TPU v7x, 32 devices: a whole 2x2x4 slice. The times are simulated.
32 devices in a mesh: group: 2 (over x), node: 16 (over z, y, core).
Axes of the slice: x: 2, y: 2, z: 4, core: 2. Of those that a mesh axis runs over, the one named last changes fastest.
Arguments:
- tokens: bfloat16 [512, 7168], P(('group', 'node')), parts along dimension 0, may hold values from -6 to 6
- expert_ids: int32 [512, 2], P(('group', 'node')), parts along dimension 0, may hold values from 0 to 3, all different within a row; in each aligned block of 16 rows (0 to 15, 16 to 31, ...) at most 12 rows name the same one
- gates: float32 [512, 2], P(('group', 'node')), parts along dimension 0, may hold values from 0.05 to 1
- placement: int32 [4], replicated, may hold values from 0 to 3, each once
- gate_weight: bfloat16 [7168, 4096], P(None, 'node'), may hold values from -0.0625 to 0.0625
- up_weight: bfloat16 [7168, 4096], P(None, 'node'), may hold values from -0.0625 to 0.0625
- down_weight: bfloat16 [4096, 7168], P('node'), may hold values from -0.1875 to 0.1875
Outputs:
- mixed: bfloat16 [512, 7168], P(('group', 'node')), parts along dimension 0
There are 2 independent parts, one for each index of `group`. A program takes and returns all parts, laid end to end along the dimension named above; an argument that names none is the same for every part. Nothing has to cross between parts.
Inputs may be any that keep to these rules, and one draw needn't show every extreme that they name: `expert_ids`: each row names 2 different experts; within the rows of one device no expert is named more than 12 times. `placement`: each block index holds one expert.
All inputs are finite; a program needn't handle non-finite values.
Results may differ from a plain program's by a relative error of at most 0.0095.
Values may be sent and summed in bfloat16 or wider, within the bound.
No kernel may reach another device: no remote copies, remote signals or barrier semaphores. Data moves between devices by JAX's collectives and lax.ppermute only.
A program may use at most 128 MiB of HBM per device.

v0:
```python
import jax
import jax.numpy as jnp
from jax import lax
from jax.sharding import PartitionSpec as P


def local(tokens, expert_ids, gates, placement, gate_weight, up_weight, down_weight):
    tok_rows, width = tokens.shape
    n_experts = placement.shape[0]
    capacity = 3 * tok_rows // 4
    picks = (
        expert_ids[:, :, None] == jnp.arange(n_experts, dtype=jnp.int32)[None, None, :]
    ).astype(jnp.int32)
    routed = jnp.sum(picks, axis=1)
    earlier = jnp.cumsum(routed, axis=0) - routed
    slot_index = jnp.sum(picks * earlier[:, None, :], axis=2)
    block_of = jnp.sum(picks * placement[None, None, :], axis=2)
    target = block_of * capacity + slot_index
    positions = jnp.arange(n_experts * capacity, dtype=jnp.int32)
    chooser = jnp.sum((target[:, :, None] == positions[None, None, :]).astype(jnp.bfloat16), axis=1)
    buckets = jnp.dot(chooser.T, tokens, preferred_element_type=jnp.float32).astype(jnp.bfloat16)
    buckets = buckets.reshape(n_experts, capacity, width)
    outgoing = jnp.repeat(buckets, 4, axis=0)
    received = lax.all_to_all(outgoing, "node", split_axis=0, concat_axis=0, tiled=True)
    n_src, count, _ = received.shape
    rows = received.reshape(n_src * count, width)
    gate_rows = jnp.dot(rows, gate_weight, preferred_element_type=jnp.float32)
    up_rows = jnp.dot(rows, up_weight, preferred_element_type=jnp.float32)
    hidden = (jax.nn.silu(gate_rows) * up_rows).astype(jnp.bfloat16)
    result = jnp.dot(hidden, down_weight, preferred_element_type=jnp.float32)
    partial_value = result.reshape(n_src, count, width)
    piece = partial_value.astype(jnp.bfloat16)
    back = lax.all_to_all(piece, "node", split_axis=0, concat_axis=0, tiled=True)
    summed = jnp.sum(back.reshape(n_experts, 4, capacity, width).astype(jnp.float32), axis=1)
    results = summed.astype(jnp.bfloat16)
    flat_results = results.reshape(n_experts * capacity, width)
    chosen = flat_results[target]
    mixed = jnp.sum(chosen.astype(jnp.float32) * gates[:, :, None], axis=1)
    return mixed.astype(jnp.bfloat16)


def solution(mesh):
    placed = (
        P(("group", "node"), None),
        P(("group", "node"), None),
        P(("group", "node"), None),
        P(),
        P(None, "node"),
        P(None, "node"),
        P("node", None),
    )
    return jax.shard_map(
        local, mesh=mesh, in_specs=placed, out_specs=P(("group", "node"), None), check_vma=False
    )
```

profile of v0, /device:TPU:13, one launch (start us, length us, event | category | flops | bytes accessed | tf_op | source)
XLA Modules:
  0.0 201.3 jit_solution(4239741670036241775)
XLA Ops:
  0.0 0.0 copy-start
  0.0 0.7 convert_reduce_fusion
  0.7 0.1 copy.16
  0.9 0.1 copy.18
  1.0 0.8 select_reduce_fusion.1
  1.7 0.1 fusion.8
  1.8 0.0 copy-done
  1.8 0.4 convolution_convert_fusion.1
  2.2 0.2 reshape.59
  2.4 0.4 broadcast_in_dim.2
  2.8 87.5 %all_to_all.10 = bf16[16,12,7168]{2,1,0:T(8,128)(2,1)} all-to-all(bf16[16,12,7168]{2,1,0:T(8,128)(2,1)S(1)} %bitcast.14), channel_id=1, replica_groups=mesh['group'=2,'node'=16] {'node'}, dimensions={0} | all-to-all | bytes 5505024 | tf_op jit(solution)/shard_map/all_to_all | solution.py:24
  90.3 3.0 %reshape.61 = bf16[192,7168]{1,0:T(8,128)(2,1)S(1)} reshape(bf16[16,12,7168]{2,1,0:T(8,128)(2,1)} %all_to_all.10) | data formatting | bytes 5505024 | tf_op jit(solution)/shard_map/reshape | solution.py:26
  93.3 2.9 %fusion.10 = f32[192,256]{1,0:T(8,128)S(1)} fusion(bf16[192,7168]{1,0:T(8,128)(2,1)S(1)} %reshape.61, bf16[7168,256]{1,0:T(8,128)(2,1)} %param.11), kind=kOutput, calls=%fused_computation.24 | convolution fusion | flops 704643072 | bytes 6619136 | tf_op jit(solution)/shard_map/dot_general | solution.py:27
  96.2 7.8 %convolution_convert_fusion = bf16[192,7168]{1,0:T(8,128)(2,1)} fusion(bf16[256,7168]{1,0:T(8,128)(2,1)} %param.13, bf16[192,7168]{1,0:T(8,128)(2,1)S(1)} %reshape.61, bf16[7168,256]{1,0:T(8,128)(2,1)} %param.12, f32[192,256]{1,0:T(8,128)S(1)} %fusion.10), kind=kOutput, calls=%fused_computation.1 | convolution fusion | flops 1410957312 | bytes 13041664 | tf_op jit(solution)/shard_map/dot_general | solution.py:30
  104.0 4.4 %convert_element_type.33 = bf16[16,12,7168]{2,1,0:T(8,128)(2,1)} reshape(bf16[192,7168]{1,0:T(8,128)(2,1)} %convolution_convert_fusion) | data formatting | bytes 5505024 | tf_op jit(solution)/shard_map/convert_element_type | solution.py:32
  108.5 0.0 copy-start.1
  108.5 5.4 %all-to-all-start.1 = ((bf16[16,12,7168]{2,1,0:T(8,128)(2,1)}), bf16[16,12,7168]{2,1,0:T(8,128)(2,1)}, u32[]{:S(2)}, u32[]{:S(2)}) async-start(bf16[16,12,7168]{2,1,0:T(8,128)(2,1)} %convert_element_type.33), calls=%async_computation.1 | async-start | bytes 7340032 | tf_op jit(solution)/shard_map/all_to_all | solution.py:33
  113.8 0.1 copy.19
  113.9 0.1 reshape.66
  114.0 0.0 copy-done.1
  114.0 0.1 copy.20
  114.1 81.0 %all-to-all-done.1 = bf16[16,12,7168]{2,1,0:T(8,128)(2,1)} async-done(((bf16[16,12,7168]{2,1,0:T(8,128)(2,1)}), bf16[16,12,7168]{2,1,0:T(8,128)(2,1)}, u32[]{:S(2)}, u32[]{:S(2)}) %all-to-all-start.1) | async-done | bytes 2752544 | tf_op jit(solution)/shard_map/all_to_all | solution.py:33
  195.1 2.7 %bitcast_reduce_fusion = bf16[4,12,7168]{2,1,0:T(8,128)(2,1)S(1)} fusion(bf16[16,12,7168]{2,1,0:T(8,128)(2,1)} %all-to-all-done.1), kind=kLoop, calls=%fused_computation.3 | loop fusion | flops 1032192 | bytes 3440640 | tf_op jit(solution)/shard_map/reduce_sum | solution.py:34
  197.7 0.2 reshape.63
  197.9 0.8 gather_fusion
  198.8 0.6 reshape.73
  199.3 1.9 multiply_reduce_fusion
  (4 shorter events, 0.1 us)
Async XLA Ops:
  0.0 1.8 copy-start
  108.5 5.5 %copy-start.1 = (f32[16,2]{0,1:T(2,128)S(1)}, f32[16,2]{0,1:T(2,128)}, u32[]{:S(2)}) copy-start(f32[16,2]{0,1:T(2,128)} %param.9) | copy-start | bytes 388
  108.5 86.6 %all-to-all-start.1 = ((bf16[16,12,7168]{2,1,0:T(8,128)(2,1)}), bf16[16,12,7168]{2,1,0:T(8,128)(2,1)}, u32[]{:S(2)}, u32[]{:S(2)}) async-start(bf16[16,12,7168]{2,1,0:T(8,128)(2,1)} %convert_element_type.33), calls=%async_computation.1 | async-start | bytes 7340032 | tf_op jit(solution)/shard_map/all_to_all | solution.py:33
where the time goes:
time: 202 us; the launch traced here: 201 us
  blocking collectives  87.5 us (43%)
  waiting for transfers between devices  81 us (40%)
  matrix products  11 us (5%)
  local copies, waits for them, and re-layouts  10.1 us (5%)
  other arithmetic  6.25 us (3%)
  starting transfers between devices  5.37 us (3%)
    all_to_all x1, blocking collectives, local(): lax.all_to_all(outgoing, 'node', split_axis=0, concat_axis=0, tiled=True)  87.5 us
    all_to_all x1, waiting for transfers between devices, local(): lax.all_to_all(piece, 'node', split_axis=0, concat_axis=0, tiled=True)  81 us
    dot_general x1, matrix products, local(): result = jnp.dot(hidden, down_weight, preferred_element_type=jnp.float32)  7.77 us
    all_to_all x1, starting transfers between devices, local(): lax.all_to_all(piece, 'node', split_axis=0, concat_axis=0, tiled=True)  5.37 us
    convert_element_type x1, local copies, waits for them, and re-layouts, local(): piece = partial_value.astype(jnp.bfloat16)  4.45 us
  transfers between devices with their start and end apart: 1, of which 1 were waited for; matrix products, arithmetic and copies ran while one was open for 0% of the time, Pallas kernels for 0%

commit v1 on v0

v1 whole, which is shorter than its diff:
```python
import jax
import jax.numpy as jnp
from jax import lax
from jax.sharding import PartitionSpec as P

LANES = 128


def block_weights(expert_ids, gates, placement):
    n_blocks = placement.shape[0]
    experts = jnp.arange(n_blocks, dtype=jnp.int32)
    picks = (expert_ids[:, :, None] == experts[None, None, :]).astype(jnp.int32)
    block_of = jnp.sum(picks * placement[None, None, :], axis=2)
    chosen = block_of[:, :, None] == experts[None, None, :]
    return jnp.sum(jnp.where(chosen, gates[:, :, None], 0.0), axis=1)


def split_three(values):
    high = lax.reduce_precision(values, 8, 7)
    rest = values - high
    middle = lax.reduce_precision(rest, 8, 7)
    return high, middle, rest - middle


def local(tokens, expert_ids, gates, placement, gate_weight, up_weight, down_weight):
    tok_rows, width = tokens.shape
    n_blocks = placement.shape[0]
    parts = lax.axis_size("node") // n_blocks
    block = lax.axis_index("node") // parts
    weights = jnp.concatenate(split_three(block_weights(expert_ids, gates, placement)), axis=1)
    weights = jnp.pad(weights, ((0, 0), (0, LANES - 3 * n_blocks))).astype(jnp.bfloat16)
    outgoing = jnp.concatenate([tokens, weights], axis=1)
    gathered = lax.all_gather(outgoing, "node", axis=0, tiled=True)
    rows = gathered[:, :width]
    tail = gathered[:, width:].astype(jnp.float32)
    lane = jnp.arange(LANES, dtype=jnp.int32)
    mine = (lane % n_blocks == block) & (lane < 3 * n_blocks)
    scale = jnp.sum(jnp.where(mine[None, :], tail, 0.0), axis=1, keepdims=True)
    gate_rows = jnp.dot(rows, gate_weight, preferred_element_type=jnp.float32)
    up_rows = jnp.dot(rows, up_weight, preferred_element_type=jnp.float32)
    hidden = (jax.nn.silu(gate_rows) * up_rows * scale).astype(jnp.bfloat16)
    piece = jnp.dot(hidden, down_weight, preferred_element_type=jnp.float32).astype(jnp.bfloat16)
    return lax.psum_scatter(piece, "node", scatter_dimension=0, tiled=True)


def solution(mesh):
    placed = (
        P(("group", "node"), None),
        P(("group", "node"), None),
        P(("group", "node"), None),
        P(),
        P(None, "node"),
        P(None, "node"),
        P("node", None),
    )
    return jax.shard_map(
        local, mesh=mesh, in_specs=placed, out_specs=P(("group", "node"), None), check_vma=False
    )
```

time: 202 us -> 151 us (0.75)
  the two profiles are of different devices: /device:TPU:13 before, /device:TPU:0 now
where the time goes in v1:
time: 151 us; the launch traced here: 150 us
  waiting for transfers between devices  118 us (78%)
  matrix products  14.3 us (9%)
  between operations  13.4 us (9%)
  other arithmetic  4.09 us (3%)
    reduce_scatter x1, waiting for transfers between devices, local(): return lax.psum_scatter(piece, 'node', scatter_dimension=0, tiled=True)  67.8 us
    all_gather x1, waiting for transfers between devices, local(): gathered = lax.all_gather(outgoing, 'node', axis=0, tiled=True)  50.6 us
    dot_general x1, matrix products, local(): jnp.dot(hidden, down_weight, preferred_element_type=jnp.float32)  10 us
    dot_general x1, matrix products, local(): gate_rows = jnp.dot(rows, gate_weight, preferred_element_type=jnp.float32)  4.27 us
  transfers between devices with their start and end apart: 2, of which 2 were waited for; matrix products, arithmetic and copies ran while one was open for 0% of the time, Pallas kernels for 0%

profile of v1, /device:TPU:0, one launch (start us, length us, event | category | flops | bytes accessed | tf_op | source)
XLA Modules:
  0.0 150.5 jit_solution(12155417637047400757)
XLA Ops:
  6.5 0.0 all-gather.2.cloned.1.call-start
  6.5 0.8 select_reduce_fusion.2
  7.3 0.7 select_reduce_fusion.1
  8.0 0.1 copy.11
  8.1 1.6 %fusion.21 = bf16[16,7296]{1,0:T(8,128)(2,1)} fusion(bf16[16,12]{1,0:T(8,128)(2,1)S(1)} %copy.11, bf16[16,7168]{1,0:T(8,128)(2,1)} %param.7), kind=kLoop, calls=%fused_computation.15 | loop fusion | flops 700416 | bytes 463232 | tf_op jit(solution)/shard_map/concatenate | solution.py:32
  9.8 0.0 all-gather.2.cloned.1.call-update
  9.8 0.0 reduce-scatter.2.cloned.1.call-start
  9.9 50.6 %all-gather.2.cloned.1.call-done = bf16[256,7296]{1,0:T(8,128)(2,1)} async-done(((bf16[16,7296]{1,0:T(8,128)(2,1)}), bf16[256,7296]{1,0:T(8,128)(2,1)}) %all-gather.2.cloned.1.call-update) | async-done | bytes 3735568 | tf_op jit(solution)/shard_map/all_gather | solution.py:33
  60.5 0.9 select_reduce_fusion
  61.4 4.3 %fusion.2 = f32[256,256]{1,0:T(8,128)S(1)} fusion(bf16[7168,256]{1,0:T(8,128)(2,1)} %param.11, bf16[256,7296]{1,0:T(8,128)(2,1)} %all-gather.2.cloned.1.call-done), kind=kOutput, calls=%fused_computation.3 | convolution fusion | flops 939524096 | bytes 7602176 | tf_op jit(solution)/shard_map/dot_general | solution.py:39
  65.7 10.0 %convolution_convert_fusion = bf16[256,7168]{1,0:T(8,128)(2,1)} fusion(bf16[256,7168]{1,0:T(8,128)(2,1)} %param.13, bf16[7168,256]{1,0:T(8,128)(2,1)} %param.12, bf16[256,7296]{1,0:T(8,128)(2,1)} %all-gather.2.cloned.1.call-done, f32[256,256]{1,0:T(8,128)S(1)} %fusion.2, f32[256]{0:T(256)S(1)} %select_reduce_fusion), kind=kOutput, calls=%fused_computation | convolution fusion | flops 1881341952 | bytes 14943232 | tf_op jit(solution)/shard_map/dot_general | solution.py:42
  75.8 0.0 reduce-scatter.2.cloned.1.call-update
  75.8 67.8 %reduce-scatter.2.cloned.1.call-done = bf16[16,7168]{1,0:T(8,128)(2,1)} async-done(((bf16[256,7168]{1,0:T(8,128)(2,1)}), bf16[16,7168]{1,0:T(8,128)(2,1)}) %reduce-scatter.2.cloned.1.call-update) | async-done | bytes 229392 | tf_op jit(solution)/shard_map/reduce_scatter | solution.py:43
  (3 shorter events, 0.0 us)
Async XLA Ops:
  6.5 54.0 %all-gather.2.cloned.1.call-start = ((), (), s32[]{:S(2)}) async-start(), calls=%async_computation.1 | async-start | bytes 3969024 | tf_op jit(solution)/shard_map/all_gather | solution.py:33
  9.8 133.8 %reduce-scatter.2.cloned.1.call-start = ((), (), s32[]{:S(2)}) async-start(), calls=%async_computation.2 | async-start | bytes 3899392 | tf_op jit(solution)/shard_map/reduce_scatter | solution.py:43
Sparse Core Ops, SparseCore 0:
  9.9 50.5 all-gather.1
  75.9 67.6 reduce-scatter.1

commit v2 on v1

v2 whole, which is shorter than its diff:
```python
import functools

import jax
import jax.numpy as jnp
from jax import lax
from jax.experimental import pallas as pl
from jax.experimental.pallas import tpu as pltpu
from jax.sharding import PartitionSpec as P

CHUNKS = 4
VMEM_BYTES = 56 * 2**20


def slots_of(expert_ids, n_blocks):
    rows, top = expert_ids.shape
    experts = lax.broadcasted_iota(jnp.int32, (rows, n_blocks), 1)
    picks = jnp.zeros((rows, n_blocks), jnp.float32)
    for k in range(top):
        picks = picks + jnp.where(expert_ids[:, k : k + 1] == experts, 1.0, 0.0)
    before = lax.broadcasted_iota(jnp.int32, (rows, rows), 1) < lax.broadcasted_iota(
        jnp.int32, (rows, rows), 0
    )
    earlier = jnp.dot(
        jnp.where(before, 1.0, 0.0).astype(jnp.bfloat16),
        picks.astype(jnp.bfloat16),
        preferred_element_type=jnp.float32,
    )
    return experts, picks, earlier


def expert_at(placement_ref, block):
    found = jnp.int32(0)
    for e in range(placement_ref.shape[0]):
        found = jnp.where(placement_ref[e] == block, jnp.int32(e), found)
    return found


def column_of(values, experts, expert):
    return jnp.sum(jnp.where(experts == expert, values, 0.0), axis=1, keepdims=True)


def bucket_row(rows, lanes):
    lane = lax.broadcasted_iota(jnp.int32, (rows, lanes), 1)
    half, quarter = rows // 2, rows // 4
    return jnp.where(lane < half, lane, half + lane % quarter).astype(jnp.float32)


def pack_kernel(n_blocks, parts, placement_ref, ids_ref, tokens_ref, *out_refs):
    rows, width = tokens_ref.shape
    half, quarter = rows // 2, rows // 4
    block = lax.axis_index("node") // parts
    experts, picks, earlier = slots_of(ids_ref[...], n_blocks)
    wanted = bucket_row(rows, rows)
    upper = lax.broadcasted_iota(jnp.int32, (half, width // 2), 0) < quarter
    for k, out_ref in enumerate(out_refs):
        expert = expert_at(placement_ref, lax.rem(block + k, n_blocks))
        named = column_of(picks, experts, expert) > 0.5
        slot = column_of(earlier, experts, expert)
        chooser = jnp.where(named & (slot == wanted), 1.0, 0.0).astype(jnp.bfloat16)
        packed = lax.dot_general(
            chooser, tokens_ref[...], (((0,), (0,)), ((), ())), preferred_element_type=jnp.float32
        )
        out_ref[:, :width] = packed[:half].astype(jnp.bfloat16)
        rest = jnp.where(upper, packed[half:, : width // 2], packed[half:, width // 2 :])
        out_ref[:, width:] = rest.astype(jnp.bfloat16)


def pack(placement, expert_ids, tokens, n_blocks, parts):
    rows, width = tokens.shape
    vmem = pl.BlockSpec(memory_space=pltpu.VMEM)
    shape = jax.ShapeDtypeStruct((rows // 2, width + width // 2), jnp.bfloat16)
    return pl.pallas_call(
        functools.partial(pack_kernel, n_blocks, parts),
        out_shape=[shape] * n_blocks,
        in_specs=[pl.BlockSpec(memory_space=pltpu.SMEM), vmem, vmem],
        out_specs=[vmem] * n_blocks,
        compiler_params=pltpu.CompilerParams(vmem_limit_bytes=VMEM_BYTES),
        cost_estimate=pl.CostEstimate(
            flops=2 * n_blocks * rows * rows * width,
            bytes_accessed=2 * (n_blocks + 1) * rows * width,
            transcendentals=0,
        ),
    )(placement, expert_ids, tokens)


def experts_kernel(count, *refs):
    pieces, (gate_hbm, up_hbm, down_hbm) = refs[:count], refs[count : count + 3]
    outs = refs[count + 3 : 2 * count + 3]
    gate_ref, up_ref, down_ref, sems = refs[2 * count + 3 :]
    width, hid = gate_hbm.shape
    height = pieces[0].shape[0]
    step = width // CHUNKS
    copies = []
    for j in range(CHUNKS):
        part = pl.ds(j * step, step)
        copies.append(
            (
                pltpu.make_async_copy(gate_hbm.at[part], gate_ref.at[part], sems.at[0, j]),
                pltpu.make_async_copy(up_hbm.at[part], up_ref.at[part], sems.at[1, j]),
            )
        )
    for pair in copies:
        for copy in pair:
            copy.start()
    down_copies = []
    for j in range(CHUNKS):
        part = pl.ds(j * step, step)
        down_copies.append(
            pltpu.make_async_copy(down_hbm.at[:, part], down_ref.at[:, part], sems.at[2, j])
        )
    order = [j for i in range(CHUNKS // 2) for j in (i, i + CHUNKS // 2)]
    for j in order:
        down_copies[j].start()

    total = count * height
    sums = {}
    for j in range(CHUNKS):
        start = j * step
        rest_start = width + (j % (CHUNKS // 2)) * step
        whole = [p[:, start : start + step] for p in pieces]
        rest = [p[:, rest_start : rest_start + step] for p in pieces]
        rows = jnp.concatenate(whole + rest, axis=0)
        side = j // (CHUNKS // 2)
        for name, ref, copy in (("g", gate_ref, copies[j][0]), ("u", up_ref, copies[j][1])):
            copy.wait()
            part = jnp.dot(
                rows, ref[start : start + step, :], preferred_element_type=jnp.float32
            )
            for key, value in (((name, 2), part[:total]), ((name, side), part[total:])):
                sums[key] = sums[key] + value if key in sums else value

    upper = lax.broadcasted_iota(jnp.int32, (total, hid), 0) % height < height // 2

    def whole_rows(name):
        left, right = sums[(name, 0)], sums[(name, 1)]
        shift = height // 2
        rest = jnp.where(
            upper,
            left + pltpu.roll(right, total - shift, axis=0),
            right + pltpu.roll(left, shift, axis=0),
        )
        return jnp.concatenate([sums[(name, 2)], rest], axis=0)

    gate_rows, up_rows = whole_rows("g"), whole_rows("u")
    hidden = (jax.nn.silu(gate_rows) * up_rows).astype(jnp.bfloat16)
    upper_out = lax.broadcasted_iota(jnp.int32, (total, step), 0) % height < height // 2
    for i in range(CHUNKS // 2):
        both = []
        for j in (i, i + CHUNKS // 2):
            down_copies[j].wait()
            part = jnp.dot(
                hidden, down_ref[:, j * step : (j + 1) * step], preferred_element_type=jnp.float32
            )
            for p, out in enumerate(outs):
                out[:, j * step : (j + 1) * step] = part[p * height : (p + 1) * height].astype(
                    jnp.bfloat16
                )
            both.append(part[total:])
        rest = jnp.where(upper_out, both[0], both[1]).astype(jnp.bfloat16)
        for p, out in enumerate(outs):
            out[:, width + i * step : width + (i + 1) * step] = rest[p * height : (p + 1) * height]


def run_experts(pieces, gate_weight, up_weight, down_weight):
    count = len(pieces)
    width, hid = gate_weight.shape
    height = pieces[0].shape[0]
    vmem = pl.BlockSpec(memory_space=pltpu.VMEM)
    hbm = pl.BlockSpec(memory_space=pl.ANY)
    return pl.pallas_call(
        functools.partial(experts_kernel, count),
        out_shape=[jax.ShapeDtypeStruct(pieces[0].shape, jnp.bfloat16)] * count,
        in_specs=[vmem] * count + [hbm] * 3,
        out_specs=[vmem] * count,
        scratch_shapes=[
            pltpu.VMEM((width, hid), jnp.bfloat16),
            pltpu.VMEM((width, hid), jnp.bfloat16),
            pltpu.VMEM((hid, width), jnp.bfloat16),
            pltpu.SemaphoreType.DMA((3, CHUNKS)),
        ],
        compiler_params=pltpu.CompilerParams(vmem_limit_bytes=VMEM_BYTES),
        cost_estimate=pl.CostEstimate(
            flops=12 * count * height * width * hid,
            bytes_accessed=6 * width * hid + 6 * count * height * width,
            transcendentals=2 * count * height * hid,
        ),
    )(*pieces, gate_weight, up_weight, down_weight)


def mix_kernel(n_blocks, parts, placement_ref, ids_ref, gates_ref, *refs):
    results, out_ref = refs[:-1], refs[-1]
    rows, width = out_ref.shape
    half, quarter = rows // 2, rows // 4
    block = lax.axis_index("node") // parts
    ids, gates = ids_ref[...], gates_ref[...]
    experts, picks, earlier = slots_of(ids, n_blocks)
    lane = lax.broadcasted_iota(jnp.int32, (rows, rows), 1)
    wanted = bucket_row(rows, rows)
    terms = []
    for k in range(n_blocks):
        expert = expert_at(placement_ref, lax.rem(block + k, n_blocks))
        named = column_of(picks, experts, expert) > 0.5
        slot = column_of(earlier, experts, expert)
        weight = jnp.sum(jnp.where(ids == expert, gates, 0.0), axis=1, keepdims=True)
        terms.append(jnp.where(named & (slot == wanted), weight, 0.0))

    def product(lhs, rhs):
        high = lhs.astype(jnp.bfloat16)
        left = lhs - high.astype(jnp.float32)
        middle = left.astype(jnp.bfloat16)
        low = (left - middle.astype(jnp.float32)).astype(jnp.bfloat16)
        both = jnp.dot(
            jnp.concatenate([high, middle, low], axis=0), rhs, preferred_element_type=jnp.float32
        )
        return both[:rows] + both[rows : 2 * rows] + both[2 * rows :]

    for side in range(2):
        begin = side * (width // 2)
        total = None
        for term, result in zip(terms, results):
            mine = (lane < half) | ((lane >= half + side * quarter) & (lane < half + (side + 1) * quarter))
            rhs = jnp.concatenate(
                [result[:, begin : begin + width // 2], result[:, width:]], axis=0
            )
            value = product(jnp.where(mine, term, 0.0), rhs)
            total = value if total is None else total + value
        out_ref[:, begin : begin + width // 2] = total.astype(jnp.bfloat16)


def mix(placement, expert_ids, gates, results, n_blocks, parts):
    rows = expert_ids.shape[0]
    width = results[0].shape[1] // 3 * 2
    vmem = pl.BlockSpec(memory_space=pltpu.VMEM)
    return pl.pallas_call(
        functools.partial(mix_kernel, n_blocks, parts),
        out_shape=jax.ShapeDtypeStruct((rows, width), jnp.bfloat16),
        in_specs=[pl.BlockSpec(memory_space=pltpu.SMEM)] + [vmem] * (2 + n_blocks),
        out_specs=vmem,
        compiler_params=pltpu.CompilerParams(vmem_limit_bytes=VMEM_BYTES),
        cost_estimate=pl.CostEstimate(
            flops=6 * n_blocks * rows * rows * width,
            bytes_accessed=2 * (n_blocks + 1) * rows * width,
            transcendentals=0,
        ),
    )(placement, expert_ids, gates, *results)


def add(*values):
    return sum(v.astype(jnp.float32) for v in values).astype(jnp.bfloat16)


def local(tokens, expert_ids, gates, placement, gate_weight, up_weight, down_weight):
    n_blocks = placement.shape[0]
    devices = lax.axis_size("node")
    parts = devices // n_blocks

    def along_z(value, k):
        pairs = [(i, (i + k * parts) % devices) for i in range(devices)]
        return lax.ppermute(value, "node", pairs)

    def along_y(value):
        return lax.ppermute(value, "node", [(i, i ^ 2) for i in range(devices)])

    def along_core(value):
        return lax.ppermute(value, "node", [(i, i ^ 1) for i in range(devices)])

    buckets = pack(placement, expert_ids, tokens, n_blocks, parts)
    straight = [buckets[0]] + [along_z(buckets[k], k) for k in range(1, n_blocks)]
    across = [along_y(piece) for piece in straight]
    mine = [piece for pair in zip(straight, across) for piece in pair]
    theirs = [along_core(piece) for piece in mine]
    outs = run_experts(mine + theirs, gate_weight, up_weight, down_weight)
    kept = outs[: len(mine)]
    returned = [along_core(piece) for piece in outs[len(mine) :]]
    results = []
    for k in range(n_blocks):
        back = along_y(add(kept[2 * k + 1], returned[2 * k + 1]))
        home = add(kept[2 * k], returned[2 * k], back)
        results.append(along_z(home, -k) if k else home)
    return mix(placement, expert_ids, gates, results, n_blocks, parts)


def solution(mesh):
    placed = (
        P(("group", "node"), None),
        P(("group", "node"), None),
        P(("group", "node"), None),
        P(),
        P(None, "node"),
        P(None, "node"),
        P("node", None),
    )
    return jax.shard_map(
        local, mesh=mesh, in_specs=placed, out_specs=P(("group", "node"), None), check_vma=False
    )
```

time: 151 us -> 82.5 us (0.55)
  waiting for transfers between devices: 118 us -> 26.3 us
  starting transfers between devices: 0.04 us -> 26.9 us
  Pallas kernels: 0 us -> 16.8 us
  matrix products: 14.3 us -> 0 us
  between operations: 13.4 us -> 0.24 us
  local copies, waits for them, and re-layouts: 0.1 us -> 3.7 us
  other arithmetic: 4.09 us -> 7.54 us
    reduce_scatter x1 -> x0, waiting for transfers between devices: 67.8 us -> none  [local(): return lax.psum_scatter(piece, 'node', scatter_dimension=0, tiled=True)]
    all_gather x1 -> x0, waiting for transfers between devices: 50.6 us -> none  [local(): gathered = lax.all_gather(outgoing, 'node', axis=0, tiled=True)]
    ppermute x0 -> x30, starting transfers between devices: none -> 26.9 us  [the longest x6 14 us: along_z(): return lax.ppermute(value, 'node', pairs)]
    ppermute x0 -> x30, waiting for transfers between devices: none -> 26.3 us  [the longest x6 13 us: along_z(): return lax.ppermute(value, 'node', pairs)]
    pallas_call x0 -> x3, Pallas kernels: none -> 16.8 us  [the longest x1 11.2 us: run_experts(): pl.pallas_call(functools.partial(experts_kernel, count), out_shape=[jax.S...]
    dot_general x2 -> x0, matrix products: 14.3 us -> none  [the longest x1 10 us: local(): jnp.dot(hidden, down_weight, preferred_element_type=jnp.float32)]
    convert_element_type x0 -> x8, other arithmetic: none -> 7.54 us  [add(): return sum((v.astype(jnp.float32) for v in values)).astype(jnp.bfloat16)]
    unnamed x1 -> x42, local copies, waits for them, and re-layouts: 0.1 us -> 3.7 us
  transfers between devices with their start and end apart: 2 -> 30, of which waited for: 2 -> 11; matrix products, arithmetic and copies ran while one was open for 0% -> 10% of each run, Pallas kernels for 0% -> 0%
where the time goes in v2:
time: 82.5 us; the launch traced here: 81.5 us
  starting transfers between devices  26.9 us (33%)
  waiting for transfers between devices  26.3 us (32%)
  Pallas kernels  16.8 us (20%)
  other arithmetic  7.54 us (9%)
  local copies, waits for them, and re-layouts  3.7 us (4%)
    ppermute x6, starting transfers between devices, along_z(): return lax.ppermute(value, 'node', pairs)  14 us
    ppermute x6, waiting for transfers between devices, along_z(): return lax.ppermute(value, 'node', pairs)  13 us
    ppermute x8, waiting for transfers between devices, along_y(): return lax.ppermute(value, 'node', [(i, i ^ 2) for i in range(devices)])  12 us
    pallas_call x1, Pallas kernels, run_experts(): pl.pallas_call(functools.partial(experts_kernel, count), out_shape=[jax.S...  11.2 us
    ppermute x8, starting transfers between devices, along_y(): return lax.ppermute(value, 'node', [(i, i ^ 2) for i in range(devices)])  9.57 us
    convert_element_type x8, other arithmetic, add(): return sum((v.astype(jnp.float32) for v in values)).astype(jnp.bfloat16)  7.54 us
    unnamed x42, local copies, waits for them, and re-layouts  3.7 us
    ppermute x16, starting transfers between devices, along_core(): return lax.ppermute(value, 'node', [(i, i ^ 1) for i in range(devices)])  3.41 us
  transfers between devices with their start and end apart: 30, of which 11 were waited for; matrix products, arithmetic and copies ran while one was open for 10% of the time, Pallas kernels for 0%

profile of v2, /device:TPU:0, one launch (start us, length us, event | category | flops | bytes accessed | tf_op | source)
XLA Modules:
  0.0 81.5 jit_solution(15903709447762320211)
XLA Ops:
  0.0 1.3 %copy.9.ids_ref = s32[16,2]{1,0:T(8,128)} copy(s32[16,2]{0,1:T(2,128)} %param.8) | data formatting | bytes 256 | tf_op args[1]
  1.3 2.3 %shard_map.73 = (bf16[8,10752]{1,0:T(8,128)(2,1)}, bf16[8,10752]{1,0:T(8,128)(2,1)}, bf16[8,10752]{1,0:T(8,128)(2,1)}, bf16[8,10752]{1,0:T(8,128)(2,1)}) custom-call(s32[4]{0:T(128)} %placement_ref.3, s32[16,2]{1,0:T(8,128)} %copy.9.ids_ref, bf16[16,7168]{1,0:T(8,128)(2,1)} %tokens_ref.1), custom_call_target="tpu_custom_call" | custom-call | flops 14680064 | bytes 1146880 | tf_op jit(solution)/shard_map/pallas_call | solution.py:72
  3.7 3.0 %collective-permute-start.1 = (bf16[8,10752]{1,0:T(8,128)(2,1)}, bf16[8,10752]{1,0:T(8,128)(2,1)S(1)}, u32[]{:S(2)}, u32[]{:S(2)}) collective-permute-start(bf16[8,10752]{1,0:T(8,128)(2,1)} %get-tuple-element.26), channel_id=1, source_target_pairs={{0,4},{1,5},{2,6},{3,7},{4,8},{5,9},{6,10},{7,11},{8,12},{9,13},{1... | collective-permute-start | bytes 516104 | tf_op jit(solution)/shard_map/ppermute | solution.py:259
  6.7 2.6 %collective-permute-start.3 = (bf16[8,10752]{1,0:T(8,128)(2,1)}, bf16[8,10752]{1,0:T(8,128)(2,1)S(1)}, u32[]{:S(2)}, u32[]{:S(2)}) collective-permute-start(bf16[8,10752]{1,0:T(8,128)(2,1)} %get-tuple-element.27), channel_id=1, source_target_pairs={{0,8},{1,9},{2,10},{3,11},{4,12},{5,13},{6,14},{7,15},{8,0},{9,1},... | collective-permute-start | bytes 516104 | tf_op jit(solution)/shard_map/ppermute | solution.py:259
  9.3 1.3 %collective-permute-start.5 = (bf16[8,10752]{1,0:T(8,128)(2,1)}, bf16[8,10752]{1,0:T(8,128)(2,1)S(1)}, u32[]{:S(2)}, u32[]{:S(2)}) collective-permute-start(bf16[8,10752]{1,0:T(8,128)(2,1)} %get-tuple-element.28), channel_id=1, source_target_pairs={{0,12},{1,13},{2,14},{3,15},{4,0},{5,1},{6,2},{7,3},{8,4},{9,5},{1... | collective-permute-start | bytes 516104 | tf_op jit(solution)/shard_map/ppermute | solution.py:259
  10.6 1.5 %collective-permute-start = (bf16[8,10752]{1,0:T(8,128)(2,1)}, bf16[8,10752]{1,0:T(8,128)(2,1)S(1)}, u32[]{:S(2)}, u32[]{:S(2)}) collective-permute-start(bf16[8,10752]{1,0:T(8,128)(2,1)} %get-tuple-element.25.refs_0_), channel_id=1, source_target_pairs={{0,2},{1,3},{2,0},{3,1},{4,6},{5,7},{6,4},{7,5},{8,10},{9,11},{10,... | collective-permute-start | bytes 516104 | tf_op jit(solution)/shard_map/ppermute | solution.py:262
  12.2 0.0 collective-permute-start.7
  12.2 2.1 %collective-permute-done.1.refs_2_ = bf16[8,10752]{1,0:T(8,128)(2,1)S(1)} collective-permute-done((bf16[8,10752]{1,0:T(8,128)(2,1)}, bf16[8,10752]{1,0:T(8,128)(2,1)S(1)}, u32[]{:S(2)}, u32[]{:S(2)}) %collective-permute-start.1) | collective-permute-done | bytes 172064 | tf_op jit(solution)/shard_map/ppermute | solution.py:259
  14.2 1.8 %collective-permute-start.2 = (bf16[8,10752]{1,0:T(8,128)(2,1)S(1)}, bf16[8,10752]{1,0:T(8,128)(2,1)S(1)}, u32[]{:S(2)}, u32[]{:S(2)}) collective-permute-start(bf16[8,10752]{1,0:T(8,128)(2,1)S(1)} %collective-permute-done.1.refs_2_), channel_id=1, source_target_pairs={{0,2},{1,3},{2,0},{3,1},{4,6},{5,7},{6,4},{7,5},{8,10},{9,11},{10,... | collective-permute-start | bytes 516104 | tf_op jit(solution)/shard_map/ppermute | solution.py:262
  16.0 4.8 %collective-permute-done.3.refs_4_ = bf16[8,10752]{1,0:T(8,128)(2,1)S(1)} collective-permute-done((bf16[8,10752]{1,0:T(8,128)(2,1)}, bf16[8,10752]{1,0:T(8,128)(2,1)S(1)}, u32[]{:S(2)}, u32[]{:S(2)}) %collective-permute-start.3) | collective-permute-done | bytes 172064 | tf_op jit(solution)/shard_map/ppermute | solution.py:259
  20.8 1.5 %collective-permute-start.4 = (bf16[8,10752]{1,0:T(8,128)(2,1)S(1)}, bf16[8,10752]{1,0:T(8,128)(2,1)S(1)}, u32[]{:S(2)}, u32[]{:S(2)}) collective-permute-start(bf16[8,10752]{1,0:T(8,128)(2,1)S(1)} %collective-permute-done.3.refs_4_), channel_id=1, source_target_pairs={{0,2},{1,3},{2,0},{3,1},{4,6},{5,7},{6,4},{7,5},{8,10},{9,11},{10,... | collective-permute-start | bytes 516104 | tf_op jit(solution)/shard_map/ppermute | solution.py:262
  22.3 0.0 collective-permute-done.5.refs_6_
  22.3 0.5 collective-permute-start.6
  22.8 0.0 collective-permute-done.refs_1_
  22.8 0.0 collective-permute-start.8
  22.8 0.5 collective-permute-start.11
  23.3 0.1 collective-permute-start.13
  23.4 4.6 %collective-permute-done.4.refs_5_ = bf16[8,10752]{1,0:T(8,128)(2,1)S(1)} collective-permute-done((bf16[8,10752]{1,0:T(8,128)(2,1)S(1)}, bf16[8,10752]{1,0:T(8,128)(2,1)S(1)}, u32[]{:S(2)}, u32[]{:S(2)}) %collective-permute-start.4) | collective-permute-done | bytes 172064 | tf_op jit(solution)/shard_map/ppermute | solution.py:262
  28.0 0.0 collective-permute-start.9
  28.0 2.6 %collective-permute-done.6.refs_7_ = bf16[8,10752]{1,0:T(8,128)(2,1)S(1)} collective-permute-done((bf16[8,10752]{1,0:T(8,128)(2,1)S(1)}, bf16[8,10752]{1,0:T(8,128)(2,1)S(1)}, u32[]{:S(2)}, u32[]{:S(2)}) %collective-permute-start.6) | collective-permute-done | bytes 172064 | tf_op jit(solution)/shard_map/ppermute | solution.py:262
  30.7 0.0 collective-permute-done.8.refs_9_
  30.7 0.5 collective-permute-start.12
  31.2 0.1 collective-permute-start.14
  31.3 0.0 collective-permute-done.13.refs_14_
  31.3 0.0 collective-permute-done.9.refs_10_
  31.3 0.8 collective-permute-done.10.refs_11_
  32.1 0.2 collective-permute-done.12.refs_13_
  32.3 0.3 collective-permute-done.14.refs_15_
  32.7 0.1 copy-done.16
  32.8 0.2 copy-done.17
  33.0 0.7 copy-done.18
  33.6 11.2 %shard_map.74 = (bf16[8,10752]{1,0:T(8,128)(2,1)}, bf16[8,10752]{1,0:T(8,128)(2,1)}, bf16[8,10752]{1,0:T(8,128)(2,1)}, bf16[8,10752]{1,0:T(8,128)(2,1)}, bf16[8,...) custom-call(bf16[8,10752]{1,0:T(8,128)(2,1)} %get-tuple-element.25.r, ...), custom_call_target="tpu_custom_call" | custom-call | flops 2818572288 | bytes 16515072 | tf_op jit(solution)/shard_map/pallas_call | solution.py:170
  44.9 0.3 collective-permute-start.27
  45.2 0.7 copy.10.gates_ref
  45.9 0.2 collective-permute-start.26
  46.1 0.3 collective-permute-start.23
  46.4 0.2 collective-permute-start.22
  46.7 0.3 collective-permute-start.19
  46.9 0.2 collective-permute-start.18
  47.2 1.0 %add_convert_fusion.1 = bf16[8,10752]{1,0:T(8,128)(2,1)S(1)} fusion(bf16[8,10752]{1,0:T(8,128)(2,1)S(1)} %collective-permute-done.27, bf16[8,10752]{1,0:T(8,128)(2,1)} %get-tuple-element.43), kind=kLoop, calls=%fused_computation.1 | loop fusion | flops 344064 | bytes 516096 | tf_op jit(solution)/shard_map/convert_element_type | solution.py:249
  48.1 0.0 collective-permute-done.23
  48.1 0.3 collective-permute-start.16
  48.5 1.0 %add_convert_fusion.3 = bf16[8,10752]{1,0:T(8,128)(2,1)S(1)} fusion(bf16[8,10752]{1,0:T(8,128)(2,1)S(1)} %collective-permute-done.23, bf16[8,10752]{1,0:T(8,128)(2,1)} %get-tuple-element.39), kind=kLoop, calls=%fused_computation.3 | loop fusion | flops 344064 | bytes 516096 | tf_op jit(solution)/shard_map/convert_element_type | solution.py:249
  49.5 0.0 collective-permute-done.19
  49.5 0.3 collective-permute-start.15
  49.8 1.0 %add_convert_fusion.5 = bf16[8,10752]{1,0:T(8,128)(2,1)S(1)} fusion(bf16[8,10752]{1,0:T(8,128)(2,1)S(1)} %collective-permute-done.19, bf16[8,10752]{1,0:T(8,128)(2,1)} %get-tuple-element.35), kind=kLoop, calls=%fused_computation.5 | loop fusion | flops 344064 | bytes 516096 | tf_op jit(solution)/shard_map/convert_element_type | solution.py:249
  50.7 1.6 %collective-permute-start.28 = (bf16[8,10752]{1,0:T(8,128)(2,1)S(1)}, bf16[8,10752]{1,0:T(8,128)(2,1)S(1)}, u32[]{:S(2)}, u32[]{:S(2)}) collective-permute-start(bf16[8,10752]{1,0:T(8,128)(2,1)S(1)} %add_convert_fusion.1), channel_id=1, source_target_pairs={{0,2},{1,3},{2,0},{3,1},{4,6},{5,7},{6,4},{7,5},{8,10},{9,11},{10,... | collective-permute-start | bytes 516104 | tf_op jit(solution)/shard_map/ppermute | solution.py:262
  52.3 1.0 %add_convert_fusion.7 = bf16[8,10752]{1,0:T(8,128)(2,1)S(1)} fusion(bf16[8,10752]{1,0:T(8,128)(2,1)S(1)} %collective-permute-done.16, bf16[8,10752]{1,0:T(8,128)(2,1)} %get-tuple-element.31), kind=kLoop, calls=%fused_computation.7 | loop fusion | flops 344064 | bytes 516096 | tf_op jit(solution)/shard_map/convert_element_type | solution.py:249
  53.3 0.6 collective-permute-start.24
  53.9 4.1 %collective-permute-done.28 = bf16[8,10752]{1,0:T(8,128)(2,1)S(1)} collective-permute-done((bf16[8,10752]{1,0:T(8,128)(2,1)S(1)}, bf16[8,10752]{1,0:T(8,128)(2,1)S(1)}, u32[]{:S(2)}, u32[]{:S(2)}) %collective-permute-start.28) | collective-permute-done | bytes 172064 | tf_op jit(solution)/shard_map/ppermute | solution.py:262
  58.0 1.5 %collective-permute-start.20 = (bf16[8,10752]{1,0:T(8,128)(2,1)S(1)}, bf16[8,10752]{1,0:T(8,128)(2,1)S(1)}, u32[]{:S(2)}, u32[]{:S(2)}) collective-permute-start(bf16[8,10752]{1,0:T(8,128)(2,1)S(1)} %add_convert_fusion.5), channel_id=1, source_target_pairs={{0,2},{1,3},{2,0},{3,1},{4,6},{5,7},{6,4},{7,5},{8,10},{9,11},{10,... | collective-permute-start | bytes 516104 | tf_op jit(solution)/shard_map/ppermute | solution.py:262
  59.5 1.0 %add_convert_fusion = bf16[8,10752]{1,0:T(8,128)(2,1)S(1)} fusion(bf16[8,10752]{1,0:T(8,128)(2,1)S(1)} %collective-permute-done.28, bf16[8,10752]{1,0:T(8,128)(2,1)S(1)} %collective-permute-done.26, bf16[8,10752]{1,0:T(8,128)(2,1)} %get-tuple-element.41), kind=kLoop, calls=%fused_computation | loop fusion | flops 516096 | bytes 688128 | tf_op jit(solution)/shard_map/convert_element_type | solution.py:249
  60.5 0.6 collective-permute-start.17
  61.1 0.6 collective-permute-done.24
  61.7 2.9 %collective-permute-start.29 = (bf16[8,10752]{1,0:T(8,128)(2,1)S(1)}, bf16[8,10752]{1,0:T(8,128)(2,1)S(1)}, u32[]{:S(2)}, u32[]{:S(2)}) collective-permute-start(bf16[8,10752]{1,0:T(8,128)(2,1)S(1)} %add_convert_fusion), channel_id=1, source_target_pairs={{0,4},{1,5},{2,6},{3,7},{4,8},{5,9},{6,10},{7,11},{8,12},{9,13},{1... | collective-permute-start | bytes 516104 | tf_op jit(solution)/shard_map/ppermute | solution.py:259
  64.6 1.0 %add_convert_fusion.2 = bf16[8,10752]{1,0:T(8,128)(2,1)S(1)} fusion(bf16[8,10752]{1,0:T(8,128)(2,1)S(1)} %collective-permute-done.24, bf16[8,10752]{1,0:T(8,128)(2,1)S(1)} %collective-permute-done.22, bf16[8,10752]{1,0:T(8,128)(2,1)} %get-tuple-element.37), kind=kLoop, calls=%fused_computation.2 | loop fusion | flops 516096 | bytes 688128 | tf_op jit(solution)/shard_map/convert_element_type | solution.py:249
  65.6 2.0 %collective-permute-start.25 = (bf16[8,10752]{1,0:T(8,128)(2,1)S(1)}, bf16[8,10752]{1,0:T(8,128)(2,1)S(1)}, u32[]{:S(2)}, u32[]{:S(2)}) collective-permute-start(bf16[8,10752]{1,0:T(8,128)(2,1)S(1)} %add_convert_fusion.2), channel_id=1, source_target_pairs={{0,8},{1,9},{2,10},{3,11},{4,12},{5,13},{6,14},{7,15},{8,0},{9,1},... | collective-permute-start | bytes 516104 | tf_op jit(solution)/shard_map/ppermute | solution.py:259
  67.6 1.0 %add_convert_fusion.4 = bf16[8,10752]{1,0:T(8,128)(2,1)S(1)} fusion(bf16[8,10752]{1,0:T(8,128)(2,1)S(1)} %collective-permute-done.20, bf16[8,10752]{1,0:T(8,128)(2,1)S(1)} %collective-permute-done.18, bf16[8,10752]{1,0:T(8,128)(2,1)} %get-tuple-element.33), kind=kLoop, calls=%fused_computation.4 | loop fusion | flops 516096 | bytes 688128 | tf_op jit(solution)/shard_map/convert_element_type | solution.py:249
  68.6 2.1 %collective-permute-start.21 = (bf16[8,10752]{1,0:T(8,128)(2,1)S(1)}, bf16[8,10752]{1,0:T(8,128)(2,1)S(1)}, u32[]{:S(2)}, u32[]{:S(2)}) collective-permute-start(bf16[8,10752]{1,0:T(8,128)(2,1)S(1)} %add_convert_fusion.4), channel_id=1, source_target_pairs={{0,12},{1,13},{2,14},{3,15},{4,0},{5,1},{6,2},{7,3},{8,4},{9,5},{1... | collective-permute-start | bytes 516104 | tf_op jit(solution)/shard_map/ppermute | solution.py:259
  70.7 0.7 add_convert_fusion.6.refs_0_
  71.4 5.4 %collective-permute-done.25.refs_2_ = bf16[8,10752]{1,0:T(8,128)(2,1)S(1)} collective-permute-done((bf16[8,10752]{1,0:T(8,128)(2,1)S(1)}, bf16[8,10752]{1,0:T(8,128)(2,1)S(1)}, u32[]{:S(2)}, u32[]{:S(2)}) %collective-permute-start.25) | collective-permute-done | bytes 172064 | tf_op jit(solution)/shard_map/ppermute | solution.py:259
  76.9 0.7 collective-permute-done.21.refs_1_
  77.6 0.7 copy-done.2
  78.3 3.2 %shard_map.75 = bf16[16,7168]{1,0:T(8,128)(2,1)} custom-call(s32[4]{0:T(128)} %placement_ref.3, s32[16,2]{1,0:T(8,128)} %copy.9.ids_ref, f32[16,2]{1,0:T(8,128)} %copy.10.gates_ref, bf16[8,10752]{1,0:T(8,128)(2,1)} %add_convert_fusion.6.refs_0_, bf16[8,10752]{1,0:T(8,128)(2,1)} %copy-done.2, bf16[8,10752]{1,0:T(8,128)(2,1)} %copy-done.1, ...), custom_call_target="tpu_custom_call" | custom-call | flops 44040192 | bytes 1146880 | tf_op jit(solution)/shard_map/pallas_call | solution.py:234
  (49 shorter events, 0.1 us)
Async XLA Ops:
  3.7 10.6 %collective-permute-start.1 = (bf16[8,10752]{1,0:T(8,128)(2,1)}, bf16[8,10752]{1,0:T(8,128)(2,1)S(1)}, u32[]{:S(2)}, u32[]{:S(2)}) collective-permute-start(bf16[8,10752]{1,0:T(8,128)(2,1)} %get-tuple-element.26), channel_id=1, source_target_pairs={{0,4},{1,5},{2,6},{3,7},{4,8},{5,9},{6,10},{7,11},{8,12},{9,13},{1... | collective-permute-start | bytes 516104 | tf_op jit(solution)/shard_map/ppermute | solution.py:259
  6.7 14.1 %collective-permute-start.3 = (bf16[8,10752]{1,0:T(8,128)(2,1)}, bf16[8,10752]{1,0:T(8,128)(2,1)S(1)}, u32[]{:S(2)}, u32[]{:S(2)}) collective-permute-start(bf16[8,10752]{1,0:T(8,128)(2,1)} %get-tuple-element.27), channel_id=1, source_target_pairs={{0,8},{1,9},{2,10},{3,11},{4,12},{5,13},{6,14},{7,15},{8,0},{9,1},... | collective-permute-start | bytes 516104 | tf_op jit(solution)/shard_map/ppermute | solution.py:259
  9.3 13.0 %collective-permute-start.5 = (bf16[8,10752]{1,0:T(8,128)(2,1)}, bf16[8,10752]{1,0:T(8,128)(2,1)S(1)}, u32[]{:S(2)}, u32[]{:S(2)}) collective-permute-start(bf16[8,10752]{1,0:T(8,128)(2,1)} %get-tuple-element.28), channel_id=1, source_target_pairs={{0,12},{1,13},{2,14},{3,15},{4,0},{5,1},{6,2},{7,3},{8,4},{9,5},{1... | collective-permute-start | bytes 516104 | tf_op jit(solution)/shard_map/ppermute | solution.py:259
  10.6 34.6 %copy-start.19 = (f32[16,2]{0,1:T(2,128)S(1)}, f32[16,2]{0,1:T(2,128)}, u32[]{:S(2)}) copy-start(f32[16,2]{0,1:T(2,128)} %param.9) | copy-start | bytes 388
  10.6 12.2 %collective-permute-start = (bf16[8,10752]{1,0:T(8,128)(2,1)}, bf16[8,10752]{1,0:T(8,128)(2,1)S(1)}, u32[]{:S(2)}, u32[]{:S(2)}) collective-permute-start(bf16[8,10752]{1,0:T(8,128)(2,1)} %get-tuple-element.25.refs_0_), channel_id=1, source_target_pairs={{0,2},{1,3},{2,0},{3,1},{4,6},{5,7},{6,4},{7,5},{8,10},{9,11},{10,... | collective-permute-start | bytes 516104 | tf_op jit(solution)/shard_map/ppermute | solution.py:262
  12.2 10.7 %collective-permute-start.7 = (bf16[8,10752]{1,0:T(8,128)(2,1)}, bf16[8,10752]{1,0:T(8,128)(2,1)S(1)}, u32[]{:S(2)}, u32[]{:S(2)}) collective-permute-start(bf16[8,10752]{1,0:T(8,128)(2,1)} %get-tuple-element.25.refs_0_), channel_id=1, source_target_pairs={{0,1},{1,0},{2,3},{3,2},{4,5},{5,4},{6,7},{7,6},{8,9},{9,8},{10,11... | collective-permute-start | bytes 516104 | tf_op jit(solution)/shard_map/ppermute | solution.py:265
  14.2 18.4 %copy-start.4 = (bf16[8,10752]{1,0:T(8,128)(2,1)}, bf16[8,10752]{1,0:T(8,128)(2,1)S(1)}, u32[]{:S(2)}) copy-start(bf16[8,10752]{1,0:T(8,128)(2,1)S(1)} %collective-permute-done.1.refs_2_) | copy-start | bytes 516100
  14.2 9.1 %collective-permute-start.2 = (bf16[8,10752]{1,0:T(8,128)(2,1)S(1)}, bf16[8,10752]{1,0:T(8,128)(2,1)S(1)}, u32[]{:S(2)}, u32[]{:S(2)}) collective-permute-start(bf16[8,10752]{1,0:T(8,128)(2,1)S(1)} %collective-permute-done.1.refs_2_), channel_id=1, source_target_pairs={{0,2},{1,3},{2,0},{3,1},{4,6},{5,7},{6,4},{7,5},{8,10},{9,11},{10,... | collective-permute-start | bytes 516104 | tf_op jit(solution)/shard_map/ppermute | solution.py:262
  20.8 11.8 %copy-start.5 = (bf16[8,10752]{1,0:T(8,128)(2,1)}, bf16[8,10752]{1,0:T(8,128)(2,1)S(1)}, u32[]{:S(2)}) copy-start(bf16[8,10752]{1,0:T(8,128)(2,1)S(1)} %collective-permute-done.3.refs_4_) | copy-start | bytes 516100
  20.8 7.3 %collective-permute-start.4 = (bf16[8,10752]{1,0:T(8,128)(2,1)S(1)}, bf16[8,10752]{1,0:T(8,128)(2,1)S(1)}, u32[]{:S(2)}, u32[]{:S(2)}) collective-permute-start(bf16[8,10752]{1,0:T(8,128)(2,1)S(1)} %collective-permute-done.3.refs_4_), channel_id=1, source_target_pairs={{0,2},{1,3},{2,0},{3,1},{4,6},{5,7},{6,4},{7,5},{8,10},{9,11},{10,... | collective-permute-start | bytes 516104 | tf_op jit(solution)/shard_map/ppermute | solution.py:262
  22.3 10.3 %copy-start.6 = (bf16[8,10752]{1,0:T(8,128)(2,1)}, bf16[8,10752]{1,0:T(8,128)(2,1)S(1)}, u32[]{:S(2)}) copy-start(bf16[8,10752]{1,0:T(8,128)(2,1)S(1)} %collective-permute-done.5.refs_6_) | copy-start | bytes 516100
  22.3 8.4 %collective-permute-start.6 = (bf16[8,10752]{1,0:T(8,128)(2,1)S(1)}, bf16[8,10752]{1,0:T(8,128)(2,1)S(1)}, u32[]{:S(2)}, u32[]{:S(2)}) collective-permute-start(bf16[8,10752]{1,0:T(8,128)(2,1)S(1)} %collective-permute-done.5.refs_6_), channel_id=1, source_target_pairs={{0,2},{1,3},{2,0},{3,1},{4,6},{5,7},{6,4},{7,5},{8,10},{9,11},{10,... | collective-permute-start | bytes 516104 | tf_op jit(solution)/shard_map/ppermute | solution.py:262
  22.8 9.8 %copy-start.7 = (bf16[8,10752]{1,0:T(8,128)(2,1)}, bf16[8,10752]{1,0:T(8,128)(2,1)S(1)}, u32[]{:S(2)}) copy-start(bf16[8,10752]{1,0:T(8,128)(2,1)S(1)} %collective-permute-done.refs_1_) | copy-start | bytes 516100
  22.8 7.9 %collective-permute-start.8 = (bf16[8,10752]{1,0:T(8,128)(2,1)S(1)}, bf16[8,10752]{1,0:T(8,128)(2,1)S(1)}, u32[]{:S(2)}, u32[]{:S(2)}) collective-permute-start(bf16[8,10752]{1,0:T(8,128)(2,1)S(1)} %collective-permute-done.refs_1_), channel_id=1, source_target_pairs={{0,1},{1,0},{2,3},{3,2},{4,5},{5,4},{6,7},{7,6},{8,9},{9,8},{10,11... | collective-permute-start | bytes 516104 | tf_op jit(solution)/shard_map/ppermute | solution.py:265
  22.8 9.8 %copy-start.8 = (bf16[8,10752]{1,0:T(8,128)(2,1)}, bf16[8,10752]{1,0:T(8,128)(2,1)S(1)}, u32[]{:S(2)}) copy-start(bf16[8,10752]{1,0:T(8,128)(2,1)S(1)} %collective-permute-done.7.refs_8_) | copy-start | bytes 516100
  22.8 8.3 %collective-permute-start.11 = (bf16[8,10752]{1,0:T(8,128)(2,1)S(1)}, bf16[8,10752]{1,0:T(8,128)(2,1)S(1)}, u32[]{:S(2)}, u32[]{:S(2)}) collective-permute-start(bf16[8,10752]{1,0:T(8,128)(2,1)S(1)} %collective-permute-done.3.refs_4_), channel_id=1, source_target_pairs={{0,1},{1,0},{2,3},{3,2},{4,5},{5,4},{6,7},{7,6},{8,9},{9,8},{10,11... | collective-permute-start | bytes 516104 | tf_op jit(solution)/shard_map/ppermute | solution.py:265
  23.3 9.3 %copy-start.9 = (bf16[8,10752]{1,0:T(8,128)(2,1)}, bf16[8,10752]{1,0:T(8,128)(2,1)S(1)}, u32[]{:S(2)}) copy-start(bf16[8,10752]{1,0:T(8,128)(2,1)S(1)} %collective-permute-done.2.refs_3_) | copy-start | bytes 516100
  23.3 7.9 %collective-permute-start.13 = (bf16[8,10752]{1,0:T(8,128)(2,1)S(1)}, bf16[8,10752]{1,0:T(8,128)(2,1)S(1)}, u32[]{:S(2)}, u32[]{:S(2)}) collective-permute-start(bf16[8,10752]{1,0:T(8,128)(2,1)S(1)} %collective-permute-done.5.refs_6_), channel_id=1, source_target_pairs={{0,1},{1,0},{2,3},{3,2},{4,5},{5,4},{6,7},{7,6},{8,9},{9,8},{10,11... | collective-permute-start | bytes 516104 | tf_op jit(solution)/shard_map/ppermute | solution.py:265
  28.0 4.6 %copy-start.10 = (bf16[8,10752]{1,0:T(8,128)(2,1)}, bf16[8,10752]{1,0:T(8,128)(2,1)S(1)}, u32[]{:S(2)}) copy-start(bf16[8,10752]{1,0:T(8,128)(2,1)S(1)} %collective-permute-done.4.refs_5_) | copy-start | bytes 516100
  28.0 3.3 %collective-permute-start.9 = (bf16[8,10752]{1,0:T(8,128)(2,1)S(1)}, bf16[8,10752]{1,0:T(8,128)(2,1)S(1)}, u32[]{:S(2)}, u32[]{:S(2)}) collective-permute-start(bf16[8,10752]{1,0:T(8,128)(2,1)S(1)} %collective-permute-done.1.refs_2_), channel_id=1, source_target_pairs={{0,1},{1,0},{2,3},{3,2},{4,5},{5,4},{6,7},{7,6},{8,9},{9,8},{10,11... | collective-permute-start | bytes 516104 | tf_op jit(solution)/shard_map/ppermute | solution.py:265
  30.7 2.0 %copy-start.11 = (bf16[8,10752]{1,0:T(8,128)(2,1)}, bf16[8,10752]{1,0:T(8,128)(2,1)S(1)}, u32[]{:S(2)}) copy-start(bf16[8,10752]{1,0:T(8,128)(2,1)S(1)} %collective-permute-done.6.refs_7_) | copy-start | bytes 516100
  30.7 1.4 %collective-permute-start.10 = (bf16[8,10752]{1,0:T(8,128)(2,1)S(1)}, bf16[8,10752]{1,0:T(8,128)(2,1)S(1)}, u32[]{:S(2)}, u32[]{:S(2)}) collective-permute-start(bf16[8,10752]{1,0:T(8,128)(2,1)S(1)} %collective-permute-done.2.refs_3_), channel_id=1, source_target_pairs={{0,1},{1,0},{2,3},{3,2},{4,5},{5,4},{6,7},{7,6},{8,9},{9,8},{10,11... | collective-permute-start | bytes 516104 | tf_op jit(solution)/shard_map/ppermute | solution.py:265
  30.7 2.0 %copy-start.12 = (bf16[8,10752]{1,0:T(8,128)(2,1)}, bf16[8,10752]{1,0:T(8,128)(2,1)S(1)}, u32[]{:S(2)}) copy-start(bf16[8,10752]{1,0:T(8,128)(2,1)S(1)} %collective-permute-done.8.refs_9_) | copy-start | bytes 516100
  30.7 1.6 %collective-permute-start.12 = (bf16[8,10752]{1,0:T(8,128)(2,1)S(1)}, bf16[8,10752]{1,0:T(8,128)(2,1)S(1)}, u32[]{:S(2)}, u32[]{:S(2)}) collective-permute-start(bf16[8,10752]{1,0:T(8,128)(2,1)S(1)} %collective-permute-done.4.refs_5_), channel_id=1, source_target_pairs={{0,1},{1,0},{2,3},{3,2},{4,5},{5,4},{6,7},{7,6},{8,9},{9,8},{10,11... | collective-permute-start | bytes 516104 | tf_op jit(solution)/shard_map/ppermute | solution.py:265
  31.2 1.5 %copy-start.13 = (bf16[8,10752]{1,0:T(8,128)(2,1)}, bf16[8,10752]{1,0:T(8,128)(2,1)S(1)}, u32[]{:S(2)}) copy-start(bf16[8,10752]{1,0:T(8,128)(2,1)S(1)} %collective-permute-done.11.refs_12_) | copy-start | bytes 516100
  31.2 1.4 %collective-permute-start.14 = (bf16[8,10752]{1,0:T(8,128)(2,1)S(1)}, bf16[8,10752]{1,0:T(8,128)(2,1)S(1)}, u32[]{:S(2)}, u32[]{:S(2)}) collective-permute-start(bf16[8,10752]{1,0:T(8,128)(2,1)S(1)} %collective-permute-done.6.refs_7_), channel_id=1, source_target_pairs={{0,1},{1,0},{2,3},{3,2},{4,5},{5,4},{6,7},{7,6},{8,9},{9,8},{10,11... | collective-permute-start | bytes 516104 | tf_op jit(solution)/shard_map/ppermute | solution.py:265
  31.3 1.4 %copy-start.14 = (bf16[8,10752]{1,0:T(8,128)(2,1)}, bf16[8,10752]{1,0:T(8,128)(2,1)S(1)}, u32[]{:S(2)}) copy-start(bf16[8,10752]{1,0:T(8,128)(2,1)S(1)} %collective-permute-done.13.refs_14_) | copy-start | bytes 516100
  31.3 1.4 %copy-start.15 = (bf16[8,10752]{1,0:T(8,128)(2,1)}, bf16[8,10752]{1,0:T(8,128)(2,1)S(1)}, u32[]{:S(2)}) copy-start(bf16[8,10752]{1,0:T(8,128)(2,1)S(1)} %collective-permute-done.9.refs_10_) | copy-start | bytes 516100
  32.1 0.7 copy-start.16
  32.3 0.7 copy-start.17
  33.0 0.7 copy-start.18
  44.9 25.8 %copy-start.3 = (bf16[8,10752]{1,0:T(8,128)(2,1)S(1)}, bf16[8,10752]{1,0:T(8,128)(2,1)}, u32[]{:S(2)}) copy-start(bf16[8,10752]{1,0:T(8,128)(2,1)} %get-tuple-element.29) | copy-start | bytes 516100
  44.9 2.0 %collective-permute-start.27 = (bf16[8,10752]{1,0:T(8,128)(2,1)}, bf16[8,10752]{1,0:T(8,128)(2,1)S(1)}, u32[]{:S(2)}, u32[]{:S(2)}) collective-permute-start(bf16[8,10752]{1,0:T(8,128)(2,1)} %get-tuple-element.44), channel_id=1, source_target_pairs={{0,1},{1,0},{2,3},{3,2},{4,5},{5,4},{6,7},{7,6},{8,9},{9,8},{10,11... | collective-permute-start | bytes 516104 | tf_op jit(solution)/shard_map/ppermute | solution.py:265
  45.9 7.4 %collective-permute-start.26 = (bf16[8,10752]{1,0:T(8,128)(2,1)}, bf16[8,10752]{1,0:T(8,128)(2,1)S(1)}, u32[]{:S(2)}, u32[]{:S(2)}) collective-permute-start(bf16[8,10752]{1,0:T(8,128)(2,1)} %get-tuple-element.42), channel_id=1, source_target_pairs={{0,1},{1,0},{2,3},{3,2},{4,5},{5,4},{6,7},{7,6},{8,9},{9,8},{10,11... | collective-permute-start | bytes 516104 | tf_op jit(solution)/shard_map/ppermute | solution.py:265
  46.1 2.0 %collective-permute-start.23 = (bf16[8,10752]{1,0:T(8,128)(2,1)}, bf16[8,10752]{1,0:T(8,128)(2,1)S(1)}, u32[]{:S(2)}, u32[]{:S(2)}) collective-permute-start(bf16[8,10752]{1,0:T(8,128)(2,1)} %get-tuple-element.40), channel_id=1, source_target_pairs={{0,1},{1,0},{2,3},{3,2},{4,5},{5,4},{6,7},{7,6},{8,9},{9,8},{10,11... | collective-permute-start | bytes 516104 | tf_op jit(solution)/shard_map/ppermute | solution.py:265
  46.4 14.1 %collective-permute-start.22 = (bf16[8,10752]{1,0:T(8,128)(2,1)}, bf16[8,10752]{1,0:T(8,128)(2,1)S(1)}, u32[]{:S(2)}, u32[]{:S(2)}) collective-permute-start(bf16[8,10752]{1,0:T(8,128)(2,1)} %get-tuple-element.38), channel_id=1, source_target_pairs={{0,1},{1,0},{2,3},{3,2},{4,5},{5,4},{6,7},{7,6},{8,9},{9,8},{10,11... | collective-permute-start | bytes 516104 | tf_op jit(solution)/shard_map/ppermute | solution.py:265
  46.7 2.8 %collective-permute-start.19 = (bf16[8,10752]{1,0:T(8,128)(2,1)}, bf16[8,10752]{1,0:T(8,128)(2,1)S(1)}, u32[]{:S(2)}, u32[]{:S(2)}) collective-permute-start(bf16[8,10752]{1,0:T(8,128)(2,1)} %get-tuple-element.36), channel_id=1, source_target_pairs={{0,1},{1,0},{2,3},{3,2},{4,5},{5,4},{6,7},{7,6},{8,9},{9,8},{10,11... | collective-permute-start | bytes 516104 | tf_op jit(solution)/shard_map/ppermute | solution.py:265
  46.9 18.6 %collective-permute-start.18 = (bf16[8,10752]{1,0:T(8,128)(2,1)}, bf16[8,10752]{1,0:T(8,128)(2,1)S(1)}, u32[]{:S(2)}, u32[]{:S(2)}) collective-permute-start(bf16[8,10752]{1,0:T(8,128)(2,1)} %get-tuple-element.34), channel_id=1, source_target_pairs={{0,1},{1,0},{2,3},{3,2},{4,5},{5,4},{6,7},{7,6},{8,9},{9,8},{10,11... | collective-permute-start | bytes 516104 | tf_op jit(solution)/shard_map/ppermute | solution.py:265
  48.1 2.6 %collective-permute-start.16 = (bf16[8,10752]{1,0:T(8,128)(2,1)}, bf16[8,10752]{1,0:T(8,128)(2,1)S(1)}, u32[]{:S(2)}, u32[]{:S(2)}) collective-permute-start(bf16[8,10752]{1,0:T(8,128)(2,1)} %get-tuple-element.32), channel_id=1, source_target_pairs={{0,1},{1,0},{2,3},{3,2},{4,5},{5,4},{6,7},{7,6},{8,9},{9,8},{10,11... | collective-permute-start | bytes 516104 | tf_op jit(solution)/shard_map/ppermute | solution.py:265
  49.5 21.2 %collective-permute-start.15 = (bf16[8,10752]{1,0:T(8,128)(2,1)}, bf16[8,10752]{1,0:T(8,128)(2,1)S(1)}, u32[]{:S(2)}, u32[]{:S(2)}) collective-permute-start(bf16[8,10752]{1,0:T(8,128)(2,1)} %get-tuple-element.30), channel_id=1, source_target_pairs={{0,1},{1,0},{2,3},{3,2},{4,5},{5,4},{6,7},{7,6},{8,9},{9,8},{10,11... | collective-permute-start | bytes 516104 | tf_op jit(solution)/shard_map/ppermute | solution.py:265
  50.7 7.3 %collective-permute-start.28 = (bf16[8,10752]{1,0:T(8,128)(2,1)S(1)}, bf16[8,10752]{1,0:T(8,128)(2,1)S(1)}, u32[]{:S(2)}, u32[]{:S(2)}) collective-permute-start(bf16[8,10752]{1,0:T(8,128)(2,1)S(1)} %add_convert_fusion.1), channel_id=1, source_target_pairs={{0,2},{1,3},{2,0},{3,1},{4,6},{5,7},{6,4},{7,5},{8,10},{9,11},{10,... | collective-permute-start | bytes 516104 | tf_op jit(solution)/shard_map/ppermute | solution.py:262
  53.3 8.4 %collective-permute-start.24 = (bf16[8,10752]{1,0:T(8,128)(2,1)S(1)}, bf16[8,10752]{1,0:T(8,128)(2,1)S(1)}, u32[]{:S(2)}, u32[]{:S(2)}) collective-permute-start(bf16[8,10752]{1,0:T(8,128)(2,1)S(1)} %add_convert_fusion.3), channel_id=1, source_target_pairs={{0,2},{1,3},{2,0},{3,1},{4,6},{5,7},{6,4},{7,5},{8,10},{9,11},{10,... | collective-permute-start | bytes 516104 | tf_op jit(solution)/shard_map/ppermute | solution.py:262
  58.0 9.6 %collective-permute-start.20 = (bf16[8,10752]{1,0:T(8,128)(2,1)S(1)}, bf16[8,10752]{1,0:T(8,128)(2,1)S(1)}, u32[]{:S(2)}, u32[]{:S(2)}) collective-permute-start(bf16[8,10752]{1,0:T(8,128)(2,1)S(1)} %add_convert_fusion.5), channel_id=1, source_target_pairs={{0,2},{1,3},{2,0},{3,1},{4,6},{5,7},{6,4},{7,5},{8,10},{9,11},{10,... | collective-permute-start | bytes 516104 | tf_op jit(solution)/shard_map/ppermute | solution.py:262
  60.5 10.2 %collective-permute-start.17 = (bf16[8,10752]{1,0:T(8,128)(2,1)S(1)}, bf16[8,10752]{1,0:T(8,128)(2,1)S(1)}, u32[]{:S(2)}, u32[]{:S(2)}) collective-permute-start(bf16[8,10752]{1,0:T(8,128)(2,1)S(1)} %add_convert_fusion.7), channel_id=1, source_target_pairs={{0,2},{1,3},{2,0},{3,1},{4,6},{5,7},{6,4},{7,5},{8,10},{9,11},{10,... | collective-permute-start | bytes 516104 | tf_op jit(solution)/shard_map/ppermute | solution.py:262
  61.7 9.7 %collective-permute-start.29 = (bf16[8,10752]{1,0:T(8,128)(2,1)S(1)}, bf16[8,10752]{1,0:T(8,128)(2,1)S(1)}, u32[]{:S(2)}, u32[]{:S(2)}) collective-permute-start(bf16[8,10752]{1,0:T(8,128)(2,1)S(1)} %add_convert_fusion), channel_id=1, source_target_pairs={{0,4},{1,5},{2,6},{3,7},{4,8},{5,9},{6,10},{7,11},{8,12},{9,13},{1... | collective-permute-start | bytes 516104 | tf_op jit(solution)/shard_map/ppermute | solution.py:259
  65.6 11.3 %collective-permute-start.25 = (bf16[8,10752]{1,0:T(8,128)(2,1)S(1)}, bf16[8,10752]{1,0:T(8,128)(2,1)S(1)}, u32[]{:S(2)}, u32[]{:S(2)}) collective-permute-start(bf16[8,10752]{1,0:T(8,128)(2,1)S(1)} %add_convert_fusion.2), channel_id=1, source_target_pairs={{0,8},{1,9},{2,10},{3,11},{4,12},{5,13},{6,14},{7,15},{8,0},{9,1},... | collective-permute-start | bytes 516104 | tf_op jit(solution)/shard_map/ppermute | solution.py:259
  68.6 9.0 %collective-permute-start.21 = (bf16[8,10752]{1,0:T(8,128)(2,1)S(1)}, bf16[8,10752]{1,0:T(8,128)(2,1)S(1)}, u32[]{:S(2)}, u32[]{:S(2)}) collective-permute-start(bf16[8,10752]{1,0:T(8,128)(2,1)S(1)} %add_convert_fusion.4), channel_id=1, source_target_pairs={{0,12},{1,13},{2,14},{3,15},{4,0},{5,1},{6,2},{7,3},{8,4},{9,5},{1... | collective-permute-start | bytes 516104 | tf_op jit(solution)/shard_map/ppermute | solution.py:259
  71.4 6.2 %copy-start = (bf16[8,10752]{1,0:T(8,128)(2,1)}, bf16[8,10752]{1,0:T(8,128)(2,1)S(1)}, u32[]{:S(2)}) copy-start(bf16[8,10752]{1,0:T(8,128)(2,1)S(1)} %collective-permute-done.29.refs_3_) | copy-start | bytes 516100
  76.9 0.8 copy-start.1
  77.6 0.7 copy-start.2

commit v3 on v1

v3 whole, which is shorter than its diff:
```python
import functools

import jax
import jax.numpy as jnp
from jax import lax
from jax.experimental import pallas as pl
from jax.experimental.pallas import tpu as pltpu
from jax.sharding import PartitionSpec as P

VMEM_BYTES = 24 * 2**20
VMEM = pl.BlockSpec(memory_space=pltpu.VMEM)
SMEM = pl.BlockSpec(memory_space=pltpu.SMEM)
ANYWHERE = pl.BlockSpec(memory_space=pl.ANY)
LOADS = 4


def in_vmem(value):
    return pltpu.with_memory_space_constraint(value, pltpu.VMEM)


def product(lhs, rhs):
    return jnp.dot(lhs, rhs, preferred_element_type=jnp.float32)


def slots_of(ids, n_blocks):
    top, rows = ids.shape
    experts = lax.broadcasted_iota(jnp.int32, (n_blocks, rows), 0)
    picks = jnp.zeros((n_blocks, rows), jnp.float32)
    for k in range(top):
        picks = picks + jnp.where(ids[k : k + 1, :] == experts, 1.0, 0.0)
    before = lax.broadcasted_iota(jnp.int32, (rows, rows), 0) < lax.broadcasted_iota(
        jnp.int32, (rows, rows), 1
    )
    earlier = product(picks.astype(jnp.bfloat16), jnp.where(before, 1.0, 0.0).astype(jnp.bfloat16))
    return experts, picks, earlier


def expert_at(placement_ref, block):
    found = jnp.int32(0)
    for e in range(placement_ref.shape[0]):
        found = jnp.where(placement_ref[e] == block, jnp.int32(e), found)
    return found


def row_of(values, experts, expert):
    return jnp.sum(jnp.where(experts == expert, values, 0.0), axis=0, keepdims=True)


def bucket_rows(rows):
    row = lax.broadcasted_iota(jnp.int32, (rows, rows), 0)
    half, quarter = rows // 2, rows // 4
    return jnp.where(row < half, row, half + row % quarter).astype(jnp.float32)


def pack_kernel(n_blocks, parts, placement_ref, ids_ref, tokens_ref, *out_refs):
    rows, width = tokens_ref.shape
    half, quarter = rows // 2, rows // 4
    block = lax.axis_index("node") // parts
    experts, picks, earlier = slots_of(ids_ref[...], n_blocks)
    wanted = bucket_rows(rows)
    upper = lax.broadcasted_iota(jnp.int32, (half, width // 2), 0) < quarter
    for k, out_ref in enumerate(out_refs):
        expert = expert_at(placement_ref, lax.rem(block + k, n_blocks))
        named = row_of(picks, experts, expert) > 0.5
        slot = row_of(earlier, experts, expert)
        chooser = jnp.where(named & (slot == wanted), 1.0, 0.0).astype(jnp.bfloat16)
        packed = product(chooser, tokens_ref[...])
        out_ref[:, :width] = packed[:half].astype(jnp.bfloat16)
        rest = jnp.where(upper, packed[half:, : width // 2], packed[half:, width // 2 :])
        out_ref[:, width:] = rest.astype(jnp.bfloat16)


def pack(placement, ids, tokens, n_blocks, parts):
    rows, width = tokens.shape
    shape = pltpu.VMEM((rows // 2, width + width // 2), jnp.bfloat16)
    return pl.pallas_call(
        functools.partial(pack_kernel, n_blocks, parts),
        out_shape=[shape] * n_blocks,
        in_specs=[SMEM, VMEM, VMEM],
        out_specs=[VMEM] * n_blocks,
        compiler_params=pltpu.CompilerParams(vmem_limit_bytes=VMEM_BYTES),
        cost_estimate=pl.CostEstimate(
            flops=2 * n_blocks * rows * rows * width,
            bytes_accessed=2 * (n_blocks + 1) * rows * width,
            transcendentals=0,
        ),
    )(placement, ids, tokens)


def load_kernel(*refs):
    sources, targets, sems = refs[:3], refs[4:7], refs[7]
    copies = []
    for i, (source, target) in enumerate(zip(sources, targets)):
        rows = source.shape[0] // LOADS
        for j in range(LOADS):
            part = pl.ds(j * rows, rows)
            copies.append(pltpu.make_async_copy(source.at[part], target.at[part], sems.at[i, j]))
    for copy in copies:
        copy.start()
    for copy in copies:
        copy.wait()


def load(weights, after):
    return pl.pallas_call(
        load_kernel,
        out_shape=[pltpu.VMEM(w.shape, w.dtype) for w in weights],
        in_specs=[pl.BlockSpec(memory_space=pltpu.HBM)] * 3 + [ANYWHERE],
        out_specs=[VMEM] * 3,
        scratch_shapes=[pltpu.SemaphoreType.DMA((3, LOADS))],
        compiler_params=pltpu.CompilerParams(vmem_limit_bytes=VMEM_BYTES),
        cost_estimate=pl.CostEstimate(
            flops=0, bytes_accessed=0, transcendentals=0
        ),
    )(*[pltpu.with_memory_space_constraint(w, pltpu.HBM) for w in weights], after)


def experts_kernel(*refs):
    straight_ref, across_ref, straight_other_ref, across_other_ref = refs[:4]
    gate_ref, up_ref, down_ref = refs[4:7]
    kept_ref, sent_ref = refs[-2:]
    pieces = (straight_ref, across_ref, straight_other_ref, across_other_ref)
    width, hid = gate_ref.shape
    middle = width // 2
    height = straight_ref.shape[0]
    total = len(pieces) * height
    rest = jnp.concatenate([p[:, width:] for p in pieces], axis=0)
    left = jnp.concatenate([p[:, :middle] for p in pieces] + [rest], axis=0)
    right = jnp.concatenate([p[:, middle:width] for p in pieces] + [rest], axis=0)
    upper = lax.broadcasted_iota(jnp.int32, (total, 1), 0) % height < height // 2
    shift = height // 2

    def whole_rows(ref):
        a, b = product(left, ref[:middle, :]), product(right, ref[middle:, :])
        tail = jnp.where(
            upper,
            a[total:] + pltpu.roll(b[total:], total - shift, axis=0),
            b[total:] + pltpu.roll(a[total:], shift, axis=0),
        )
        return jnp.concatenate([a[:total] + b[:total], tail], axis=0)

    gate_rows, up_rows = whole_rows(gate_ref), whole_rows(up_ref)
    hidden = (jax.nn.silu(gate_rows) * up_rows).astype(jnp.bfloat16)

    def store(start, values):
        values = values.astype(jnp.bfloat16)
        stop = start + values.shape[1]
        kept_ref[:, start:stop] = values[: 2 * height]
        sent_ref[:, start:stop] = values[2 * height :]

    step = middle // 4
    for i in range(4):
        begin = i * step
        a = product(hidden, down_ref[:, begin : begin + step])
        b = product(hidden, down_ref[:, middle + begin : middle + begin + step])
        store(begin, a[:total])
        store(middle + begin, b[:total])
        store(width + begin, jnp.where(upper, a[total:], b[total:]))


def run_experts(pieces, weights, after):
    width, hid = weights[0].shape
    height, packed_width = pieces[0].shape
    rows = len(pieces) * height
    shape = pltpu.VMEM((rows // 2, packed_width), jnp.bfloat16)
    operands = [in_vmem(p) for p in pieces] + [in_vmem(w) for w in weights]
    return pl.pallas_call(
        experts_kernel,
        out_shape=[shape] * 2,
        in_specs=[VMEM] * 7 + [ANYWHERE] * len(after),
        out_specs=[VMEM] * 2,
        compiler_params=pltpu.CompilerParams(vmem_limit_bytes=VMEM_BYTES),
        cost_estimate=pl.CostEstimate(
            flops=0, bytes_accessed=0, transcendentals=0
        ),
    )(*operands, *after)


def mix_kernel(n_blocks, parts, placement_ref, ids_ref, gates_ref, *refs):
    results, out_ref = refs[:-1], refs[-1]
    rows, width = out_ref.shape
    half, quarter, middle = rows // 2, rows // 4, width // 2
    block = lax.axis_index("node") // parts
    ids, gates = ids_ref[...], gates_ref[...]
    experts, picks, earlier = slots_of(ids, n_blocks)
    wanted = bucket_rows(rows)
    terms = []
    for k in range(n_blocks):
        expert = expert_at(placement_ref, lax.rem(block + k, n_blocks))
        named = row_of(picks, experts, expert) > 0.5
        slot = row_of(earlier, experts, expert)
        weight = jnp.sum(jnp.where(ids == expert, gates, 0.0), axis=0, keepdims=True)
        terms.append(jnp.where(named & (slot == wanted), weight, 0.0))
    term = jnp.concatenate(terms, axis=0)
    row = lax.broadcasted_iota(jnp.int32, term.shape, 0) % rows
    rest = jnp.concatenate([r[:, width:] for r in results], axis=0)
    for side in range(2):
        first = half + side * quarter
        mine = jnp.where((row < half) | ((row >= first) & (row < first + quarter)), term, 0.0)
        high = mine.astype(jnp.bfloat16)
        lower = mine - high.astype(jnp.float32)
        mid = lower.astype(jnp.bfloat16)
        low = (lower - mid.astype(jnp.float32)).astype(jnp.bfloat16)
        lhs = jnp.concatenate([high, mid, low], axis=1)
        pieces = []
        for r in results:
            pieces += [r[:, side * middle : (side + 1) * middle], r[:, width:]]
        rhs = jnp.concatenate(pieces, axis=0)
        value = lax.dot_general(
            lhs, rhs, (((0,), (0,)), ((), ())), preferred_element_type=jnp.float32
        )
        value = value[:rows] + value[rows : 2 * rows] + value[2 * rows :]
        out_ref[:, side * middle : (side + 1) * middle] = value.astype(jnp.bfloat16)


def mix(placement, ids, gates, results, n_blocks, parts):
    rows = ids.shape[1]
    width = results[0].shape[1] // 3 * 2
    return pl.pallas_call(
        functools.partial(mix_kernel, n_blocks, parts),
        out_shape=jax.ShapeDtypeStruct((rows, width), jnp.bfloat16),
        in_specs=[SMEM] + [VMEM] * (2 + n_blocks),
        out_specs=VMEM,
        compiler_params=pltpu.CompilerParams(vmem_limit_bytes=VMEM_BYTES),
        cost_estimate=pl.CostEstimate(
            flops=6 * n_blocks * rows * rows * width,
            bytes_accessed=2 * (n_blocks + 1) * rows * width,
            transcendentals=0,
        ),
    )(placement, ids, gates, *[in_vmem(r) for r in results])


def add(*values):
    return sum(v.astype(jnp.float32) for v in values).astype(jnp.bfloat16)


def local(tokens, expert_ids, gates, placement, gate_weight, up_weight, down_weight):
    n_blocks = placement.shape[0]
    devices = lax.axis_size("node")
    parts = devices // n_blocks
    half = tokens.shape[0] // 2

    def along_z(value, k):
        pairs = [(i, (i + k * parts) % devices) for i in range(devices)]
        return lax.ppermute(value, "node", pairs)

    def along_y(value):
        return lax.ppermute(value, "node", [(i, i ^ 2) for i in range(devices)])

    def along_core(value):
        return lax.ppermute(value, "node", [(i, i ^ 1) for i in range(devices)])

    order = sorted(range(n_blocks), key=lambda k: (min(k, n_blocks - k), k))
    ids = expert_ids.T
    buckets = pack(placement, ids, tokens, n_blocks, parts)
    across, straight = {0: along_y(buckets[0])}, {0: buckets[0]}
    for k in order[1:]:
        straight[k] = along_z(buckets[k], k)
    weights = load((gate_weight, up_weight, down_weight), buckets[0])
    results = [None] * n_blocks
    after = []
    for k in order:
        if k:
            across[k] = along_y(straight[k])
        pieces = [straight[k], across[k], along_core(straight[k]), along_core(across[k])]
        kept, sent = run_experts(pieces, weights, after)
        returned = along_core(sent)
        both = add(kept[half:], returned[half:])
        after = [both]
        back = along_y(both)
        home = add(kept[:half], returned[:half], back)
        results[k] = along_z(home, -k) if k else home
    return mix(placement, ids, gates.T, results, n_blocks, parts)


def solution(mesh):
    placed = (
        P(("group", "node"), None),
        P(("group", "node"), None),
        P(("group", "node"), None),
        P(),
        P(None, "node"),
        P(None, "node"),
        P("node", None),
    )
    return jax.shard_map(
        local, mesh=mesh, in_specs=placed, out_specs=P(("group", "node"), None), check_vma=False
    )
```

time: 151 us -> 82.3 us (0.55)
  waiting for transfers between devices: 118 us -> 43.5 us
  starting transfers between devices: 0.04 us -> 20.2 us
  Pallas kernels: 0 us -> 15.4 us
  matrix products: 14.3 us -> 0 us
  between operations: 13.4 us -> 0.22 us
  other arithmetic: 4.09 us -> 0.43 us
  local copies, waits for them, and re-layouts: 0.1 us -> 2.29 us
    reduce_scatter x1 -> x0, waiting for transfers between devices: 67.8 us -> none  [local(): return lax.psum_scatter(piece, 'node', scatter_dimension=0, tiled=True)]
    all_gather x1 -> x0, waiting for transfers between devices: 50.6 us -> none  [local(): gathered = lax.all_gather(outgoing, 'node', axis=0, tiled=True)]
    ppermute x0 -> x26, waiting for transfers between devices: none -> 43.5 us  [the longest x8 28 us: along_y(): return lax.ppermute(value, 'node', [(i, i ^ 2) for i in range(devices)])]
    ppermute x0 -> x26, starting transfers between devices: none -> 20.2 us  [the longest x8 10.7 us: along_y(): return lax.ppermute(value, 'node', [(i, i ^ 2) for i in range(devices)])]
    pallas_call x0 -> x7, Pallas kernels: none -> 15.4 us  [the longest x4 8.28 us: run_experts(): pl.pallas_call(experts_kernel, out_shape=[shape] * 2, in_specs=[VMEM] * 7...]
    dot_general x2 -> x0, matrix products: 14.3 us -> none  [the longest x1 10 us: local(): jnp.dot(hidden, down_weight, preferred_element_type=jnp.float32)]
    reduce_sum x3 -> x0, other arithmetic: 2.41 us -> none  [the longest x1 0.94 us: local(): scale = jnp.sum(jnp.where(mine[None, :], tail, 0.0), axis=1, keepdims=True)]
    unnamed x1 -> x12, local copies, waits for them, and re-layouts: 0.1 us -> 2.29 us
  transfers between devices with their start and end apart: 2 -> 26, of which waited for: 2 -> 13; matrix products, arithmetic and copies ran while one was open for 0% -> 1% of each run, Pallas kernels for 0% -> 15%
where the time goes in v3:
time: 82.3 us; the launch traced here: 82.1 us
  waiting for transfers between devices  43.5 us (53%)
  starting transfers between devices  20.2 us (25%)
  Pallas kernels  15.4 us (19%)
  local copies, waits for them, and re-layouts  2.29 us (3%)
    ppermute x8, waiting for transfers between devices, along_y(): return lax.ppermute(value, 'node', [(i, i ^ 2) for i in range(devices)])  28 us
    ppermute x6, waiting for transfers between devices, along_z(): return lax.ppermute(value, 'node', pairs)  12.8 us
    ppermute x8, starting transfers between devices, along_y(): return lax.ppermute(value, 'node', [(i, i ^ 2) for i in range(devices)])  10.7 us
    ppermute x6, starting transfers between devices, along_z(): return lax.ppermute(value, 'node', pairs)  8.71 us
    pallas_call x4, Pallas kernels, run_experts(): pl.pallas_call(experts_kernel, out_shape=[shape] * 2, in_specs=[VMEM] * 7...  8.28 us
    pallas_call x1, Pallas kernels, load(): pl.pallas_call(load_kernel, out_shape=[pltpu.VMEM(w.shape, w.dtype) for w...  4.24 us
    ppermute x12, waiting for transfers between devices, along_core(): return lax.ppermute(value, 'node', [(i, i ^ 1) for i in range(devices)])  2.71 us
    unnamed x12, local copies, waits for them, and re-layouts  2.29 us
  transfers between devices with their start and end apart: 26, of which 13 were waited for; matrix products, arithmetic and copies ran while one was open for 1% of the time, Pallas kernels for 15%

profile of v3, /device:TPU:0, one launch (start us, length us, event | category | flops | bytes accessed | tf_op | source)
XLA Modules:
  0.0 82.1 jit_solution(16409607723518960510)
XLA Ops:
  0.0 0.9 %copy-done = bf16[16,7168]{1,0:T(8,128)(2,1)S(1)} copy-done((bf16[16,7168]{1,0:T(8,128)(2,1)S(1)}, bf16[16,7168]{1,0:T(8,128)(2,1)}, u32[]{:S(2)}) %copy-start) | copy-done | bytes 229400
  0.9 0.7 copy-done.1
  1.6 0.7 copy-done.3
  2.3 1.0 %shard_map.73 = (bf16[8,10752]{1,0:T(8,128)(2,1)S(1)}, bf16[8,10752]{1,0:T(8,128)(2,1)S(1)}, bf16[8,10752]{1,0:T(8,128)(2,1)S(1)}, bf16[8,10752]{1,0:T(8,128)(2,1)S(1)}) custom-call(s32[4]{0:T(128)S(1)} %copy-done.3, s32[2,16]{1,0:T(2,128)S(1)} %bitcast.2, bf16[16,7168]{1,0:T(8,128)(2,1)S(1)} %copy-done), custom_call_target="tpu_custom_call" | custom-call | flops 14680064 | bytes 1146880 | tf_op jit(solution)/shard_map/pallas_call | solution.py:76
  3.3 3.0 %collective-permute-start = (bf16[8,10752]{1,0:T(8,128)(2,1)S(1)}, bf16[8,10752]{1,0:T(8,128)(2,1)S(1)}, u32[]{:S(2)}, u32[]{:S(2)}) collective-permute-start(bf16[8,10752]{1,0:T(8,128)(2,1)S(1)} %get-tuple-element.20.refs_3_.refs_0_), channel_id=1, source_target_pairs={{0,2},{1,3},{2,0},{3,1},{4,6},{5,7},{6,4},{7,5},{8,10},{9,11},{10,... | collective-permute-start | bytes 516104 | tf_op jit(solution)/shard_map/ppermute | solution.py:248
  6.3 0.0 collective-permute-start.1
  6.4 4.4 %collective-permute-done.refs_1_ = bf16[8,10752]{1,0:T(8,128)(2,1)S(1)} collective-permute-done((bf16[8,10752]{1,0:T(8,128)(2,1)S(1)}, bf16[8,10752]{1,0:T(8,128)(2,1)S(1)}, u32[]{:S(2)}, u32[]{:S(2)}) %collective-permute-start) | collective-permute-done | bytes 172064 | tf_op jit(solution)/shard_map/ppermute | solution.py:248
  10.7 0.0 collective-permute-start.2
  10.7 1.8 %collective-permute-start.5 = (bf16[8,10752]{1,0:T(8,128)(2,1)S(1)}, bf16[8,10752]{1,0:T(8,128)(2,1)S(1)}, u32[]{:S(2)}, u32[]{:S(2)}) collective-permute-start(bf16[8,10752]{1,0:T(8,128)(2,1)S(1)} %get-tuple-element.26), channel_id=1, source_target_pairs={{0,4},{1,5},{2,6},{3,7},{4,8},{5,9},{6,10},{7,11},{8,12},{9,13},{1... | collective-permute-start | bytes 516104 | tf_op jit(solution)/shard_map/ppermute | solution.py:245
  12.5 4.2 %shard_map.74 = (bf16[7168,256]{1,0:T(8,128)(2,1)S(1)}, bf16[7168,256]{1,0:T(8,128)(2,1)S(1)}, bf16[256,7168]{1,0:T(8,128)(2,1)S(1)}) custom-call(bf16[7168,256]{1,0:T(8,128)(2,1)} %refs_0_.1, bf16[7168,256]{1,0:T(8,128)(2,1)} %refs_1_.1, bf16[256,7168]{1,0:T(8,128)(2,1)} %refs_2_.1, bf16[8,10752]{1,0:T(8,128)(2,1)S(1)} %get-tuple-element.20.refs_3_.refs_0_), custom_call_target="tpu_custom_call" | custom-call | tf_op jit(solution)/shard_map/pallas_call | solution.py:105
  16.8 0.0 collective-permute-done.1.refs_2_
  16.8 0.0 collective-permute-done.2.refs_3_
  16.8 2.1 %shard_map.75 = (bf16[16,10752]{1,0:T(8,128)(2,1)S(1)}, bf16[16,10752]{1,0:T(8,128)(2,1)S(1)}) custom-call(bf16[8,10752]{1,0:T(8,128)(2,1)S(1)} %get-tuple-element.20.refs_3_.refs_0_, bf16[8,10752]{1,0:T(8,128)(2,1)S(1)} %collective-permute-done.refs_1_, bf16[8,10752]{1,0:T(8,128)(2,1)S(1)} %collective-permute-done.1.refs_2_, ...), custom_call_target="tpu_custom_call" | custom-call | tf_op jit(solution)/shard_map/pallas_call | solution.py:167
  18.9 0.3 collective-permute-start.3
  19.2 0.4 collective-permute-done.5.refs_0_
  19.6 1.5 %collective-permute-start.6 = (bf16[8,10752]{1,0:T(8,128)(2,1)S(1)}, bf16[8,10752]{1,0:T(8,128)(2,1)S(1)}, u32[]{:S(2)}, u32[]{:S(2)}) collective-permute-start(bf16[8,10752]{1,0:T(8,128)(2,1)S(1)} %collective-permute-done.5.refs_0_), channel_id=1, source_target_pairs={{0,2},{1,3},{2,0},{3,1},{4,6},{5,7},{6,4},{7,5},{8,10},{9,11},{10,... | collective-permute-start | bytes 516104 | tf_op jit(solution)/shard_map/ppermute | solution.py:248
  21.1 1.9 %collective-permute-start.16 = (bf16[8,10752]{1,0:T(8,128)(2,1)S(1)}, bf16[8,10752]{1,0:T(8,128)(2,1)S(1)}, u32[]{:S(2)}, u32[]{:S(2)}) collective-permute-start(bf16[8,10752]{1,0:T(8,128)(2,1)S(1)} %get-tuple-element.30), channel_id=1, source_target_pairs={{0,12},{1,13},{2,14},{3,15},{4,0},{5,1},{6,2},{7,3},{8,4},{9,5},{1... | collective-permute-start | bytes 516104 | tf_op jit(solution)/shard_map/ppermute | solution.py:245
  23.0 0.0 collective-permute-start.7
  23.0 2.8 %collective-permute-done.6.refs_1_ = bf16[8,10752]{1,0:T(8,128)(2,1)S(1)} collective-permute-done((bf16[8,10752]{1,0:T(8,128)(2,1)S(1)}, bf16[8,10752]{1,0:T(8,128)(2,1)S(1)}, u32[]{:S(2)}, u32[]{:S(2)}) %collective-permute-start.6) | collective-permute-done | bytes 172064 | tf_op jit(solution)/shard_map/ppermute | solution.py:248
  25.8 0.0 collective-permute-start.8
  25.8 0.0 collective-permute-done.3
  25.8 0.0 collective-permute-done.7.refs_2_
  25.9 1.3 %collective-permute-done.8.refs_3_ = bf16[8,10752]{1,0:T(8,128)(2,1)S(1)} collective-permute-done((bf16[8,10752]{1,0:T(8,128)(2,1)S(1)}, bf16[8,10752]{1,0:T(8,128)(2,1)S(1)}, u32[]{:S(2)}, u32[]{:S(2)}) %collective-permute-start.8) | collective-permute-done | bytes 172064 | tf_op jit(solution)/shard_map/ppermute | solution.py:251
  27.2 2.1 %shard_map.76 = (bf16[16,10752]{1,0:T(8,128)(2,1)S(1)}, bf16[16,10752]{1,0:T(8,128)(2,1)S(1)}) custom-call(bf16[8,10752]{1,0:T(8,128)(2,1)S(1)} %collective-permute-done.5.refs_0_, bf16[8,10752]{1,0:T(8,128)(2,1)S(1)} %collective-permute-done.6.refs_1_, bf16[8,10752]{1,0:T(8,128)(2,1)S(1)} %collective-permute-done.7.refs_2_, ...), custom_call_target="tpu_custom_call" | custom-call | tf_op jit(solution)/shard_map/pallas_call | solution.py:167
  29.3 0.2 collective-permute-start.9
  29.5 0.0 collective-permute-done.16.refs_0_
  29.5 1.5 %collective-permute-start.17 = (bf16[8,10752]{1,0:T(8,128)(2,1)S(1)}, bf16[8,10752]{1,0:T(8,128)(2,1)S(1)}, u32[]{:S(2)}, u32[]{:S(2)}) collective-permute-start(bf16[8,10752]{1,0:T(8,128)(2,1)S(1)} %collective-permute-done.16.refs_0_), channel_id=1, source_target_pairs={{0,2},{1,3},{2,0},{3,1},{4,6},{5,7},{6,4},{7,5},{8,10},{9,11},{10,... | collective-permute-start | bytes 516104 | tf_op jit(solution)/shard_map/ppermute | solution.py:248
  31.0 2.6 %collective-permute-start.12 = (bf16[8,10752]{1,0:T(8,128)(2,1)S(1)}, bf16[8,10752]{1,0:T(8,128)(2,1)S(1)}, u32[]{:S(2)}, u32[]{:S(2)}) collective-permute-start(bf16[8,10752]{1,0:T(8,128)(2,1)S(1)} %get-tuple-element.29), channel_id=1, source_target_pairs={{0,8},{1,9},{2,10},{3,11},{4,12},{5,13},{6,14},{7,15},{8,0},{9,1},... | collective-permute-start | bytes 516104 | tf_op jit(solution)/shard_map/ppermute | solution.py:245
  33.6 2.6 %collective-permute-done.17.refs_1_ = bf16[8,10752]{1,0:T(8,128)(2,1)S(1)} collective-permute-done((bf16[8,10752]{1,0:T(8,128)(2,1)S(1)}, bf16[8,10752]{1,0:T(8,128)(2,1)S(1)}, u32[]{:S(2)}, u32[]{:S(2)}) %collective-permute-start.17) | collective-permute-done | bytes 172064 | tf_op jit(solution)/shard_map/ppermute | solution.py:248
  36.1 0.0 collective-permute-start.19
  36.1 0.0 collective-permute-done.9
  36.2 0.0 collective-permute-done.18.refs_2_
  36.2 1.3 %collective-permute-done.19.refs_3_ = bf16[8,10752]{1,0:T(8,128)(2,1)S(1)} collective-permute-done((bf16[8,10752]{1,0:T(8,128)(2,1)S(1)}, bf16[8,10752]{1,0:T(8,128)(2,1)S(1)}, u32[]{:S(2)}, u32[]{:S(2)}) %collective-permute-start.19) | collective-permute-done | bytes 172064 | tf_op jit(solution)/shard_map/ppermute | solution.py:251
  37.5 2.1 %shard_map.77 = (bf16[16,10752]{1,0:T(8,128)(2,1)S(1)}, bf16[16,10752]{1,0:T(8,128)(2,1)S(1)}) custom-call(bf16[8,10752]{1,0:T(8,128)(2,1)S(1)} %collective-permute-done.16.refs_0_, bf16[8,10752]{1,0:T(8,128)(2,1)S(1)} %collective-permute-done.17.refs_1_, bf16[8,10752]{1,0:T(8,128)(2,1)S(1)} %collective-permute-done.18.refs_2_, ...), custom_call_target="tpu_custom_call" | custom-call | tf_op jit(solution)/shard_map/pallas_call | solution.py:167
  39.6 0.2 collective-permute-start.20
  39.8 2.1 %collective-permute-done.12.refs_0_ = bf16[8,10752]{1,0:T(8,128)(2,1)S(1)} collective-permute-done((bf16[8,10752]{1,0:T(8,128)(2,1)S(1)}, bf16[8,10752]{1,0:T(8,128)(2,1)S(1)}, u32[]{:S(2)}, u32[]{:S(2)}) %collective-permute-start.12) | collective-permute-done | bytes 172064 | tf_op jit(solution)/shard_map/ppermute | solution.py:245
  41.9 0.6 collective-permute-start.13
  42.5 4.9 %collective-permute-done.13.refs_1_ = bf16[8,10752]{1,0:T(8,128)(2,1)S(1)} collective-permute-done((bf16[8,10752]{1,0:T(8,128)(2,1)S(1)}, bf16[8,10752]{1,0:T(8,128)(2,1)S(1)}, u32[]{:S(2)}, u32[]{:S(2)}) %collective-permute-start.13) | collective-permute-done | bytes 172064 | tf_op jit(solution)/shard_map/ppermute | solution.py:248
  47.4 0.6 collective-permute-start.4
  48.0 1.5 %collective-permute-start.10 = (bf16[8,10752]{1,0:T(8,128)(2,1)S(1)}, bf16[8,10752]{1,0:T(8,128)(2,1)S(1)}, u32[]{:S(2)}, u32[]{:S(2)}) collective-permute-start(bf16[8,10752]{1,0:T(8,128)(2,1)S(1)} %add_convert_fusion.5.refs_7_), channel_id=1, source_target_pairs={{0,2},{1,3},{2,0},{3,1},{4,6},{5,7},{6,4},{7,5},{8,10},{9,11},{10,... | collective-permute-start | bytes 516104 | tf_op jit(solution)/shard_map/ppermute | solution.py:248
  49.4 0.0 collective-permute-done.20
  49.5 0.0 copy-start.2
  49.5 0.0 copy-start.4
  49.5 0.0 copy-start.5
  49.5 0.0 collective-permute-done.15.refs_3_
  49.5 2.1 %shard_map.78 = (bf16[16,10752]{1,0:T(8,128)(2,1)S(1)}, bf16[16,10752]{1,0:T(8,128)(2,1)S(1)}) custom-call(bf16[8,10752]{1,0:T(8,128)(2,1)S(1)} %collective-permute-done.12.refs_0_, bf16[8,10752]{1,0:T(8,128)(2,1)S(1)} %collective-permute-done.13.refs_1_, bf16[8,10752]{1,0:T(8,128)(2,1)S(1)} %collective-permute-done.14.refs_2_, ...), custom_call_target="tpu_custom_call" | custom-call | tf_op jit(solution)/shard_map/pallas_call | solution.py:167
  51.6 0.1 collective-permute-start.21
  51.7 6.2 %collective-permute-done.10 = bf16[8,10752]{1,0:T(8,128)(2,1)S(1)} collective-permute-done((bf16[8,10752]{1,0:T(8,128)(2,1)S(1)}, bf16[8,10752]{1,0:T(8,128)(2,1)S(1)}, u32[]{:S(2)}, u32[]{:S(2)}) %collective-permute-start.10) | collective-permute-done | bytes 172064 | tf_op jit(solution)/shard_map/ppermute | solution.py:248
  57.9 0.1 add_convert_fusion.4
  58.0 2.3 %collective-permute-start.11 = (bf16[8,10752]{1,0:T(8,128)(2,1)S(1)}, bf16[8,10752]{1,0:T(8,128)(2,1)S(1)}, u32[]{:S(2)}, u32[]{:S(2)}) collective-permute-start(bf16[8,10752]{1,0:T(8,128)(2,1)S(1)} %add_convert_fusion.4), channel_id=1, source_target_pairs={{0,12},{1,13},{2,14},{3,15},{4,0},{5,1},{6,2},{7,3},{8,4},{9,5},{1... | collective-permute-start | bytes 516104 | tf_op jit(solution)/shard_map/ppermute | solution.py:245
  60.3 0.5 collective-permute-start.24
  60.8 0.0 collective-permute-done.21
  60.8 1.6 %collective-permute-start.22 = (bf16[8,10752]{1,0:T(8,128)(2,1)S(1)}, bf16[8,10752]{1,0:T(8,128)(2,1)S(1)}, u32[]{:S(2)}, u32[]{:S(2)}) collective-permute-start(bf16[8,10752]{1,0:T(8,128)(2,1)S(1)} %add_convert_fusion.2), channel_id=1, source_target_pairs={{0,2},{1,3},{2,0},{3,1},{4,6},{5,7},{6,4},{7,5},{8,10},{9,11},{10,... | collective-permute-start | bytes 516104 | tf_op jit(solution)/shard_map/ppermute | solution.py:248
  62.4 5.2 %collective-permute-done.24 = bf16[8,10752]{1,0:T(8,128)(2,1)S(1)} collective-permute-done((bf16[8,10752]{1,0:T(8,128)(2,1)S(1)}, bf16[8,10752]{1,0:T(8,128)(2,1)S(1)}, u32[]{:S(2)}, u32[]{:S(2)}) %collective-permute-start.24) | collective-permute-done | bytes 172064 | tf_op jit(solution)/shard_map/ppermute | solution.py:248
  67.6 0.1 add_convert_fusion
  67.6 0.1 collective-permute-start.25
  67.7 2.0 %collective-permute-done.22 = bf16[8,10752]{1,0:T(8,128)(2,1)S(1)} collective-permute-done((bf16[8,10752]{1,0:T(8,128)(2,1)S(1)}, bf16[8,10752]{1,0:T(8,128)(2,1)S(1)}, u32[]{:S(2)}, u32[]{:S(2)}) %collective-permute-start.22) | collective-permute-done | bytes 172064 | tf_op jit(solution)/shard_map/ppermute | solution.py:248
  69.7 0.1 add_convert_fusion.1
  69.8 0.1 collective-permute-start.23
  69.8 0.1 add_convert_fusion.6.refs_0_
  69.9 0.0 collective-permute-done.11.refs_1_
  69.9 5.0 %collective-permute-done.25.refs_3_ = bf16[8,10752]{1,0:T(8,128)(2,1)S(1)} collective-permute-done((bf16[8,10752]{1,0:T(8,128)(2,1)S(1)}, bf16[8,10752]{1,0:T(8,128)(2,1)S(1)}, u32[]{:S(2)}, u32[]{:S(2)}) %collective-permute-start.25) | collective-permute-done | bytes 172064 | tf_op jit(solution)/shard_map/ppermute | solution.py:245
  74.9 5.3 %collective-permute-done.23.refs_2_ = bf16[8,10752]{1,0:T(8,128)(2,1)S(1)} collective-permute-done((bf16[8,10752]{1,0:T(8,128)(2,1)S(1)}, bf16[8,10752]{1,0:T(8,128)(2,1)S(1)}, u32[]{:S(2)}, u32[]{:S(2)}) %collective-permute-start.23) | collective-permute-done | bytes 172064 | tf_op jit(solution)/shard_map/ppermute | solution.py:245
  80.3 1.9 %shard_map.79 = bf16[16,7168]{1,0:T(8,128)(2,1)} custom-call(s32[4]{0:T(128)S(1)} %copy-done.4, s32[2,16]{1,0:T(2,128)S(1)} %bitcast.3, f32[2,16]{1,0:T(2,128)S(1)} %bitcast.4, bf16[8,10752]{1,0:T(8,128)(2,1)S(1)} %add_convert_fusion.6.refs_0_, bf16[8,10752]{1,0:T(8,128)(2,1)S(1)} %collective-permute-done.11.refs_1_, ...), custom_call_target="tpu_custom_call" | custom-call | flops 44040192 | bytes 1146880 | tf_op jit(solution)/shard_map/pallas_call | solution.py:219
  (15 shorter events, 0.2 us)
Async XLA Ops:
  0.0 0.9 %copy-start = (bf16[16,7168]{1,0:T(8,128)(2,1)S(1)}, bf16[16,7168]{1,0:T(8,128)(2,1)}, u32[]{:S(2)}) copy-start(bf16[16,7168]{1,0:T(8,128)(2,1)} %tokens_ref.1) | copy-start | bytes 688132
  0.9 0.7 copy-start.1
  1.6 0.7 copy-start.3
  3.3 7.4 %collective-permute-start = (bf16[8,10752]{1,0:T(8,128)(2,1)S(1)}, bf16[8,10752]{1,0:T(8,128)(2,1)S(1)}, u32[]{:S(2)}, u32[]{:S(2)}) collective-permute-start(bf16[8,10752]{1,0:T(8,128)(2,1)S(1)} %get-tuple-element.20.refs_3_.refs_0_), channel_id=1, source_target_pairs={{0,2},{1,3},{2,0},{3,1},{4,6},{5,7},{6,4},{7,5},{8,10},{9,11},{10,... | collective-permute-start | bytes 516104 | tf_op jit(solution)/shard_map/ppermute | solution.py:248
  6.3 10.4 %collective-permute-start.1 = (bf16[8,10752]{1,0:T(8,128)(2,1)S(1)}, bf16[8,10752]{1,0:T(8,128)(2,1)S(1)}, u32[]{:S(2)}, u32[]{:S(2)}) collective-permute-start(bf16[8,10752]{1,0:T(8,128)(2,1)S(1)} %get-tuple-element.20.refs_3_.refs_0_), channel_id=1, source_target_pairs={{0,1},{1,0},{2,3},{3,2},{4,5},{5,4},{6,7},{7,6},{8,9},{9,8},{10,11... | collective-permute-start | bytes 516104 | tf_op jit(solution)/shard_map/ppermute | solution.py:251
  10.7 6.1 %collective-permute-start.2 = (bf16[8,10752]{1,0:T(8,128)(2,1)S(1)}, bf16[8,10752]{1,0:T(8,128)(2,1)S(1)}, u32[]{:S(2)}, u32[]{:S(2)}) collective-permute-start(bf16[8,10752]{1,0:T(8,128)(2,1)S(1)} %collective-permute-done.refs_1_), channel_id=1, source_target_pairs={{0,1},{1,0},{2,3},{3,2},{4,5},{5,4},{6,7},{7,6},{8,9},{9,8},{10,11... | collective-permute-start | bytes 516104 | tf_op jit(solution)/shard_map/ppermute | solution.py:251
  10.7 8.9 %collective-permute-start.5 = (bf16[8,10752]{1,0:T(8,128)(2,1)S(1)}, bf16[8,10752]{1,0:T(8,128)(2,1)S(1)}, u32[]{:S(2)}, u32[]{:S(2)}) collective-permute-start(bf16[8,10752]{1,0:T(8,128)(2,1)S(1)} %get-tuple-element.26), channel_id=1, source_target_pairs={{0,4},{1,5},{2,6},{3,7},{4,8},{5,9},{6,10},{7,11},{8,12},{9,13},{1... | collective-permute-start | bytes 516104 | tf_op jit(solution)/shard_map/ppermute | solution.py:245
  18.9 6.9 %collective-permute-start.3 = (bf16[16,10752]{1,0:T(8,128)(2,1)S(1)}, bf16[16,10752]{1,0:T(8,128)(2,1)S(1)}, u32[]{:S(2)}, u32[]{:S(2)}) collective-permute-start(bf16[16,10752]{1,0:T(8,128)(2,1)S(1)} %get-tuple-element.25), channel_id=1, source_target_pairs={{0,1},{1,0},{2,3},{3,2},{4,5},{5,4},{6,7},{7,6},{8,9},{9,8},{10,11... | collective-permute-start | bytes 1032200 | tf_op jit(solution)/shard_map/ppermute | solution.py:251
  19.6 6.2 %collective-permute-start.6 = (bf16[8,10752]{1,0:T(8,128)(2,1)S(1)}, bf16[8,10752]{1,0:T(8,128)(2,1)S(1)}, u32[]{:S(2)}, u32[]{:S(2)}) collective-permute-start(bf16[8,10752]{1,0:T(8,128)(2,1)S(1)} %collective-permute-done.5.refs_0_), channel_id=1, source_target_pairs={{0,2},{1,3},{2,0},{3,1},{4,6},{5,7},{6,4},{7,5},{8,10},{9,11},{10,... | collective-permute-start | bytes 516104 | tf_op jit(solution)/shard_map/ppermute | solution.py:248
  21.1 8.4 %collective-permute-start.16 = (bf16[8,10752]{1,0:T(8,128)(2,1)S(1)}, bf16[8,10752]{1,0:T(8,128)(2,1)S(1)}, u32[]{:S(2)}, u32[]{:S(2)}) collective-permute-start(bf16[8,10752]{1,0:T(8,128)(2,1)S(1)} %get-tuple-element.30), channel_id=1, source_target_pairs={{0,12},{1,13},{2,14},{3,15},{4,0},{5,1},{6,2},{7,3},{8,4},{9,5},{1... | collective-permute-start | bytes 516104 | tf_op jit(solution)/shard_map/ppermute | solution.py:245
  23.0 2.9 %collective-permute-start.7 = (bf16[8,10752]{1,0:T(8,128)(2,1)S(1)}, bf16[8,10752]{1,0:T(8,128)(2,1)S(1)}, u32[]{:S(2)}, u32[]{:S(2)}) collective-permute-start(bf16[8,10752]{1,0:T(8,128)(2,1)S(1)} %collective-permute-done.5.refs_0_), channel_id=1, source_target_pairs={{0,1},{1,0},{2,3},{3,2},{4,5},{5,4},{6,7},{7,6},{8,9},{9,8},{10,11... | collective-permute-start | bytes 516104 | tf_op jit(solution)/shard_map/ppermute | solution.py:251
  25.8 1.4 %collective-permute-start.8 = (bf16[8,10752]{1,0:T(8,128)(2,1)S(1)}, bf16[8,10752]{1,0:T(8,128)(2,1)S(1)}, u32[]{:S(2)}, u32[]{:S(2)}) collective-permute-start(bf16[8,10752]{1,0:T(8,128)(2,1)S(1)} %collective-permute-done.6.refs_1_), channel_id=1, source_target_pairs={{0,1},{1,0},{2,3},{3,2},{4,5},{5,4},{6,7},{7,6},{8,9},{9,8},{10,11... | collective-permute-start | bytes 516104 | tf_op jit(solution)/shard_map/ppermute | solution.py:251
  29.3 6.9 %collective-permute-start.9 = (bf16[16,10752]{1,0:T(8,128)(2,1)S(1)}, bf16[16,10752]{1,0:T(8,128)(2,1)S(1)}, u32[]{:S(2)}, u32[]{:S(2)}) collective-permute-start(bf16[16,10752]{1,0:T(8,128)(2,1)S(1)} %get-tuple-element.28), channel_id=1, source_target_pairs={{0,1},{1,0},{2,3},{3,2},{4,5},{5,4},{6,7},{7,6},{8,9},{9,8},{10,11... | collective-permute-start | bytes 1032200 | tf_op jit(solution)/shard_map/ppermute | solution.py:251
  29.5 6.6 %collective-permute-start.17 = (bf16[8,10752]{1,0:T(8,128)(2,1)S(1)}, bf16[8,10752]{1,0:T(8,128)(2,1)S(1)}, u32[]{:S(2)}, u32[]{:S(2)}) collective-permute-start(bf16[8,10752]{1,0:T(8,128)(2,1)S(1)} %collective-permute-done.16.refs_0_), channel_id=1, source_target_pairs={{0,2},{1,3},{2,0},{3,1},{4,6},{5,7},{6,4},{7,5},{8,10},{9,11},{10,... | collective-permute-start | bytes 516104 | tf_op jit(solution)/shard_map/ppermute | solution.py:248
  31.0 10.9 %collective-permute-start.12 = (bf16[8,10752]{1,0:T(8,128)(2,1)S(1)}, bf16[8,10752]{1,0:T(8,128)(2,1)S(1)}, u32[]{:S(2)}, u32[]{:S(2)}) collective-permute-start(bf16[8,10752]{1,0:T(8,128)(2,1)S(1)} %get-tuple-element.29), channel_id=1, source_target_pairs={{0,8},{1,9},{2,10},{3,11},{4,12},{5,13},{6,14},{7,15},{8,0},{9,1},... | collective-permute-start | bytes 516104 | tf_op jit(solution)/shard_map/ppermute | solution.py:245
  33.6 2.6 %collective-permute-start.18 = (bf16[8,10752]{1,0:T(8,128)(2,1)S(1)}, bf16[8,10752]{1,0:T(8,128)(2,1)S(1)}, u32[]{:S(2)}, u32[]{:S(2)}) collective-permute-start(bf16[8,10752]{1,0:T(8,128)(2,1)S(1)} %collective-permute-done.16.refs_0_), channel_id=1, source_target_pairs={{0,1},{1,0},{2,3},{3,2},{4,5},{5,4},{6,7},{7,6},{8,9},{9,8},{10,11... | collective-permute-start | bytes 516104 | tf_op jit(solution)/shard_map/ppermute | solution.py:251
  36.1 1.4 %collective-permute-start.19 = (bf16[8,10752]{1,0:T(8,128)(2,1)S(1)}, bf16[8,10752]{1,0:T(8,128)(2,1)S(1)}, u32[]{:S(2)}, u32[]{:S(2)}) collective-permute-start(bf16[8,10752]{1,0:T(8,128)(2,1)S(1)} %collective-permute-done.17.refs_1_), channel_id=1, source_target_pairs={{0,1},{1,0},{2,3},{3,2},{4,5},{5,4},{6,7},{7,6},{8,9},{9,8},{10,11... | collective-permute-start | bytes 516104 | tf_op jit(solution)/shard_map/ppermute | solution.py:251
  39.6 9.8 %collective-permute-start.20 = (bf16[16,10752]{1,0:T(8,128)(2,1)S(1)}, bf16[16,10752]{1,0:T(8,128)(2,1)S(1)}, u32[]{:S(2)}, u32[]{:S(2)}) collective-permute-start(bf16[16,10752]{1,0:T(8,128)(2,1)S(1)} %get-tuple-element.32), channel_id=1, source_target_pairs={{0,1},{1,0},{2,3},{3,2},{4,5},{5,4},{6,7},{7,6},{8,9},{9,8},{10,11... | collective-permute-start | bytes 1032200 | tf_op jit(solution)/shard_map/ppermute | solution.py:251
  41.9 5.5 %collective-permute-start.13 = (bf16[8,10752]{1,0:T(8,128)(2,1)S(1)}, bf16[8,10752]{1,0:T(8,128)(2,1)S(1)}, u32[]{:S(2)}, u32[]{:S(2)}) collective-permute-start(bf16[8,10752]{1,0:T(8,128)(2,1)S(1)} %collective-permute-done.12.refs_0_), channel_id=1, source_target_pairs={{0,2},{1,3},{2,0},{3,1},{4,6},{5,7},{6,4},{7,5},{8,10},{9,11},{10,... | collective-permute-start | bytes 516104 | tf_op jit(solution)/shard_map/ppermute | solution.py:248
  42.5 7.1 %collective-permute-start.14 = (bf16[8,10752]{1,0:T(8,128)(2,1)S(1)}, bf16[8,10752]{1,0:T(8,128)(2,1)S(1)}, u32[]{:S(2)}, u32[]{:S(2)}) collective-permute-start(bf16[8,10752]{1,0:T(8,128)(2,1)S(1)} %collective-permute-done.12.refs_0_), channel_id=1, source_target_pairs={{0,1},{1,0},{2,3},{3,2},{4,5},{5,4},{6,7},{7,6},{8,9},{9,8},{10,11... | collective-permute-start | bytes 516104 | tf_op jit(solution)/shard_map/ppermute | solution.py:251
  47.4 2.1 %collective-permute-start.15 = (bf16[8,10752]{1,0:T(8,128)(2,1)S(1)}, bf16[8,10752]{1,0:T(8,128)(2,1)S(1)}, u32[]{:S(2)}, u32[]{:S(2)}) collective-permute-start(bf16[8,10752]{1,0:T(8,128)(2,1)S(1)} %collective-permute-done.13.refs_1_), channel_id=1, source_target_pairs={{0,1},{1,0},{2,3},{3,2},{4,5},{5,4},{6,7},{7,6},{8,9},{9,8},{10,11... | collective-permute-start | bytes 516104 | tf_op jit(solution)/shard_map/ppermute | solution.py:251
  47.4 22.4 %collective-permute-start.4 = (bf16[8,10752]{1,0:T(8,128)(2,1)S(1)}, bf16[8,10752]{1,0:T(8,128)(2,1)S(1)}, u32[]{:S(2)}, u32[]{:S(2)}) collective-permute-start(bf16[8,10752]{1,0:T(8,128)(2,1)S(1)} %add_convert_fusion.7.refs_7_), channel_id=1, source_target_pairs={{0,2},{1,3},{2,0},{3,1},{4,6},{5,7},{6,4},{7,5},{8,10},{9,11},{10,... | collective-permute-start | bytes 516104 | tf_op jit(solution)/shard_map/ppermute | solution.py:248
  48.0 9.9 %collective-permute-start.10 = (bf16[8,10752]{1,0:T(8,128)(2,1)S(1)}, bf16[8,10752]{1,0:T(8,128)(2,1)S(1)}, u32[]{:S(2)}, u32[]{:S(2)}) collective-permute-start(bf16[8,10752]{1,0:T(8,128)(2,1)S(1)} %add_convert_fusion.5.refs_7_), channel_id=1, source_target_pairs={{0,2},{1,3},{2,0},{3,1},{4,6},{5,7},{6,4},{7,5},{8,10},{9,11},{10,... | collective-permute-start | bytes 516104 | tf_op jit(solution)/shard_map/ppermute | solution.py:248
  49.5 30.8 %copy-start.2 = (s32[16,2]{0,1:T(2,128)S(1)}, s32[16,2]{0,1:T(2,128)}, u32[]{:S(2)}) copy-start(s32[16,2]{0,1:T(2,128)} %param.8) | copy-start | bytes 388
  49.5 30.8 %copy-start.4 = (s32[4]{0:T(128)S(1)}, s32[4]{0:T(128)}, u32[]{:S(2)}) copy-start(s32[4]{0:T(128)} %placement_ref.3) | copy-start | bytes 52
  49.5 30.7 %copy-start.5 = (f32[16,2]{0,1:T(2,128)S(1)}, f32[16,2]{0,1:T(2,128)}, u32[]{:S(2)}) copy-start(f32[16,2]{0,1:T(2,128)} %param.9) | copy-start | bytes 388
  51.6 9.2 %collective-permute-start.21 = (bf16[16,10752]{1,0:T(8,128)(2,1)S(1)}, bf16[16,10752]{1,0:T(8,128)(2,1)S(1)}, u32[]{:S(2)}, u32[]{:S(2)}) collective-permute-start(bf16[16,10752]{1,0:T(8,128)(2,1)S(1)} %get-tuple-element.34), channel_id=1, source_target_pairs={{0,1},{1,0},{2,3},{3,2},{4,5},{5,4},{6,7},{7,6},{8,9},{9,8},{10,11... | collective-permute-start | bytes 1032200 | tf_op jit(solution)/shard_map/ppermute | solution.py:251
  58.0 12.0 %collective-permute-start.11 = (bf16[8,10752]{1,0:T(8,128)(2,1)S(1)}, bf16[8,10752]{1,0:T(8,128)(2,1)S(1)}, u32[]{:S(2)}, u32[]{:S(2)}) collective-permute-start(bf16[8,10752]{1,0:T(8,128)(2,1)S(1)} %add_convert_fusion.4), channel_id=1, source_target_pairs={{0,12},{1,13},{2,14},{3,15},{4,0},{5,1},{6,2},{7,3},{8,4},{9,5},{1... | collective-permute-start | bytes 516104 | tf_op jit(solution)/shard_map/ppermute | solution.py:245
  60.3 7.3 %collective-permute-start.24 = (bf16[8,10752]{1,0:T(8,128)(2,1)S(1)}, bf16[8,10752]{1,0:T(8,128)(2,1)S(1)}, u32[]{:S(2)}, u32[]{:S(2)}) collective-permute-start(bf16[8,10752]{1,0:T(8,128)(2,1)S(1)} %add_convert_fusion.3.refs_7_), channel_id=1, source_target_pairs={{0,2},{1,3},{2,0},{3,1},{4,6},{5,7},{6,4},{7,5},{8,10},{9,11},{10,... | collective-permute-start | bytes 516104 | tf_op jit(solution)/shard_map/ppermute | solution.py:248
  60.8 8.8 %collective-permute-start.22 = (bf16[8,10752]{1,0:T(8,128)(2,1)S(1)}, bf16[8,10752]{1,0:T(8,128)(2,1)S(1)}, u32[]{:S(2)}, u32[]{:S(2)}) collective-permute-start(bf16[8,10752]{1,0:T(8,128)(2,1)S(1)} %add_convert_fusion.2), channel_id=1, source_target_pairs={{0,2},{1,3},{2,0},{3,1},{4,6},{5,7},{6,4},{7,5},{8,10},{9,11},{10,... | collective-permute-start | bytes 516104 | tf_op jit(solution)/shard_map/ppermute | solution.py:248
  67.6 7.3 %collective-permute-start.25 = (bf16[8,10752]{1,0:T(8,128)(2,1)S(1)}, bf16[8,10752]{1,0:T(8,128)(2,1)S(1)}, u32[]{:S(2)}, u32[]{:S(2)}) collective-permute-start(bf16[8,10752]{1,0:T(8,128)(2,1)S(1)} %add_convert_fusion), channel_id=1, source_target_pairs={{0,4},{1,5},{2,6},{3,7},{4,8},{5,9},{6,10},{7,11},{8,12},{9,13},{1... | collective-permute-start | bytes 516104 | tf_op jit(solution)/shard_map/ppermute | solution.py:245
  69.8 10.5 %collective-permute-start.23 = (bf16[8,10752]{1,0:T(8,128)(2,1)S(1)}, bf16[8,10752]{1,0:T(8,128)(2,1)S(1)}, u32[]{:S(2)}, u32[]{:S(2)}) collective-permute-start(bf16[8,10752]{1,0:T(8,128)(2,1)S(1)} %add_convert_fusion.1), channel_id=1, source_target_pairs={{0,8},{1,9},{2,10},{3,11},{4,12},{5,13},{6,14},{7,15},{8,0},{9,1},... | collective-permute-start | bytes 516104 | tf_op jit(solution)/shard_map/ppermute | solution.py:245

commit v4 on v3

--- a/solution.py
+++ b/solution.py
@@ -12,10 +12,15 @@
 SMEM = pl.BlockSpec(memory_space=pltpu.SMEM)
 ANYWHERE = pl.BlockSpec(memory_space=pl.ANY)
 LOADS = 4
+NO_COST = pl.CostEstimate(flops=0, bytes_accessed=0, transcendentals=0)
 
 
 def in_vmem(value):
     return pltpu.with_memory_space_constraint(value, pltpu.VMEM)
+
+
+def in_hbm(value):
+    return pltpu.with_memory_space_constraint(value, pltpu.HBM)
 
 
 def product(lhs, rhs):
@@ -52,14 +57,14 @@
     return jnp.where(row < half, row, half + row % quarter).astype(jnp.float32)
 
 
-def pack_kernel(n_blocks, parts, placement_ref, ids_ref, tokens_ref, *out_refs):
+def pack_kernel(n_blocks, parts, distances, placement_ref, ids_ref, tokens_ref, *refs):
     rows, width = tokens_ref.shape
     half, quarter = rows // 2, rows // 4
     block = lax.axis_index("node") // parts
     experts, picks, earlier = slots_of(ids_ref[...], n_blocks)
     wanted = bucket_rows(rows)
     upper = lax.broadcasted_iota(jnp.int32, (half, width // 2), 0) < quarter
-    for k, out_ref in enumerate(out_refs):
+    for k, out_ref in zip(distances, refs[-len(distances) :]):
         expert = expert_at(placement_ref, lax.rem(block + k, n_blocks))
         named = row_of(picks, experts, expert) > 0.5
         slot = row_of(earlier, experts, expert)
@@ -70,21 +75,34 @@
         out_ref[:, width:] = rest.astype(jnp.bfloat16)
 
 
-def pack(placement, ids, tokens, n_blocks, parts):
+def pack(placement, ids, tokens, n_blocks, parts, distances, after):
     rows, width = tokens.shape
     shape = pltpu.VMEM((rows // 2, width + width // 2), jnp.bfloat16)
+    out = pl.pallas_call(
+        functools.partial(pack_kernel, n_blocks, parts, distances),
+        out_shape=[shape] * len(distances),
+        in_specs=[SMEM, VMEM, VMEM] + [ANYWHERE] * len(after),
+        out_specs=[VMEM] * len(distances),
+        compiler_params=pltpu.CompilerParams(vmem_limit_bytes=VMEM_BYTES),
+        cost_estimate=NO_COST,
+    )(in_hbm(placement), in_hbm(ids), in_hbm(tokens), *after)
+    return dict(zip(distances, out))
+
+
+def nothing(*refs):
+    pass
+
+
+def when(value, after):
     return pl.pallas_call(
-        functools.partial(pack_kernel, n_blocks, parts),
-        out_shape=[shape] * n_blocks,
-        in_specs=[SMEM, VMEM, VMEM],
-        out_specs=[VMEM] * n_blocks,
-        compiler_params=pltpu.CompilerParams(vmem_limit_bytes=VMEM_BYTES),
-        cost_estimate=pl.CostEstimate(
-            flops=2 * n_blocks * rows * rows * width,
-            bytes_accessed=2 * (n_blocks + 1) * rows * width,
-            transcendentals=0,
-        ),
-    )(placement, ids, tokens)
+        nothing,
+        out_shape=pltpu.VMEM(value.shape, value.dtype),
+        in_specs=[ANYWHERE] * (1 + len(after)),
+        out_specs=ANYWHERE,
+        input_output_aliases={0: 0},
+        compiler_params=pltpu.CompilerParams(vmem_limit_bytes=VMEM_BYTES),
+        cost_estimate=NO_COST,
+    )(in_vmem(value), *after)
 
 
 def load_kernel(*refs):
@@ -109,9 +127,7 @@
         out_specs=[VMEM] * 3,
         scratch_shapes=[pltpu.SemaphoreType.DMA((3, LOADS))],
         compiler_params=pltpu.CompilerParams(vmem_limit_bytes=VMEM_BYTES),
-        cost_estimate=pl.CostEstimate(
-            flops=0, bytes_accessed=0, transcendentals=0
-        ),
+        cost_estimate=NO_COST,
     )(*[pltpu.with_memory_space_constraint(w, pltpu.HBM) for w in weights], after)
 
 
@@ -170,9 +186,7 @@
         in_specs=[VMEM] * 7 + [ANYWHERE] * len(after),
         out_specs=[VMEM] * 2,
         compiler_params=pltpu.CompilerParams(vmem_limit_bytes=VMEM_BYTES),
-        cost_estimate=pl.CostEstimate(
-            flops=0, bytes_accessed=0, transcendentals=0
-        ),
+        cost_estimate=NO_COST,
     )(*operands, *after)
 
 
@@ -250,27 +264,52 @@
     def along_core(value):
         return lax.ppermute(value, "node", [(i, i ^ 1) for i in range(devices)])
 
-    order = sorted(range(n_blocks), key=lambda k: (min(k, n_blocks - k), k))
     ids = expert_ids.T
-    buckets = pack(placement, ids, tokens, n_blocks, parts)
-    across, straight = {0: along_y(buckets[0])}, {0: buckets[0]}
-    for k in order[1:]:
+    groups = [sorted({d, n_blocks - d}) for d in range(1, n_blocks // 2 + 1)]
+    buckets = pack(placement, ids, tokens, n_blocks, parts, [0] + groups[0], [])
+    straight, across, theirs = {0: buckets[0]}, {0: along_y(buckets[0])}, {}
+    results, both, home, kept, sent, returned = {}, {}, {}, {}, {}, {}
+    for k in groups[0]:
         straight[k] = along_z(buckets[k], k)
     weights = load((gate_weight, up_weight, down_weight), buckets[0])
-    results = [None] * n_blocks
-    after = []
-    for k in order:
+
+    def compute(k, after):
+        theirs[k] = [along_core(straight[k]), along_core(across[k])]
+        pieces = [straight[k], across[k]] + theirs[k]
+        kept[k], sent[k] = run_experts(pieces, weights, after)
+        returned[k] = along_core(sent[k])
+        both[k] = add(kept[k][half:], returned[k][half:])
+
+    def go_home(k, after):
+        back = along_y(both[k] if k else when(both[k], after))
+        home[k] = add(kept[k][:half], returned[k][:half], back)
         if k:
+            value = when(home[k], after) if after else home[k]
+            results[k] = along_z(value, -k)
+        else:
+            results[k] = home[k]
+
+    compute(0, [])
+    for g, group in enumerate(groups):
+        if g:
+            earlier = groups[g - 1]
+            after = [straight[k] for k in earlier] + [across[0], weights[0]][: 2 if g == 1 else 0]
+            buckets = pack(placement, ids, tokens, n_blocks, parts, group, after)
+            after = [across[k] for k in earlier] + [both[earlier[0]]]
+            for k in group:
+                straight[k] = when(along_z(buckets[k], k), after)
+        for k in group:
             across[k] = along_y(straight[k])
-        pieces = [straight[k], across[k], along_core(straight[k]), along_core(across[k])]
-        kept, sent = run_experts(pieces, weights, after)
-        returned = along_core(sent)
-        both = add(kept[half:], returned[half:])
-        after = [both]
-        back = along_y(both)
-        home = add(kept[:half], returned[:half], back)
-        results[k] = along_z(home, -k) if k else home
-    return mix(placement, ids, gates.T, results, n_blocks, parts)
+        if g:
+            after = [home[earlier[0]]] + [both[k] for k in earlier[1:]]
+        else:
+            after = [sent[0]]
+        for k in group:
+            compute(k, after)
+        for k in group:
+            go_home(k, [results[earlier[0]]] if g else [])
+    go_home(0, [home[groups[-1][-1]]])
+    return mix(placement, ids, gates.T, [results[k] for k in range(n_blocks)], n_blocks, parts)
 
 
 def solution(mesh):

time: 82.3 us -> 77.2 us (0.938)
  waiting for transfers between devices: 43.5 us -> 35.1 us
  starting transfers between devices: 20.2 us -> 24.3 us
  local copies, waits for them, and re-layouts: 2.29 us -> 0.02 us
  Pallas kernels: 15.4 us -> 17.1 us
    ppermute x8, waiting for transfers between devices: 28 us -> 11.8 us  [along_y(): return lax.ppermute(value, 'node', [(i, i ^ 2) for i in range(devices)])]
    ppermute x6, waiting for transfers between devices: 12.8 us -> 20.7 us  [along_z(): return lax.ppermute(value, 'node', pairs)]
    ppermute x6, starting transfers between devices: 8.71 us -> 11 us  [along_z(): return lax.ppermute(value, 'node', pairs)]
    unnamed x12 -> x6, local copies, waits for them, and re-layouts: 2.29 us -> 0.02 us
    pallas_call x1 -> x5, Pallas kernels: 1.03 us -> 2.68 us  [the longest x2 2.67 us: pack(): pl.pallas_call(functools.partial(pack_kernel, n_blocks, parts, distances)...]
    ppermute x12, starting transfers between devices: 0.81 us -> 1.97 us  [along_core(): return lax.ppermute(value, 'node', [(i, i ^ 1) for i in range(devices)])]
  transfers between devices with their start and end apart: 26 -> 26, of which waited for: 13 -> 11; matrix products, arithmetic and copies ran while one was open for 1% -> 1% of each run, Pallas kernels for 15% -> 15%
where the time goes in v4:
time: 77.2 us; the launch traced here: 77.1 us
  waiting for transfers between devices  35.1 us (45%)
  starting transfers between devices  24.3 us (31%)
  Pallas kernels  17.1 us (22%)
    ppermute x6, waiting for transfers between devices, along_z(): return lax.ppermute(value, 'node', pairs)  20.7 us
    ppermute x8, waiting for transfers between devices, along_y(): return lax.ppermute(value, 'node', [(i, i ^ 2) for i in range(devices)])  11.8 us
    ppermute x8, starting transfers between devices, along_y(): return lax.ppermute(value, 'node', [(i, i ^ 2) for i in range(devices)])  11.3 us
    ppermute x6, starting transfers between devices, along_z(): return lax.ppermute(value, 'node', pairs)  11 us
    pallas_call x4, Pallas kernels, run_experts(): pl.pallas_call(experts_kernel, out_shape=[shape] * 2, in_specs=[VMEM] * 7...  8.27 us
    pallas_call x1, Pallas kernels, load(): pl.pallas_call(load_kernel, out_shape=[pltpu.VMEM(w.shape, w.dtype) for w...  4.25 us
    pallas_call x2, Pallas kernels, pack(): pl.pallas_call(functools.partial(pack_kernel, n_blocks, parts, distances)...  2.67 us
    ppermute x12, waiting for transfers between devices, along_core(): return lax.ppermute(value, 'node', [(i, i ^ 1) for i in range(devices)])  2.49 us
  transfers between devices with their start and end apart: 26, of which 11 were waited for; matrix products, arithmetic and copies ran while one was open for 1% of the time, Pallas kernels for 15%

profile of v4, /device:TPU:0, one launch (start us, length us, event | category | flops | bytes accessed | tf_op | source)
XLA Modules:
  0.0 77.1 jit_solution(7451712877806389825)
XLA Ops:
  0.0 1.4 %shard_map.73 = (bf16[8,10752]{1,0:T(8,128)(2,1)S(1)}, bf16[8,10752]{1,0:T(8,128)(2,1)S(1)}, bf16[8,10752]{1,0:T(8,128)(2,1)S(1)}) custom-call(s32[4]{0:T(128)} %placement_ref.5, s32[2,16]{1,0:T(2,128)} %bitcast.2, bf16[16,7168]{1,0:T(8,128)(2,1)} %tokens_ref.3), custom_call_target="tpu_custom_call" | custom-call | tf_op jit(solution)/shard_map/pallas_call | solution.py:81
  1.4 3.1 %collective-permute-start.4 = (bf16[8,10752]{1,0:T(8,128)(2,1)S(1)}, bf16[8,10752]{1,0:T(8,128)(2,1)S(1)}, u32[]{:S(2)}, u32[]{:S(2)}) collective-permute-start(bf16[8,10752]{1,0:T(8,128)(2,1)S(1)} %get-tuple-element.25), channel_id=1, source_target_pairs={{0,4},{1,5},{2,6},{3,7},{4,8},{5,9},{6,10},{7,11},{8,12},{9,13},{1... | collective-permute-start | bytes 516104 | tf_op jit(solution)/shard_map/ppermute | solution.py:259
  4.5 1.5 %collective-permute-start = (bf16[8,10752]{1,0:T(8,128)(2,1)S(1)}, bf16[8,10752]{1,0:T(8,128)(2,1)S(1)}, u32[]{:S(2)}, u32[]{:S(2)}) collective-permute-start(bf16[8,10752]{1,0:T(8,128)(2,1)S(1)} %get-tuple-element.19.refs_3_.refs_0_), channel_id=1, source_target_pairs={{0,2},{1,3},{2,0},{3,1},{4,6},{5,7},{6,4},{7,5},{8,10},{9,11},{10,... | collective-permute-start | bytes 516104 | tf_op jit(solution)/shard_map/ppermute | solution.py:262
  6.0 4.9 %collective-permute-done.4.refs_0_ = bf16[8,10752]{1,0:T(8,128)(2,1)S(1)} collective-permute-done((bf16[8,10752]{1,0:T(8,128)(2,1)S(1)}, bf16[8,10752]{1,0:T(8,128)(2,1)S(1)}, u32[]{:S(2)}, u32[]{:S(2)}) %collective-permute-start.4) | collective-permute-done | bytes 172064 | tf_op jit(solution)/shard_map/ppermute | solution.py:259
  10.9 1.5 %collective-permute-start.7 = (bf16[8,10752]{1,0:T(8,128)(2,1)S(1)}, bf16[8,10752]{1,0:T(8,128)(2,1)S(1)}, u32[]{:S(2)}, u32[]{:S(2)}) collective-permute-start(bf16[8,10752]{1,0:T(8,128)(2,1)S(1)} %collective-permute-done.4.refs_0_), channel_id=1, source_target_pairs={{0,2},{1,3},{2,0},{3,1},{4,6},{5,7},{6,4},{7,5},{8,10},{9,11},{10,... | collective-permute-start | bytes 516104 | tf_op jit(solution)/shard_map/ppermute | solution.py:262
  12.4 1.7 %collective-permute-start.5 = (bf16[8,10752]{1,0:T(8,128)(2,1)S(1)}, bf16[8,10752]{1,0:T(8,128)(2,1)S(1)}, u32[]{:S(2)}, u32[]{:S(2)}) collective-permute-start(bf16[8,10752]{1,0:T(8,128)(2,1)S(1)} %get-tuple-element.26), channel_id=1, source_target_pairs={{0,12},{1,13},{2,14},{3,15},{4,0},{5,1},{6,2},{7,3},{8,4},{9,5},{1... | collective-permute-start | bytes 516104 | tf_op jit(solution)/shard_map/ppermute | solution.py:259
  14.1 0.0 collective-permute-start.1
  14.1 0.0 collective-permute-done.refs_1_.refs_2_
  14.1 0.5 collective-permute-start.2
  14.7 0.0 collective-permute-start.9
  14.7 1.8 %collective-permute-done.7.refs_1_ = bf16[8,10752]{1,0:T(8,128)(2,1)S(1)} collective-permute-done((bf16[8,10752]{1,0:T(8,128)(2,1)S(1)}, bf16[8,10752]{1,0:T(8,128)(2,1)S(1)}, u32[]{:S(2)}, u32[]{:S(2)}) %collective-permute-start.7) | collective-permute-done | bytes 172064 | tf_op jit(solution)/shard_map/ppermute | solution.py:262
  16.4 0.0 collective-permute-start.10
  16.4 4.2 %shard_map.74 = (bf16[7168,256]{1,0:T(8,128)(2,1)S(1)}, bf16[7168,256]{1,0:T(8,128)(2,1)S(1)}, bf16[256,7168]{1,0:T(8,128)(2,1)S(1)}) custom-call(bf16[7168,256]{1,0:T(8,128)(2,1)} %refs_0_.1, bf16[7168,256]{1,0:T(8,128)(2,1)} %refs_1_.1, bf16[256,7168]{1,0:T(8,128)(2,1)} %refs_2_.1, bf16[8,10752]{1,0:T(8,128)(2,1)S(1)} %get-tuple-element.19.refs_3_.refs_0_), custom_call_target="tpu_custom_call" | custom-call | tf_op jit(solution)/shard_map/pallas_call | solution.py:123
  20.7 0.0 collective-permute-done.5.refs_1_.refs_0_
  20.7 1.4 %collective-permute-start.8 = (bf16[8,10752]{1,0:T(8,128)(2,1)S(1)}, bf16[8,10752]{1,0:T(8,128)(2,1)S(1)}, u32[]{:S(2)}, u32[]{:S(2)}) collective-permute-start(bf16[8,10752]{1,0:T(8,128)(2,1)S(1)} %collective-permute-done.5.refs_1_.refs_0_), channel_id=1, source_target_pairs={{0,2},{1,3},{2,0},{3,1},{4,6},{5,7},{6,4},{7,5},{8,10},{9,11},{10,... | collective-permute-start | bytes 516104 | tf_op jit(solution)/shard_map/ppermute | solution.py:262
  22.1 0.0 collective-permute-done.1.refs_2_
  22.1 0.0 collective-permute-done.2.refs_3_
  22.1 2.1 %shard_map.75 = (bf16[16,10752]{1,0:T(8,128)(2,1)S(1)}, bf16[16,10752]{1,0:T(8,128)(2,1)S(1)}) custom-call(bf16[8,10752]{1,0:T(8,128)(2,1)S(1)} %get-tuple-element.19.refs_3_.refs_0_, bf16[8,10752]{1,0:T(8,128)(2,1)S(1)} %collective-permute-done.refs_1_.refs_2_, bf16[8,10752]{1,0:T(8,128)(2,1)S(1)} %collective-permute-done.1.refs_2_, ...), custom_call_target="tpu_custom_call" | custom-call | tf_op jit(solution)/shard_map/pallas_call | solution.py:183
  24.2 0.0 collective-permute-done.9.refs_2_
  24.2 0.0 collective-permute-done.10.refs_3_
  24.2 2.1 %shard_map.77 = (bf16[16,10752]{1,0:T(8,128)(2,1)S(1)}, bf16[16,10752]{1,0:T(8,128)(2,1)S(1)}) custom-call(bf16[8,10752]{1,0:T(8,128)(2,1)S(1)} %collective-permute-done.4.refs_0_, bf16[8,10752]{1,0:T(8,128)(2,1)S(1)} %collective-permute-done.7.refs_1_, bf16[8,10752]{1,0:T(8,128)(2,1)S(1)} %collective-permute-done.9.refs_2_, ...), custom_call_target="tpu_custom_call" | custom-call | tf_op jit(solution)/shard_map/pallas_call | solution.py:183
  26.3 0.3 collective-permute-start.11
  26.6 0.3 collective-permute-start.16
  26.9 0.7 collective-permute-done.8.refs_2_.refs_1_
  27.6 0.0 collective-permute-start.17
  27.6 1.3 %shard_map.76 = bf16[8,10752]{1,0:T(8,128)(2,1)S(1)} custom-call(s32[4]{0:T(128)} %placement_ref.5, s32[2,16]{1,0:T(2,128)} %bitcast.3, bf16[16,7168]{1,0:T(8,128)(2,1)} %tokens_ref.3, bf16[8,10752]{1,0:T(8,128)(2,1)S(1)} %collective-permute-done.4.refs_0_, bf16[8,10752]{1,0:T(8,128)(2,1)S(1)} %collective-permute-done.5.refs_1_.refs_0_, ...), custom_call_target="tpu_custom_call" | custom-call | tf_op jit(solution)/shard_map/pallas_call | solution.py:81
  28.8 0.6 collective-permute-start.6
  29.5 0.0 collective-permute-done.16.refs_2_
  29.5 0.0 collective-permute-done.17.refs_3_
  29.5 2.1 %shard_map.79 = (bf16[16,10752]{1,0:T(8,128)(2,1)S(1)}, bf16[16,10752]{1,0:T(8,128)(2,1)S(1)}) custom-call(bf16[8,10752]{1,0:T(8,128)(2,1)S(1)} %collective-permute-done.5.refs_1_.refs_0_, bf16[8,10752]{1,0:T(8,128)(2,1)S(1)} %collective-permute-done.8.refs_2_.refs_1_, bf16[8,10752]{1,0:T(8,128)(2,1)S(1)} %collective-permute-done.16.refs_2_, ...), custom_call_target="tpu_custom_call" | custom-call | tf_op jit(solution)/shard_map/pallas_call | solution.py:183
  31.6 0.3 collective-permute-start.18
  31.9 0.0 collective-permute-done.11
  31.9 1.6 %collective-permute-start.15 = (bf16[8,10752]{1,0:T(8,128)(2,1)S(1)}, bf16[8,10752]{1,0:T(8,128)(2,1)S(1)}, u32[]{:S(2)}, u32[]{:S(2)}) collective-permute-start(bf16[8,10752]{1,0:T(8,128)(2,1)S(1)} %add_convert_fusion.6.refs_3_), channel_id=1, source_target_pairs={{0,2},{1,3},{2,0},{3,1},{4,6},{5,7},{6,4},{7,5},{8,10},{9,11},{10,... | collective-permute-start | bytes 516104 | tf_op jit(solution)/shard_map/ppermute | solution.py:262
  33.5 5.8 %collective-permute-done.6.refs_0_ = bf16[8,10752]{1,0:T(8,128)(2,1)S(1)} collective-permute-done((bf16[8,10752]{1,0:T(8,128)(2,1)S(1)}, bf16[8,10752]{1,0:T(8,128)(2,1)S(1)}, u32[]{:S(2)}, u32[]{:S(2)}) %collective-permute-start.6) | collective-permute-done | bytes 172064 | tf_op jit(solution)/shard_map/ppermute | solution.py:259
  39.3 1.5 %collective-permute-start.12 = (bf16[8,10752]{1,0:T(8,128)(2,1)S(1)}, bf16[8,10752]{1,0:T(8,128)(2,1)S(1)}, u32[]{:S(2)}, u32[]{:S(2)}) collective-permute-start(bf16[8,10752]{1,0:T(8,128)(2,1)S(1)} %shard_map.78.refs_0_), channel_id=1, source_target_pairs={{0,2},{1,3},{2,0},{3,1},{4,6},{5,7},{6,4},{7,5},{8,10},{9,11},{10,... | collective-permute-start | bytes 516104 | tf_op jit(solution)/shard_map/ppermute | solution.py:262
  40.8 0.0 collective-permute-start.13
  40.9 4.8 %collective-permute-done.12.refs_1_ = bf16[8,10752]{1,0:T(8,128)(2,1)S(1)} collective-permute-done((bf16[8,10752]{1,0:T(8,128)(2,1)S(1)}, bf16[8,10752]{1,0:T(8,128)(2,1)S(1)}, u32[]{:S(2)}, u32[]{:S(2)}) %collective-permute-start.12) | collective-permute-done | bytes 172064 | tf_op jit(solution)/shard_map/ppermute | solution.py:262
  45.6 0.0 collective-permute-start.14
  45.6 0.0 collective-permute-done.15
  45.6 0.1 add_convert_fusion.5.refs_7_
  45.7 1.3 %collective-permute-done.14.refs_3_ = bf16[8,10752]{1,0:T(8,128)(2,1)S(1)} collective-permute-done((bf16[8,10752]{1,0:T(8,128)(2,1)S(1)}, bf16[8,10752]{1,0:T(8,128)(2,1)S(1)}, u32[]{:S(2)}, u32[]{:S(2)}) %collective-permute-start.14) | collective-permute-done | bytes 172064 | tf_op jit(solution)/shard_map/ppermute | solution.py:265
  47.0 2.1 %shard_map.80 = (bf16[16,10752]{1,0:T(8,128)(2,1)S(1)}, bf16[16,10752]{1,0:T(8,128)(2,1)S(1)}) custom-call(bf16[8,10752]{1,0:T(8,128)(2,1)S(1)} %shard_map.78.refs_0_, bf16[8,10752]{1,0:T(8,128)(2,1)S(1)} %collective-permute-done.12.refs_1_, bf16[8,10752]{1,0:T(8,128)(2,1)S(1)} %collective-permute-done.13.refs_2_, ...), custom_call_target="tpu_custom_call" | custom-call | tf_op jit(solution)/shard_map/pallas_call | solution.py:183
  49.1 0.0 copy-start
  49.1 0.0 copy-start.1
  49.1 0.0 copy-start.2
  49.1 0.2 collective-permute-start.19
  49.4 0.4 collective-permute-start.3
  49.7 1.1 %collective-permute-done.19 = bf16[16,10752]{1,0:T(8,128)(2,1)S(1)} collective-permute-done((bf16[16,10752]{1,0:T(8,128)(2,1)S(1)}, bf16[16,10752]{1,0:T(8,128)(2,1)S(1)}, u32[]{:S(2)}, u32[]{:S(2)}) %collective-permute-start.19) | collective-permute-done | bytes 344096 | tf_op jit(solution)/shard_map/ppermute | solution.py:265
  50.9 1.6 %collective-permute-start.20 = (bf16[8,10752]{1,0:T(8,128)(2,1)S(1)}, bf16[8,10752]{1,0:T(8,128)(2,1)S(1)}, u32[]{:S(2)}, u32[]{:S(2)}) collective-permute-start(bf16[8,10752]{1,0:T(8,128)(2,1)S(1)} %add_convert_fusion.3), channel_id=1, source_target_pairs={{0,2},{1,3},{2,0},{3,1},{4,6},{5,7},{6,4},{7,5},{8,10},{9,11},{10,... | collective-permute-start | bytes 516104 | tf_op jit(solution)/shard_map/ppermute | solution.py:262
  52.5 0.0 collective-permute-done.3
  52.6 0.6 collective-permute-start.24
  53.1 2.5 %collective-permute-start.22 = (bf16[8,10752]{1,0:T(8,128)(2,1)S(1)}, bf16[8,10752]{1,0:T(8,128)(2,1)S(1)}, u32[]{:S(2)}, u32[]{:S(2)}) collective-permute-start(bf16[8,10752]{1,0:T(8,128)(2,1)S(1)} %add_convert_fusion.5.refs_7_), channel_id=1, source_target_pairs={{0,12},{1,13},{2,14},{3,15},{4,0},{5,1},{6,2},{7,3},{8,4},{9,5},{1... | collective-permute-start | bytes 516104 | tf_op jit(solution)/shard_map/ppermute | solution.py:259
  55.6 2.6 %collective-permute-done.20 = bf16[8,10752]{1,0:T(8,128)(2,1)S(1)} collective-permute-done((bf16[8,10752]{1,0:T(8,128)(2,1)S(1)}, bf16[8,10752]{1,0:T(8,128)(2,1)S(1)}, u32[]{:S(2)}, u32[]{:S(2)}) %collective-permute-start.20) | collective-permute-done | bytes 172064 | tf_op jit(solution)/shard_map/ppermute | solution.py:262
  58.2 0.1 add_convert_fusion.2.refs_1_.refs_0_
  58.3 1.6 %collective-permute-start.21 = (bf16[8,10752]{1,0:T(8,128)(2,1)S(1)}, bf16[8,10752]{1,0:T(8,128)(2,1)S(1)}, u32[]{:S(2)}, u32[]{:S(2)}) collective-permute-start(bf16[8,10752]{1,0:T(8,128)(2,1)S(1)} %shard_map.81), channel_id=1, source_target_pairs={{0,2},{1,3},{2,0},{3,1},{4,6},{5,7},{6,4},{7,5},{8,10},{9,11},{10,... | collective-permute-start | bytes 516104 | tf_op jit(solution)/shard_map/ppermute | solution.py:262
  59.9 2.0 %collective-permute-done.24 = bf16[8,10752]{1,0:T(8,128)(2,1)S(1)} collective-permute-done((bf16[8,10752]{1,0:T(8,128)(2,1)S(1)}, bf16[8,10752]{1,0:T(8,128)(2,1)S(1)}, u32[]{:S(2)}, u32[]{:S(2)}) %collective-permute-start.24) | collective-permute-done | bytes 172064 | tf_op jit(solution)/shard_map/ppermute | solution.py:262
  61.9 0.1 add_convert_fusion
  62.0 0.1 collective-permute-start.25
  62.0 0.0 collective-permute-done.22.refs_1_
  62.0 3.0 %collective-permute-start.23 = (bf16[8,10752]{1,0:T(8,128)(2,1)S(1)}, bf16[8,10752]{1,0:T(8,128)(2,1)S(1)}, u32[]{:S(2)}, u32[]{:S(2)}) collective-permute-start(bf16[8,10752]{1,0:T(8,128)(2,1)S(1)} %shard_map.82), channel_id=1, source_target_pairs={{0,8},{1,9},{2,10},{3,11},{4,12},{5,13},{6,14},{7,15},{8,0},{9,1},... | collective-permute-start | bytes 516104 | tf_op jit(solution)/shard_map/ppermute | solution.py:259
  65.1 0.1 add_convert_fusion.1.refs_0_
  65.1 5.4 %collective-permute-done.25.refs_3_ = bf16[8,10752]{1,0:T(8,128)(2,1)S(1)} collective-permute-done((bf16[8,10752]{1,0:T(8,128)(2,1)S(1)}, bf16[8,10752]{1,0:T(8,128)(2,1)S(1)}, u32[]{:S(2)}, u32[]{:S(2)}) %collective-permute-start.25) | collective-permute-done | bytes 172064 | tf_op jit(solution)/shard_map/ppermute | solution.py:259
  70.6 4.6 %collective-permute-done.23.refs_2_ = bf16[8,10752]{1,0:T(8,128)(2,1)S(1)} collective-permute-done((bf16[8,10752]{1,0:T(8,128)(2,1)S(1)}, bf16[8,10752]{1,0:T(8,128)(2,1)S(1)}, u32[]{:S(2)}, u32[]{:S(2)}) %collective-permute-start.23) | collective-permute-done | bytes 172064 | tf_op jit(solution)/shard_map/ppermute | solution.py:259
  75.2 1.9 %shard_map.83 = bf16[16,7168]{1,0:T(8,128)(2,1)} custom-call(s32[4]{0:T(128)S(1)} %copy-done.1, s32[2,16]{1,0:T(2,128)S(1)} %bitcast.4, f32[2,16]{1,0:T(2,128)S(1)} %bitcast.5, bf16[8,10752]{1,0:T(8,128)(2,1)S(1)} %add_convert_fusion.1.refs_0_, bf16[8,10752]{1,0:T(8,128)(2,1)S(1)} %collective-permute-done.22.refs_1_, ...), custom_call_target="tpu_custom_call" | custom-call | flops 44040192 | bytes 1146880 | tf_op jit(solution)/shard_map/pallas_call | solution.py:233
  (13 shorter events, 0.2 us)
Async XLA Ops:
  1.4 9.5 %collective-permute-start.4 = (bf16[8,10752]{1,0:T(8,128)(2,1)S(1)}, bf16[8,10752]{1,0:T(8,128)(2,1)S(1)}, u32[]{:S(2)}, u32[]{:S(2)}) collective-permute-start(bf16[8,10752]{1,0:T(8,128)(2,1)S(1)} %get-tuple-element.25), channel_id=1, source_target_pairs={{0,4},{1,5},{2,6},{3,7},{4,8},{5,9},{6,10},{7,11},{8,12},{9,13},{1... | collective-permute-start | bytes 516104 | tf_op jit(solution)/shard_map/ppermute | solution.py:259
  4.5 9.7 %collective-permute-start = (bf16[8,10752]{1,0:T(8,128)(2,1)S(1)}, bf16[8,10752]{1,0:T(8,128)(2,1)S(1)}, u32[]{:S(2)}, u32[]{:S(2)}) collective-permute-start(bf16[8,10752]{1,0:T(8,128)(2,1)S(1)} %get-tuple-element.19.refs_3_.refs_0_), channel_id=1, source_target_pairs={{0,2},{1,3},{2,0},{3,1},{4,6},{5,7},{6,4},{7,5},{8,10},{9,11},{10,... | collective-permute-start | bytes 516104 | tf_op jit(solution)/shard_map/ppermute | solution.py:262
  10.9 5.6 %collective-permute-start.7 = (bf16[8,10752]{1,0:T(8,128)(2,1)S(1)}, bf16[8,10752]{1,0:T(8,128)(2,1)S(1)}, u32[]{:S(2)}, u32[]{:S(2)}) collective-permute-start(bf16[8,10752]{1,0:T(8,128)(2,1)S(1)} %collective-permute-done.4.refs_0_), channel_id=1, source_target_pairs={{0,2},{1,3},{2,0},{3,1},{4,6},{5,7},{6,4},{7,5},{8,10},{9,11},{10,... | collective-permute-start | bytes 516104 | tf_op jit(solution)/shard_map/ppermute | solution.py:262
  12.4 8.3 %collective-permute-start.5 = (bf16[8,10752]{1,0:T(8,128)(2,1)S(1)}, bf16[8,10752]{1,0:T(8,128)(2,1)S(1)}, u32[]{:S(2)}, u32[]{:S(2)}) collective-permute-start(bf16[8,10752]{1,0:T(8,128)(2,1)S(1)} %get-tuple-element.26), channel_id=1, source_target_pairs={{0,12},{1,13},{2,14},{3,15},{4,0},{5,1},{6,2},{7,3},{8,4},{9,5},{1... | collective-permute-start | bytes 516104 | tf_op jit(solution)/shard_map/ppermute | solution.py:259
  14.1 8.0 %collective-permute-start.1 = (bf16[8,10752]{1,0:T(8,128)(2,1)S(1)}, bf16[8,10752]{1,0:T(8,128)(2,1)S(1)}, u32[]{:S(2)}, u32[]{:S(2)}) collective-permute-start(bf16[8,10752]{1,0:T(8,128)(2,1)S(1)} %get-tuple-element.19.refs_3_.refs_0_), channel_id=1, source_target_pairs={{0,1},{1,0},{2,3},{3,2},{4,5},{5,4},{6,7},{7,6},{8,9},{9,8},{10,11... | collective-permute-start | bytes 516104 | tf_op jit(solution)/shard_map/ppermute | solution.py:265
  14.1 8.0 %collective-permute-start.2 = (bf16[8,10752]{1,0:T(8,128)(2,1)S(1)}, bf16[8,10752]{1,0:T(8,128)(2,1)S(1)}, u32[]{:S(2)}, u32[]{:S(2)}) collective-permute-start(bf16[8,10752]{1,0:T(8,128)(2,1)S(1)} %collective-permute-done.refs_1_.refs_2_), channel_id=1, source_target_pairs={{0,1},{1,0},{2,3},{3,2},{4,5},{5,4},{6,7},{7,6},{8,9},{9,8},{10,11... | collective-permute-start | bytes 516104 | tf_op jit(solution)/shard_map/ppermute | solution.py:265
  14.7 9.6 %collective-permute-start.9 = (bf16[8,10752]{1,0:T(8,128)(2,1)S(1)}, bf16[8,10752]{1,0:T(8,128)(2,1)S(1)}, u32[]{:S(2)}, u32[]{:S(2)}) collective-permute-start(bf16[8,10752]{1,0:T(8,128)(2,1)S(1)} %collective-permute-done.4.refs_0_), channel_id=1, source_target_pairs={{0,1},{1,0},{2,3},{3,2},{4,5},{5,4},{6,7},{7,6},{8,9},{9,8},{10,11... | collective-permute-start | bytes 516104 | tf_op jit(solution)/shard_map/ppermute | solution.py:265
  16.4 7.8 %collective-permute-start.10 = (bf16[8,10752]{1,0:T(8,128)(2,1)S(1)}, bf16[8,10752]{1,0:T(8,128)(2,1)S(1)}, u32[]{:S(2)}, u32[]{:S(2)}) collective-permute-start(bf16[8,10752]{1,0:T(8,128)(2,1)S(1)} %collective-permute-done.7.refs_1_), channel_id=1, source_target_pairs={{0,1},{1,0},{2,3},{3,2},{4,5},{5,4},{6,7},{7,6},{8,9},{9,8},{10,11... | collective-permute-start | bytes 516104 | tf_op jit(solution)/shard_map/ppermute | solution.py:265
  20.7 6.9 %collective-permute-start.8 = (bf16[8,10752]{1,0:T(8,128)(2,1)S(1)}, bf16[8,10752]{1,0:T(8,128)(2,1)S(1)}, u32[]{:S(2)}, u32[]{:S(2)}) collective-permute-start(bf16[8,10752]{1,0:T(8,128)(2,1)S(1)} %collective-permute-done.5.refs_1_.refs_0_), channel_id=1, source_target_pairs={{0,2},{1,3},{2,0},{3,1},{4,6},{5,7},{6,4},{7,5},{8,10},{9,11},{10,... | collective-permute-start | bytes 516104 | tf_op jit(solution)/shard_map/ppermute | solution.py:262
  26.3 5.5 %collective-permute-start.11 = (bf16[16,10752]{1,0:T(8,128)(2,1)S(1)}, bf16[16,10752]{1,0:T(8,128)(2,1)S(1)}, u32[]{:S(2)}, u32[]{:S(2)}) collective-permute-start(bf16[16,10752]{1,0:T(8,128)(2,1)S(1)} %get-tuple-element.28), channel_id=1, source_target_pairs={{0,1},{1,0},{2,3},{3,2},{4,5},{5,4},{6,7},{7,6},{8,9},{9,8},{10,11... | collective-permute-start | bytes 1032200 | tf_op jit(solution)/shard_map/ppermute | solution.py:265
  26.6 2.9 %collective-permute-start.16 = (bf16[8,10752]{1,0:T(8,128)(2,1)S(1)}, bf16[8,10752]{1,0:T(8,128)(2,1)S(1)}, u32[]{:S(2)}, u32[]{:S(2)}) collective-permute-start(bf16[8,10752]{1,0:T(8,128)(2,1)S(1)} %collective-permute-done.5.refs_1_.refs_0_), channel_id=1, source_target_pairs={{0,1},{1,0},{2,3},{3,2},{4,5},{5,4},{6,7},{7,6},{8,9},{9,8},{10,11... | collective-permute-start | bytes 516104 | tf_op jit(solution)/shard_map/ppermute | solution.py:265
  27.6 1.9 %collective-permute-start.17 = (bf16[8,10752]{1,0:T(8,128)(2,1)S(1)}, bf16[8,10752]{1,0:T(8,128)(2,1)S(1)}, u32[]{:S(2)}, u32[]{:S(2)}) collective-permute-start(bf16[8,10752]{1,0:T(8,128)(2,1)S(1)} %collective-permute-done.8.refs_2_.refs_1_), channel_id=1, source_target_pairs={{0,1},{1,0},{2,3},{3,2},{4,5},{5,4},{6,7},{7,6},{8,9},{9,8},{10,11... | collective-permute-start | bytes 516104 | tf_op jit(solution)/shard_map/ppermute | solution.py:265
  28.8 10.4 %collective-permute-start.6 = (bf16[8,10752]{1,0:T(8,128)(2,1)S(1)}, bf16[8,10752]{1,0:T(8,128)(2,1)S(1)}, u32[]{:S(2)}, u32[]{:S(2)}) collective-permute-start(bf16[8,10752]{1,0:T(8,128)(2,1)S(1)} %shard_map.76), channel_id=1, source_target_pairs={{0,8},{1,9},{2,10},{3,11},{4,12},{5,13},{6,14},{7,15},{8,0},{9,1},... | collective-permute-start | bytes 516104 | tf_op jit(solution)/shard_map/ppermute | solution.py:259
  31.6 9.3 %collective-permute-start.18 = (bf16[16,10752]{1,0:T(8,128)(2,1)S(1)}, bf16[16,10752]{1,0:T(8,128)(2,1)S(1)}, u32[]{:S(2)}, u32[]{:S(2)}) collective-permute-start(bf16[16,10752]{1,0:T(8,128)(2,1)S(1)} %get-tuple-element.30), channel_id=1, source_target_pairs={{0,1},{1,0},{2,3},{3,2},{4,5},{5,4},{6,7},{7,6},{8,9},{9,8},{10,11... | collective-permute-start | bytes 1032200 | tf_op jit(solution)/shard_map/ppermute | solution.py:265
  31.9 13.7 %collective-permute-start.15 = (bf16[8,10752]{1,0:T(8,128)(2,1)S(1)}, bf16[8,10752]{1,0:T(8,128)(2,1)S(1)}, u32[]{:S(2)}, u32[]{:S(2)}) collective-permute-start(bf16[8,10752]{1,0:T(8,128)(2,1)S(1)} %add_convert_fusion.6.refs_3_), channel_id=1, source_target_pairs={{0,2},{1,3},{2,0},{3,1},{4,6},{5,7},{6,4},{7,5},{8,10},{9,11},{10,... | collective-permute-start | bytes 516104 | tf_op jit(solution)/shard_map/ppermute | solution.py:262
  39.3 6.4 %collective-permute-start.12 = (bf16[8,10752]{1,0:T(8,128)(2,1)S(1)}, bf16[8,10752]{1,0:T(8,128)(2,1)S(1)}, u32[]{:S(2)}, u32[]{:S(2)}) collective-permute-start(bf16[8,10752]{1,0:T(8,128)(2,1)S(1)} %shard_map.78.refs_0_), channel_id=1, source_target_pairs={{0,2},{1,3},{2,0},{3,1},{4,6},{5,7},{6,4},{7,5},{8,10},{9,11},{10,... | collective-permute-start | bytes 516104 | tf_op jit(solution)/shard_map/ppermute | solution.py:262
  40.8 4.9 %collective-permute-start.13 = (bf16[8,10752]{1,0:T(8,128)(2,1)S(1)}, bf16[8,10752]{1,0:T(8,128)(2,1)S(1)}, u32[]{:S(2)}, u32[]{:S(2)}) collective-permute-start(bf16[8,10752]{1,0:T(8,128)(2,1)S(1)} %shard_map.78.refs_0_), channel_id=1, source_target_pairs={{0,1},{1,0},{2,3},{3,2},{4,5},{5,4},{6,7},{7,6},{8,9},{9,8},{10,11... | collective-permute-start | bytes 516104 | tf_op jit(solution)/shard_map/ppermute | solution.py:265
  45.6 1.4 %collective-permute-start.14 = (bf16[8,10752]{1,0:T(8,128)(2,1)S(1)}, bf16[8,10752]{1,0:T(8,128)(2,1)S(1)}, u32[]{:S(2)}, u32[]{:S(2)}) collective-permute-start(bf16[8,10752]{1,0:T(8,128)(2,1)S(1)} %collective-permute-done.12.refs_1_), channel_id=1, source_target_pairs={{0,1},{1,0},{2,3},{3,2},{4,5},{5,4},{6,7},{7,6},{8,9},{9,8},{10,11... | collective-permute-start | bytes 516104 | tf_op jit(solution)/shard_map/ppermute | solution.py:265
  49.1 26.1 %copy-start = (s32[16,2]{0,1:T(2,128)S(1)}, s32[16,2]{0,1:T(2,128)}, u32[]{:S(2)}) copy-start(s32[16,2]{0,1:T(2,128)} %param.8) | copy-start | bytes 388
  49.1 26.1 %copy-start.1 = (s32[4]{0:T(128)S(1)}, s32[4]{0:T(128)}, u32[]{:S(2)}) copy-start(s32[4]{0:T(128)} %placement_ref.5) | copy-start | bytes 52
  49.1 26.1 %copy-start.2 = (f32[16,2]{0,1:T(2,128)S(1)}, f32[16,2]{0,1:T(2,128)}, u32[]{:S(2)}) copy-start(f32[16,2]{0,1:T(2,128)} %param.9) | copy-start | bytes 388
  49.1 1.7 %collective-permute-start.19 = (bf16[16,10752]{1,0:T(8,128)(2,1)S(1)}, bf16[16,10752]{1,0:T(8,128)(2,1)S(1)}, u32[]{:S(2)}, u32[]{:S(2)}) collective-permute-start(bf16[16,10752]{1,0:T(8,128)(2,1)S(1)} %get-tuple-element.32), channel_id=1, source_target_pairs={{0,1},{1,0},{2,3},{3,2},{4,5},{5,4},{6,7},{7,6},{8,9},{9,8},{10,11... | collective-permute-start | bytes 1032200 | tf_op jit(solution)/shard_map/ppermute | solution.py:265
  49.4 3.1 %collective-permute-start.3 = (bf16[16,10752]{1,0:T(8,128)(2,1)S(1)}, bf16[16,10752]{1,0:T(8,128)(2,1)S(1)}, u32[]{:S(2)}, u32[]{:S(2)}) collective-permute-start(bf16[16,10752]{1,0:T(8,128)(2,1)S(1)} %get-tuple-element.24.refs_7_), channel_id=1, source_target_pairs={{0,1},{1,0},{2,3},{3,2},{4,5},{5,4},{6,7},{7,6},{8,9},{9,8},{10,11... | collective-permute-start | bytes 1032200 | tf_op jit(solution)/shard_map/ppermute | solution.py:265
  50.9 7.3 %collective-permute-start.20 = (bf16[8,10752]{1,0:T(8,128)(2,1)S(1)}, bf16[8,10752]{1,0:T(8,128)(2,1)S(1)}, u32[]{:S(2)}, u32[]{:S(2)}) collective-permute-start(bf16[8,10752]{1,0:T(8,128)(2,1)S(1)} %add_convert_fusion.3), channel_id=1, source_target_pairs={{0,2},{1,3},{2,0},{3,1},{4,6},{5,7},{6,4},{7,5},{8,10},{9,11},{10,... | collective-permute-start | bytes 516104 | tf_op jit(solution)/shard_map/ppermute | solution.py:262
  52.6 9.3 %collective-permute-start.24 = (bf16[8,10752]{1,0:T(8,128)(2,1)S(1)}, bf16[8,10752]{1,0:T(8,128)(2,1)S(1)}, u32[]{:S(2)}, u32[]{:S(2)}) collective-permute-start(bf16[8,10752]{1,0:T(8,128)(2,1)S(1)} %add_convert_fusion.4.refs_8_), channel_id=1, source_target_pairs={{0,2},{1,3},{2,0},{3,1},{4,6},{5,7},{6,4},{7,5},{8,10},{9,11},{10,... | collective-permute-start | bytes 516104 | tf_op jit(solution)/shard_map/ppermute | solution.py:262
  53.1 8.9 %collective-permute-start.22 = (bf16[8,10752]{1,0:T(8,128)(2,1)S(1)}, bf16[8,10752]{1,0:T(8,128)(2,1)S(1)}, u32[]{:S(2)}, u32[]{:S(2)}) collective-permute-start(bf16[8,10752]{1,0:T(8,128)(2,1)S(1)} %add_convert_fusion.5.refs_7_), channel_id=1, source_target_pairs={{0,12},{1,13},{2,14},{3,15},{4,0},{5,1},{6,2},{7,3},{8,4},{9,5},{1... | collective-permute-start | bytes 516104 | tf_op jit(solution)/shard_map/ppermute | solution.py:259
  58.3 6.8 %collective-permute-start.21 = (bf16[8,10752]{1,0:T(8,128)(2,1)S(1)}, bf16[8,10752]{1,0:T(8,128)(2,1)S(1)}, u32[]{:S(2)}, u32[]{:S(2)}) collective-permute-start(bf16[8,10752]{1,0:T(8,128)(2,1)S(1)} %shard_map.81), channel_id=1, source_target_pairs={{0,2},{1,3},{2,0},{3,1},{4,6},{5,7},{6,4},{7,5},{8,10},{9,11},{10,... | collective-permute-start | bytes 516104 | tf_op jit(solution)/shard_map/ppermute | solution.py:262
  62.0 8.6 %collective-permute-start.25 = (bf16[8,10752]{1,0:T(8,128)(2,1)S(1)}, bf16[8,10752]{1,0:T(8,128)(2,1)S(1)}, u32[]{:S(2)}, u32[]{:S(2)}) collective-permute-start(bf16[8,10752]{1,0:T(8,128)(2,1)S(1)} %add_convert_fusion), channel_id=1, source_target_pairs={{0,4},{1,5},{2,6},{3,7},{4,8},{5,9},{6,10},{7,11},{8,12},{9,13},{1... | collective-permute-start | bytes 516104 | tf_op jit(solution)/shard_map/ppermute | solution.py:259
  62.0 13.2 %collective-permute-start.23 = (bf16[8,10752]{1,0:T(8,128)(2,1)S(1)}, bf16[8,10752]{1,0:T(8,128)(2,1)S(1)}, u32[]{:S(2)}, u32[]{:S(2)}) collective-permute-start(bf16[8,10752]{1,0:T(8,128)(2,1)S(1)} %shard_map.82), channel_id=1, source_target_pairs={{0,8},{1,9},{2,10},{3,11},{4,12},{5,13},{6,14},{7,15},{8,0},{9,1},... | collective-permute-start | bytes 516104 | tf_op jit(solution)/shard_map/ppermute | solution.py:259

commit v5 on v4

--- a/solution.py
+++ b/solution.py
@@ -65,7 +65,7 @@
     wanted = bucket_rows(rows)
     upper = lax.broadcasted_iota(jnp.int32, (half, width // 2), 0) < quarter
     for k, out_ref in zip(distances, refs[-len(distances) :]):
-        expert = expert_at(placement_ref, lax.rem(block + k, n_blocks))
+        expert = expert_at(placement_ref, lax.bitwise_xor(block, jnp.int32(k)))
         named = row_of(picks, experts, expert) > 0.5
         slot = row_of(earlier, experts, expert)
         chooser = jnp.where(named & (slot == wanted), 1.0, 0.0).astype(jnp.bfloat16)
@@ -94,6 +94,8 @@
 
 
 def when(value, after):
+    if not after:
+        return value
     return pl.pallas_call(
         nothing,
         out_shape=pltpu.VMEM(value.shape, value.dtype),
@@ -186,7 +188,9 @@
         in_specs=[VMEM] * 7 + [ANYWHERE] * len(after),
         out_specs=[VMEM] * 2,
         compiler_params=pltpu.CompilerParams(vmem_limit_bytes=VMEM_BYTES),
-        cost_estimate=NO_COST,
+        cost_estimate=pl.CostEstimate(
+            flops=0, bytes_accessed=4 * width * hid, transcendentals=0
+        ),
     )(*operands, *after)
 
 
@@ -200,7 +204,7 @@
     wanted = bucket_rows(rows)
     terms = []
     for k in range(n_blocks):
-        expert = expert_at(placement_ref, lax.rem(block + k, n_blocks))
+        expert = expert_at(placement_ref, lax.bitwise_xor(block, jnp.int32(k)))
         named = row_of(picks, experts, expert) > 0.5
         slot = row_of(earlier, experts, expert)
         weight = jnp.sum(jnp.where(ids == expert, gates, 0.0), axis=0, keepdims=True)
@@ -255,7 +259,7 @@
     half = tokens.shape[0] // 2
 
     def along_z(value, k):
-        pairs = [(i, (i + k * parts) % devices) for i in range(devices)]
+        pairs = [(i, i ^ (k * parts)) for i in range(devices)]
         return lax.ppermute(value, "node", pairs)
 
     def along_y(value):
@@ -265,50 +269,39 @@
         return lax.ppermute(value, "node", [(i, i ^ 1) for i in range(devices)])
 
     ids = expert_ids.T
-    groups = [sorted({d, n_blocks - d}) for d in range(1, n_blocks // 2 + 1)]
-    buckets = pack(placement, ids, tokens, n_blocks, parts, [0] + groups[0], [])
-    straight, across, theirs = {0: buckets[0]}, {0: along_y(buckets[0])}, {}
-    results, both, home, kept, sent, returned = {}, {}, {}, {}, {}, {}
-    for k in groups[0]:
-        straight[k] = along_z(buckets[k], k)
-    weights = load((gate_weight, up_weight, down_weight), buckets[0])
+    groups = [[n_blocks - d, d] for d in range(1, n_blocks // 2)] + [[n_blocks // 2]]
+    last = groups[-1][0]
+    straight, arrived, across, results = {}, {}, {}, {}
+    both, home, kept, sent, returned = {}, {}, {}, {}, {}
 
     def compute(k, after):
-        theirs[k] = [along_core(straight[k]), along_core(across[k])]
-        pieces = [straight[k], across[k]] + theirs[k]
-        kept[k], sent[k] = run_experts(pieces, weights, after)
+        theirs = [along_core(straight[k]), along_core(across[k])]
+        kept[k], sent[k] = run_experts([straight[k], across[k]] + theirs, weights, after)
         returned[k] = along_core(sent[k])
         both[k] = add(kept[k][half:], returned[k][half:])
 
-    def go_home(k, after):
-        back = along_y(both[k] if k else when(both[k], after))
+    def go_home(k, after_y, after_z):
+        back = along_y(when(both[k], after_y))
         home[k] = add(kept[k][:half], returned[k][:half], back)
-        if k:
-            value = when(home[k], after) if after else home[k]
-            results[k] = along_z(value, -k)
-        else:
-            results[k] = home[k]
-
-    compute(0, [])
+        results[k] = along_z(when(home[k], after_z), k) if k else home[k]
+
     for g, group in enumerate(groups):
-        if g:
-            earlier = groups[g - 1]
-            after = [straight[k] for k in earlier] + [across[0], weights[0]][: 2 if g == 1 else 0]
-            buckets = pack(placement, ids, tokens, n_blocks, parts, group, after)
-            after = [across[k] for k in earlier] + [both[earlier[0]]]
-            for k in group:
-                straight[k] = when(along_z(buckets[k], k), after)
+        members = [0] + group if g == 0 else group
+        after = [arrived[k] for k in groups[g - 1]] + [weights[0]] if g else []
+        buckets = pack(placement, ids, tokens, n_blocks, parts, members, after)
+        if g == 0:
+            straight[0] = buckets[0]
+            across[0] = along_y(straight[0])
+            weights = load((gate_weight, up_weight, down_weight), buckets[0])
         for k in group:
+            straight[k] = arrived[k] = along_z(buckets[k], k)
+        if g == 0:
+            compute(0, [])
+        for i, k in enumerate(group):
             across[k] = along_y(straight[k])
-        if g:
-            after = [home[earlier[0]]] + [both[k] for k in earlier[1:]]
-        else:
-            after = [sent[0]]
-        for k in group:
-            compute(k, after)
-        for k in group:
-            go_home(k, [results[earlier[0]]] if g else [])
-    go_home(0, [home[groups[-1][-1]]])
+            compute(k, [both[j] for j in groups[g - 1]] if g else [sent[0]][:i])
+            go_home(k, [], [results[j] for j in groups[g - 1]] if g else [])
+    go_home(0, [home[last]], [])
     return mix(placement, ids, gates.T, [results[k] for k in range(n_blocks)], n_blocks, parts)
 
 

time: 77.2 us -> 69.3 us (0.90)
  waiting for transfers between devices: 35.1 us -> 27 us
    ppermute x6, waiting for transfers between devices: 20.7 us -> 17.4 us  [along_z(): return lax.ppermute(value, 'node', pairs)]
    ppermute x12, waiting for transfers between devices: 2.49 us -> 0.03 us  [along_core(): return lax.ppermute(value, 'node', [(i, i ^ 1) for i in range(devices)])]
    ppermute x8, waiting for transfers between devices: 11.8 us -> 9.59 us  [along_y(): return lax.ppermute(value, 'node', [(i, i ^ 2) for i in range(devices)])]
  transfers between devices with their start and end apart: 26 -> 26, of which waited for: 11 -> 9; matrix products, arithmetic and copies ran while one was open for 1% -> 1% of each run, Pallas kernels for 15% -> 20%
where the time goes in v5:
time: 69.3 us; the launch traced here: 69.1 us
  waiting for transfers between devices  27 us (39%)
  starting transfers between devices  24.4 us (35%)
  Pallas kernels  17.1 us (25%)
    ppermute x6, waiting for transfers between devices, along_z(): return lax.ppermute(value, 'node', pairs)  17.4 us
    ppermute x6, starting transfers between devices, along_z(): return lax.ppermute(value, 'node', pairs)  11.5 us
    ppermute x8, starting transfers between devices, along_y(): return lax.ppermute(value, 'node', [(i, i ^ 2) for i in range(devices)])  11 us
    ppermute x8, waiting for transfers between devices, along_y(): return lax.ppermute(value, 'node', [(i, i ^ 2) for i in range(devices)])  9.59 us
    pallas_call x4, Pallas kernels, run_experts(): pl.pallas_call(experts_kernel, out_shape=[shape] * 2, in_specs=[VMEM] * 7...  8.28 us
    pallas_call x1, Pallas kernels, load(): pl.pallas_call(load_kernel, out_shape=[pltpu.VMEM(w.shape, w.dtype) for w...  4.24 us
    pallas_call x2, Pallas kernels, pack(): pl.pallas_call(functools.partial(pack_kernel, n_blocks, parts, distances)...  2.67 us
    ppermute x12, starting transfers between devices, along_core(): return lax.ppermute(value, 'node', [(i, i ^ 1) for i in range(devices)])  1.88 us
  transfers between devices with their start and end apart: 26, of which 9 were waited for; matrix products, arithmetic and copies ran while one was open for 1% of the time, Pallas kernels for 20%

profile of v5, /device:TPU:0, one launch (start us, length us, event | category | flops | bytes accessed | tf_op | source)
XLA Modules:
  0.0 69.1 jit_solution(13634153158361945072)
XLA Ops:
  0.0 1.4 %shard_map.73 = (bf16[8,10752]{1,0:T(8,128)(2,1)S(1)}, bf16[8,10752]{1,0:T(8,128)(2,1)S(1)}, bf16[8,10752]{1,0:T(8,128)(2,1)S(1)}) custom-call(s32[4]{0:T(128)} %placement_ref.5, s32[2,16]{1,0:T(2,128)} %bitcast.2, bf16[16,7168]{1,0:T(8,128)(2,1)} %tokens_ref.3), custom_call_target="tpu_custom_call" | custom-call | tf_op jit(solution)/shard_map/pallas_call | solution.py:81
  1.4 3.0 %collective-permute-start = (bf16[8,10752]{1,0:T(8,128)(2,1)S(1)}, bf16[8,10752]{1,0:T(8,128)(2,1)S(1)}, u32[]{:S(2)}, u32[]{:S(2)}) collective-permute-start(bf16[8,10752]{1,0:T(8,128)(2,1)S(1)} %get-tuple-element.19.refs_3_.refs_0_), channel_id=1, source_target_pairs={{0,2},{1,3},{2,0},{3,1},{4,6},{5,7},{6,4},{7,5},{8,10},{9,11},{10,... | collective-permute-start | bytes 516104 | tf_op jit(solution)/shard_map/ppermute | solution.py:266
  4.4 3.6 %collective-permute-start.4 = (bf16[8,10752]{1,0:T(8,128)(2,1)S(1)}, bf16[8,10752]{1,0:T(8,128)(2,1)S(1)}, u32[]{:S(2)}, u32[]{:S(2)}) collective-permute-start(bf16[8,10752]{1,0:T(8,128)(2,1)S(1)} %get-tuple-element.25), channel_id=1, source_target_pairs={{0,12},{1,13},{2,14},{3,15},{4,8},{5,9},{6,10},{7,11},{8,4},{9,5},... | collective-permute-start | bytes 516104 | tf_op jit(solution)/shard_map/ppermute | solution.py:263
  8.0 0.0 collective-permute-start.5
  8.0 0.0 collective-permute-start.1
  8.0 0.8 %collective-permute-done.refs_1_ = bf16[8,10752]{1,0:T(8,128)(2,1)S(1)} collective-permute-done((bf16[8,10752]{1,0:T(8,128)(2,1)S(1)}, bf16[8,10752]{1,0:T(8,128)(2,1)S(1)}, u32[]{:S(2)}, u32[]{:S(2)}) %collective-permute-start) | collective-permute-done | bytes 172064 | tf_op jit(solution)/shard_map/ppermute | solution.py:266
  8.8 0.0 collective-permute-start.2
  8.8 4.7 %collective-permute-done.4.refs_0_ = bf16[8,10752]{1,0:T(8,128)(2,1)S(1)} collective-permute-done((bf16[8,10752]{1,0:T(8,128)(2,1)S(1)}, bf16[8,10752]{1,0:T(8,128)(2,1)S(1)}, u32[]{:S(2)}, u32[]{:S(2)}) %collective-permute-start.4) | collective-permute-done | bytes 172064 | tf_op jit(solution)/shard_map/ppermute | solution.py:263
  13.5 0.3 collective-permute-start.10
  13.8 4.2 %shard_map.74 = (bf16[7168,256]{1,0:T(8,128)(2,1)S(1)}, bf16[7168,256]{1,0:T(8,128)(2,1)S(1)}, bf16[256,7168]{1,0:T(8,128)(2,1)S(1)}) custom-call(bf16[7168,256]{1,0:T(8,128)(2,1)} %refs_0_.1, bf16[7168,256]{1,0:T(8,128)(2,1)} %refs_1_.1, bf16[256,7168]{1,0:T(8,128)(2,1)} %refs_2_.1, bf16[8,10752]{1,0:T(8,128)(2,1)S(1)} %get-tuple-element.19.refs_3_.refs_0_), custom_call_target="tpu_custom_call" | custom-call | tf_op jit(solution)/shard_map/pallas_call | solution.py:125
  18.0 0.1 collective-permute-start.11
  18.1 0.0 collective-permute-done.5.refs_1_.refs_0_
  18.1 1.8 %collective-permute-start.14 = (bf16[8,10752]{1,0:T(8,128)(2,1)S(1)}, bf16[8,10752]{1,0:T(8,128)(2,1)S(1)}, u32[]{:S(2)}, u32[]{:S(2)}) collective-permute-start(bf16[8,10752]{1,0:T(8,128)(2,1)S(1)} %collective-permute-done.5.refs_1_.refs_0_), channel_id=1, source_target_pairs={{0,2},{1,3},{2,0},{3,1},{4,6},{5,7},{6,4},{7,5},{8,10},{9,11},{10,... | collective-permute-start | bytes 516104 | tf_op jit(solution)/shard_map/ppermute | solution.py:266
  20.0 1.3 %shard_map.76 = bf16[8,10752]{1,0:T(8,128)(2,1)S(1)} custom-call(s32[4]{0:T(128)} %placement_ref.5, s32[2,16]{1,0:T(2,128)} %bitcast.3, bf16[16,7168]{1,0:T(8,128)(2,1)} %tokens_ref.3, bf16[8,10752]{1,0:T(8,128)(2,1)S(1)} %collective-permute-done.4.refs_0_, bf16[8,10752]{1,0:T(8,128)(2,1)S(1)} %collective-permute-done.5.refs_1_.refs_0_, ...), custom_call_target="tpu_custom_call" | custom-call | tf_op jit(solution)/shard_map/pallas_call | solution.py:81
  21.3 0.0 collective-permute-done.1.refs_2_
  21.3 3.1 %collective-permute-start.6 = (bf16[8,10752]{1,0:T(8,128)(2,1)S(1)}, bf16[8,10752]{1,0:T(8,128)(2,1)S(1)}, u32[]{:S(2)}, u32[]{:S(2)}) collective-permute-start(bf16[8,10752]{1,0:T(8,128)(2,1)S(1)} %shard_map.76), channel_id=1, source_target_pairs={{0,8},{1,9},{2,10},{3,11},{4,12},{5,13},{6,14},{7,15},{8,0},{9,1},... | collective-permute-start | bytes 516104 | tf_op jit(solution)/shard_map/ppermute | solution.py:263
  24.3 0.0 collective-permute-done.2.refs_3_
  24.3 2.1 %shard_map.75 = (bf16[16,10752]{1,0:T(8,128)(2,1)S(1)}, bf16[16,10752]{1,0:T(8,128)(2,1)S(1)}) custom-call(bf16[8,10752]{1,0:T(8,128)(2,1)S(1)} %get-tuple-element.19.refs_3_.refs_0_, bf16[8,10752]{1,0:T(8,128)(2,1)S(1)} %collective-permute-done.refs_1_, bf16[8,10752]{1,0:T(8,128)(2,1)S(1)} %collective-permute-done.1.refs_2_, ...), custom_call_target="tpu_custom_call" | custom-call | bytes 7340032 | tf_op jit(solution)/shard_map/pallas_call | solution.py:185
  26.4 0.1 collective-permute-start.3
  26.5 0.0 collective-permute-done.10.refs_1_
  26.5 0.5 collective-permute-start.12
  27.0 0.0 collective-permute-done.11.refs_2_
  27.0 0.1 collective-permute-start.15
  27.1 0.0 collective-permute-done.14.refs_1_
  27.1 0.4 collective-permute-start.16
  27.5 5.2 %collective-permute-done.6.refs_0_ = bf16[8,10752]{1,0:T(8,128)(2,1)S(1)} collective-permute-done((bf16[8,10752]{1,0:T(8,128)(2,1)S(1)}, bf16[8,10752]{1,0:T(8,128)(2,1)S(1)}, u32[]{:S(2)}, u32[]{:S(2)}) %collective-permute-start.6) | collective-permute-done | bytes 172064 | tf_op jit(solution)/shard_map/ppermute | solution.py:263
  32.7 0.5 collective-permute-start.7
  33.2 0.0 collective-permute-done.12.refs_3_
  33.2 0.0 collective-permute-start.8
  33.2 2.1 %shard_map.77 = (bf16[16,10752]{1,0:T(8,128)(2,1)S(1)}, bf16[16,10752]{1,0:T(8,128)(2,1)S(1)}) custom-call(bf16[8,10752]{1,0:T(8,128)(2,1)S(1)} %collective-permute-done.4.refs_0_, bf16[8,10752]{1,0:T(8,128)(2,1)S(1)} %collective-permute-done.10.refs_1_, bf16[8,10752]{1,0:T(8,128)(2,1)S(1)} %collective-permute-done.11.refs_2_, ...), custom_call_target="tpu_custom_call" | custom-call | bytes 7340032 | tf_op jit(solution)/shard_map/pallas_call | solution.py:185
  35.3 0.6 collective-permute-start.13
  35.9 0.0 collective-permute-done.16.refs_3_
  35.9 2.1 %shard_map.78 = (bf16[16,10752]{1,0:T(8,128)(2,1)S(1)}, bf16[16,10752]{1,0:T(8,128)(2,1)S(1)}) custom-call(bf16[8,10752]{1,0:T(8,128)(2,1)S(1)} %collective-permute-done.5.refs_1_.refs_0_, bf16[8,10752]{1,0:T(8,128)(2,1)S(1)} %collective-permute-done.14.refs_1_, bf16[8,10752]{1,0:T(8,128)(2,1)S(1)} %collective-permute-done.15.refs_2_, ...), custom_call_target="tpu_custom_call" | custom-call | bytes 7340032 | tf_op jit(solution)/shard_map/pallas_call | solution.py:185
  38.0 0.1 collective-permute-start.17
  38.1 0.6 collective-permute-done.7.refs_1_
  38.6 0.0 collective-permute-start.9
  38.6 0.0 collective-permute-done.3
  38.8 1.5 %collective-permute-start.23 = (bf16[8,10752]{1,0:T(8,128)(2,1)S(1)}, bf16[8,10752]{1,0:T(8,128)(2,1)S(1)}, u32[]{:S(2)}, u32[]{:S(2)}) collective-permute-start(bf16[8,10752]{1,0:T(8,128)(2,1)S(1)} %add_convert_fusion.6.refs_7_), channel_id=1, source_target_pairs={{0,2},{1,3},{2,0},{3,1},{4,6},{5,7},{6,4},{7,5},{8,10},{9,11},{10,... | collective-permute-start | bytes 516104 | tf_op jit(solution)/shard_map/ppermute | solution.py:266
  40.3 1.0 %collective-permute-start.21 = (bf16[8,10752]{1,0:T(8,128)(2,1)S(1)}, bf16[8,10752]{1,0:T(8,128)(2,1)S(1)}, u32[]{:S(2)}, u32[]{:S(2)}) collective-permute-start(bf16[8,10752]{1,0:T(8,128)(2,1)S(1)} %add_convert_fusion.5.refs_8_), channel_id=1, source_target_pairs={{0,2},{1,3},{2,0},{3,1},{4,6},{5,7},{6,4},{7,5},{8,10},{9,11},{10,... | collective-permute-start | bytes 516104 | tf_op jit(solution)/shard_map/ppermute | solution.py:266
  41.3 0.0 collective-permute-done.8.refs_2_
  41.3 0.0 collective-permute-done.9.refs_3_
  41.3 2.1 %shard_map.79 = (bf16[16,10752]{1,0:T(8,128)(2,1)S(1)}, bf16[16,10752]{1,0:T(8,128)(2,1)S(1)}) custom-call(bf16[8,10752]{1,0:T(8,128)(2,1)S(1)} %collective-permute-done.6.refs_0_, bf16[8,10752]{1,0:T(8,128)(2,1)S(1)} %collective-permute-done.7.refs_1_, bf16[8,10752]{1,0:T(8,128)(2,1)S(1)} %collective-permute-done.8.refs_2_, ...), custom_call_target="tpu_custom_call" | custom-call | bytes 7340032 | tf_op jit(solution)/shard_map/pallas_call | solution.py:185
  43.4 0.0 copy-start
  43.4 0.0 copy-start.1
  43.4 0.0 copy-start.2
  43.4 0.1 collective-permute-start.18
  43.5 2.5 %collective-permute-done.23 = bf16[8,10752]{1,0:T(8,128)(2,1)S(1)} collective-permute-done((bf16[8,10752]{1,0:T(8,128)(2,1)S(1)}, bf16[8,10752]{1,0:T(8,128)(2,1)S(1)}, u32[]{:S(2)}, u32[]{:S(2)}) %collective-permute-start.23) | collective-permute-done | bytes 172064 | tf_op jit(solution)/shard_map/ppermute | solution.py:266
  46.0 0.1 add_convert_fusion
  46.1 3.4 %collective-permute-start.24 = (bf16[8,10752]{1,0:T(8,128)(2,1)S(1)}, bf16[8,10752]{1,0:T(8,128)(2,1)S(1)}, u32[]{:S(2)}, u32[]{:S(2)}) collective-permute-start(bf16[8,10752]{1,0:T(8,128)(2,1)S(1)} %add_convert_fusion), channel_id=1, source_target_pairs={{0,12},{1,13},{2,14},{3,15},{4,8},{5,9},{6,10},{7,11},{8,4},{9,5},... | collective-permute-start | bytes 516104 | tf_op jit(solution)/shard_map/ppermute | solution.py:263
  49.5 0.0 collective-permute-done.18
  49.5 1.4 %collective-permute-start.19 = (bf16[8,10752]{1,0:T(8,128)(2,1)S(1)}, bf16[8,10752]{1,0:T(8,128)(2,1)S(1)}, u32[]{:S(2)}, u32[]{:S(2)}) collective-permute-start(bf16[8,10752]{1,0:T(8,128)(2,1)S(1)} %add_convert_fusion.4), channel_id=1, source_target_pairs={{0,2},{1,3},{2,0},{3,1},{4,6},{5,7},{6,4},{7,5},{8,10},{9,11},{10,... | collective-permute-start | bytes 516104 | tf_op jit(solution)/shard_map/ppermute | solution.py:266
  51.0 0.0 collective-permute-done.21
  51.0 0.1 add_convert_fusion.1
  51.0 0.1 collective-permute-start.22
  51.1 3.9 %collective-permute-done.19 = bf16[8,10752]{1,0:T(8,128)(2,1)S(1)} collective-permute-done((bf16[8,10752]{1,0:T(8,128)(2,1)S(1)}, bf16[8,10752]{1,0:T(8,128)(2,1)S(1)}, u32[]{:S(2)}, u32[]{:S(2)}) %collective-permute-start.19) | collective-permute-done | bytes 172064 | tf_op jit(solution)/shard_map/ppermute | solution.py:266
  55.0 0.1 add_convert_fusion.3.refs_1_.refs_0_
  55.1 1.4 %collective-permute-start.20 = (bf16[8,10752]{1,0:T(8,128)(2,1)S(1)}, bf16[8,10752]{1,0:T(8,128)(2,1)S(1)}, u32[]{:S(2)}, u32[]{:S(2)}) collective-permute-start(bf16[8,10752]{1,0:T(8,128)(2,1)S(1)} %shard_map.80), channel_id=1, source_target_pairs={{0,2},{1,3},{2,0},{3,1},{4,6},{5,7},{6,4},{7,5},{8,10},{9,11},{10,... | collective-permute-start | bytes 516104 | tf_op jit(solution)/shard_map/ppermute | solution.py:266
  56.5 0.0 collective-permute-done.24.refs_1_.refs_3_
  56.5 0.8 %collective-permute-done.22.refs_2_.refs_1_ = bf16[8,10752]{1,0:T(8,128)(2,1)S(1)} collective-permute-done((bf16[8,10752]{1,0:T(8,128)(2,1)S(1)}, bf16[8,10752]{1,0:T(8,128)(2,1)S(1)}, u32[]{:S(2)}, u32[]{:S(2)}) %collective-permute-start.22) | collective-permute-done | bytes 172064 | tf_op jit(solution)/shard_map/ppermute | solution.py:263
  57.3 1.3 %collective-permute-start.25 = (bf16[8,10752]{1,0:T(8,128)(2,1)S(1)}, bf16[8,10752]{1,0:T(8,128)(2,1)S(1)}, u32[]{:S(2)}, u32[]{:S(2)}) collective-permute-start(bf16[8,10752]{1,0:T(8,128)(2,1)S(1)} %shard_map.81), channel_id=1, source_target_pairs={{0,8},{1,9},{2,10},{3,11},{4,12},{5,13},{6,14},{7,15},{8,0},{9,1},... | collective-permute-start | bytes 516104 | tf_op jit(solution)/shard_map/ppermute | solution.py:263
  58.7 1.9 %collective-permute-done.20 = bf16[8,10752]{1,0:T(8,128)(2,1)S(1)} collective-permute-done((bf16[8,10752]{1,0:T(8,128)(2,1)S(1)}, bf16[8,10752]{1,0:T(8,128)(2,1)S(1)}, u32[]{:S(2)}, u32[]{:S(2)}) %collective-permute-start.20) | collective-permute-done | bytes 172064 | tf_op jit(solution)/shard_map/ppermute | solution.py:266
  60.5 0.1 add_convert_fusion.2.refs_0_
  60.6 6.6 %collective-permute-done.25.refs_2_ = bf16[8,10752]{1,0:T(8,128)(2,1)S(1)} collective-permute-done((bf16[8,10752]{1,0:T(8,128)(2,1)S(1)}, bf16[8,10752]{1,0:T(8,128)(2,1)S(1)}, u32[]{:S(2)}, u32[]{:S(2)}) %collective-permute-start.25) | collective-permute-done | bytes 172064 | tf_op jit(solution)/shard_map/ppermute | solution.py:263
  67.2 1.9 %shard_map.82 = bf16[16,7168]{1,0:T(8,128)(2,1)} custom-call(s32[4]{0:T(128)S(1)} %copy-done.1, s32[2,16]{1,0:T(2,128)S(1)} %bitcast.4, f32[2,16]{1,0:T(2,128)S(1)} %bitcast.5, bf16[8,10752]{1,0:T(8,128)(2,1)S(1)} %add_convert_fusion.2.refs_0_, bf16[8,10752]{1,0:T(8,128)(2,1)S(1)} %collective-permute-done.22.refs_2_.refs_1_, ...), custom_call_target="tpu_custom_call" | custom-call | flops 44040192 | bytes 1146880 | tf_op jit(solution)/shard_map/pallas_call | solution.py:237
  (12 shorter events, 0.2 us)
Async XLA Ops:
  1.4 7.4 %collective-permute-start = (bf16[8,10752]{1,0:T(8,128)(2,1)S(1)}, bf16[8,10752]{1,0:T(8,128)(2,1)S(1)}, u32[]{:S(2)}, u32[]{:S(2)}) collective-permute-start(bf16[8,10752]{1,0:T(8,128)(2,1)S(1)} %get-tuple-element.19.refs_3_.refs_0_), channel_id=1, source_target_pairs={{0,2},{1,3},{2,0},{3,1},{4,6},{5,7},{6,4},{7,5},{8,10},{9,11},{10,... | collective-permute-start | bytes 516104 | tf_op jit(solution)/shard_map/ppermute | solution.py:266
  4.4 9.1 %collective-permute-start.4 = (bf16[8,10752]{1,0:T(8,128)(2,1)S(1)}, bf16[8,10752]{1,0:T(8,128)(2,1)S(1)}, u32[]{:S(2)}, u32[]{:S(2)}) collective-permute-start(bf16[8,10752]{1,0:T(8,128)(2,1)S(1)} %get-tuple-element.25), channel_id=1, source_target_pairs={{0,12},{1,13},{2,14},{3,15},{4,8},{5,9},{6,10},{7,11},{8,4},{9,5},... | collective-permute-start | bytes 516104 | tf_op jit(solution)/shard_map/ppermute | solution.py:263
  8.0 10.1 %collective-permute-start.5 = (bf16[8,10752]{1,0:T(8,128)(2,1)S(1)}, bf16[8,10752]{1,0:T(8,128)(2,1)S(1)}, u32[]{:S(2)}, u32[]{:S(2)}) collective-permute-start(bf16[8,10752]{1,0:T(8,128)(2,1)S(1)} %get-tuple-element.26), channel_id=1, source_target_pairs={{0,4},{1,5},{2,6},{3,7},{4,0},{5,1},{6,2},{7,3},{8,12},{9,13},{10,... | collective-permute-start | bytes 516104 | tf_op jit(solution)/shard_map/ppermute | solution.py:263
  8.0 13.2 %collective-permute-start.1 = (bf16[8,10752]{1,0:T(8,128)(2,1)S(1)}, bf16[8,10752]{1,0:T(8,128)(2,1)S(1)}, u32[]{:S(2)}, u32[]{:S(2)}) collective-permute-start(bf16[8,10752]{1,0:T(8,128)(2,1)S(1)} %get-tuple-element.19.refs_3_.refs_0_), channel_id=1, source_target_pairs={{0,1},{1,0},{2,3},{3,2},{4,5},{5,4},{6,7},{7,6},{8,9},{9,8},{10,11... | collective-permute-start | bytes 516104 | tf_op jit(solution)/shard_map/ppermute | solution.py:269
  8.8 15.5 %collective-permute-start.2 = (bf16[8,10752]{1,0:T(8,128)(2,1)S(1)}, bf16[8,10752]{1,0:T(8,128)(2,1)S(1)}, u32[]{:S(2)}, u32[]{:S(2)}) collective-permute-start(bf16[8,10752]{1,0:T(8,128)(2,1)S(1)} %collective-permute-done.refs_1_), channel_id=1, source_target_pairs={{0,1},{1,0},{2,3},{3,2},{4,5},{5,4},{6,7},{7,6},{8,9},{9,8},{10,11... | collective-permute-start | bytes 516104 | tf_op jit(solution)/shard_map/ppermute | solution.py:269
  13.5 13.0 %collective-permute-start.10 = (bf16[8,10752]{1,0:T(8,128)(2,1)S(1)}, bf16[8,10752]{1,0:T(8,128)(2,1)S(1)}, u32[]{:S(2)}, u32[]{:S(2)}) collective-permute-start(bf16[8,10752]{1,0:T(8,128)(2,1)S(1)} %collective-permute-done.4.refs_0_), channel_id=1, source_target_pairs={{0,2},{1,3},{2,0},{3,1},{4,6},{5,7},{6,4},{7,5},{8,10},{9,11},{10,... | collective-permute-start | bytes 516104 | tf_op jit(solution)/shard_map/ppermute | solution.py:266
  18.0 9.0 %collective-permute-start.11 = (bf16[8,10752]{1,0:T(8,128)(2,1)S(1)}, bf16[8,10752]{1,0:T(8,128)(2,1)S(1)}, u32[]{:S(2)}, u32[]{:S(2)}) collective-permute-start(bf16[8,10752]{1,0:T(8,128)(2,1)S(1)} %collective-permute-done.4.refs_0_), channel_id=1, source_target_pairs={{0,1},{1,0},{2,3},{3,2},{4,5},{5,4},{6,7},{7,6},{8,9},{9,8},{10,11... | collective-permute-start | bytes 516104 | tf_op jit(solution)/shard_map/ppermute | solution.py:269
  18.1 9.0 %collective-permute-start.14 = (bf16[8,10752]{1,0:T(8,128)(2,1)S(1)}, bf16[8,10752]{1,0:T(8,128)(2,1)S(1)}, u32[]{:S(2)}, u32[]{:S(2)}) collective-permute-start(bf16[8,10752]{1,0:T(8,128)(2,1)S(1)} %collective-permute-done.5.refs_1_.refs_0_), channel_id=1, source_target_pairs={{0,2},{1,3},{2,0},{3,1},{4,6},{5,7},{6,4},{7,5},{8,10},{9,11},{10,... | collective-permute-start | bytes 516104 | tf_op jit(solution)/shard_map/ppermute | solution.py:266
  21.3 11.5 %collective-permute-start.6 = (bf16[8,10752]{1,0:T(8,128)(2,1)S(1)}, bf16[8,10752]{1,0:T(8,128)(2,1)S(1)}, u32[]{:S(2)}, u32[]{:S(2)}) collective-permute-start(bf16[8,10752]{1,0:T(8,128)(2,1)S(1)} %shard_map.76), channel_id=1, source_target_pairs={{0,8},{1,9},{2,10},{3,11},{4,12},{5,13},{6,14},{7,15},{8,0},{9,1},... | collective-permute-start | bytes 516104 | tf_op jit(solution)/shard_map/ppermute | solution.py:263
  26.4 12.2 %collective-permute-start.3 = (bf16[16,10752]{1,0:T(8,128)(2,1)S(1)}, bf16[16,10752]{1,0:T(8,128)(2,1)S(1)}, u32[]{:S(2)}, u32[]{:S(2)}) collective-permute-start(bf16[16,10752]{1,0:T(8,128)(2,1)S(1)} %get-tuple-element.24.refs_7_), channel_id=1, source_target_pairs={{0,1},{1,0},{2,3},{3,2},{4,5},{5,4},{6,7},{7,6},{8,9},{9,8},{10,11... | collective-permute-start | bytes 1032200 | tf_op jit(solution)/shard_map/ppermute | solution.py:269
  26.5 6.7 %collective-permute-start.12 = (bf16[8,10752]{1,0:T(8,128)(2,1)S(1)}, bf16[8,10752]{1,0:T(8,128)(2,1)S(1)}, u32[]{:S(2)}, u32[]{:S(2)}) collective-permute-start(bf16[8,10752]{1,0:T(8,128)(2,1)S(1)} %collective-permute-done.10.refs_1_), channel_id=1, source_target_pairs={{0,1},{1,0},{2,3},{3,2},{4,5},{5,4},{6,7},{7,6},{8,9},{9,8},{10,11... | collective-permute-start | bytes 516104 | tf_op jit(solution)/shard_map/ppermute | solution.py:269
  27.0 8.3 %collective-permute-start.15 = (bf16[8,10752]{1,0:T(8,128)(2,1)S(1)}, bf16[8,10752]{1,0:T(8,128)(2,1)S(1)}, u32[]{:S(2)}, u32[]{:S(2)}) collective-permute-start(bf16[8,10752]{1,0:T(8,128)(2,1)S(1)} %collective-permute-done.5.refs_1_.refs_0_), channel_id=1, source_target_pairs={{0,1},{1,0},{2,3},{3,2},{4,5},{5,4},{6,7},{7,6},{8,9},{9,8},{10,11... | collective-permute-start | bytes 516104 | tf_op jit(solution)/shard_map/ppermute | solution.py:269
  27.1 8.8 %collective-permute-start.16 = (bf16[8,10752]{1,0:T(8,128)(2,1)S(1)}, bf16[8,10752]{1,0:T(8,128)(2,1)S(1)}, u32[]{:S(2)}, u32[]{:S(2)}) collective-permute-start(bf16[8,10752]{1,0:T(8,128)(2,1)S(1)} %collective-permute-done.14.refs_1_), channel_id=1, source_target_pairs={{0,1},{1,0},{2,3},{3,2},{4,5},{5,4},{6,7},{7,6},{8,9},{9,8},{10,11... | collective-permute-start | bytes 516104 | tf_op jit(solution)/shard_map/ppermute | solution.py:269
  32.7 5.9 %collective-permute-start.7 = (bf16[8,10752]{1,0:T(8,128)(2,1)S(1)}, bf16[8,10752]{1,0:T(8,128)(2,1)S(1)}, u32[]{:S(2)}, u32[]{:S(2)}) collective-permute-start(bf16[8,10752]{1,0:T(8,128)(2,1)S(1)} %collective-permute-done.6.refs_0_), channel_id=1, source_target_pairs={{0,2},{1,3},{2,0},{3,1},{4,6},{5,7},{6,4},{7,5},{8,10},{9,11},{10,... | collective-permute-start | bytes 516104 | tf_op jit(solution)/shard_map/ppermute | solution.py:266
  33.2 8.1 %collective-permute-start.8 = (bf16[8,10752]{1,0:T(8,128)(2,1)S(1)}, bf16[8,10752]{1,0:T(8,128)(2,1)S(1)}, u32[]{:S(2)}, u32[]{:S(2)}) collective-permute-start(bf16[8,10752]{1,0:T(8,128)(2,1)S(1)} %collective-permute-done.6.refs_0_), channel_id=1, source_target_pairs={{0,1},{1,0},{2,3},{3,2},{4,5},{5,4},{6,7},{7,6},{8,9},{9,8},{10,11... | collective-permute-start | bytes 516104 | tf_op jit(solution)/shard_map/ppermute | solution.py:269
  35.3 3.4 %collective-permute-start.13 = (bf16[16,10752]{1,0:T(8,128)(2,1)S(1)}, bf16[16,10752]{1,0:T(8,128)(2,1)S(1)}, u32[]{:S(2)}, u32[]{:S(2)}) collective-permute-start(bf16[16,10752]{1,0:T(8,128)(2,1)S(1)} %get-tuple-element.28), channel_id=1, source_target_pairs={{0,1},{1,0},{2,3},{3,2},{4,5},{5,4},{6,7},{7,6},{8,9},{9,8},{10,11... | collective-permute-start | bytes 1032200 | tf_op jit(solution)/shard_map/ppermute | solution.py:269
  38.0 2.3 %collective-permute-start.17 = (bf16[16,10752]{1,0:T(8,128)(2,1)S(1)}, bf16[16,10752]{1,0:T(8,128)(2,1)S(1)}, u32[]{:S(2)}, u32[]{:S(2)}) collective-permute-start(bf16[16,10752]{1,0:T(8,128)(2,1)S(1)} %get-tuple-element.30), channel_id=1, source_target_pairs={{0,1},{1,0},{2,3},{3,2},{4,5},{5,4},{6,7},{7,6},{8,9},{9,8},{10,11... | collective-permute-start | bytes 1032200 | tf_op jit(solution)/shard_map/ppermute | solution.py:269
  38.6 2.7 %collective-permute-start.9 = (bf16[8,10752]{1,0:T(8,128)(2,1)S(1)}, bf16[8,10752]{1,0:T(8,128)(2,1)S(1)}, u32[]{:S(2)}, u32[]{:S(2)}) collective-permute-start(bf16[8,10752]{1,0:T(8,128)(2,1)S(1)} %collective-permute-done.7.refs_1_), channel_id=1, source_target_pairs={{0,1},{1,0},{2,3},{3,2},{4,5},{5,4},{6,7},{7,6},{8,9},{9,8},{10,11... | collective-permute-start | bytes 516104 | tf_op jit(solution)/shard_map/ppermute | solution.py:269
  38.8 7.2 %collective-permute-start.23 = (bf16[8,10752]{1,0:T(8,128)(2,1)S(1)}, bf16[8,10752]{1,0:T(8,128)(2,1)S(1)}, u32[]{:S(2)}, u32[]{:S(2)}) collective-permute-start(bf16[8,10752]{1,0:T(8,128)(2,1)S(1)} %add_convert_fusion.6.refs_7_), channel_id=1, source_target_pairs={{0,2},{1,3},{2,0},{3,1},{4,6},{5,7},{6,4},{7,5},{8,10},{9,11},{10,... | collective-permute-start | bytes 516104 | tf_op jit(solution)/shard_map/ppermute | solution.py:266
  40.3 10.7 %collective-permute-start.21 = (bf16[8,10752]{1,0:T(8,128)(2,1)S(1)}, bf16[8,10752]{1,0:T(8,128)(2,1)S(1)}, u32[]{:S(2)}, u32[]{:S(2)}) collective-permute-start(bf16[8,10752]{1,0:T(8,128)(2,1)S(1)} %add_convert_fusion.5.refs_8_), channel_id=1, source_target_pairs={{0,2},{1,3},{2,0},{3,1},{4,6},{5,7},{6,4},{7,5},{8,10},{9,11},{10,... | collective-permute-start | bytes 516104 | tf_op jit(solution)/shard_map/ppermute | solution.py:266
  43.4 23.8 %copy-start = (s32[16,2]{0,1:T(2,128)S(1)}, s32[16,2]{0,1:T(2,128)}, u32[]{:S(2)}) copy-start(s32[16,2]{0,1:T(2,128)} %param.8) | copy-start | bytes 388
  43.4 23.8 %copy-start.1 = (s32[4]{0:T(128)S(1)}, s32[4]{0:T(128)}, u32[]{:S(2)}) copy-start(s32[4]{0:T(128)} %placement_ref.5) | copy-start | bytes 52
  43.4 23.8 %copy-start.2 = (f32[16,2]{0,1:T(2,128)S(1)}, f32[16,2]{0,1:T(2,128)}, u32[]{:S(2)}) copy-start(f32[16,2]{0,1:T(2,128)} %param.9) | copy-start | bytes 388
  43.4 6.0 %collective-permute-start.18 = (bf16[16,10752]{1,0:T(8,128)(2,1)S(1)}, bf16[16,10752]{1,0:T(8,128)(2,1)S(1)}, u32[]{:S(2)}, u32[]{:S(2)}) collective-permute-start(bf16[16,10752]{1,0:T(8,128)(2,1)S(1)} %get-tuple-element.32), channel_id=1, source_target_pairs={{0,1},{1,0},{2,3},{3,2},{4,5},{5,4},{6,7},{7,6},{8,9},{9,8},{10,11... | collective-permute-start | bytes 1032200 | tf_op jit(solution)/shard_map/ppermute | solution.py:269
  46.1 10.5 %collective-permute-start.24 = (bf16[8,10752]{1,0:T(8,128)(2,1)S(1)}, bf16[8,10752]{1,0:T(8,128)(2,1)S(1)}, u32[]{:S(2)}, u32[]{:S(2)}) collective-permute-start(bf16[8,10752]{1,0:T(8,128)(2,1)S(1)} %add_convert_fusion), channel_id=1, source_target_pairs={{0,12},{1,13},{2,14},{3,15},{4,8},{5,9},{6,10},{7,11},{8,4},{9,5},... | collective-permute-start | bytes 516104 | tf_op jit(solution)/shard_map/ppermute | solution.py:263
  49.5 5.5 %collective-permute-start.19 = (bf16[8,10752]{1,0:T(8,128)(2,1)S(1)}, bf16[8,10752]{1,0:T(8,128)(2,1)S(1)}, u32[]{:S(2)}, u32[]{:S(2)}) collective-permute-start(bf16[8,10752]{1,0:T(8,128)(2,1)S(1)} %add_convert_fusion.4), channel_id=1, source_target_pairs={{0,2},{1,3},{2,0},{3,1},{4,6},{5,7},{6,4},{7,5},{8,10},{9,11},{10,... | collective-permute-start | bytes 516104 | tf_op jit(solution)/shard_map/ppermute | solution.py:266
  51.0 6.3 %collective-permute-start.22 = (bf16[8,10752]{1,0:T(8,128)(2,1)S(1)}, bf16[8,10752]{1,0:T(8,128)(2,1)S(1)}, u32[]{:S(2)}, u32[]{:S(2)}) collective-permute-start(bf16[8,10752]{1,0:T(8,128)(2,1)S(1)} %add_convert_fusion.1), channel_id=1, source_target_pairs={{0,4},{1,5},{2,6},{3,7},{4,0},{5,1},{6,2},{7,3},{8,12},{9,13},{10,... | collective-permute-start | bytes 516104 | tf_op jit(solution)/shard_map/ppermute | solution.py:263
  55.1 5.5 %collective-permute-start.20 = (bf16[8,10752]{1,0:T(8,128)(2,1)S(1)}, bf16[8,10752]{1,0:T(8,128)(2,1)S(1)}, u32[]{:S(2)}, u32[]{:S(2)}) collective-permute-start(bf16[8,10752]{1,0:T(8,128)(2,1)S(1)} %shard_map.80), channel_id=1, source_target_pairs={{0,2},{1,3},{2,0},{3,1},{4,6},{5,7},{6,4},{7,5},{8,10},{9,11},{10,... | collective-permute-start | bytes 516104 | tf_op jit(solution)/shard_map/ppermute | solution.py:266
  57.3 9.9 %collective-permute-start.25 = (bf16[8,10752]{1,0:T(8,128)(2,1)S(1)}, bf16[8,10752]{1,0:T(8,128)(2,1)S(1)}, u32[]{:S(2)}, u32[]{:S(2)}) collective-permute-start(bf16[8,10752]{1,0:T(8,128)(2,1)S(1)} %shard_map.81), channel_id=1, source_target_pairs={{0,8},{1,9},{2,10},{3,11},{4,12},{5,13},{6,14},{7,15},{8,0},{9,1},... | collective-permute-start | bytes 516104 | tf_op jit(solution)/shard_map/ppermute | solution.py:263

commit v6 on v5

--- a/solution.py
+++ b/solution.py
@@ -12,6 +12,7 @@
 SMEM = pl.BlockSpec(memory_space=pltpu.SMEM)
 ANYWHERE = pl.BlockSpec(memory_space=pl.ANY)
 LOADS = 4
+N1, N2, N3, N4 = 30,30,30,30
 NO_COST = pl.CostEstimate(flops=0, bytes_accessed=0, transcendentals=0)
 
 
@@ -57,14 +58,14 @@
     return jnp.where(row < half, row, half + row % quarter).astype(jnp.float32)
 
 
-def pack_kernel(n_blocks, parts, distances, placement_ref, ids_ref, tokens_ref, *refs):
+def pack_kernel(n_blocks, parts, placement_ref, ids_ref, tokens_ref, *out_refs):
     rows, width = tokens_ref.shape
     half, quarter = rows // 2, rows // 4
     block = lax.axis_index("node") // parts
     experts, picks, earlier = slots_of(ids_ref[...], n_blocks)
     wanted = bucket_rows(rows)
     upper = lax.broadcasted_iota(jnp.int32, (half, width // 2), 0) < quarter
-    for k, out_ref in zip(distances, refs[-len(distances) :]):
+    for k, out_ref in enumerate(out_refs):
         expert = expert_at(placement_ref, lax.bitwise_xor(block, jnp.int32(k)))
         named = row_of(picks, experts, expert) > 0.5
         slot = row_of(earlier, experts, expert)
@@ -75,18 +76,17 @@
         out_ref[:, width:] = rest.astype(jnp.bfloat16)
 
 
-def pack(placement, ids, tokens, n_blocks, parts, distances, after):
+def pack(placement, ids, tokens, n_blocks, parts):
     rows, width = tokens.shape
     shape = pltpu.VMEM((rows // 2, width + width // 2), jnp.bfloat16)
-    out = pl.pallas_call(
-        functools.partial(pack_kernel, n_blocks, parts, distances),
-        out_shape=[shape] * len(distances),
-        in_specs=[SMEM, VMEM, VMEM] + [ANYWHERE] * len(after),
-        out_specs=[VMEM] * len(distances),
+    return pl.pallas_call(
+        functools.partial(pack_kernel, n_blocks, parts),
+        out_shape=[shape] * n_blocks,
+        in_specs=[SMEM, VMEM, VMEM],
+        out_specs=[VMEM] * n_blocks,
         compiler_params=pltpu.CompilerParams(vmem_limit_bytes=VMEM_BYTES),
         cost_estimate=NO_COST,
-    )(in_hbm(placement), in_hbm(ids), in_hbm(tokens), *after)
-    return dict(zip(distances, out))
+    )(in_hbm(placement), in_hbm(ids), in_hbm(tokens))
 
 
 def nothing(*refs):
@@ -285,22 +285,28 @@
         home[k] = add(kept[k][:half], returned[k][:half], back)
         results[k] = along_z(when(home[k], after_z), k) if k else home[k]
 
+    buckets = list(pack(placement, ids, tokens, n_blocks, parts))
+    straight[0] = buckets[0]
+    across[0] = along_y(straight[0])
     for g, group in enumerate(groups):
-        members = [0] + group if g == 0 else group
-        after = [arrived[k] for k in groups[g - 1]] + [weights[0]] if g else []
-        buckets = pack(placement, ids, tokens, n_blocks, parts, members, after)
-        if g == 0:
-            straight[0] = buckets[0]
-            across[0] = along_y(straight[0])
-            weights = load((gate_weight, up_weight, down_weight), buckets[0])
+        previous = groups[g - 1] if g else []
+        if g:
+            after = [arrived[k] for k in previous] + [across[0]]
+            for k in group:
+                buckets[k] = when(buckets[k], after)
         for k in group:
             straight[k] = arrived[k] = along_z(buckets[k], k)
-        if g == 0:
-            compute(0, [])
+    for k in groups[0]:
+        across[k] = along_y(straight[k])
+    weights = load((gate_weight, up_weight, down_weight), across[groups[0][0]])
+    compute(0, [])
+    for g, group in enumerate(groups):
+        previous = groups[g - 1] if g else []
         for i, k in enumerate(group):
-            across[k] = along_y(straight[k])
-            compute(k, [both[j] for j in groups[g - 1]] if g else [sent[0]][:i])
-            go_home(k, [], [results[j] for j in groups[g - 1]] if g else [])
+            if g:
+                across[k] = along_y(straight[k])
+            compute(k, [both[j] for j in previous] if g else [sent[0]][:i])
+            go_home(k, [], [results[j] for j in previous])
     go_home(0, [home[last]], [])
     return mix(placement, ids, gates.T, [results[k] for k in range(n_blocks)], n_blocks, parts)
 

time: 69.3 us -> 63.6 us (0.918)
  waiting for transfers between devices: 27 us -> 20.9 us
  starting transfers between devices: 24.4 us -> 26 us
  Pallas kernels: 17.1 us -> 15.8 us
    ppermute x6, waiting for transfers between devices: 17.4 us -> 11.9 us  [along_z(): return lax.ppermute(value, 'node', pairs)]
    ppermute x6, starting transfers between devices: 11.5 us -> 13.9 us  [along_z(): return lax.ppermute(value, 'node', pairs)]
    ppermute x8, starting transfers between devices: 11 us -> 9.72 us  [along_y(): return lax.ppermute(value, 'node', [(i, i ^ 2) for i in range(devices)])]
    pallas_call x2 -> x1, Pallas kernels: 2.67 us -> 1.46 us  [pack(): pl.pallas_call(functools.partial(pack_kernel, n_blocks, parts), out_shape...]
    ppermute x8, waiting for transfers between devices: 9.59 us -> 8.64 us  [along_y(): return lax.ppermute(value, 'node', [(i, i ^ 2) for i in range(devices)])]
where the time goes in v6:
time: 63.6 us; the launch traced here: 63.4 us
  starting transfers between devices  26 us (41%)
  waiting for transfers between devices  20.9 us (33%)
  Pallas kernels  15.8 us (25%)
    ppermute x6, starting transfers between devices, along_z(): return lax.ppermute(value, 'node', pairs)  13.9 us
    ppermute x6, waiting for transfers between devices, along_z(): return lax.ppermute(value, 'node', pairs)  11.9 us
    ppermute x8, starting transfers between devices, along_y(): return lax.ppermute(value, 'node', [(i, i ^ 2) for i in range(devices)])  9.72 us
    ppermute x8, waiting for transfers between devices, along_y(): return lax.ppermute(value, 'node', [(i, i ^ 2) for i in range(devices)])  8.64 us
    pallas_call x4, Pallas kernels, run_experts(): pl.pallas_call(experts_kernel, out_shape=[shape] * 2, in_specs=[VMEM] * 7...  8.29 us
    pallas_call x1, Pallas kernels, load(): pl.pallas_call(load_kernel, out_shape=[pltpu.VMEM(w.shape, w.dtype) for w...  4.24 us
    ppermute x12, starting transfers between devices, along_core(): return lax.ppermute(value, 'node', [(i, i ^ 1) for i in range(devices)])  2.44 us
    pallas_call x1, Pallas kernels, mix(): pl.pallas_call(functools.partial(mix_kernel, n_blocks, parts), out_shape=...  1.85 us
  transfers between devices with their start and end apart: 26, of which 9 were waited for; matrix products, arithmetic and copies ran while one was open for 1% of the time, Pallas kernels for 20%

profile of v6, /device:TPU:0, one launch (start us, length us, event | category | flops | bytes accessed | tf_op | source)
XLA Modules:
  0.0 63.4 jit_solution(8870400156719476387)
XLA Ops:
  0.0 1.5 %shard_map.73 = (bf16[8,10752]{1,0:T(8,128)(2,1)S(1)}, bf16[8,10752]{1,0:T(8,128)(2,1)S(1)}, bf16[8,10752]{1,0:T(8,128)(2,1)S(1)}, bf16[8,10752]{1,0:T(8,128)(2,1)S(1)}) custom-call(s32[4]{0:T(128)} %placement_ref.3, s32[2,16]{1,0:T(2,128)} %bitcast.2, bf16[16,7168]{1,0:T(8,128)(2,1)} %tokens_ref.1), custom_call_target="tpu_custom_call" | custom-call | tf_op jit(solution)/shard_map/pallas_call | solution.py:82
  1.5 5.1 %collective-permute-start.3 = (bf16[8,10752]{1,0:T(8,128)(2,1)S(1)}, bf16[8,10752]{1,0:T(8,128)(2,1)S(1)}, u32[]{:S(2)}, u32[]{:S(2)}) collective-permute-start(bf16[8,10752]{1,0:T(8,128)(2,1)S(1)} %get-tuple-element.21), channel_id=1, source_target_pairs={{0,12},{1,13},{2,14},{3,15},{4,8},{5,9},{6,10},{7,11},{8,4},{9,5},... | collective-permute-start | bytes 516104 | tf_op jit(solution)/shard_map/ppermute | solution.py:263
  6.6 1.5 %collective-permute-start = (bf16[8,10752]{1,0:T(8,128)(2,1)S(1)}, bf16[8,10752]{1,0:T(8,128)(2,1)S(1)}, u32[]{:S(2)}, u32[]{:S(2)}) collective-permute-start(bf16[8,10752]{1,0:T(8,128)(2,1)S(1)} %get-tuple-element.20.refs_0_), channel_id=1, source_target_pairs={{0,2},{1,3},{2,0},{3,1},{4,6},{5,7},{6,4},{7,5},{8,10},{9,11},{10,... | collective-permute-start | bytes 516104 | tf_op jit(solution)/shard_map/ppermute | solution.py:266
  8.1 0.0 collective-permute-start.6
  8.1 3.7 %collective-permute-done.3.refs_1_.refs_0_ = bf16[8,10752]{1,0:T(8,128)(2,1)S(1)} collective-permute-done((bf16[8,10752]{1,0:T(8,128)(2,1)S(1)}, bf16[8,10752]{1,0:T(8,128)(2,1)S(1)}, u32[]{:S(2)}, u32[]{:S(2)}) %collective-permute-start.3) | collective-permute-done | bytes 172064 | tf_op jit(solution)/shard_map/ppermute | solution.py:263
  11.8 1.7 %collective-permute-start.4 = (bf16[8,10752]{1,0:T(8,128)(2,1)S(1)}, bf16[8,10752]{1,0:T(8,128)(2,1)S(1)}, u32[]{:S(2)}, u32[]{:S(2)}) collective-permute-start(bf16[8,10752]{1,0:T(8,128)(2,1)S(1)} %collective-permute-done.3.refs_1_.refs_0_), channel_id=1, source_target_pairs={{0,2},{1,3},{2,0},{3,1},{4,6},{5,7},{6,4},{7,5},{8,10},{9,11},{10,... | collective-permute-start | bytes 516104 | tf_op jit(solution)/shard_map/ppermute | solution.py:266
  13.6 0.0 collective-permute-start.1
  13.6 0.0 collective-permute-done.refs_1_.refs_3_
  13.6 0.5 collective-permute-start.2
  14.1 0.7 %collective-permute-done.6.refs_2_.refs_0_ = bf16[8,10752]{1,0:T(8,128)(2,1)S(1)} collective-permute-done((bf16[8,10752]{1,0:T(8,128)(2,1)S(1)}, bf16[8,10752]{1,0:T(8,128)(2,1)S(1)}, u32[]{:S(2)}, u32[]{:S(2)}) %collective-permute-start.6) | collective-permute-done | bytes 172064 | tf_op jit(solution)/shard_map/ppermute | solution.py:263
  14.7 2.7 %collective-permute-start.7 = (bf16[8,10752]{1,0:T(8,128)(2,1)S(1)}, bf16[8,10752]{1,0:T(8,128)(2,1)S(1)}, u32[]{:S(2)}, u32[]{:S(2)}) collective-permute-start(bf16[8,10752]{1,0:T(8,128)(2,1)S(1)} %shard_map.76), channel_id=1, source_target_pairs={{0,8},{1,9},{2,10},{3,11},{4,12},{5,13},{6,14},{7,15},{8,0},{9,1},... | collective-permute-start | bytes 516104 | tf_op jit(solution)/shard_map/ppermute | solution.py:263
  17.4 0.0 collective-permute-start.11
  17.4 0.0 collective-permute-done.4.refs_3_.refs_1_
  17.4 1.6 %collective-permute-start.14 = (bf16[8,10752]{1,0:T(8,128)(2,1)S(1)}, bf16[8,10752]{1,0:T(8,128)(2,1)S(1)}, u32[]{:S(2)}, u32[]{:S(2)}) collective-permute-start(bf16[8,10752]{1,0:T(8,128)(2,1)S(1)} %collective-permute-done.6.refs_2_.refs_0_), channel_id=1, source_target_pairs={{0,2},{1,3},{2,0},{3,1},{4,6},{5,7},{6,4},{7,5},{8,10},{9,11},{10,... | collective-permute-start | bytes 516104 | tf_op jit(solution)/shard_map/ppermute | solution.py:266
  19.0 4.2 %shard_map.74 = (bf16[7168,256]{1,0:T(8,128)(2,1)S(1)}, bf16[7168,256]{1,0:T(8,128)(2,1)S(1)}, bf16[256,7168]{1,0:T(8,128)(2,1)S(1)}) custom-call(bf16[7168,256]{1,0:T(8,128)(2,1)} %refs_0_.1, bf16[7168,256]{1,0:T(8,128)(2,1)} %refs_1_.1, bf16[256,7168]{1,0:T(8,128)(2,1)} %refs_2_.1, bf16[8,10752]{1,0:T(8,128)(2,1)S(1)} %collective-permute-done.4.refs_3_.refs_1_), custom_call_target="tpu_custom_call" | custom-call | tf_op jit(solution)/shard_map/pallas_call | solution.py:125
  23.2 0.0 collective-permute-done.1.refs_2_
  23.2 0.0 collective-permute-done.2.refs_3_
  23.2 2.1 %shard_map.75 = (bf16[16,10752]{1,0:T(8,128)(2,1)S(1)}, bf16[16,10752]{1,0:T(8,128)(2,1)S(1)}) custom-call(bf16[8,10752]{1,0:T(8,128)(2,1)S(1)} %get-tuple-element.20.refs_0_, bf16[8,10752]{1,0:T(8,128)(2,1)S(1)} %collective-permute-done.refs_1_.refs_3_, bf16[8,10752]{1,0:T(8,128)(2,1)S(1)} %collective-permute-done.1.refs_2_, ...), custom_call_target="tpu_custom_call" | custom-call | bytes 7340032 | tf_op jit(solution)/shard_map/pallas_call | solution.py:185
  25.3 0.1 collective-permute-start.5
  25.4 0.5 collective-permute-start.12
  25.9 0.0 collective-permute-done.11.refs_2_
  25.9 0.1 collective-permute-start.15
  26.0 0.0 collective-permute-done.14.refs_1_
  26.0 0.4 collective-permute-start.16
  26.4 0.0 collective-permute-done.7.refs_0_
  26.4 0.5 collective-permute-start.8
  26.9 0.3 collective-permute-done.12.refs_3_
  27.3 0.1 collective-permute-start.9
  27.4 2.1 %shard_map.77 = (bf16[16,10752]{1,0:T(8,128)(2,1)S(1)}, bf16[16,10752]{1,0:T(8,128)(2,1)S(1)}) custom-call(bf16[8,10752]{1,0:T(8,128)(2,1)S(1)} %collective-permute-done.3.refs_1_.refs_0_, bf16[8,10752]{1,0:T(8,128)(2,1)S(1)} %collective-permute-done.4.refs_3_.refs_1_, bf16[8,10752]{1,0:T(8,128)(2,1)S(1)} %collective-permute-done.11.refs_2_, ...), custom_call_target="tpu_custom_call" | custom-call | bytes 7340032 | tf_op jit(solution)/shard_map/pallas_call | solution.py:185
  29.5 0.0 collective-permute-done.15.refs_2_
  29.5 0.4 collective-permute-start.13
  29.9 0.0 collective-permute-done.16.refs_3_
  29.9 2.1 %shard_map.78 = (bf16[16,10752]{1,0:T(8,128)(2,1)S(1)}, bf16[16,10752]{1,0:T(8,128)(2,1)S(1)}) custom-call(bf16[8,10752]{1,0:T(8,128)(2,1)S(1)} %collective-permute-done.6.refs_2_.refs_0_, bf16[8,10752]{1,0:T(8,128)(2,1)S(1)} %collective-permute-done.14.refs_1_, bf16[8,10752]{1,0:T(8,128)(2,1)S(1)} %collective-permute-done.15.refs_2_, ...), custom_call_target="tpu_custom_call" | custom-call | bytes 7340032 | tf_op jit(solution)/shard_map/pallas_call | solution.py:185
  32.0 0.2 collective-permute-start.17
  32.2 0.5 collective-permute-done.8.refs_1_
  32.8 0.0 collective-permute-start.10
  32.8 0.0 collective-permute-done.5
  32.8 0.0 collective-permute-done.13
  32.9 1.1 %collective-permute-start.23 = (bf16[8,10752]{1,0:T(8,128)(2,1)S(1)}, bf16[8,10752]{1,0:T(8,128)(2,1)S(1)}, u32[]{:S(2)}, u32[]{:S(2)}) collective-permute-start(bf16[8,10752]{1,0:T(8,128)(2,1)S(1)} %add_convert_fusion.6.refs_7_), channel_id=1, source_target_pairs={{0,2},{1,3},{2,0},{3,1},{4,6},{5,7},{6,4},{7,5},{8,10},{9,11},{10,... | collective-permute-start | bytes 516104 | tf_op jit(solution)/shard_map/ppermute | solution.py:266
  34.0 0.0 collective-permute-done.17
  34.0 1.1 %collective-permute-start.21 = (bf16[8,10752]{1,0:T(8,128)(2,1)S(1)}, bf16[8,10752]{1,0:T(8,128)(2,1)S(1)}, u32[]{:S(2)}, u32[]{:S(2)}) collective-permute-start(bf16[8,10752]{1,0:T(8,128)(2,1)S(1)} %add_convert_fusion.5.refs_8_), channel_id=1, source_target_pairs={{0,2},{1,3},{2,0},{3,1},{4,6},{5,7},{6,4},{7,5},{8,10},{9,11},{10,... | collective-permute-start | bytes 516104 | tf_op jit(solution)/shard_map/ppermute | solution.py:266
  35.1 0.0 collective-permute-done.9.refs_2_
  35.1 0.0 collective-permute-done.10.refs_3_
  35.1 2.1 %shard_map.79 = (bf16[16,10752]{1,0:T(8,128)(2,1)S(1)}, bf16[16,10752]{1,0:T(8,128)(2,1)S(1)}) custom-call(bf16[8,10752]{1,0:T(8,128)(2,1)S(1)} %collective-permute-done.7.refs_0_, bf16[8,10752]{1,0:T(8,128)(2,1)S(1)} %collective-permute-done.8.refs_1_, bf16[8,10752]{1,0:T(8,128)(2,1)S(1)} %collective-permute-done.9.refs_2_, ...), custom_call_target="tpu_custom_call" | custom-call | bytes 7340032 | tf_op jit(solution)/shard_map/pallas_call | solution.py:185
  37.2 0.0 copy-start
  37.2 0.0 copy-start.1
  37.2 0.0 copy-start.2
  37.2 0.1 collective-permute-start.18
  37.3 2.8 %collective-permute-done.23 = bf16[8,10752]{1,0:T(8,128)(2,1)S(1)} collective-permute-done((bf16[8,10752]{1,0:T(8,128)(2,1)S(1)}, bf16[8,10752]{1,0:T(8,128)(2,1)S(1)}, u32[]{:S(2)}, u32[]{:S(2)}) %collective-permute-start.23) | collective-permute-done | bytes 172064 | tf_op jit(solution)/shard_map/ppermute | solution.py:266
  40.1 0.1 add_convert_fusion
  40.2 3.7 %collective-permute-start.24 = (bf16[8,10752]{1,0:T(8,128)(2,1)S(1)}, bf16[8,10752]{1,0:T(8,128)(2,1)S(1)}, u32[]{:S(2)}, u32[]{:S(2)}) collective-permute-start(bf16[8,10752]{1,0:T(8,128)(2,1)S(1)} %add_convert_fusion), channel_id=1, source_target_pairs={{0,12},{1,13},{2,14},{3,15},{4,8},{5,9},{6,10},{7,11},{8,4},{9,5},... | collective-permute-start | bytes 516104 | tf_op jit(solution)/shard_map/ppermute | solution.py:263
  43.9 0.0 collective-permute-done.18
  43.9 1.1 %collective-permute-start.19 = (bf16[8,10752]{1,0:T(8,128)(2,1)S(1)}, bf16[8,10752]{1,0:T(8,128)(2,1)S(1)}, u32[]{:S(2)}, u32[]{:S(2)}) collective-permute-start(bf16[8,10752]{1,0:T(8,128)(2,1)S(1)} %add_convert_fusion.4), channel_id=1, source_target_pairs={{0,2},{1,3},{2,0},{3,1},{4,6},{5,7},{6,4},{7,5},{8,10},{9,11},{10,... | collective-permute-start | bytes 516104 | tf_op jit(solution)/shard_map/ppermute | solution.py:266
  45.0 0.1 add_convert_fusion.1
  45.1 0.8 %collective-permute-start.22 = (bf16[8,10752]{1,0:T(8,128)(2,1)S(1)}, bf16[8,10752]{1,0:T(8,128)(2,1)S(1)}, u32[]{:S(2)}, u32[]{:S(2)}) collective-permute-start(bf16[8,10752]{1,0:T(8,128)(2,1)S(1)} %add_convert_fusion.1), channel_id=1, source_target_pairs={{0,4},{1,5},{2,6},{3,7},{4,0},{5,1},{6,2},{7,3},{8,12},{9,13},{10,... | collective-permute-start | bytes 516104 | tf_op jit(solution)/shard_map/ppermute | solution.py:263
  45.9 3.5 %collective-permute-done.19 = bf16[8,10752]{1,0:T(8,128)(2,1)S(1)} collective-permute-done((bf16[8,10752]{1,0:T(8,128)(2,1)S(1)}, bf16[8,10752]{1,0:T(8,128)(2,1)S(1)}, u32[]{:S(2)}, u32[]{:S(2)}) %collective-permute-start.19) | collective-permute-done | bytes 172064 | tf_op jit(solution)/shard_map/ppermute | solution.py:266
  49.4 0.1 add_convert_fusion.3.refs_1_.refs_0_
  49.5 1.1 %collective-permute-start.20 = (bf16[8,10752]{1,0:T(8,128)(2,1)S(1)}, bf16[8,10752]{1,0:T(8,128)(2,1)S(1)}, u32[]{:S(2)}, u32[]{:S(2)}) collective-permute-start(bf16[8,10752]{1,0:T(8,128)(2,1)S(1)} %shard_map.80), channel_id=1, source_target_pairs={{0,2},{1,3},{2,0},{3,1},{4,6},{5,7},{6,4},{7,5},{8,10},{9,11},{10,... | collective-permute-start | bytes 516104 | tf_op jit(solution)/shard_map/ppermute | solution.py:266
  50.6 0.9 %collective-permute-done.22.refs_2_.refs_1_ = bf16[8,10752]{1,0:T(8,128)(2,1)S(1)} collective-permute-done((bf16[8,10752]{1,0:T(8,128)(2,1)S(1)}, bf16[8,10752]{1,0:T(8,128)(2,1)S(1)}, u32[]{:S(2)}, u32[]{:S(2)}) %collective-permute-start.22) | collective-permute-done | bytes 172064 | tf_op jit(solution)/shard_map/ppermute | solution.py:263
  51.5 1.6 %collective-permute-start.25 = (bf16[8,10752]{1,0:T(8,128)(2,1)S(1)}, bf16[8,10752]{1,0:T(8,128)(2,1)S(1)}, u32[]{:S(2)}, u32[]{:S(2)}) collective-permute-start(bf16[8,10752]{1,0:T(8,128)(2,1)S(1)} %shard_map.81), channel_id=1, source_target_pairs={{0,8},{1,9},{2,10},{3,11},{4,12},{5,13},{6,14},{7,15},{8,0},{9,1},... | collective-permute-start | bytes 516104 | tf_op jit(solution)/shard_map/ppermute | solution.py:263
  53.2 1.8 %collective-permute-done.20 = bf16[8,10752]{1,0:T(8,128)(2,1)S(1)} collective-permute-done((bf16[8,10752]{1,0:T(8,128)(2,1)S(1)}, bf16[8,10752]{1,0:T(8,128)(2,1)S(1)}, u32[]{:S(2)}, u32[]{:S(2)}) %collective-permute-start.20) | collective-permute-done | bytes 172064 | tf_op jit(solution)/shard_map/ppermute | solution.py:266
  54.9 0.1 add_convert_fusion.2.refs_0_
  55.0 6.5 %collective-permute-done.25.refs_2_ = bf16[8,10752]{1,0:T(8,128)(2,1)S(1)} collective-permute-done((bf16[8,10752]{1,0:T(8,128)(2,1)S(1)}, bf16[8,10752]{1,0:T(8,128)(2,1)S(1)}, u32[]{:S(2)}, u32[]{:S(2)}) %collective-permute-start.25) | collective-permute-done | bytes 172064 | tf_op jit(solution)/shard_map/ppermute | solution.py:263
  61.6 1.9 %shard_map.82 = bf16[16,7168]{1,0:T(8,128)(2,1)} custom-call(s32[4]{0:T(128)S(1)} %copy-done.1, s32[2,16]{1,0:T(2,128)S(1)} %bitcast.3, f32[2,16]{1,0:T(2,128)S(1)} %bitcast.4, bf16[8,10752]{1,0:T(8,128)(2,1)S(1)} %add_convert_fusion.2.refs_0_, bf16[8,10752]{1,0:T(8,128)(2,1)S(1)} %collective-permute-done.22.refs_2_.refs_1_, ...), custom_call_target="tpu_custom_call" | custom-call | flops 44040192 | bytes 1146880 | tf_op jit(solution)/shard_map/pallas_call | solution.py:237
  (12 shorter events, 0.2 us)
Async XLA Ops:
  1.5 10.4 %collective-permute-start.3 = (bf16[8,10752]{1,0:T(8,128)(2,1)S(1)}, bf16[8,10752]{1,0:T(8,128)(2,1)S(1)}, u32[]{:S(2)}, u32[]{:S(2)}) collective-permute-start(bf16[8,10752]{1,0:T(8,128)(2,1)S(1)} %get-tuple-element.21), channel_id=1, source_target_pairs={{0,12},{1,13},{2,14},{3,15},{4,8},{5,9},{6,10},{7,11},{8,4},{9,5},... | collective-permute-start | bytes 516104 | tf_op jit(solution)/shard_map/ppermute | solution.py:263
  6.6 7.0 %collective-permute-start = (bf16[8,10752]{1,0:T(8,128)(2,1)S(1)}, bf16[8,10752]{1,0:T(8,128)(2,1)S(1)}, u32[]{:S(2)}, u32[]{:S(2)}) collective-permute-start(bf16[8,10752]{1,0:T(8,128)(2,1)S(1)} %get-tuple-element.20.refs_0_), channel_id=1, source_target_pairs={{0,2},{1,3},{2,0},{3,1},{4,6},{5,7},{6,4},{7,5},{8,10},{9,11},{10,... | collective-permute-start | bytes 516104 | tf_op jit(solution)/shard_map/ppermute | solution.py:266
  8.1 6.6 %collective-permute-start.6 = (bf16[8,10752]{1,0:T(8,128)(2,1)S(1)}, bf16[8,10752]{1,0:T(8,128)(2,1)S(1)}, u32[]{:S(2)}, u32[]{:S(2)}) collective-permute-start(bf16[8,10752]{1,0:T(8,128)(2,1)S(1)} %get-tuple-element.28), channel_id=1, source_target_pairs={{0,4},{1,5},{2,6},{3,7},{4,0},{5,1},{6,2},{7,3},{8,12},{9,13},{10,... | collective-permute-start | bytes 516104 | tf_op jit(solution)/shard_map/ppermute | solution.py:263
  11.8 5.6 %collective-permute-start.4 = (bf16[8,10752]{1,0:T(8,128)(2,1)S(1)}, bf16[8,10752]{1,0:T(8,128)(2,1)S(1)}, u32[]{:S(2)}, u32[]{:S(2)}) collective-permute-start(bf16[8,10752]{1,0:T(8,128)(2,1)S(1)} %collective-permute-done.3.refs_1_.refs_0_), channel_id=1, source_target_pairs={{0,2},{1,3},{2,0},{3,1},{4,6},{5,7},{6,4},{7,5},{8,10},{9,11},{10,... | collective-permute-start | bytes 516104 | tf_op jit(solution)/shard_map/ppermute | solution.py:266
  13.6 9.7 %collective-permute-start.1 = (bf16[8,10752]{1,0:T(8,128)(2,1)S(1)}, bf16[8,10752]{1,0:T(8,128)(2,1)S(1)}, u32[]{:S(2)}, u32[]{:S(2)}) collective-permute-start(bf16[8,10752]{1,0:T(8,128)(2,1)S(1)} %get-tuple-element.20.refs_0_), channel_id=1, source_target_pairs={{0,1},{1,0},{2,3},{3,2},{4,5},{5,4},{6,7},{7,6},{8,9},{9,8},{10,11... | collective-permute-start | bytes 516104 | tf_op jit(solution)/shard_map/ppermute | solution.py:269
  13.6 9.7 %collective-permute-start.2 = (bf16[8,10752]{1,0:T(8,128)(2,1)S(1)}, bf16[8,10752]{1,0:T(8,128)(2,1)S(1)}, u32[]{:S(2)}, u32[]{:S(2)}) collective-permute-start(bf16[8,10752]{1,0:T(8,128)(2,1)S(1)} %collective-permute-done.refs_1_.refs_3_), channel_id=1, source_target_pairs={{0,1},{1,0},{2,3},{3,2},{4,5},{5,4},{6,7},{7,6},{8,9},{9,8},{10,11... | collective-permute-start | bytes 516104 | tf_op jit(solution)/shard_map/ppermute | solution.py:269
  14.7 11.7 %collective-permute-start.7 = (bf16[8,10752]{1,0:T(8,128)(2,1)S(1)}, bf16[8,10752]{1,0:T(8,128)(2,1)S(1)}, u32[]{:S(2)}, u32[]{:S(2)}) collective-permute-start(bf16[8,10752]{1,0:T(8,128)(2,1)S(1)} %shard_map.76), channel_id=1, source_target_pairs={{0,8},{1,9},{2,10},{3,11},{4,12},{5,13},{6,14},{7,15},{8,0},{9,1},... | collective-permute-start | bytes 516104 | tf_op jit(solution)/shard_map/ppermute | solution.py:263
  17.4 8.5 %collective-permute-start.11 = (bf16[8,10752]{1,0:T(8,128)(2,1)S(1)}, bf16[8,10752]{1,0:T(8,128)(2,1)S(1)}, u32[]{:S(2)}, u32[]{:S(2)}) collective-permute-start(bf16[8,10752]{1,0:T(8,128)(2,1)S(1)} %collective-permute-done.3.refs_1_.refs_0_), channel_id=1, source_target_pairs={{0,1},{1,0},{2,3},{3,2},{4,5},{5,4},{6,7},{7,6},{8,9},{9,8},{10,11... | collective-permute-start | bytes 516104 | tf_op jit(solution)/shard_map/ppermute | solution.py:269
  17.4 8.6 %collective-permute-start.14 = (bf16[8,10752]{1,0:T(8,128)(2,1)S(1)}, bf16[8,10752]{1,0:T(8,128)(2,1)S(1)}, u32[]{:S(2)}, u32[]{:S(2)}) collective-permute-start(bf16[8,10752]{1,0:T(8,128)(2,1)S(1)} %collective-permute-done.6.refs_2_.refs_0_), channel_id=1, source_target_pairs={{0,2},{1,3},{2,0},{3,1},{4,6},{5,7},{6,4},{7,5},{8,10},{9,11},{10,... | collective-permute-start | bytes 516104 | tf_op jit(solution)/shard_map/ppermute | solution.py:266
  25.3 7.5 %collective-permute-start.5 = (bf16[16,10752]{1,0:T(8,128)(2,1)S(1)}, bf16[16,10752]{1,0:T(8,128)(2,1)S(1)}, u32[]{:S(2)}, u32[]{:S(2)}) collective-permute-start(bf16[16,10752]{1,0:T(8,128)(2,1)S(1)} %get-tuple-element.26.refs_7_), channel_id=1, source_target_pairs={{0,1},{1,0},{2,3},{3,2},{4,5},{5,4},{6,7},{7,6},{8,9},{9,8},{10,11... | collective-permute-start | bytes 1032200 | tf_op jit(solution)/shard_map/ppermute | solution.py:269
  25.4 1.9 %collective-permute-start.12 = (bf16[8,10752]{1,0:T(8,128)(2,1)S(1)}, bf16[8,10752]{1,0:T(8,128)(2,1)S(1)}, u32[]{:S(2)}, u32[]{:S(2)}) collective-permute-start(bf16[8,10752]{1,0:T(8,128)(2,1)S(1)} %collective-permute-done.4.refs_3_.refs_1_), channel_id=1, source_target_pairs={{0,1},{1,0},{2,3},{3,2},{4,5},{5,4},{6,7},{7,6},{8,9},{9,8},{10,11... | collective-permute-start | bytes 516104 | tf_op jit(solution)/shard_map/ppermute | solution.py:269
  25.9 3.6 %collective-permute-start.15 = (bf16[8,10752]{1,0:T(8,128)(2,1)S(1)}, bf16[8,10752]{1,0:T(8,128)(2,1)S(1)}, u32[]{:S(2)}, u32[]{:S(2)}) collective-permute-start(bf16[8,10752]{1,0:T(8,128)(2,1)S(1)} %collective-permute-done.6.refs_2_.refs_0_), channel_id=1, source_target_pairs={{0,1},{1,0},{2,3},{3,2},{4,5},{5,4},{6,7},{7,6},{8,9},{9,8},{10,11... | collective-permute-start | bytes 516104 | tf_op jit(solution)/shard_map/ppermute | solution.py:269
  26.0 4.0 %collective-permute-start.16 = (bf16[8,10752]{1,0:T(8,128)(2,1)S(1)}, bf16[8,10752]{1,0:T(8,128)(2,1)S(1)}, u32[]{:S(2)}, u32[]{:S(2)}) collective-permute-start(bf16[8,10752]{1,0:T(8,128)(2,1)S(1)} %collective-permute-done.14.refs_1_), channel_id=1, source_target_pairs={{0,1},{1,0},{2,3},{3,2},{4,5},{5,4},{6,7},{7,6},{8,9},{9,8},{10,11... | collective-permute-start | bytes 516104 | tf_op jit(solution)/shard_map/ppermute | solution.py:269
  26.4 6.4 %collective-permute-start.8 = (bf16[8,10752]{1,0:T(8,128)(2,1)S(1)}, bf16[8,10752]{1,0:T(8,128)(2,1)S(1)}, u32[]{:S(2)}, u32[]{:S(2)}) collective-permute-start(bf16[8,10752]{1,0:T(8,128)(2,1)S(1)} %collective-permute-done.7.refs_0_), channel_id=1, source_target_pairs={{0,2},{1,3},{2,0},{3,1},{4,6},{5,7},{6,4},{7,5},{8,10},{9,11},{10,... | collective-permute-start | bytes 516104 | tf_op jit(solution)/shard_map/ppermute | solution.py:266
  27.3 7.8 %collective-permute-start.9 = (bf16[8,10752]{1,0:T(8,128)(2,1)S(1)}, bf16[8,10752]{1,0:T(8,128)(2,1)S(1)}, u32[]{:S(2)}, u32[]{:S(2)}) collective-permute-start(bf16[8,10752]{1,0:T(8,128)(2,1)S(1)} %collective-permute-done.7.refs_0_), channel_id=1, source_target_pairs={{0,1},{1,0},{2,3},{3,2},{4,5},{5,4},{6,7},{7,6},{8,9},{9,8},{10,11... | collective-permute-start | bytes 516104 | tf_op jit(solution)/shard_map/ppermute | solution.py:269
  29.5 3.3 %collective-permute-start.13 = (bf16[16,10752]{1,0:T(8,128)(2,1)S(1)}, bf16[16,10752]{1,0:T(8,128)(2,1)S(1)}, u32[]{:S(2)}, u32[]{:S(2)}) collective-permute-start(bf16[16,10752]{1,0:T(8,128)(2,1)S(1)} %get-tuple-element.30), channel_id=1, source_target_pairs={{0,1},{1,0},{2,3},{3,2},{4,5},{5,4},{6,7},{7,6},{8,9},{9,8},{10,11... | collective-permute-start | bytes 1032200 | tf_op jit(solution)/shard_map/ppermute | solution.py:269
  32.0 1.9 %collective-permute-start.17 = (bf16[16,10752]{1,0:T(8,128)(2,1)S(1)}, bf16[16,10752]{1,0:T(8,128)(2,1)S(1)}, u32[]{:S(2)}, u32[]{:S(2)}) collective-permute-start(bf16[16,10752]{1,0:T(8,128)(2,1)S(1)} %get-tuple-element.32), channel_id=1, source_target_pairs={{0,1},{1,0},{2,3},{3,2},{4,5},{5,4},{6,7},{7,6},{8,9},{9,8},{10,11... | collective-permute-start | bytes 1032200 | tf_op jit(solution)/shard_map/ppermute | solution.py:269
  32.8 2.3 %collective-permute-start.10 = (bf16[8,10752]{1,0:T(8,128)(2,1)S(1)}, bf16[8,10752]{1,0:T(8,128)(2,1)S(1)}, u32[]{:S(2)}, u32[]{:S(2)}) collective-permute-start(bf16[8,10752]{1,0:T(8,128)(2,1)S(1)} %collective-permute-done.8.refs_1_), channel_id=1, source_target_pairs={{0,1},{1,0},{2,3},{3,2},{4,5},{5,4},{6,7},{7,6},{8,9},{9,8},{10,11... | collective-permute-start | bytes 516104 | tf_op jit(solution)/shard_map/ppermute | solution.py:269
  32.9 7.2 %collective-permute-start.23 = (bf16[8,10752]{1,0:T(8,128)(2,1)S(1)}, bf16[8,10752]{1,0:T(8,128)(2,1)S(1)}, u32[]{:S(2)}, u32[]{:S(2)}) collective-permute-start(bf16[8,10752]{1,0:T(8,128)(2,1)S(1)} %add_convert_fusion.6.refs_7_), channel_id=1, source_target_pairs={{0,2},{1,3},{2,0},{3,1},{4,6},{5,7},{6,4},{7,5},{8,10},{9,11},{10,... | collective-permute-start | bytes 516104 | tf_op jit(solution)/shard_map/ppermute | solution.py:266
  34.0 11.0 %collective-permute-start.21 = (bf16[8,10752]{1,0:T(8,128)(2,1)S(1)}, bf16[8,10752]{1,0:T(8,128)(2,1)S(1)}, u32[]{:S(2)}, u32[]{:S(2)}) collective-permute-start(bf16[8,10752]{1,0:T(8,128)(2,1)S(1)} %add_convert_fusion.5.refs_8_), channel_id=1, source_target_pairs={{0,2},{1,3},{2,0},{3,1},{4,6},{5,7},{6,4},{7,5},{8,10},{9,11},{10,... | collective-permute-start | bytes 516104 | tf_op jit(solution)/shard_map/ppermute | solution.py:266
  37.2 24.4 %copy-start = (s32[16,2]{0,1:T(2,128)S(1)}, s32[16,2]{0,1:T(2,128)}, u32[]{:S(2)}) copy-start(s32[16,2]{0,1:T(2,128)} %param.8) | copy-start | bytes 388
  37.2 24.4 %copy-start.1 = (s32[4]{0:T(128)S(1)}, s32[4]{0:T(128)}, u32[]{:S(2)}) copy-start(s32[4]{0:T(128)} %placement_ref.3) | copy-start | bytes 52
  37.2 24.4 %copy-start.2 = (f32[16,2]{0,1:T(2,128)S(1)}, f32[16,2]{0,1:T(2,128)}, u32[]{:S(2)}) copy-start(f32[16,2]{0,1:T(2,128)} %param.9) | copy-start | bytes 388
  37.2 6.7 %collective-permute-start.18 = (bf16[16,10752]{1,0:T(8,128)(2,1)S(1)}, bf16[16,10752]{1,0:T(8,128)(2,1)S(1)}, u32[]{:S(2)}, u32[]{:S(2)}) collective-permute-start(bf16[16,10752]{1,0:T(8,128)(2,1)S(1)} %get-tuple-element.34), channel_id=1, source_target_pairs={{0,1},{1,0},{2,3},{3,2},{4,5},{5,4},{6,7},{7,6},{8,9},{9,8},{10,11... | collective-permute-start | bytes 1032200 | tf_op jit(solution)/shard_map/ppermute | solution.py:269
  40.2 10.4 %collective-permute-start.24 = (bf16[8,10752]{1,0:T(8,128)(2,1)S(1)}, bf16[8,10752]{1,0:T(8,128)(2,1)S(1)}, u32[]{:S(2)}, u32[]{:S(2)}) collective-permute-start(bf16[8,10752]{1,0:T(8,128)(2,1)S(1)} %add_convert_fusion), channel_id=1, source_target_pairs={{0,12},{1,13},{2,14},{3,15},{4,8},{5,9},{6,10},{7,11},{8,4},{9,5},... | collective-permute-start | bytes 516104 | tf_op jit(solution)/shard_map/ppermute | solution.py:263
  43.9 5.5 %collective-permute-start.19 = (bf16[8,10752]{1,0:T(8,128)(2,1)S(1)}, bf16[8,10752]{1,0:T(8,128)(2,1)S(1)}, u32[]{:S(2)}, u32[]{:S(2)}) collective-permute-start(bf16[8,10752]{1,0:T(8,128)(2,1)S(1)} %add_convert_fusion.4), channel_id=1, source_target_pairs={{0,2},{1,3},{2,0},{3,1},{4,6},{5,7},{6,4},{7,5},{8,10},{9,11},{10,... | collective-permute-start | bytes 516104 | tf_op jit(solution)/shard_map/ppermute | solution.py:266
  45.1 6.4 %collective-permute-start.22 = (bf16[8,10752]{1,0:T(8,128)(2,1)S(1)}, bf16[8,10752]{1,0:T(8,128)(2,1)S(1)}, u32[]{:S(2)}, u32[]{:S(2)}) collective-permute-start(bf16[8,10752]{1,0:T(8,128)(2,1)S(1)} %add_convert_fusion.1), channel_id=1, source_target_pairs={{0,4},{1,5},{2,6},{3,7},{4,0},{5,1},{6,2},{7,3},{8,12},{9,13},{10,... | collective-permute-start | bytes 516104 | tf_op jit(solution)/shard_map/ppermute | solution.py:263
  49.5 5.5 %collective-permute-start.20 = (bf16[8,10752]{1,0:T(8,128)(2,1)S(1)}, bf16[8,10752]{1,0:T(8,128)(2,1)S(1)}, u32[]{:S(2)}, u32[]{:S(2)}) collective-permute-start(bf16[8,10752]{1,0:T(8,128)(2,1)S(1)} %shard_map.80), channel_id=1, source_target_pairs={{0,2},{1,3},{2,0},{3,1},{4,6},{5,7},{6,4},{7,5},{8,10},{9,11},{10,... | collective-permute-start | bytes 516104 | tf_op jit(solution)/shard_map/ppermute | solution.py:266
  51.5 10.0 %collective-permute-start.25 = (bf16[8,10752]{1,0:T(8,128)(2,1)S(1)}, bf16[8,10752]{1,0:T(8,128)(2,1)S(1)}, u32[]{:S(2)}, u32[]{:S(2)}) collective-permute-start(bf16[8,10752]{1,0:T(8,128)(2,1)S(1)} %shard_map.81), channel_id=1, source_target_pairs={{0,8},{1,9},{2,10},{3,11},{4,12},{5,13},{6,14},{7,15},{8,0},{9,1},... | collective-permute-start | bytes 516104 | tf_op jit(solution)/shard_map/ppermute | solution.py:263

commit v7 on v6

--- a/solution.py
+++ b/solution.py
@@ -136,7 +136,7 @@
 def experts_kernel(*refs):
     straight_ref, across_ref, straight_other_ref, across_other_ref = refs[:4]
     gate_ref, up_ref, down_ref = refs[4:7]
-    kept_ref, sent_ref = refs[-2:]
+    out_refs = refs[-4:]
     pieces = (straight_ref, across_ref, straight_other_ref, across_other_ref)
     width, hid = gate_ref.shape
     middle = width // 2
@@ -163,8 +163,8 @@
     def store(start, values):
         values = values.astype(jnp.bfloat16)
         stop = start + values.shape[1]
-        kept_ref[:, start:stop] = values[: 2 * height]
-        sent_ref[:, start:stop] = values[2 * height :]
+        for i, out_ref in enumerate(out_refs):
+            out_ref[:, start:stop] = values[i * height : (i + 1) * height]
 
     step = middle // 4
     for i in range(4):
@@ -180,13 +180,13 @@
     width, hid = weights[0].shape
     height, packed_width = pieces[0].shape
     rows = len(pieces) * height
-    shape = pltpu.VMEM((rows // 2, packed_width), jnp.bfloat16)
+    shape = pltpu.VMEM((height, packed_width), jnp.bfloat16)
     operands = [in_vmem(p) for p in pieces] + [in_vmem(w) for w in weights]
     return pl.pallas_call(
         experts_kernel,
-        out_shape=[shape] * 2,
+        out_shape=[shape] * len(pieces),
         in_specs=[VMEM] * 7 + [ANYWHERE] * len(after),
-        out_specs=[VMEM] * 2,
+        out_specs=[VMEM] * len(pieces),
         compiler_params=pltpu.CompilerParams(vmem_limit_bytes=VMEM_BYTES),
         cost_estimate=pl.CostEstimate(
             flops=0, bytes_accessed=4 * width * hid, transcendentals=0
@@ -256,7 +256,6 @@
     n_blocks = placement.shape[0]
     devices = lax.axis_size("node")
     parts = devices // n_blocks
-    half = tokens.shape[0] // 2
 
     def along_z(value, k):
         pairs = [(i, i ^ (k * parts)) for i in range(devices)]
@@ -271,43 +270,50 @@
     ids = expert_ids.T
     groups = [[n_blocks - d, d] for d in range(1, n_blocks // 2)] + [[n_blocks // 2]]
     last = groups[-1][0]
-    straight, arrived, across, results = {}, {}, {}, {}
-    both, home, kept, sent, returned = {}, {}, {}, {}, {}
+    straight, across, results = {}, {}, {}
+    both, home, kept, sent = {}, {}, {}, {}
 
     def compute(k, after):
         theirs = [along_core(straight[k]), along_core(across[k])]
-        kept[k], sent[k] = run_experts([straight[k], across[k]] + theirs, weights, after)
-        returned[k] = along_core(sent[k])
-        both[k] = add(kept[k][half:], returned[k][half:])
-
-    def go_home(k, after_y, after_z):
-        back = along_y(when(both[k], after_y))
-        home[k] = add(kept[k][:half], returned[k][:half], back)
-        results[k] = along_z(when(home[k], after_z), k) if k else home[k]
+        out = run_experts([straight[k], across[k]] + theirs, weights, after)
+        sent[k] = out[3]
+        both[k] = add(out[1], along_core(out[3]))
+        kept[k] = out[0], along_core(out[2])
+
+    def go_home(k, after):
+        back = along_y(both[k] if k else when(both[k], after))
+        home[k] = add(*kept[k], back)
+        results[k] = along_z(when(home[k], after), k) if k else home[k]
 
     buckets = list(pack(placement, ids, tokens, n_blocks, parts))
+    weights = load((gate_weight, up_weight, down_weight), buckets[0])
     straight[0] = buckets[0]
     across[0] = along_y(straight[0])
+    compute(0, [])
+    second = None
     for g, group in enumerate(groups):
-        previous = groups[g - 1] if g else []
-        if g:
-            after = [arrived[k] for k in previous] + [across[0]]
-            for k in group:
-                buckets[k] = when(buckets[k], after)
-        for k in group:
-            straight[k] = arrived[k] = along_z(buckets[k], k)
-    for k in groups[0]:
-        across[k] = along_y(straight[k])
-    weights = load((gate_weight, up_weight, down_weight), across[groups[0][0]])
-    compute(0, [])
-    for g, group in enumerate(groups):
-        previous = groups[g - 1] if g else []
-        for i, k in enumerate(group):
-            if g:
-                across[k] = along_y(straight[k])
-            compute(k, [both[j] for j in previous] if g else [sent[0]][:i])
-            go_home(k, [], [results[j] for j in previous])
-    go_home(0, [home[last]], [])
+        first = group[0]
+        if g == 0:
+            straight[first] = along_z(buckets[first], first)
+            across[first] = along_y(straight[first])
+            compute(first, [])
+            go_home(first, [])
+        else:
+            previous = groups[g - 1][0]
+            straight[first] = along_z(when(buckets[first], [straight[previous], across[0]]), first)
+            after = [sent[0]] + ([across[second]] if second else [])
+            straight[first] = when(straight[first], after)
+            across[first] = along_y(straight[first])
+            compute(first, [])
+            go_home(first, [results[previous]])
+        if second:
+            compute(second, [sent[first]] + ([both[previous]] if g else []))
+            go_home(second, [])
+        second = group[1] if len(group) > 1 else None
+        if second:
+            straight[second] = along_z(when(buckets[second], [weights[0]] if g == 0 else []), second)
+            across[second] = along_y(straight[second])
+    go_home(0, [home[last]])
     return mix(placement, ids, gates.T, [results[k] for k in range(n_blocks)], n_blocks, parts)
 
 

time: 63.6 us -> 63.4 us (level)
  starting transfers between devices: 26 us -> 24.1 us
  waiting for transfers between devices: 20.9 us -> 22.6 us
    ppermute x8, starting transfers between devices: 9.72 us -> 7.32 us  [along_y(): return lax.ppermute(value, 'node', [(i, i ^ 2) for i in range(devices)])]
    ppermute x12 -> x16, waiting for transfers between devices: 0.37 us -> 2.1 us  [along_core(): return lax.ppermute(value, 'node', [(i, i ^ 1) for i in range(devices)])]
    ppermute x12 -> x16, starting transfers between devices: 2.44 us -> 3.53 us  [along_core(): return lax.ppermute(value, 'node', [(i, i ^ 1) for i in range(devices)])]
  transfers between devices with their start and end apart: 26 -> 30, of which waited for: 9 -> 12; matrix products, arithmetic and copies ran while one was open for 1% -> 1% of each run, Pallas kernels for 20% -> 20%
where the time goes in v7:
time: 63.4 us; the launch traced here: 63.2 us
  starting transfers between devices  24.1 us (38%)
  waiting for transfers between devices  22.6 us (36%)
  Pallas kernels  15.8 us (25%)
    ppermute x6, starting transfers between devices, along_z(): return lax.ppermute(value, 'node', pairs)  13.3 us
    ppermute x6, waiting for transfers between devices, along_z(): return lax.ppermute(value, 'node', pairs)  11.7 us
    ppermute x8, waiting for transfers between devices, along_y(): return lax.ppermute(value, 'node', [(i, i ^ 2) for i in range(devices)])  8.8 us
    pallas_call x4, Pallas kernels, run_experts(): pl.pallas_call(experts_kernel, out_shape=[shape] * len(pieces), in_specs=...  8.27 us
    ppermute x8, starting transfers between devices, along_y(): return lax.ppermute(value, 'node', [(i, i ^ 2) for i in range(devices)])  7.32 us
    pallas_call x1, Pallas kernels, load(): pl.pallas_call(load_kernel, out_shape=[pltpu.VMEM(w.shape, w.dtype) for w...  4.24 us
    ppermute x16, starting transfers between devices, along_core(): return lax.ppermute(value, 'node', [(i, i ^ 1) for i in range(devices)])  3.53 us
    ppermute x16, waiting for transfers between devices, along_core(): return lax.ppermute(value, 'node', [(i, i ^ 1) for i in range(devices)])  2.1 us
  transfers between devices with their start and end apart: 30, of which 12 were waited for; matrix products, arithmetic and copies ran while one was open for 1% of the time, Pallas kernels for 20%

profile of v7, /device:TPU:0, one launch (start us, length us, event | category | flops | bytes accessed | tf_op | source)
XLA Modules:
  0.0 63.2 jit_solution(10302538241145078151)
XLA Ops:
  0.0 1.5 %shard_map.73 = (bf16[8,10752]{1,0:T(8,128)(2,1)S(1)}, bf16[8,10752]{1,0:T(8,128)(2,1)S(1)}, bf16[8,10752]{1,0:T(8,128)(2,1)S(1)}, bf16[8,10752]{1,0:T(8,128)(2,1)S(1)}) custom-call(s32[4]{0:T(128)} %placement_ref.3, s32[2,16]{1,0:T(2,128)} %bitcast.2, bf16[16,7168]{1,0:T(8,128)(2,1)} %tokens_ref.1), custom_call_target="tpu_custom_call" | custom-call | tf_op jit(solution)/shard_map/pallas_call | solution.py:82
  1.5 5.1 %collective-permute-start.5 = (bf16[8,10752]{1,0:T(8,128)(2,1)S(1)}, bf16[8,10752]{1,0:T(8,128)(2,1)S(1)}, u32[]{:S(2)}, u32[]{:S(2)}) collective-permute-start(bf16[8,10752]{1,0:T(8,128)(2,1)S(1)} %get-tuple-element.37), channel_id=1, source_target_pairs={{0,12},{1,13},{2,14},{3,15},{4,8},{5,9},{6,10},{7,11},{8,4},{9,5},... | collective-permute-start | bytes 516104 | tf_op jit(solution)/shard_map/ppermute | solution.py:262
  6.6 1.5 %collective-permute-start = (bf16[8,10752]{1,0:T(8,128)(2,1)S(1)}, bf16[8,10752]{1,0:T(8,128)(2,1)S(1)}, u32[]{:S(2)}, u32[]{:S(2)}) collective-permute-start(bf16[8,10752]{1,0:T(8,128)(2,1)S(1)} %get-tuple-element.28.refs_3_.refs_0_), channel_id=1, source_target_pairs={{0,2},{1,3},{2,0},{3,1},{4,6},{5,7},{6,4},{7,5},{8,10},{9,11},{10,... | collective-permute-start | bytes 516104 | tf_op jit(solution)/shard_map/ppermute | solution.py:265
  8.1 4.2 %shard_map.74 = (bf16[7168,256]{1,0:T(8,128)(2,1)S(1)}, bf16[7168,256]{1,0:T(8,128)(2,1)S(1)}, bf16[256,7168]{1,0:T(8,128)(2,1)S(1)}) custom-call(bf16[7168,256]{1,0:T(8,128)(2,1)} %refs_0_.1, bf16[7168,256]{1,0:T(8,128)(2,1)} %refs_1_.1, bf16[256,7168]{1,0:T(8,128)(2,1)} %refs_2_.1, bf16[8,10752]{1,0:T(8,128)(2,1)S(1)} %get-tuple-element.28.refs_3_.refs_0_), custom_call_target="tpu_custom_call" | custom-call | tf_op jit(solution)/shard_map/pallas_call | solution.py:125
  12.4 0.1 collective-permute-start.7
  12.4 0.1 collective-permute-start.1
  12.5 0.6 collective-permute-start.18
  13.1 0.0 collective-permute-done.refs_1_.refs_2_
  13.1 0.2 collective-permute-start.2
  13.3 3.6 %collective-permute-start.6 = (bf16[8,10752]{1,0:T(8,128)(2,1)S(1)}, bf16[8,10752]{1,0:T(8,128)(2,1)S(1)}, u32[]{:S(2)}, u32[]{:S(2)}) collective-permute-start(bf16[8,10752]{1,0:T(8,128)(2,1)S(1)} %shard_map.76), channel_id=1, source_target_pairs={{0,8},{1,9},{2,10},{3,11},{4,12},{5,13},{6,14},{7,15},{8,0},{9,1},... | collective-permute-start | bytes 516104 | tf_op jit(solution)/shard_map/ppermute | solution.py:262
  16.9 1.1 %collective-permute-done.7.refs_0_ = bf16[8,10752]{1,0:T(8,128)(2,1)S(1)} collective-permute-done((bf16[8,10752]{1,0:T(8,128)(2,1)S(1)}, bf16[8,10752]{1,0:T(8,128)(2,1)S(1)}, u32[]{:S(2)}, u32[]{:S(2)}) %collective-permute-start.7) | collective-permute-done | bytes 172064 | tf_op jit(solution)/shard_map/ppermute | solution.py:262
  18.0 0.5 collective-permute-start.8
  18.5 0.0 collective-permute-done.1.refs_2_
  18.5 0.0 collective-permute-start.19
  18.5 0.8 %collective-permute-done.18.refs_1_ = bf16[8,10752]{1,0:T(8,128)(2,1)S(1)} collective-permute-done((bf16[8,10752]{1,0:T(8,128)(2,1)S(1)}, bf16[8,10752]{1,0:T(8,128)(2,1)S(1)}, u32[]{:S(2)}, u32[]{:S(2)}) %collective-permute-start.18) | collective-permute-done | bytes 172064 | tf_op jit(solution)/shard_map/ppermute | solution.py:265
  19.3 0.0 collective-permute-start.20
  19.3 2.1 %shard_map.75 = (bf16[8,10752]{1,0:T(8,128)(2,1)S(1)}, bf16[8,10752]{1,0:T(8,128)(2,1)S(1)}, bf16[8,10752]{1,0:T(8,128)(2,1)S(1)}, bf16[8,10752]{1,0:T(8,128)(2,1)S(1)}) custom-call(bf16[8,10752]{1,0:T(8,128)(2,1)S(1)} %get-tuple-element.28.refs_3_.refs_0_, bf16[8,10752]{1,0:T(8,128)(2,1)S(1)} %collective-permute-done.refs_1_.refs_2_, ...), custom_call_target="tpu_custom_call" | custom-call | bytes 7340032 | tf_op jit(solution)/shard_map/pallas_call | solution.py:185
  21.4 0.6 collective-permute-start.4
  22.0 3.7 %collective-permute-done.6.refs_0_ = bf16[8,10752]{1,0:T(8,128)(2,1)S(1)} collective-permute-done((bf16[8,10752]{1,0:T(8,128)(2,1)S(1)}, bf16[8,10752]{1,0:T(8,128)(2,1)S(1)}, u32[]{:S(2)}, u32[]{:S(2)}) %collective-permute-start.6) | collective-permute-done | bytes 172064 | tf_op jit(solution)/shard_map/ppermute | solution.py:262
  25.6 0.0 collective-permute-done.8.refs_2_.refs_1_
  25.6 0.5 collective-permute-start.9
  26.1 0.5 collective-permute-start.10
  26.6 0.0 collective-permute-done.20.refs_3_
  26.6 0.1 collective-permute-start.3
  26.7 2.1 %shard_map.81 = (bf16[8,10752]{1,0:T(8,128)(2,1)S(1)}, bf16[8,10752]{1,0:T(8,128)(2,1)S(1)}, bf16[8,10752]{1,0:T(8,128)(2,1)S(1)}, bf16[8,10752]{1,0:T(8,128)(2,1)S(1)}) custom-call(bf16[8,10752]{1,0:T(8,128)(2,1)S(1)} %collective-permute-done.5.refs_1_.refs_0_, bf16[8,10752]{1,0:T(8,128)(2,1)S(1)} %collective-permute-done.18.refs_1_, ...), custom_call_target="tpu_custom_call" | custom-call | bytes 7340032 | tf_op jit(solution)/shard_map/pallas_call | solution.py:185
  28.8 0.0 collective-permute-done.4
  28.8 0.5 collective-permute-start.21
  29.3 2.5 %collective-permute-done.9.refs_1_ = bf16[8,10752]{1,0:T(8,128)(2,1)S(1)} collective-permute-done((bf16[8,10752]{1,0:T(8,128)(2,1)S(1)}, bf16[8,10752]{1,0:T(8,128)(2,1)S(1)}, u32[]{:S(2)}, u32[]{:S(2)}) %collective-permute-start.9) | collective-permute-done | bytes 172064 | tf_op jit(solution)/shard_map/ppermute | solution.py:265
  31.9 0.0 collective-permute-done.10.refs_2_
  31.9 0.6 collective-permute-start.17
  32.5 0.8 %collective-permute-done.11.refs_3_ = bf16[8,10752]{1,0:T(8,128)(2,1)S(1)} collective-permute-done((bf16[8,10752]{1,0:T(8,128)(2,1)S(1)}, bf16[8,10752]{1,0:T(8,128)(2,1)S(1)}, u32[]{:S(2)}, u32[]{:S(2)}) %collective-permute-start.11) | collective-permute-done | bytes 172064 | tf_op jit(solution)/shard_map/ppermute | solution.py:268
  33.2 0.1 collective-permute-start.26
  33.4 2.1 %shard_map.79 = (bf16[8,10752]{1,0:T(8,128)(2,1)S(1)}, bf16[8,10752]{1,0:T(8,128)(2,1)S(1)}, bf16[8,10752]{1,0:T(8,128)(2,1)S(1)}, bf16[8,10752]{1,0:T(8,128)(2,1)S(1)}) custom-call(bf16[8,10752]{1,0:T(8,128)(2,1)S(1)} %shard_map.78.refs_0_, bf16[8,10752]{1,0:T(8,128)(2,1)S(1)} %collective-permute-done.9.refs_1_, ...), custom_call_target="tpu_custom_call" | custom-call | bytes 7340032 | tf_op jit(solution)/shard_map/pallas_call | solution.py:185
  35.5 0.0 collective-permute-done.21
  35.5 0.4 collective-permute-start.13
  35.9 0.0 collective-permute-done.16.refs_2_
  36.0 0.2 collective-permute-start.12
  36.2 0.0 collective-permute-done.17.refs_3_
  36.2 0.3 collective-permute-start.27
  36.5 2.1 %shard_map.82 = (bf16[8,10752]{1,0:T(8,128)(2,1)S(1)}, bf16[8,10752]{1,0:T(8,128)(2,1)S(1)}, bf16[8,10752]{1,0:T(8,128)(2,1)S(1)}, bf16[8,10752]{1,0:T(8,128)(2,1)S(1)}) custom-call(bf16[8,10752]{1,0:T(8,128)(2,1)S(1)} %collective-permute-done.7.refs_0_, bf16[8,10752]{1,0:T(8,128)(2,1)S(1)} %collective-permute-done.8.refs_2_.refs_1_, ...), custom_call_target="tpu_custom_call" | custom-call | bytes 7340032 | tf_op jit(solution)/shard_map/pallas_call | solution.py:185
  38.5 0.0 copy-start
  38.6 0.0 copy-start.1
  38.6 0.0 copy-start.2
  38.6 0.1 collective-permute-start.23
  38.8 1.3 %collective-permute-done.23 = bf16[8,10752]{1,0:T(8,128)(2,1)S(1)} collective-permute-done((bf16[8,10752]{1,0:T(8,128)(2,1)S(1)}, bf16[8,10752]{1,0:T(8,128)(2,1)S(1)}, u32[]{:S(2)}, u32[]{:S(2)}) %collective-permute-start.23) | collective-permute-done | bytes 172064 | tf_op jit(solution)/shard_map/ppermute | solution.py:268
  40.1 0.1 collective-permute-start.22
  40.3 1.8 %collective-permute-start.14 = (bf16[8,10752]{1,0:T(8,128)(2,1)S(1)}, bf16[8,10752]{1,0:T(8,128)(2,1)S(1)}, u32[]{:S(2)}, u32[]{:S(2)}) collective-permute-start(bf16[8,10752]{1,0:T(8,128)(2,1)S(1)} %add_convert_fusion.6), channel_id=1, source_target_pairs={{0,2},{1,3},{2,0},{3,1},{4,6},{5,7},{6,4},{7,5},{8,10},{9,11},{10,... | collective-permute-start | bytes 516104 | tf_op jit(solution)/shard_map/ppermute | solution.py:265
  42.1 0.7 %collective-permute-done.27 = bf16[8,10752]{1,0:T(8,128)(2,1)S(1)} collective-permute-done((bf16[8,10752]{1,0:T(8,128)(2,1)S(1)}, bf16[8,10752]{1,0:T(8,128)(2,1)S(1)}, u32[]{:S(2)}, u32[]{:S(2)}) %collective-permute-start.27) | collective-permute-done | bytes 172064 | tf_op jit(solution)/shard_map/ppermute | solution.py:265
  42.8 0.3 collective-permute-start.24
  43.1 0.1 add_convert_fusion
  43.2 0.0 collective-permute-done.12
  43.2 2.0 %collective-permute-start.28 = (bf16[8,10752]{1,0:T(8,128)(2,1)S(1)}, bf16[8,10752]{1,0:T(8,128)(2,1)S(1)}, u32[]{:S(2)}, u32[]{:S(2)}) collective-permute-start(bf16[8,10752]{1,0:T(8,128)(2,1)S(1)} %add_convert_fusion), channel_id=1, source_target_pairs={{0,12},{1,13},{2,14},{3,15},{4,8},{5,9},{6,10},{7,11},{8,4},{9,5},... | collective-permute-start | bytes 516104 | tf_op jit(solution)/shard_map/ppermute | solution.py:262
  45.1 2.4 %collective-permute-done.14 = bf16[8,10752]{1,0:T(8,128)(2,1)S(1)} collective-permute-done((bf16[8,10752]{1,0:T(8,128)(2,1)S(1)}, bf16[8,10752]{1,0:T(8,128)(2,1)S(1)}, u32[]{:S(2)}, u32[]{:S(2)}) %collective-permute-start.14) | collective-permute-done | bytes 172064 | tf_op jit(solution)/shard_map/ppermute | solution.py:265
  47.5 0.1 add_convert_fusion.5.refs_1_.refs_0_
  47.6 1.8 %collective-permute-start.15 = (bf16[8,10752]{1,0:T(8,128)(2,1)S(1)}, bf16[8,10752]{1,0:T(8,128)(2,1)S(1)}, u32[]{:S(2)}, u32[]{:S(2)}) collective-permute-start(bf16[8,10752]{1,0:T(8,128)(2,1)S(1)} %shard_map.80), channel_id=1, source_target_pairs={{0,2},{1,3},{2,0},{3,1},{4,6},{5,7},{6,4},{7,5},{8,10},{9,11},{10,... | collective-permute-start | bytes 516104 | tf_op jit(solution)/shard_map/ppermute | solution.py:265
  49.4 1.8 %collective-permute-done.24 = bf16[8,10752]{1,0:T(8,128)(2,1)S(1)} collective-permute-done((bf16[8,10752]{1,0:T(8,128)(2,1)S(1)}, bf16[8,10752]{1,0:T(8,128)(2,1)S(1)}, u32[]{:S(2)}, u32[]{:S(2)}) %collective-permute-start.24) | collective-permute-done | bytes 172064 | tf_op jit(solution)/shard_map/ppermute | solution.py:265
  51.2 0.1 add_convert_fusion.1
  51.3 0.2 collective-permute-start.25
  51.5 2.4 %collective-permute-start.29 = (bf16[8,10752]{1,0:T(8,128)(2,1)S(1)}, bf16[8,10752]{1,0:T(8,128)(2,1)S(1)}, u32[]{:S(2)}, u32[]{:S(2)}) collective-permute-start(bf16[8,10752]{1,0:T(8,128)(2,1)S(1)} %shard_map.83), channel_id=1, source_target_pairs={{0,8},{1,9},{2,10},{3,11},{4,12},{5,13},{6,14},{7,15},{8,0},{9,1},... | collective-permute-start | bytes 516104 | tf_op jit(solution)/shard_map/ppermute | solution.py:262
  53.8 0.5 collective-permute-done.15
  54.4 0.1 add_convert_fusion.4.refs_0_
  54.4 5.3 %collective-permute-done.25.refs_1_ = bf16[8,10752]{1,0:T(8,128)(2,1)S(1)} collective-permute-done((bf16[8,10752]{1,0:T(8,128)(2,1)S(1)}, bf16[8,10752]{1,0:T(8,128)(2,1)S(1)}, u32[]{:S(2)}, u32[]{:S(2)}) %collective-permute-start.25) | collective-permute-done | bytes 172064 | tf_op jit(solution)/shard_map/ppermute | solution.py:262
  59.7 1.7 %collective-permute-done.29.refs_2_ = bf16[8,10752]{1,0:T(8,128)(2,1)S(1)} collective-permute-done((bf16[8,10752]{1,0:T(8,128)(2,1)S(1)}, bf16[8,10752]{1,0:T(8,128)(2,1)S(1)}, u32[]{:S(2)}, u32[]{:S(2)}) %collective-permute-start.29) | collective-permute-done | bytes 172064 | tf_op jit(solution)/shard_map/ppermute | solution.py:262
  61.4 1.9 %shard_map.84 = bf16[16,7168]{1,0:T(8,128)(2,1)} custom-call(s32[4]{0:T(128)S(1)} %copy-done.1, s32[2,16]{1,0:T(2,128)S(1)} %bitcast.3, f32[2,16]{1,0:T(2,128)S(1)} %bitcast.4, bf16[8,10752]{1,0:T(8,128)(2,1)S(1)} %add_convert_fusion.4.refs_0_, bf16[8,10752]{1,0:T(8,128)(2,1)S(1)} %collective-permute-done.25.refs_1_, ...), custom_call_target="tpu_custom_call" | custom-call | flops 44040192 | bytes 1146880 | tf_op jit(solution)/shard_map/pallas_call | solution.py:237
  (22 shorter events, 0.2 us)
Async XLA Ops:
  1.5 11.1 %collective-permute-start.5 = (bf16[8,10752]{1,0:T(8,128)(2,1)S(1)}, bf16[8,10752]{1,0:T(8,128)(2,1)S(1)}, u32[]{:S(2)}, u32[]{:S(2)}) collective-permute-start(bf16[8,10752]{1,0:T(8,128)(2,1)S(1)} %get-tuple-element.37), channel_id=1, source_target_pairs={{0,12},{1,13},{2,14},{3,15},{4,8},{5,9},{6,10},{7,11},{8,4},{9,5},... | collective-permute-start | bytes 516104 | tf_op jit(solution)/shard_map/ppermute | solution.py:262
  6.6 6.5 %collective-permute-start = (bf16[8,10752]{1,0:T(8,128)(2,1)S(1)}, bf16[8,10752]{1,0:T(8,128)(2,1)S(1)}, u32[]{:S(2)}, u32[]{:S(2)}) collective-permute-start(bf16[8,10752]{1,0:T(8,128)(2,1)S(1)} %get-tuple-element.28.refs_3_.refs_0_), channel_id=1, source_target_pairs={{0,2},{1,3},{2,0},{3,1},{4,6},{5,7},{6,4},{7,5},{8,10},{9,11},{10,... | collective-permute-start | bytes 516104 | tf_op jit(solution)/shard_map/ppermute | solution.py:265
  12.4 5.6 %collective-permute-start.7 = (bf16[8,10752]{1,0:T(8,128)(2,1)S(1)}, bf16[8,10752]{1,0:T(8,128)(2,1)S(1)}, u32[]{:S(2)}, u32[]{:S(2)}) collective-permute-start(bf16[8,10752]{1,0:T(8,128)(2,1)S(1)} %shard_map.77), channel_id=1, source_target_pairs={{0,4},{1,5},{2,6},{3,7},{4,0},{5,1},{6,2},{7,3},{8,12},{9,13},{10,... | collective-permute-start | bytes 516104 | tf_op jit(solution)/shard_map/ppermute | solution.py:262
  12.4 6.0 %collective-permute-start.1 = (bf16[8,10752]{1,0:T(8,128)(2,1)S(1)}, bf16[8,10752]{1,0:T(8,128)(2,1)S(1)}, u32[]{:S(2)}, u32[]{:S(2)}) collective-permute-start(bf16[8,10752]{1,0:T(8,128)(2,1)S(1)} %get-tuple-element.28.refs_3_.refs_0_), channel_id=1, source_target_pairs={{0,1},{1,0},{2,3},{3,2},{4,5},{5,4},{6,7},{7,6},{8,9},{9,8},{10,11... | collective-permute-start | bytes 516104 | tf_op jit(solution)/shard_map/ppermute | solution.py:268
  12.5 6.8 %collective-permute-start.18 = (bf16[8,10752]{1,0:T(8,128)(2,1)S(1)}, bf16[8,10752]{1,0:T(8,128)(2,1)S(1)}, u32[]{:S(2)}, u32[]{:S(2)}) collective-permute-start(bf16[8,10752]{1,0:T(8,128)(2,1)S(1)} %collective-permute-done.5.refs_1_.refs_0_), channel_id=1, source_target_pairs={{0,2},{1,3},{2,0},{3,1},{4,6},{5,7},{6,4},{7,5},{8,10},{9,11},{10,... | collective-permute-start | bytes 516104 | tf_op jit(solution)/shard_map/ppermute | solution.py:265
  13.1 6.2 %collective-permute-start.2 = (bf16[8,10752]{1,0:T(8,128)(2,1)S(1)}, bf16[8,10752]{1,0:T(8,128)(2,1)S(1)}, u32[]{:S(2)}, u32[]{:S(2)}) collective-permute-start(bf16[8,10752]{1,0:T(8,128)(2,1)S(1)} %collective-permute-done.refs_1_.refs_2_), channel_id=1, source_target_pairs={{0,1},{1,0},{2,3},{3,2},{4,5},{5,4},{6,7},{7,6},{8,9},{9,8},{10,11... | collective-permute-start | bytes 516104 | tf_op jit(solution)/shard_map/ppermute | solution.py:268
  13.3 12.4 %collective-permute-start.6 = (bf16[8,10752]{1,0:T(8,128)(2,1)S(1)}, bf16[8,10752]{1,0:T(8,128)(2,1)S(1)}, u32[]{:S(2)}, u32[]{:S(2)}) collective-permute-start(bf16[8,10752]{1,0:T(8,128)(2,1)S(1)} %shard_map.76), channel_id=1, source_target_pairs={{0,8},{1,9},{2,10},{3,11},{4,12},{5,13},{6,14},{7,15},{8,0},{9,1},... | collective-permute-start | bytes 516104 | tf_op jit(solution)/shard_map/ppermute | solution.py:262
  18.0 7.7 %collective-permute-start.8 = (bf16[8,10752]{1,0:T(8,128)(2,1)S(1)}, bf16[8,10752]{1,0:T(8,128)(2,1)S(1)}, u32[]{:S(2)}, u32[]{:S(2)}) collective-permute-start(bf16[8,10752]{1,0:T(8,128)(2,1)S(1)} %collective-permute-done.7.refs_0_), channel_id=1, source_target_pairs={{0,2},{1,3},{2,0},{3,1},{4,6},{5,7},{6,4},{7,5},{8,10},{9,11},{10,... | collective-permute-start | bytes 516104 | tf_op jit(solution)/shard_map/ppermute | solution.py:265
  18.5 7.7 %collective-permute-start.19 = (bf16[8,10752]{1,0:T(8,128)(2,1)S(1)}, bf16[8,10752]{1,0:T(8,128)(2,1)S(1)}, u32[]{:S(2)}, u32[]{:S(2)}) collective-permute-start(bf16[8,10752]{1,0:T(8,128)(2,1)S(1)} %collective-permute-done.5.refs_1_.refs_0_), channel_id=1, source_target_pairs={{0,1},{1,0},{2,3},{3,2},{4,5},{5,4},{6,7},{7,6},{8,9},{9,8},{10,11... | collective-permute-start | bytes 516104 | tf_op jit(solution)/shard_map/ppermute | solution.py:268
  19.3 7.3 %collective-permute-start.20 = (bf16[8,10752]{1,0:T(8,128)(2,1)S(1)}, bf16[8,10752]{1,0:T(8,128)(2,1)S(1)}, u32[]{:S(2)}, u32[]{:S(2)}) collective-permute-start(bf16[8,10752]{1,0:T(8,128)(2,1)S(1)} %collective-permute-done.18.refs_1_), channel_id=1, source_target_pairs={{0,1},{1,0},{2,3},{3,2},{4,5},{5,4},{6,7},{7,6},{8,9},{9,8},{10,11... | collective-permute-start | bytes 516104 | tf_op jit(solution)/shard_map/ppermute | solution.py:268
  21.4 7.4 %collective-permute-start.4 = (bf16[8,10752]{1,0:T(8,128)(2,1)S(1)}, bf16[8,10752]{1,0:T(8,128)(2,1)S(1)}, u32[]{:S(2)}, u32[]{:S(2)}) collective-permute-start(bf16[8,10752]{1,0:T(8,128)(2,1)S(1)} %get-tuple-element.35.refs_1_), channel_id=1, source_target_pairs={{0,1},{1,0},{2,3},{3,2},{4,5},{5,4},{6,7},{7,6},{8,9},{9,8},{10,11... | collective-permute-start | bytes 516104 | tf_op jit(solution)/shard_map/ppermute | solution.py:268
  25.6 6.2 %collective-permute-start.9 = (bf16[8,10752]{1,0:T(8,128)(2,1)S(1)}, bf16[8,10752]{1,0:T(8,128)(2,1)S(1)}, u32[]{:S(2)}, u32[]{:S(2)}) collective-permute-start(bf16[8,10752]{1,0:T(8,128)(2,1)S(1)} %shard_map.78.refs_0_), channel_id=1, source_target_pairs={{0,2},{1,3},{2,0},{3,1},{4,6},{5,7},{6,4},{7,5},{8,10},{9,11},{10,... | collective-permute-start | bytes 516104 | tf_op jit(solution)/shard_map/ppermute | solution.py:265
  26.1 9.8 %collective-permute-start.16 = (bf16[8,10752]{1,0:T(8,128)(2,1)S(1)}, bf16[8,10752]{1,0:T(8,128)(2,1)S(1)}, u32[]{:S(2)}, u32[]{:S(2)}) collective-permute-start(bf16[8,10752]{1,0:T(8,128)(2,1)S(1)} %collective-permute-done.7.refs_0_), channel_id=1, source_target_pairs={{0,1},{1,0},{2,3},{3,2},{4,5},{5,4},{6,7},{7,6},{8,9},{9,8},{10,11... | collective-permute-start | bytes 516104 | tf_op jit(solution)/shard_map/ppermute | solution.py:268
  26.1 5.8 %collective-permute-start.10 = (bf16[8,10752]{1,0:T(8,128)(2,1)S(1)}, bf16[8,10752]{1,0:T(8,128)(2,1)S(1)}, u32[]{:S(2)}, u32[]{:S(2)}) collective-permute-start(bf16[8,10752]{1,0:T(8,128)(2,1)S(1)} %shard_map.78.refs_0_), channel_id=1, source_target_pairs={{0,1},{1,0},{2,3},{3,2},{4,5},{5,4},{6,7},{7,6},{8,9},{9,8},{10,11... | collective-permute-start | bytes 516104 | tf_op jit(solution)/shard_map/ppermute | solution.py:268
  26.6 27.2 %collective-permute-start.3 = (bf16[8,10752]{1,0:T(8,128)(2,1)S(1)}, bf16[8,10752]{1,0:T(8,128)(2,1)S(1)}, u32[]{:S(2)}, u32[]{:S(2)}) collective-permute-start(bf16[8,10752]{1,0:T(8,128)(2,1)S(1)} %get-tuple-element.33), channel_id=1, source_target_pairs={{0,1},{1,0},{2,3},{3,2},{4,5},{5,4},{6,7},{7,6},{8,9},{9,8},{10,11... | collective-permute-start | bytes 516104 | tf_op jit(solution)/shard_map/ppermute | solution.py:268
  28.8 6.7 %collective-permute-start.21 = (bf16[8,10752]{1,0:T(8,128)(2,1)S(1)}, bf16[8,10752]{1,0:T(8,128)(2,1)S(1)}, u32[]{:S(2)}, u32[]{:S(2)}) collective-permute-start(bf16[8,10752]{1,0:T(8,128)(2,1)S(1)} %get-tuple-element.44), channel_id=1, source_target_pairs={{0,1},{1,0},{2,3},{3,2},{4,5},{5,4},{6,7},{7,6},{8,9},{9,8},{10,11... | collective-permute-start | bytes 516104 | tf_op jit(solution)/shard_map/ppermute | solution.py:268
  31.8 1.4 %collective-permute-start.11 = (bf16[8,10752]{1,0:T(8,128)(2,1)S(1)}, bf16[8,10752]{1,0:T(8,128)(2,1)S(1)}, u32[]{:S(2)}, u32[]{:S(2)}) collective-permute-start(bf16[8,10752]{1,0:T(8,128)(2,1)S(1)} %collective-permute-done.9.refs_1_), channel_id=1, source_target_pairs={{0,1},{1,0},{2,3},{3,2},{4,5},{5,4},{6,7},{7,6},{8,9},{9,8},{10,11... | collective-permute-start | bytes 516104 | tf_op jit(solution)/shard_map/ppermute | solution.py:268
  31.9 4.3 %collective-permute-start.17 = (bf16[8,10752]{1,0:T(8,128)(2,1)S(1)}, bf16[8,10752]{1,0:T(8,128)(2,1)S(1)}, u32[]{:S(2)}, u32[]{:S(2)}) collective-permute-start(bf16[8,10752]{1,0:T(8,128)(2,1)S(1)} %collective-permute-done.8.refs_2_.refs_1_), channel_id=1, source_target_pairs={{0,1},{1,0},{2,3},{3,2},{4,5},{5,4},{6,7},{7,6},{8,9},{9,8},{10,11... | collective-permute-start | bytes 516104 | tf_op jit(solution)/shard_map/ppermute | solution.py:268
  33.2 7.0 %collective-permute-start.26 = (bf16[8,10752]{1,0:T(8,128)(2,1)S(1)}, bf16[8,10752]{1,0:T(8,128)(2,1)S(1)}, u32[]{:S(2)}, u32[]{:S(2)}) collective-permute-start(bf16[8,10752]{1,0:T(8,128)(2,1)S(1)} %get-tuple-element.50), channel_id=1, source_target_pairs={{0,1},{1,0},{2,3},{3,2},{4,5},{5,4},{6,7},{7,6},{8,9},{9,8},{10,11... | collective-permute-start | bytes 516104 | tf_op jit(solution)/shard_map/ppermute | solution.py:268
  35.5 3.1 %collective-permute-start.13 = (bf16[8,10752]{1,0:T(8,128)(2,1)S(1)}, bf16[8,10752]{1,0:T(8,128)(2,1)S(1)}, u32[]{:S(2)}, u32[]{:S(2)}) collective-permute-start(bf16[8,10752]{1,0:T(8,128)(2,1)S(1)} %get-tuple-element.42.refs_7_), channel_id=1, source_target_pairs={{0,1},{1,0},{2,3},{3,2},{4,5},{5,4},{6,7},{7,6},{8,9},{9,8},{10,11... | collective-permute-start | bytes 516104 | tf_op jit(solution)/shard_map/ppermute | solution.py:268
  36.0 7.2 %collective-permute-start.12 = (bf16[8,10752]{1,0:T(8,128)(2,1)S(1)}, bf16[8,10752]{1,0:T(8,128)(2,1)S(1)}, u32[]{:S(2)}, u32[]{:S(2)}) collective-permute-start(bf16[8,10752]{1,0:T(8,128)(2,1)S(1)} %get-tuple-element.40), channel_id=1, source_target_pairs={{0,1},{1,0},{2,3},{3,2},{4,5},{5,4},{6,7},{7,6},{8,9},{9,8},{10,11... | collective-permute-start | bytes 516104 | tf_op jit(solution)/shard_map/ppermute | solution.py:268
  36.2 6.6 %collective-permute-start.27 = (bf16[8,10752]{1,0:T(8,128)(2,1)S(1)}, bf16[8,10752]{1,0:T(8,128)(2,1)S(1)}, u32[]{:S(2)}, u32[]{:S(2)}) collective-permute-start(bf16[8,10752]{1,0:T(8,128)(2,1)S(1)} %add_convert_fusion.3.refs_8_), channel_id=1, source_target_pairs={{0,2},{1,3},{2,0},{3,1},{4,6},{5,7},{6,4},{7,5},{8,10},{9,11},{10,... | collective-permute-start | bytes 516104 | tf_op jit(solution)/shard_map/ppermute | solution.py:265
  38.5 22.8 %copy-start = (s32[16,2]{0,1:T(2,128)S(1)}, s32[16,2]{0,1:T(2,128)}, u32[]{:S(2)}) copy-start(s32[16,2]{0,1:T(2,128)} %param.8) | copy-start | bytes 388
  38.6 22.8 %copy-start.1 = (s32[4]{0:T(128)S(1)}, s32[4]{0:T(128)}, u32[]{:S(2)}) copy-start(s32[4]{0:T(128)} %placement_ref.3) | copy-start | bytes 52
  38.6 22.8 %copy-start.2 = (f32[16,2]{0,1:T(2,128)S(1)}, f32[16,2]{0,1:T(2,128)}, u32[]{:S(2)}) copy-start(f32[16,2]{0,1:T(2,128)} %param.9) | copy-start | bytes 388
  38.6 1.5 %collective-permute-start.23 = (bf16[8,10752]{1,0:T(8,128)(2,1)S(1)}, bf16[8,10752]{1,0:T(8,128)(2,1)S(1)}, u32[]{:S(2)}, u32[]{:S(2)}) collective-permute-start(bf16[8,10752]{1,0:T(8,128)(2,1)S(1)} %get-tuple-element.48), channel_id=1, source_target_pairs={{0,1},{1,0},{2,3},{3,2},{4,5},{5,4},{6,7},{7,6},{8,9},{9,8},{10,11... | collective-permute-start | bytes 516104 | tf_op jit(solution)/shard_map/ppermute | solution.py:268
  40.1 9.4 %collective-permute-start.22 = (bf16[8,10752]{1,0:T(8,128)(2,1)S(1)}, bf16[8,10752]{1,0:T(8,128)(2,1)S(1)}, u32[]{:S(2)}, u32[]{:S(2)}) collective-permute-start(bf16[8,10752]{1,0:T(8,128)(2,1)S(1)} %get-tuple-element.46), channel_id=1, source_target_pairs={{0,1},{1,0},{2,3},{3,2},{4,5},{5,4},{6,7},{7,6},{8,9},{9,8},{10,11... | collective-permute-start | bytes 516104 | tf_op jit(solution)/shard_map/ppermute | solution.py:268
  40.3 7.3 %collective-permute-start.14 = (bf16[8,10752]{1,0:T(8,128)(2,1)S(1)}, bf16[8,10752]{1,0:T(8,128)(2,1)S(1)}, u32[]{:S(2)}, u32[]{:S(2)}) collective-permute-start(bf16[8,10752]{1,0:T(8,128)(2,1)S(1)} %add_convert_fusion.6), channel_id=1, source_target_pairs={{0,2},{1,3},{2,0},{3,1},{4,6},{5,7},{6,4},{7,5},{8,10},{9,11},{10,... | collective-permute-start | bytes 516104 | tf_op jit(solution)/shard_map/ppermute | solution.py:265
  42.8 8.4 %collective-permute-start.24 = (bf16[8,10752]{1,0:T(8,128)(2,1)S(1)}, bf16[8,10752]{1,0:T(8,128)(2,1)S(1)}, u32[]{:S(2)}, u32[]{:S(2)}) collective-permute-start(bf16[8,10752]{1,0:T(8,128)(2,1)S(1)} %add_convert_fusion.2), channel_id=1, source_target_pairs={{0,2},{1,3},{2,0},{3,1},{4,6},{5,7},{6,4},{7,5},{8,10},{9,11},{10,... | collective-permute-start | bytes 516104 | tf_op jit(solution)/shard_map/ppermute | solution.py:265
  43.2 8.3 %collective-permute-start.28 = (bf16[8,10752]{1,0:T(8,128)(2,1)S(1)}, bf16[8,10752]{1,0:T(8,128)(2,1)S(1)}, u32[]{:S(2)}, u32[]{:S(2)}) collective-permute-start(bf16[8,10752]{1,0:T(8,128)(2,1)S(1)} %add_convert_fusion), channel_id=1, source_target_pairs={{0,12},{1,13},{2,14},{3,15},{4,8},{5,9},{6,10},{7,11},{8,4},{9,5},... | collective-permute-start | bytes 516104 | tf_op jit(solution)/shard_map/ppermute | solution.py:262
  47.6 6.7 %collective-permute-start.15 = (bf16[8,10752]{1,0:T(8,128)(2,1)S(1)}, bf16[8,10752]{1,0:T(8,128)(2,1)S(1)}, u32[]{:S(2)}, u32[]{:S(2)}) collective-permute-start(bf16[8,10752]{1,0:T(8,128)(2,1)S(1)} %shard_map.80), channel_id=1, source_target_pairs={{0,2},{1,3},{2,0},{3,1},{4,6},{5,7},{6,4},{7,5},{8,10},{9,11},{10,... | collective-permute-start | bytes 516104 | tf_op jit(solution)/shard_map/ppermute | solution.py:265
  51.3 8.4 %collective-permute-start.25 = (bf16[8,10752]{1,0:T(8,128)(2,1)S(1)}, bf16[8,10752]{1,0:T(8,128)(2,1)S(1)}, u32[]{:S(2)}, u32[]{:S(2)}) collective-permute-start(bf16[8,10752]{1,0:T(8,128)(2,1)S(1)} %add_convert_fusion.1), channel_id=1, source_target_pairs={{0,4},{1,5},{2,6},{3,7},{4,0},{5,1},{6,2},{7,3},{8,12},{9,13},{10,... | collective-permute-start | bytes 516104 | tf_op jit(solution)/shard_map/ppermute | solution.py:262
  51.5 9.9 %collective-permute-start.29 = (bf16[8,10752]{1,0:T(8,128)(2,1)S(1)}, bf16[8,10752]{1,0:T(8,128)(2,1)S(1)}, u32[]{:S(2)}, u32[]{:S(2)}) collective-permute-start(bf16[8,10752]{1,0:T(8,128)(2,1)S(1)} %shard_map.83), channel_id=1, source_target_pairs={{0,8},{1,9},{2,10},{3,11},{4,12},{5,13},{6,14},{7,15},{8,0},{9,1},... | collective-permute-start | bytes 516104 | tf_op jit(solution)/shard_map/ppermute | solution.py:262

commit v8 on v7

--- a/solution.py
+++ b/solution.py
@@ -195,7 +195,7 @@
 
 
 def mix_kernel(n_blocks, parts, placement_ref, ids_ref, gates_ref, *refs):
-    results, out_ref = refs[:-1], refs[-1]
+    results, out_ref = refs[:n_blocks], refs[-1]
     rows, width = out_ref.shape
     half, quarter, middle = rows // 2, rows // 4, width // 2
     block = lax.axis_index("node") // parts
@@ -231,13 +231,13 @@
         out_ref[:, side * middle : (side + 1) * middle] = value.astype(jnp.bfloat16)
 
 
-def mix(placement, ids, gates, results, n_blocks, parts):
+def mix(placement, ids, gates, results, after, n_blocks, parts):
     rows = ids.shape[1]
     width = results[0].shape[1] // 3 * 2
     return pl.pallas_call(
         functools.partial(mix_kernel, n_blocks, parts),
         out_shape=jax.ShapeDtypeStruct((rows, width), jnp.bfloat16),
-        in_specs=[SMEM] + [VMEM] * (2 + n_blocks),
+        in_specs=[SMEM] + [VMEM] * (2 + n_blocks) + [ANYWHERE] * len(after),
         out_specs=VMEM,
         compiler_params=pltpu.CompilerParams(vmem_limit_bytes=VMEM_BYTES),
         cost_estimate=pl.CostEstimate(
@@ -245,11 +245,25 @@
             bytes_accessed=2 * (n_blocks + 1) * rows * width,
             transcendentals=0,
         ),
-    )(placement, ids, gates, *[in_vmem(r) for r in results])
+    )(placement, ids, gates, *[in_vmem(r) for r in results], *after)
+
+
+def add_kernel(*refs):
+    total = refs[0][...].astype(jnp.float32)
+    for ref in refs[1:-1]:
+        total = total + ref[...].astype(jnp.float32)
+    refs[-1][...] = total.astype(refs[-1].dtype)
 
 
 def add(*values):
-    return sum(v.astype(jnp.float32) for v in values).astype(jnp.bfloat16)
+    return pl.pallas_call(
+        add_kernel,
+        out_shape=pltpu.VMEM(values[0].shape, values[0].dtype),
+        in_specs=[VMEM] * len(values),
+        out_specs=VMEM,
+        compiler_params=pltpu.CompilerParams(vmem_limit_bytes=VMEM_BYTES),
+        cost_estimate=NO_COST,
+    )(*[in_vmem(v) for v in values])
 
 
 def local(tokens, expert_ids, gates, placement, gate_weight, up_weight, down_weight):
@@ -290,7 +304,7 @@
     straight[0] = buckets[0]
     across[0] = along_y(straight[0])
     compute(0, [])
-    second = None
+    second, marks = None, []
     for g, group in enumerate(groups):
         first = group[0]
         if g == 0:
@@ -304,17 +318,18 @@
             after = [sent[0]] + ([across[second]] if second else [])
             straight[first] = when(straight[first], after)
             across[first] = along_y(straight[first])
-            compute(first, [])
-            go_home(first, [results[previous]])
+            compute(first, [both[previous]])
+            go_home(first, [])
+            marks.append(along_core(results[previous]))
         if second:
-            compute(second, [sent[first]] + ([both[previous]] if g else []))
+            compute(second, [sent[first]])
             go_home(second, [])
         second = group[1] if len(group) > 1 else None
         if second:
             straight[second] = along_z(when(buckets[second], [weights[0]] if g == 0 else []), second)
             across[second] = along_y(straight[second])
     go_home(0, [home[last]])
-    return mix(placement, ids, gates.T, [results[k] for k in range(n_blocks)], n_blocks, parts)
+    return mix(placement, ids, gates.T, [results[k] for k in range(n_blocks)], marks, n_blocks, parts)
 
 
 def solution(mesh):

time: 63.4 us -> 64.4 us (1.016)
  waiting for transfers between devices: 22.6 us -> 23.3 us
    ppermute x6, waiting for transfers between devices: 11.7 us -> 15.8 us  [along_z(): return lax.ppermute(value, 'node', pairs)]
    ppermute x6, starting transfers between devices: 13.3 us -> 15.7 us  [along_z(): return lax.ppermute(value, 'node', pairs)]
    ppermute x8, waiting for transfers between devices: 8.8 us -> 6.62 us  [along_y(): return lax.ppermute(value, 'node', [(i, i ^ 2) for i in range(devices)])]
    ppermute x16 -> x17, waiting for transfers between devices: 2.1 us -> 0.87 us  [along_core(): return lax.ppermute(value, 'node', [(i, i ^ 1) for i in range(devices)])]
    ppermute x8, starting transfers between devices: 7.32 us -> 6.13 us  [along_y(): return lax.ppermute(value, 'node', [(i, i ^ 2) for i in range(devices)])]
    ppermute x16 -> x17, starting transfers between devices: 3.53 us -> 2.62 us  [along_core(): return lax.ppermute(value, 'node', [(i, i ^ 1) for i in range(devices)])]
  transfers between devices with their start and end apart: 30 -> 31, of which waited for: 12 -> 10; matrix products, arithmetic and copies ran while one was open for 1% -> 0% of each run, Pallas kernels for 20% -> 20%
where the time goes in v8:
time: 64.4 us; the launch traced here: 64.3 us
  starting transfers between devices  24.5 us (38%)
  waiting for transfers between devices  23.3 us (36%)
  Pallas kernels  16.3 us (25%)
    ppermute x6, waiting for transfers between devices, along_z(): return lax.ppermute(value, 'node', pairs)  15.8 us
    ppermute x6, starting transfers between devices, along_z(): return lax.ppermute(value, 'node', pairs)  15.7 us
    pallas_call x4, Pallas kernels, run_experts(): pl.pallas_call(experts_kernel, out_shape=[shape] * len(pieces), in_specs=...  8.28 us
    ppermute x8, waiting for transfers between devices, along_y(): return lax.ppermute(value, 'node', [(i, i ^ 2) for i in range(devices)])  6.62 us
    ppermute x8, starting transfers between devices, along_y(): return lax.ppermute(value, 'node', [(i, i ^ 2) for i in range(devices)])  6.13 us
    pallas_call x1, Pallas kernels, load(): pl.pallas_call(load_kernel, out_shape=[pltpu.VMEM(w.shape, w.dtype) for w...  4.24 us
    ppermute x17, starting transfers between devices, along_core(): return lax.ppermute(value, 'node', [(i, i ^ 1) for i in range(devices)])  2.62 us
    pallas_call x1, Pallas kernels, mix(): pl.pallas_call(functools.partial(mix_kernel, n_blocks, parts), out_shape=...  1.85 us
  transfers between devices with their start and end apart: 31, of which 10 were waited for; matrix products, arithmetic and copies ran while one was open for 0% of the time, Pallas kernels for 20%

profile of v8, /device:TPU:0, one launch (start us, length us, event | category | flops | bytes accessed | tf_op | source)
XLA Modules:
  0.0 64.3 jit_solution(1345417835546930564)
XLA Ops:
  0.0 1.5 %shard_map.73 = (bf16[8,10752]{1,0:T(8,128)(2,1)S(1)}, bf16[8,10752]{1,0:T(8,128)(2,1)S(1)}, bf16[8,10752]{1,0:T(8,128)(2,1)S(1)}, bf16[8,10752]{1,0:T(8,128)(2,1)S(1)}) custom-call(s32[4]{0:T(128)} %placement_ref.3, s32[2,16]{1,0:T(2,128)} %bitcast.2, bf16[16,7168]{1,0:T(8,128)(2,1)} %tokens_ref.1), custom_call_target="tpu_custom_call" | custom-call | tf_op jit(solution)/shard_map/pallas_call | solution.py:82
  1.5 5.1 %collective-permute-start.5 = (bf16[8,10752]{1,0:T(8,128)(2,1)S(1)}, bf16[8,10752]{1,0:T(8,128)(2,1)S(1)}, u32[]{:S(2)}, u32[]{:S(2)}) collective-permute-start(bf16[8,10752]{1,0:T(8,128)(2,1)S(1)} %get-tuple-element.37), channel_id=1, source_target_pairs={{0,12},{1,13},{2,14},{3,15},{4,8},{5,9},{6,10},{7,11},{8,4},{9,5},... | collective-permute-start | bytes 516104 | tf_op jit(solution)/shard_map/ppermute | solution.py:276
  6.6 1.5 %collective-permute-start = (bf16[8,10752]{1,0:T(8,128)(2,1)S(1)}, bf16[8,10752]{1,0:T(8,128)(2,1)S(1)}, u32[]{:S(2)}, u32[]{:S(2)}) collective-permute-start(bf16[8,10752]{1,0:T(8,128)(2,1)S(1)} %get-tuple-element.28.refs_3_.refs_0_), channel_id=1, source_target_pairs={{0,2},{1,3},{2,0},{3,1},{4,6},{5,7},{6,4},{7,5},{8,10},{9,11},{10,... | collective-permute-start | bytes 516104 | tf_op jit(solution)/shard_map/ppermute | solution.py:279
  8.1 4.2 %shard_map.74 = (bf16[7168,256]{1,0:T(8,128)(2,1)S(1)}, bf16[7168,256]{1,0:T(8,128)(2,1)S(1)}, bf16[256,7168]{1,0:T(8,128)(2,1)S(1)}) custom-call(bf16[7168,256]{1,0:T(8,128)(2,1)} %refs_0_.1, bf16[7168,256]{1,0:T(8,128)(2,1)} %refs_1_.1, bf16[256,7168]{1,0:T(8,128)(2,1)} %refs_2_.1, bf16[8,10752]{1,0:T(8,128)(2,1)S(1)} %get-tuple-element.28.refs_3_.refs_0_), custom_call_target="tpu_custom_call" | custom-call | tf_op jit(solution)/shard_map/pallas_call | solution.py:125
  12.4 0.1 collective-permute-start.7
  12.4 0.1 collective-permute-start.1
  12.5 0.0 collective-permute-done.5.refs_1_.refs_0_
  12.5 0.6 collective-permute-start.12
  13.1 0.0 collective-permute-done.refs_1_.refs_2_
  13.1 0.2 collective-permute-start.2
  13.3 3.6 %collective-permute-start.6 = (bf16[8,10752]{1,0:T(8,128)(2,1)S(1)}, bf16[8,10752]{1,0:T(8,128)(2,1)S(1)}, u32[]{:S(2)}, u32[]{:S(2)}) collective-permute-start(bf16[8,10752]{1,0:T(8,128)(2,1)S(1)} %shard_map.77), channel_id=1, source_target_pairs={{0,8},{1,9},{2,10},{3,11},{4,12},{5,13},{6,14},{7,15},{8,0},{9,1},... | collective-permute-start | bytes 516104 | tf_op jit(solution)/shard_map/ppermute | solution.py:276
  16.9 1.1 %collective-permute-done.7.refs_0_ = bf16[8,10752]{1,0:T(8,128)(2,1)S(1)} collective-permute-done((bf16[8,10752]{1,0:T(8,128)(2,1)S(1)}, bf16[8,10752]{1,0:T(8,128)(2,1)S(1)}, u32[]{:S(2)}, u32[]{:S(2)}) %collective-permute-start.7) | collective-permute-done | bytes 172064 | tf_op jit(solution)/shard_map/ppermute | solution.py:276
  18.0 0.5 collective-permute-start.8
  18.5 0.8 %collective-permute-done.12.refs_1_ = bf16[8,10752]{1,0:T(8,128)(2,1)S(1)} collective-permute-done((bf16[8,10752]{1,0:T(8,128)(2,1)S(1)}, bf16[8,10752]{1,0:T(8,128)(2,1)S(1)}, u32[]{:S(2)}, u32[]{:S(2)}) %collective-permute-start.12) | collective-permute-done | bytes 172064 | tf_op jit(solution)/shard_map/ppermute | solution.py:279
  19.3 0.0 collective-permute-done.2.refs_3_
  19.3 2.1 %shard_map.75 = (bf16[8,10752]{1,0:T(8,128)(2,1)S(1)}, bf16[8,10752]{1,0:T(8,128)(2,1)S(1)}, bf16[8,10752]{1,0:T(8,128)(2,1)S(1)}, bf16[8,10752]{1,0:T(8,128)(2,1)S(1)}) custom-call(bf16[8,10752]{1,0:T(8,128)(2,1)S(1)} %get-tuple-element.28.refs_3_.refs_0_, bf16[8,10752]{1,0:T(8,128)(2,1)S(1)} %collective-permute-done.refs_1_.refs_2_, ...), custom_call_target="tpu_custom_call" | custom-call | bytes 7340032 | tf_op jit(solution)/shard_map/pallas_call | solution.py:185
  21.4 4.2 %collective-permute-done.6.refs_0_ = bf16[8,10752]{1,0:T(8,128)(2,1)S(1)} collective-permute-done((bf16[8,10752]{1,0:T(8,128)(2,1)S(1)}, bf16[8,10752]{1,0:T(8,128)(2,1)S(1)}, u32[]{:S(2)}, u32[]{:S(2)}) %collective-permute-start.6) | collective-permute-done | bytes 172064 | tf_op jit(solution)/shard_map/ppermute | solution.py:276
  25.6 0.5 collective-permute-start.9
  26.1 0.0 collective-permute-done.13.refs_2_
  26.1 0.0 collective-permute-done.14.refs_3_
  26.1 2.1 %shard_map.80 = (bf16[8,10752]{1,0:T(8,128)(2,1)S(1)}, bf16[8,10752]{1,0:T(8,128)(2,1)S(1)}, bf16[8,10752]{1,0:T(8,128)(2,1)S(1)}, bf16[8,10752]{1,0:T(8,128)(2,1)S(1)}) custom-call(bf16[8,10752]{1,0:T(8,128)(2,1)S(1)} %collective-permute-done.5.refs_1_.refs_0_, bf16[8,10752]{1,0:T(8,128)(2,1)S(1)} %collective-permute-done.12.refs_1_, ...), custom_call_target="tpu_custom_call" | custom-call | bytes 7340032 | tf_op jit(solution)/shard_map/pallas_call | solution.py:185
  28.2 0.1 collective-permute-start.15
  28.3 0.5 collective-permute-start.10
  28.8 3.0 %collective-permute-done.9.refs_1_ = bf16[8,10752]{1,0:T(8,128)(2,1)S(1)} collective-permute-done((bf16[8,10752]{1,0:T(8,128)(2,1)S(1)}, bf16[8,10752]{1,0:T(8,128)(2,1)S(1)}, u32[]{:S(2)}, u32[]{:S(2)}) %collective-permute-start.9) | collective-permute-done | bytes 172064 | tf_op jit(solution)/shard_map/ppermute | solution.py:279
  31.8 0.0 collective-permute-start.11
  31.8 0.5 collective-permute-start.20
  32.3 0.0 collective-permute-start.21
  32.4 0.0 collective-permute-done.15.refs_1_
  32.4 0.8 %collective-permute-done.11.refs_3_ = bf16[8,10752]{1,0:T(8,128)(2,1)S(1)} collective-permute-done((bf16[8,10752]{1,0:T(8,128)(2,1)S(1)}, bf16[8,10752]{1,0:T(8,128)(2,1)S(1)}, u32[]{:S(2)}, u32[]{:S(2)}) %collective-permute-start.11) | collective-permute-done | bytes 172064 | tf_op jit(solution)/shard_map/ppermute | solution.py:282
  33.2 2.1 %shard_map.82 = (bf16[8,10752]{1,0:T(8,128)(2,1)S(1)}, bf16[8,10752]{1,0:T(8,128)(2,1)S(1)}, bf16[8,10752]{1,0:T(8,128)(2,1)S(1)}, bf16[8,10752]{1,0:T(8,128)(2,1)S(1)}) custom-call(bf16[8,10752]{1,0:T(8,128)(2,1)S(1)} %shard_map.79.refs_0_, bf16[8,10752]{1,0:T(8,128)(2,1)S(1)} %collective-permute-done.9.refs_1_, ...), custom_call_target="tpu_custom_call" | custom-call | bytes 7340032 | tf_op jit(solution)/shard_map/pallas_call | solution.py:185
  35.3 0.2 collective-permute-start.17
  35.5 0.4 collective-permute-start.27
  35.9 0.3 collective-permute-start.28
  36.2 2.1 %shard_map.87 = (bf16[8,10752]{1,0:T(8,128)(2,1)S(1)}, bf16[8,10752]{1,0:T(8,128)(2,1)S(1)}, bf16[8,10752]{1,0:T(8,128)(2,1)S(1)}, bf16[8,10752]{1,0:T(8,128)(2,1)S(1)}) custom-call(bf16[8,10752]{1,0:T(8,128)(2,1)S(1)} %collective-permute-done.7.refs_0_, bf16[8,10752]{1,0:T(8,128)(2,1)S(1)} %collective-permute-done.8.refs_2_.refs_1_, ...), custom_call_target="tpu_custom_call" | custom-call | bytes 7340032 | tf_op jit(solution)/shard_map/pallas_call | solution.py:185
  38.3 0.0 copy-start
  38.3 0.0 copy-start.1
  38.3 0.0 copy-start.2
  38.3 0.1 collective-permute-start.23
  38.4 0.5 collective-permute-start.4
  38.9 0.1 collective-permute-start.16
  39.0 0.0 collective-permute-done.27.refs_1_
  39.0 1.8 %collective-permute-start.18 = (bf16[8,10752]{1,0:T(8,128)(2,1)S(1)}, bf16[8,10752]{1,0:T(8,128)(2,1)S(1)}, u32[]{:S(2)}, u32[]{:S(2)}) collective-permute-start(bf16[8,10752]{1,0:T(8,128)(2,1)S(1)} %shard_map.83), channel_id=1, source_target_pairs={{0,2},{1,3},{2,0},{3,1},{4,6},{5,7},{6,4},{7,5},{8,10},{9,11},{10,... | collective-permute-start | bytes 516104 | tf_op jit(solution)/shard_map/ppermute | solution.py:279
  40.8 1.6 %collective-permute-done.28.refs_2_ = bf16[8,10752]{1,0:T(8,128)(2,1)S(1)} collective-permute-done((bf16[8,10752]{1,0:T(8,128)(2,1)S(1)}, bf16[8,10752]{1,0:T(8,128)(2,1)S(1)}, u32[]{:S(2)}, u32[]{:S(2)}) %collective-permute-start.28) | collective-permute-done | bytes 172064 | tf_op jit(solution)/shard_map/ppermute | solution.py:279
  42.5 0.0 collective-permute-start.22
  42.5 0.1 shard_map.90
  42.5 0.0 collective-permute-done.23.refs_1_
  42.5 1.7 %collective-permute-start.29 = (bf16[8,10752]{1,0:T(8,128)(2,1)S(1)}, bf16[8,10752]{1,0:T(8,128)(2,1)S(1)}, u32[]{:S(2)}, u32[]{:S(2)}) collective-permute-start(bf16[8,10752]{1,0:T(8,128)(2,1)S(1)} %shard_map.90), channel_id=1, source_target_pairs={{0,12},{1,13},{2,14},{3,15},{4,8},{5,9},{6,10},{7,11},{8,4},{9,5},... | collective-permute-start | bytes 516104 | tf_op jit(solution)/shard_map/ppermute | solution.py:276
  44.3 0.0 collective-permute-done.4.refs_1_
  44.3 0.5 collective-permute-start.24
  44.8 0.1 collective-permute-start.3
  44.9 1.1 %collective-permute-done.18.refs_2_ = bf16[8,10752]{1,0:T(8,128)(2,1)S(1)} collective-permute-done((bf16[8,10752]{1,0:T(8,128)(2,1)S(1)}, bf16[8,10752]{1,0:T(8,128)(2,1)S(1)}, u32[]{:S(2)}, u32[]{:S(2)}) %collective-permute-start.18) | collective-permute-done | bytes 172064 | tf_op jit(solution)/shard_map/ppermute | solution.py:279
  46.0 0.1 shard_map.84.refs_1_
  46.1 1.2 %collective-permute-start.26 = (bf16[8,10752]{1,0:T(8,128)(2,1)S(1)}, bf16[8,10752]{1,0:T(8,128)(2,1)S(1)}, u32[]{:S(2)}, u32[]{:S(2)}) collective-permute-start(bf16[8,10752]{1,0:T(8,128)(2,1)S(1)} %shard_map.84.refs_1_), channel_id=1, source_target_pairs={{0,8},{1,9},{2,10},{3,11},{4,12},{5,13},{6,14},{7,15},{8,0},{9,1},... | collective-permute-start | bytes 516104 | tf_op jit(solution)/shard_map/ppermute | solution.py:276
  47.3 0.0 collective-permute-done.22.refs_1_
  47.3 0.5 collective-permute-start.19
  47.8 3.9 %collective-permute-done.29.refs_3_ = bf16[8,10752]{1,0:T(8,128)(2,1)S(1)} collective-permute-done((bf16[8,10752]{1,0:T(8,128)(2,1)S(1)}, bf16[8,10752]{1,0:T(8,128)(2,1)S(1)}, u32[]{:S(2)}, u32[]{:S(2)}) %collective-permute-start.29) | collective-permute-done | bytes 172064 | tf_op jit(solution)/shard_map/ppermute | solution.py:276
  51.7 0.0 collective-permute-start.30
  51.7 0.1 shard_map.89
  51.7 4.0 %collective-permute-start.25 = (bf16[8,10752]{1,0:T(8,128)(2,1)S(1)}, bf16[8,10752]{1,0:T(8,128)(2,1)S(1)}, u32[]{:S(2)}, u32[]{:S(2)}) collective-permute-start(bf16[8,10752]{1,0:T(8,128)(2,1)S(1)} %shard_map.89), channel_id=1, source_target_pairs={{0,4},{1,5},{2,6},{3,7},{4,0},{5,1},{6,2},{7,3},{8,12},{9,13},{10,... | collective-permute-start | bytes 516104 | tf_op jit(solution)/shard_map/ppermute | solution.py:276
  55.7 0.0 collective-permute-done.3.refs_1_
  55.7 0.1 shard_map.86.refs_0_
  55.8 3.0 %collective-permute-done.26.refs_2_ = bf16[8,10752]{1,0:T(8,128)(2,1)S(1)} collective-permute-done((bf16[8,10752]{1,0:T(8,128)(2,1)S(1)}, bf16[8,10752]{1,0:T(8,128)(2,1)S(1)}, u32[]{:S(2)}, u32[]{:S(2)}) %collective-permute-start.26) | collective-permute-done | bytes 172064 | tf_op jit(solution)/shard_map/ppermute | solution.py:276
  58.8 3.6 %collective-permute-done.25.refs_1_ = bf16[8,10752]{1,0:T(8,128)(2,1)S(1)} collective-permute-done((bf16[8,10752]{1,0:T(8,128)(2,1)S(1)}, bf16[8,10752]{1,0:T(8,128)(2,1)S(1)}, u32[]{:S(2)}, u32[]{:S(2)}) %collective-permute-start.25) | collective-permute-done | bytes 172064 | tf_op jit(solution)/shard_map/ppermute | solution.py:276
  62.4 1.9 %shard_map.91 = bf16[16,7168]{1,0:T(8,128)(2,1)} custom-call(s32[4]{0:T(128)S(1)} %copy-done.1, s32[2,16]{1,0:T(2,128)S(1)} %bitcast.3, f32[2,16]{1,0:T(2,128)S(1)} %bitcast.4, bf16[8,10752]{1,0:T(8,128)(2,1)S(1)} %shard_map.86.refs_0_, bf16[8,10752]{1,0:T(8,128)(2,1)S(1)} %collective-permute-done.25.refs_1_, ...), custom_call_target="tpu_custom_call" | custom-call | flops 44040192 | bytes 1146880 | tf_op jit(solution)/shard_map/pallas_call | solution.py:237
  (23 shorter events, 0.2 us)
Async XLA Ops:
  1.5 11.1 %collective-permute-start.5 = (bf16[8,10752]{1,0:T(8,128)(2,1)S(1)}, bf16[8,10752]{1,0:T(8,128)(2,1)S(1)}, u32[]{:S(2)}, u32[]{:S(2)}) collective-permute-start(bf16[8,10752]{1,0:T(8,128)(2,1)S(1)} %get-tuple-element.37), channel_id=1, source_target_pairs={{0,12},{1,13},{2,14},{3,15},{4,8},{5,9},{6,10},{7,11},{8,4},{9,5},... | collective-permute-start | bytes 516104 | tf_op jit(solution)/shard_map/ppermute | solution.py:276
  6.6 6.5 %collective-permute-start = (bf16[8,10752]{1,0:T(8,128)(2,1)S(1)}, bf16[8,10752]{1,0:T(8,128)(2,1)S(1)}, u32[]{:S(2)}, u32[]{:S(2)}) collective-permute-start(bf16[8,10752]{1,0:T(8,128)(2,1)S(1)} %get-tuple-element.28.refs_3_.refs_0_), channel_id=1, source_target_pairs={{0,2},{1,3},{2,0},{3,1},{4,6},{5,7},{6,4},{7,5},{8,10},{9,11},{10,... | collective-permute-start | bytes 516104 | tf_op jit(solution)/shard_map/ppermute | solution.py:279
  12.4 5.6 %collective-permute-start.7 = (bf16[8,10752]{1,0:T(8,128)(2,1)S(1)}, bf16[8,10752]{1,0:T(8,128)(2,1)S(1)}, u32[]{:S(2)}, u32[]{:S(2)}) collective-permute-start(bf16[8,10752]{1,0:T(8,128)(2,1)S(1)} %shard_map.78), channel_id=1, source_target_pairs={{0,4},{1,5},{2,6},{3,7},{4,0},{5,1},{6,2},{7,3},{8,12},{9,13},{10,... | collective-permute-start | bytes 516104 | tf_op jit(solution)/shard_map/ppermute | solution.py:276
  12.4 6.0 %collective-permute-start.1 = (bf16[8,10752]{1,0:T(8,128)(2,1)S(1)}, bf16[8,10752]{1,0:T(8,128)(2,1)S(1)}, u32[]{:S(2)}, u32[]{:S(2)}) collective-permute-start(bf16[8,10752]{1,0:T(8,128)(2,1)S(1)} %get-tuple-element.28.refs_3_.refs_0_), channel_id=1, source_target_pairs={{0,1},{1,0},{2,3},{3,2},{4,5},{5,4},{6,7},{7,6},{8,9},{9,8},{10,11... | collective-permute-start | bytes 516104 | tf_op jit(solution)/shard_map/ppermute | solution.py:282
  12.5 6.8 %collective-permute-start.12 = (bf16[8,10752]{1,0:T(8,128)(2,1)S(1)}, bf16[8,10752]{1,0:T(8,128)(2,1)S(1)}, u32[]{:S(2)}, u32[]{:S(2)}) collective-permute-start(bf16[8,10752]{1,0:T(8,128)(2,1)S(1)} %collective-permute-done.5.refs_1_.refs_0_), channel_id=1, source_target_pairs={{0,2},{1,3},{2,0},{3,1},{4,6},{5,7},{6,4},{7,5},{8,10},{9,11},{10,... | collective-permute-start | bytes 516104 | tf_op jit(solution)/shard_map/ppermute | solution.py:279
  13.1 6.2 %collective-permute-start.2 = (bf16[8,10752]{1,0:T(8,128)(2,1)S(1)}, bf16[8,10752]{1,0:T(8,128)(2,1)S(1)}, u32[]{:S(2)}, u32[]{:S(2)}) collective-permute-start(bf16[8,10752]{1,0:T(8,128)(2,1)S(1)} %collective-permute-done.refs_1_.refs_2_), channel_id=1, source_target_pairs={{0,1},{1,0},{2,3},{3,2},{4,5},{5,4},{6,7},{7,6},{8,9},{9,8},{10,11... | collective-permute-start | bytes 516104 | tf_op jit(solution)/shard_map/ppermute | solution.py:282
  13.3 12.4 %collective-permute-start.6 = (bf16[8,10752]{1,0:T(8,128)(2,1)S(1)}, bf16[8,10752]{1,0:T(8,128)(2,1)S(1)}, u32[]{:S(2)}, u32[]{:S(2)}) collective-permute-start(bf16[8,10752]{1,0:T(8,128)(2,1)S(1)} %shard_map.77), channel_id=1, source_target_pairs={{0,8},{1,9},{2,10},{3,11},{4,12},{5,13},{6,14},{7,15},{8,0},{9,1},... | collective-permute-start | bytes 516104 | tf_op jit(solution)/shard_map/ppermute | solution.py:276
  18.0 7.7 %collective-permute-start.8 = (bf16[8,10752]{1,0:T(8,128)(2,1)S(1)}, bf16[8,10752]{1,0:T(8,128)(2,1)S(1)}, u32[]{:S(2)}, u32[]{:S(2)}) collective-permute-start(bf16[8,10752]{1,0:T(8,128)(2,1)S(1)} %collective-permute-done.7.refs_0_), channel_id=1, source_target_pairs={{0,2},{1,3},{2,0},{3,1},{4,6},{5,7},{6,4},{7,5},{8,10},{9,11},{10,... | collective-permute-start | bytes 516104 | tf_op jit(solution)/shard_map/ppermute | solution.py:279
  18.5 7.7 %collective-permute-start.13 = (bf16[8,10752]{1,0:T(8,128)(2,1)S(1)}, bf16[8,10752]{1,0:T(8,128)(2,1)S(1)}, u32[]{:S(2)}, u32[]{:S(2)}) collective-permute-start(bf16[8,10752]{1,0:T(8,128)(2,1)S(1)} %collective-permute-done.5.refs_1_.refs_0_), channel_id=1, source_target_pairs={{0,1},{1,0},{2,3},{3,2},{4,5},{5,4},{6,7},{7,6},{8,9},{9,8},{10,11... | collective-permute-start | bytes 516104 | tf_op jit(solution)/shard_map/ppermute | solution.py:282
  19.3 6.8 %collective-permute-start.14 = (bf16[8,10752]{1,0:T(8,128)(2,1)S(1)}, bf16[8,10752]{1,0:T(8,128)(2,1)S(1)}, u32[]{:S(2)}, u32[]{:S(2)}) collective-permute-start(bf16[8,10752]{1,0:T(8,128)(2,1)S(1)} %collective-permute-done.12.refs_1_), channel_id=1, source_target_pairs={{0,1},{1,0},{2,3},{3,2},{4,5},{5,4},{6,7},{7,6},{8,9},{9,8},{10,11... | collective-permute-start | bytes 516104 | tf_op jit(solution)/shard_map/ppermute | solution.py:282
  25.6 6.2 %collective-permute-start.9 = (bf16[8,10752]{1,0:T(8,128)(2,1)S(1)}, bf16[8,10752]{1,0:T(8,128)(2,1)S(1)}, u32[]{:S(2)}, u32[]{:S(2)}) collective-permute-start(bf16[8,10752]{1,0:T(8,128)(2,1)S(1)} %shard_map.79.refs_0_), channel_id=1, source_target_pairs={{0,2},{1,3},{2,0},{3,1},{4,6},{5,7},{6,4},{7,5},{8,10},{9,11},{10,... | collective-permute-start | bytes 516104 | tf_op jit(solution)/shard_map/ppermute | solution.py:279
  28.2 4.1 %collective-permute-start.15 = (bf16[8,10752]{1,0:T(8,128)(2,1)S(1)}, bf16[8,10752]{1,0:T(8,128)(2,1)S(1)}, u32[]{:S(2)}, u32[]{:S(2)}) collective-permute-start(bf16[8,10752]{1,0:T(8,128)(2,1)S(1)} %get-tuple-element.40), channel_id=1, source_target_pairs={{0,1},{1,0},{2,3},{3,2},{4,5},{5,4},{6,7},{7,6},{8,9},{9,8},{10,11... | collective-permute-start | bytes 516104 | tf_op jit(solution)/shard_map/ppermute | solution.py:282
  28.3 4.1 %collective-permute-start.10 = (bf16[8,10752]{1,0:T(8,128)(2,1)S(1)}, bf16[8,10752]{1,0:T(8,128)(2,1)S(1)}, u32[]{:S(2)}, u32[]{:S(2)}) collective-permute-start(bf16[8,10752]{1,0:T(8,128)(2,1)S(1)} %shard_map.79.refs_0_), channel_id=1, source_target_pairs={{0,1},{1,0},{2,3},{3,2},{4,5},{5,4},{6,7},{7,6},{8,9},{9,8},{10,11... | collective-permute-start | bytes 516104 | tf_op jit(solution)/shard_map/ppermute | solution.py:282
  31.8 1.4 %collective-permute-start.11 = (bf16[8,10752]{1,0:T(8,128)(2,1)S(1)}, bf16[8,10752]{1,0:T(8,128)(2,1)S(1)}, u32[]{:S(2)}, u32[]{:S(2)}) collective-permute-start(bf16[8,10752]{1,0:T(8,128)(2,1)S(1)} %collective-permute-done.9.refs_1_), channel_id=1, source_target_pairs={{0,1},{1,0},{2,3},{3,2},{4,5},{5,4},{6,7},{7,6},{8,9},{9,8},{10,11... | collective-permute-start | bytes 516104 | tf_op jit(solution)/shard_map/ppermute | solution.py:282
  31.8 4.3 %collective-permute-start.20 = (bf16[8,10752]{1,0:T(8,128)(2,1)S(1)}, bf16[8,10752]{1,0:T(8,128)(2,1)S(1)}, u32[]{:S(2)}, u32[]{:S(2)}) collective-permute-start(bf16[8,10752]{1,0:T(8,128)(2,1)S(1)} %collective-permute-done.7.refs_0_), channel_id=1, source_target_pairs={{0,1},{1,0},{2,3},{3,2},{4,5},{5,4},{6,7},{7,6},{8,9},{9,8},{10,11... | collective-permute-start | bytes 516104 | tf_op jit(solution)/shard_map/ppermute | solution.py:282
  32.3 3.8 %collective-permute-start.21 = (bf16[8,10752]{1,0:T(8,128)(2,1)S(1)}, bf16[8,10752]{1,0:T(8,128)(2,1)S(1)}, u32[]{:S(2)}, u32[]{:S(2)}) collective-permute-start(bf16[8,10752]{1,0:T(8,128)(2,1)S(1)} %collective-permute-done.8.refs_2_.refs_1_), channel_id=1, source_target_pairs={{0,1},{1,0},{2,3},{3,2},{4,5},{5,4},{6,7},{7,6},{8,9},{9,8},{10,11... | collective-permute-start | bytes 516104 | tf_op jit(solution)/shard_map/ppermute | solution.py:282
  35.3 3.6 %collective-permute-start.17 = (bf16[8,10752]{1,0:T(8,128)(2,1)S(1)}, bf16[8,10752]{1,0:T(8,128)(2,1)S(1)}, u32[]{:S(2)}, u32[]{:S(2)}) collective-permute-start(bf16[8,10752]{1,0:T(8,128)(2,1)S(1)} %get-tuple-element.44.refs_7_), channel_id=1, source_target_pairs={{0,1},{1,0},{2,3},{3,2},{4,5},{5,4},{6,7},{7,6},{8,9},{9,8},{10,11... | collective-permute-start | bytes 516104 | tf_op jit(solution)/shard_map/ppermute | solution.py:282
  35.5 3.5 %collective-permute-start.27 = (bf16[8,10752]{1,0:T(8,128)(2,1)S(1)}, bf16[8,10752]{1,0:T(8,128)(2,1)S(1)}, u32[]{:S(2)}, u32[]{:S(2)}) collective-permute-start(bf16[8,10752]{1,0:T(8,128)(2,1)S(1)} %get-tuple-element.50), channel_id=1, source_target_pairs={{0,1},{1,0},{2,3},{3,2},{4,5},{5,4},{6,7},{7,6},{8,9},{9,8},{10,11... | collective-permute-start | bytes 516104 | tf_op jit(solution)/shard_map/ppermute | solution.py:282
  35.9 6.6 %collective-permute-start.28 = (bf16[8,10752]{1,0:T(8,128)(2,1)S(1)}, bf16[8,10752]{1,0:T(8,128)(2,1)S(1)}, u32[]{:S(2)}, u32[]{:S(2)}) collective-permute-start(bf16[8,10752]{1,0:T(8,128)(2,1)S(1)} %shard_map.81.refs_7_), channel_id=1, source_target_pairs={{0,2},{1,3},{2,0},{3,1},{4,6},{5,7},{6,4},{7,5},{8,10},{9,11},{10,... | collective-permute-start | bytes 516104 | tf_op jit(solution)/shard_map/ppermute | solution.py:279
  38.3 24.1 %copy-start = (s32[16,2]{0,1:T(2,128)S(1)}, s32[16,2]{0,1:T(2,128)}, u32[]{:S(2)}) copy-start(s32[16,2]{0,1:T(2,128)} %param.8) | copy-start | bytes 388
  38.3 24.1 %copy-start.1 = (s32[4]{0:T(128)S(1)}, s32[4]{0:T(128)}, u32[]{:S(2)}) copy-start(s32[4]{0:T(128)} %placement_ref.3) | copy-start | bytes 52
  38.3 24.1 %copy-start.2 = (f32[16,2]{0,1:T(2,128)S(1)}, f32[16,2]{0,1:T(2,128)}, u32[]{:S(2)}) copy-start(f32[16,2]{0,1:T(2,128)} %param.9) | copy-start | bytes 388
  38.3 4.2 %collective-permute-start.23 = (bf16[8,10752]{1,0:T(8,128)(2,1)S(1)}, bf16[8,10752]{1,0:T(8,128)(2,1)S(1)}, u32[]{:S(2)}, u32[]{:S(2)}) collective-permute-start(bf16[8,10752]{1,0:T(8,128)(2,1)S(1)} %get-tuple-element.48), channel_id=1, source_target_pairs={{0,1},{1,0},{2,3},{3,2},{4,5},{5,4},{6,7},{7,6},{8,9},{9,8},{10,11... | collective-permute-start | bytes 516104 | tf_op jit(solution)/shard_map/ppermute | solution.py:282
  38.4 5.9 %collective-permute-start.4 = (bf16[8,10752]{1,0:T(8,128)(2,1)S(1)}, bf16[8,10752]{1,0:T(8,128)(2,1)S(1)}, u32[]{:S(2)}, u32[]{:S(2)}) collective-permute-start(bf16[8,10752]{1,0:T(8,128)(2,1)S(1)} %get-tuple-element.35.refs_1_), channel_id=1, source_target_pairs={{0,1},{1,0},{2,3},{3,2},{4,5},{5,4},{6,7},{7,6},{8,9},{9,8},{10,11... | collective-permute-start | bytes 516104 | tf_op jit(solution)/shard_map/ppermute | solution.py:282
  38.9 5.9 %collective-permute-start.16 = (bf16[8,10752]{1,0:T(8,128)(2,1)S(1)}, bf16[8,10752]{1,0:T(8,128)(2,1)S(1)}, u32[]{:S(2)}, u32[]{:S(2)}) collective-permute-start(bf16[8,10752]{1,0:T(8,128)(2,1)S(1)} %get-tuple-element.42), channel_id=1, source_target_pairs={{0,1},{1,0},{2,3},{3,2},{4,5},{5,4},{6,7},{7,6},{8,9},{9,8},{10,11... | collective-permute-start | bytes 516104 | tf_op jit(solution)/shard_map/ppermute | solution.py:282
  39.0 7.0 %collective-permute-start.18 = (bf16[8,10752]{1,0:T(8,128)(2,1)S(1)}, bf16[8,10752]{1,0:T(8,128)(2,1)S(1)}, u32[]{:S(2)}, u32[]{:S(2)}) collective-permute-start(bf16[8,10752]{1,0:T(8,128)(2,1)S(1)} %shard_map.83), channel_id=1, source_target_pairs={{0,2},{1,3},{2,0},{3,1},{4,6},{5,7},{6,4},{7,5},{8,10},{9,11},{10,... | collective-permute-start | bytes 516104 | tf_op jit(solution)/shard_map/ppermute | solution.py:279
  42.5 4.9 %collective-permute-start.22 = (bf16[8,10752]{1,0:T(8,128)(2,1)S(1)}, bf16[8,10752]{1,0:T(8,128)(2,1)S(1)}, u32[]{:S(2)}, u32[]{:S(2)}) collective-permute-start(bf16[8,10752]{1,0:T(8,128)(2,1)S(1)} %get-tuple-element.46), channel_id=1, source_target_pairs={{0,1},{1,0},{2,3},{3,2},{4,5},{5,4},{6,7},{7,6},{8,9},{9,8},{10,11... | collective-permute-start | bytes 516104 | tf_op jit(solution)/shard_map/ppermute | solution.py:282
  42.5 9.1 %collective-permute-start.29 = (bf16[8,10752]{1,0:T(8,128)(2,1)S(1)}, bf16[8,10752]{1,0:T(8,128)(2,1)S(1)}, u32[]{:S(2)}, u32[]{:S(2)}) collective-permute-start(bf16[8,10752]{1,0:T(8,128)(2,1)S(1)} %shard_map.90), channel_id=1, source_target_pairs={{0,12},{1,13},{2,14},{3,15},{4,8},{5,9},{6,10},{7,11},{8,4},{9,5},... | collective-permute-start | bytes 516104 | tf_op jit(solution)/shard_map/ppermute | solution.py:276
  44.3 7.4 %collective-permute-start.24 = (bf16[8,10752]{1,0:T(8,128)(2,1)S(1)}, bf16[8,10752]{1,0:T(8,128)(2,1)S(1)}, u32[]{:S(2)}, u32[]{:S(2)}) collective-permute-start(bf16[8,10752]{1,0:T(8,128)(2,1)S(1)} %shard_map.88), channel_id=1, source_target_pairs={{0,2},{1,3},{2,0},{3,1},{4,6},{5,7},{6,4},{7,5},{8,10},{9,11},{10,... | collective-permute-start | bytes 516104 | tf_op jit(solution)/shard_map/ppermute | solution.py:279
  44.8 10.9 %collective-permute-start.3 = (bf16[8,10752]{1,0:T(8,128)(2,1)S(1)}, bf16[8,10752]{1,0:T(8,128)(2,1)S(1)}, u32[]{:S(2)}, u32[]{:S(2)}) collective-permute-start(bf16[8,10752]{1,0:T(8,128)(2,1)S(1)} %get-tuple-element.33), channel_id=1, source_target_pairs={{0,1},{1,0},{2,3},{3,2},{4,5},{5,4},{6,7},{7,6},{8,9},{9,8},{10,11... | collective-permute-start | bytes 516104 | tf_op jit(solution)/shard_map/ppermute | solution.py:282
  46.1 12.7 %collective-permute-start.26 = (bf16[8,10752]{1,0:T(8,128)(2,1)S(1)}, bf16[8,10752]{1,0:T(8,128)(2,1)S(1)}, u32[]{:S(2)}, u32[]{:S(2)}) collective-permute-start(bf16[8,10752]{1,0:T(8,128)(2,1)S(1)} %shard_map.84.refs_1_), channel_id=1, source_target_pairs={{0,8},{1,9},{2,10},{3,11},{4,12},{5,13},{6,14},{7,15},{8,0},{9,1},... | collective-permute-start | bytes 516104 | tf_op jit(solution)/shard_map/ppermute | solution.py:276
  47.3 8.4 %collective-permute-start.19 = (bf16[8,10752]{1,0:T(8,128)(2,1)S(1)}, bf16[8,10752]{1,0:T(8,128)(2,1)S(1)}, u32[]{:S(2)}, u32[]{:S(2)}) collective-permute-start(bf16[8,10752]{1,0:T(8,128)(2,1)S(1)} %shard_map.85), channel_id=1, source_target_pairs={{0,2},{1,3},{2,0},{3,1},{4,6},{5,7},{6,4},{7,5},{8,10},{9,11},{10,... | collective-permute-start | bytes 516104 | tf_op jit(solution)/shard_map/ppermute | solution.py:279
  51.7 4.1 %collective-permute-start.30 = (bf16[8,10752]{1,0:T(8,128)(2,1)S(1)}, bf16[8,10752]{1,0:T(8,128)(2,1)S(1)}, u32[]{:S(2)}, u32[]{:S(2)}) collective-permute-start(bf16[8,10752]{1,0:T(8,128)(2,1)S(1)} %collective-permute-done.29.refs_3_), channel_id=1, source_target_pairs={{0,1},{1,0},{2,3},{3,2},{4,5},{5,4},{6,7},{7,6},{8,9},{9,8},{10,11... | collective-permute-start | bytes 516104 | tf_op jit(solution)/shard_map/ppermute | solution.py:282
  51.7 10.6 %collective-permute-start.25 = (bf16[8,10752]{1,0:T(8,128)(2,1)S(1)}, bf16[8,10752]{1,0:T(8,128)(2,1)S(1)}, u32[]{:S(2)}, u32[]{:S(2)}) collective-permute-start(bf16[8,10752]{1,0:T(8,128)(2,1)S(1)} %shard_map.89), channel_id=1, source_target_pairs={{0,4},{1,5},{2,6},{3,7},{4,0},{5,1},{6,2},{7,3},{8,12},{9,13},{10,... | collective-permute-start | bytes 516104 | tf_op jit(solution)/shard_map/ppermute | solution.py:276

commit v9 on v8

--- a/solution.py
+++ b/solution.py
@@ -12,6 +12,7 @@
 SMEM = pl.BlockSpec(memory_space=pltpu.SMEM)
 ANYWHERE = pl.BlockSpec(memory_space=pl.ANY)
 LOADS = 4
+SHARE = 95
 N1, N2, N3, N4 = 30,30,30,30
 NO_COST = pl.CostEstimate(flops=0, bytes_accessed=0, transcendentals=0)
 
@@ -93,6 +94,22 @@
     pass
 
 
+def clear(*refs):
+    refs[-1][...] = jnp.zeros_like(refs[-1])
+
+
+def token(after):
+    rows, width = after.shape
+    return pl.pallas_call(
+        clear,
+        out_shape=pltpu.VMEM((rows, width * SHARE // 12800 * 128), after.dtype),
+        in_specs=[ANYWHERE],
+        out_specs=VMEM,
+        compiler_params=pltpu.CompilerParams(vmem_limit_bytes=VMEM_BYTES),
+        cost_estimate=NO_COST,
+    )(after)
+
+
 def when(value, after):
     if not after:
         return value
@@ -133,18 +150,39 @@
     )(*[pltpu.with_memory_space_constraint(w, pltpu.HBM) for w in weights], after)
 
 
+def split_kernel(whole_ref, *part_refs):
+    width = part_refs[0].shape[1]
+    for i, part_ref in enumerate(part_refs):
+        part_ref[...] = whole_ref[:, i * width : (i + 1) * width]
+
+
+def split(value):
+    rows, width = value.shape
+    return pl.pallas_call(
+        split_kernel,
+        out_shape=[pltpu.VMEM((rows, width // 3), value.dtype)] * 3,
+        in_specs=[VMEM],
+        out_specs=[VMEM] * 3,
+        compiler_params=pltpu.CompilerParams(vmem_limit_bytes=VMEM_BYTES),
+        cost_estimate=NO_COST,
+    )(in_vmem(value))
+
+
 def experts_kernel(*refs):
-    straight_ref, across_ref, straight_other_ref, across_other_ref = refs[:4]
-    gate_ref, up_ref, down_ref = refs[4:7]
-    out_refs = refs[-4:]
-    pieces = (straight_ref, across_ref, straight_other_ref, across_other_ref)
+    whole, parts = refs[:3], refs[3:6]
+    gate_ref, up_ref, down_ref = refs[6:9]
+    out_whole, out_parts = refs[-6:-3], refs[-3:]
     width, hid = gate_ref.shape
     middle = width // 2
-    height = straight_ref.shape[0]
-    total = len(pieces) * height
-    rest = jnp.concatenate([p[:, width:] for p in pieces], axis=0)
-    left = jnp.concatenate([p[:, :middle] for p in pieces] + [rest], axis=0)
-    right = jnp.concatenate([p[:, middle:width] for p in pieces] + [rest], axis=0)
+    height = whole[0].shape[0]
+    total = 4 * height
+
+    def third(i):
+        return [p[:, i * middle : (i + 1) * middle] for p in whole] + [parts[i][...]]
+
+    rest = third(2)
+    left = jnp.concatenate(third(0) + rest, axis=0)
+    right = jnp.concatenate(third(1) + rest, axis=0)
     upper = lax.broadcasted_iota(jnp.int32, (total, 1), 0) % height < height // 2
     shift = height // 2
 
@@ -160,37 +198,35 @@
     gate_rows, up_rows = whole_rows(gate_ref), whole_rows(up_ref)
     hidden = (jax.nn.silu(gate_rows) * up_rows).astype(jnp.bfloat16)
 
-    def store(start, values):
+    def store(i, begin, values):
         values = values.astype(jnp.bfloat16)
-        stop = start + values.shape[1]
-        for i, out_ref in enumerate(out_refs):
-            out_ref[:, start:stop] = values[i * height : (i + 1) * height]
+        stop = begin + values.shape[1]
+        for p, out_ref in enumerate(out_whole):
+            out_ref[:, i * middle + begin : i * middle + stop] = values[p * height : (p + 1) * height]
+        out_parts[i][:, begin:stop] = values[3 * height :]
 
     step = middle // 4
-    for i in range(4):
-        begin = i * step
+    for j in range(4):
+        begin = j * step
         a = product(hidden, down_ref[:, begin : begin + step])
         b = product(hidden, down_ref[:, middle + begin : middle + begin + step])
-        store(begin, a[:total])
-        store(middle + begin, b[:total])
-        store(width + begin, jnp.where(upper, a[total:], b[total:]))
-
-
-def run_experts(pieces, weights, after):
-    width, hid = weights[0].shape
-    height, packed_width = pieces[0].shape
-    rows = len(pieces) * height
-    shape = pltpu.VMEM((height, packed_width), jnp.bfloat16)
-    operands = [in_vmem(p) for p in pieces] + [in_vmem(w) for w in weights]
+        store(0, begin, a[:total])
+        store(1, begin, b[:total])
+        store(2, begin, jnp.where(upper, a[total:], b[total:]))
+
+
+def run_experts(whole, parts, weights, after):
+    rows, width = whole[0].shape
+    shapes = [pltpu.VMEM((rows, width), jnp.bfloat16)] * 3
+    shapes += [pltpu.VMEM((rows, width // 3), jnp.bfloat16)] * 3
+    operands = [in_vmem(value) for value in [*whole, *parts, *weights]]
     return pl.pallas_call(
         experts_kernel,
-        out_shape=[shape] * len(pieces),
-        in_specs=[VMEM] * 7 + [ANYWHERE] * len(after),
-        out_specs=[VMEM] * len(pieces),
-        compiler_params=pltpu.CompilerParams(vmem_limit_bytes=VMEM_BYTES),
-        cost_estimate=pl.CostEstimate(
-            flops=0, bytes_accessed=4 * width * hid, transcendentals=0
-        ),
+        out_shape=shapes,
+        in_specs=[VMEM] * len(operands) + [ANYWHERE] * len(after),
+        out_specs=[VMEM] * len(shapes),
+        compiler_params=pltpu.CompilerParams(vmem_limit_bytes=VMEM_BYTES),
+        cost_estimate=NO_COST,
     )(*operands, *after)
 
 
@@ -211,7 +247,6 @@
         terms.append(jnp.where(named & (slot == wanted), weight, 0.0))
     term = jnp.concatenate(terms, axis=0)
     row = lax.broadcasted_iota(jnp.int32, term.shape, 0) % rows
-    rest = jnp.concatenate([r[:, width:] for r in results], axis=0)
     for side in range(2):
         first = half + side * quarter
         mine = jnp.where((row < half) | ((row >= first) & (row < first + quarter)), term, 0.0)
@@ -223,7 +258,7 @@
         pieces = []
         for r in results:
             pieces += [r[:, side * middle : (side + 1) * middle], r[:, width:]]
-        rhs = jnp.concatenate(pieces, axis=0)
+        rhs = jnp.concatenate([p.astype(jnp.bfloat16) for p in pieces], axis=0)
         value = lax.dot_general(
             lhs, rhs, (((0,), (0,)), ((), ())), preferred_element_type=jnp.float32
         )
@@ -255,9 +290,17 @@
     refs[-1][...] = total.astype(refs[-1].dtype)
 
 
-def add(*values):
-    return pl.pallas_call(
-        add_kernel,
+def add_parts_kernel(whole_ref, *refs):
+    width = refs[0].shape[1]
+    for i, part_ref in enumerate(refs[:-1]):
+        columns = slice(i * width, (i + 1) * width)
+        total = whole_ref[:, columns].astype(jnp.float32) + part_ref[...].astype(jnp.float32)
+        refs[-1][:, columns] = total.astype(refs[-1].dtype)
+
+
+def add(kernel, *values):
+    return pl.pallas_call(
+        kernel,
         out_shape=pltpu.VMEM(values[0].shape, values[0].dtype),
         in_specs=[VMEM] * len(values),
         out_specs=VMEM,
@@ -288,16 +331,22 @@
     both, home, kept, sent = {}, {}, {}, {}
 
     def compute(k, after):
-        theirs = [along_core(straight[k]), along_core(across[k])]
-        out = run_experts([straight[k], across[k]] + theirs, weights, after)
+        whole = [straight[k], across[k], along_core(straight[k])]
+        parts = [along_core(part) for part in split(across[k])]
+        out = run_experts(whole, parts, weights, after)
         sent[k] = out[3]
-        both[k] = add(out[1], along_core(out[3]))
+        both[k] = add(add_parts_kernel, out[1], *[along_core(part) for part in out[3:]])
         kept[k] = out[0], along_core(out[2])
 
     def go_home(k, after):
         back = along_y(both[k] if k else when(both[k], after))
-        home[k] = add(*kept[k], back)
-        results[k] = along_z(when(home[k], after), k) if k else home[k]
+        early = k in [group[0] for group in groups[:-1]]
+        home[k] = add(add_kernel, *kept[k], back)
+        results[k] = along_z(home[k], k) if k else home[k]
+        if early:
+            marks.append(along_core(token(results[k])))
+        if k == last:
+            results[k] = results[k].astype(jnp.float32)
 
     buckets = list(pack(placement, ids, tokens, n_blocks, parts))
     weights = load((gate_weight, up_weight, down_weight), buckets[0])
@@ -320,7 +369,6 @@
             across[first] = along_y(straight[first])
             compute(first, [both[previous]])
             go_home(first, [])
-            marks.append(along_core(results[previous]))
         if second:
             compute(second, [sent[first]])
             go_home(second, [])

time: 64.4 us -> 64.8 us (level)
  starting transfers between devices: 24.5 us -> 31.5 us
  waiting for transfers between devices: 23.3 us -> 16.4 us
    ppermute x6, waiting for transfers between devices: 15.8 us -> 9.97 us  [along_z(): return lax.ppermute(value, 'node', pairs)]
    ppermute x17 -> x33, starting transfers between devices: 2.62 us -> 8.26 us  [along_core(): return lax.ppermute(value, 'node', [(i, i ^ 1) for i in range(devices)])]
    ppermute x8, starting transfers between devices: 6.13 us -> 9.44 us  [along_y(): return lax.ppermute(value, 'node', [(i, i ^ 2) for i in range(devices)])]
    ppermute x8, waiting for transfers between devices: 6.62 us -> 3.37 us  [along_y(): return lax.ppermute(value, 'node', [(i, i ^ 2) for i in range(devices)])]
    ppermute x17 -> x33, waiting for transfers between devices: 0.87 us -> 3.07 us  [along_core(): return lax.ppermute(value, 'node', [(i, i ^ 1) for i in range(devices)])]
    ppermute x6, starting transfers between devices: 15.7 us -> 13.8 us  [along_z(): return lax.ppermute(value, 'node', pairs)]
    pallas_call x12 -> x17, Pallas kernels: 8.72 us -> 8.78 us  [the longest x4 8.28 us: run_experts(): pl.pallas_call(experts_kernel, out_shape=shapes, in_specs=[VMEM] * len(op...]
  transfers between devices with their start and end apart: 31 -> 47, of which waited for: 10 -> 12; matrix products, arithmetic and copies ran while one was open for 0% -> 0% of each run, Pallas kernels for 20% -> 20%
where the time goes in v9:
time: 64.8 us; the launch traced here: 64.6 us
  starting transfers between devices  31.5 us (49%)
  waiting for transfers between devices  16.4 us (25%)
  Pallas kernels  16.3 us (25%)
    ppermute x6, starting transfers between devices, along_z(): return lax.ppermute(value, 'node', pairs)  13.8 us
    ppermute x6, waiting for transfers between devices, along_z(): return lax.ppermute(value, 'node', pairs)  9.97 us
    ppermute x8, starting transfers between devices, along_y(): return lax.ppermute(value, 'node', [(i, i ^ 2) for i in range(devices)])  9.44 us
    pallas_call x4, Pallas kernels, run_experts(): pl.pallas_call(experts_kernel, out_shape=shapes, in_specs=[VMEM] * len(op...  8.28 us
    ppermute x33, starting transfers between devices, along_core(): return lax.ppermute(value, 'node', [(i, i ^ 1) for i in range(devices)])  8.26 us
    pallas_call x1, Pallas kernels, load(): pl.pallas_call(load_kernel, out_shape=[pltpu.VMEM(w.shape, w.dtype) for w...  4.24 us
    ppermute x8, waiting for transfers between devices, along_y(): return lax.ppermute(value, 'node', [(i, i ^ 2) for i in range(devices)])  3.37 us
    ppermute x33, waiting for transfers between devices, along_core(): return lax.ppermute(value, 'node', [(i, i ^ 1) for i in range(devices)])  3.07 us
  transfers between devices with their start and end apart: 47, of which 12 were waited for; matrix products, arithmetic and copies ran while one was open for 0% of the time, Pallas kernels for 20%

profile of v9, /device:TPU:0, one launch (start us, length us, event | category | flops | bytes accessed | tf_op | source)
XLA Modules:
  0.0 64.6 jit_solution(5572064654140772216)
XLA Ops:
  0.0 1.5 %shard_map.73 = (bf16[8,10752]{1,0:T(8,128)(2,1)S(1)}, bf16[8,10752]{1,0:T(8,128)(2,1)S(1)}, bf16[8,10752]{1,0:T(8,128)(2,1)S(1)}, bf16[8,10752]{1,0:T(8,128)(2,1)S(1)}) custom-call(s32[4]{0:T(128)} %placement_ref.3, s32[2,16]{1,0:T(2,128)} %bitcast.2, bf16[16,7168]{1,0:T(8,128)(2,1)} %tokens_ref.1), custom_call_target="tpu_custom_call" | custom-call | tf_op jit(solution)/shard_map/pallas_call | solution.py:83
  1.5 3.0 %collective-permute-start = (bf16[8,10752]{1,0:T(8,128)(2,1)S(1)}, bf16[8,10752]{1,0:T(8,128)(2,1)S(1)}, u32[]{:S(2)}, u32[]{:S(2)}) collective-permute-start(bf16[8,10752]{1,0:T(8,128)(2,1)S(1)} %get-tuple-element.48.refs_3_.refs_0_), channel_id=1, source_target_pairs={{0,2},{1,3},{2,0},{3,1},{4,6},{5,7},{6,4},{7,5},{8,10},{9,11},{10,... | collective-permute-start | bytes 516104 | tf_op jit(solution)/shard_map/ppermute | solution.py:322
  4.5 3.6 %collective-permute-start.9 = (bf16[8,10752]{1,0:T(8,128)(2,1)S(1)}, bf16[8,10752]{1,0:T(8,128)(2,1)S(1)}, u32[]{:S(2)}, u32[]{:S(2)}) collective-permute-start(bf16[8,10752]{1,0:T(8,128)(2,1)S(1)} %get-tuple-element.62), channel_id=1, source_target_pairs={{0,12},{1,13},{2,14},{3,15},{4,8},{5,9},{6,10},{7,11},{8,4},{9,5},... | collective-permute-start | bytes 516104 | tf_op jit(solution)/shard_map/ppermute | solution.py:319
  8.1 4.2 %shard_map.75 = (bf16[7168,256]{1,0:T(8,128)(2,1)S(1)}, bf16[7168,256]{1,0:T(8,128)(2,1)S(1)}, bf16[256,7168]{1,0:T(8,128)(2,1)S(1)}) custom-call(bf16[7168,256]{1,0:T(8,128)(2,1)} %refs_0_.1, bf16[7168,256]{1,0:T(8,128)(2,1)} %refs_1_.1, bf16[256,7168]{1,0:T(8,128)(2,1)} %refs_2_.1, bf16[8,10752]{1,0:T(8,128)(2,1)S(1)} %get-tuple-element.48.refs_3_.refs_0_), custom_call_target="tpu_custom_call" | custom-call | tf_op jit(solution)/shard_map/pallas_call | solution.py:142
  12.4 0.1 collective-permute-start.11
  12.4 0.1 collective-permute-start.1
  12.5 0.5 collective-permute-start.2
  13.1 3.5 %collective-permute-start.10 = (bf16[8,10752]{1,0:T(8,128)(2,1)S(1)}, bf16[8,10752]{1,0:T(8,128)(2,1)S(1)}, u32[]{:S(2)}, u32[]{:S(2)}) collective-permute-start(bf16[8,10752]{1,0:T(8,128)(2,1)S(1)} %shard_map.78), channel_id=1, source_target_pairs={{0,8},{1,9},{2,10},{3,11},{4,12},{5,13},{6,14},{7,15},{8,0},{9,1},... | collective-permute-start | bytes 516104 | tf_op jit(solution)/shard_map/ppermute | solution.py:319
  16.6 2.8 %collective-permute-done.11.refs_0_ = bf16[8,10752]{1,0:T(8,128)(2,1)S(1)} collective-permute-done((bf16[8,10752]{1,0:T(8,128)(2,1)S(1)}, bf16[8,10752]{1,0:T(8,128)(2,1)S(1)}, u32[]{:S(2)}, u32[]{:S(2)}) %collective-permute-start.11) | collective-permute-done | bytes 172064 | tf_op jit(solution)/shard_map/ppermute | solution.py:319
  19.4 0.5 collective-permute-start.12
  19.9 1.5 %collective-permute-start.18 = (bf16[8,10752]{1,0:T(8,128)(2,1)S(1)}, bf16[8,10752]{1,0:T(8,128)(2,1)S(1)}, u32[]{:S(2)}, u32[]{:S(2)}) collective-permute-start(bf16[8,10752]{1,0:T(8,128)(2,1)S(1)} %collective-permute-done.9.refs_1_.refs_0_), channel_id=1, source_target_pairs={{0,2},{1,3},{2,0},{3,1},{4,6},{5,7},{6,4},{7,5},{8,10},{9,11},{10,... | collective-permute-start | bytes 516104 | tf_op jit(solution)/shard_map/ppermute | solution.py:322
  21.5 0.5 collective-permute-start.3
  22.0 1.0 %collective-permute-done.3.refs_4_ = bf16[8,3584]{1,0:T(8,128)(2,1)S(1)} collective-permute-done((bf16[8,3584]{1,0:T(8,128)(2,1)S(1)}, bf16[8,3584]{1,0:T(8,128)(2,1)S(1)}, u32[]{:S(2)}, u32[]{:S(2)}) %collective-permute-start.3) | collective-permute-done | bytes 57376 | tf_op jit(solution)/shard_map/ppermute | solution.py:325
  22.9 0.3 collective-permute-start.4
  23.2 1.0 %collective-permute-done.4.refs_5_ = bf16[8,3584]{1,0:T(8,128)(2,1)S(1)} collective-permute-done((bf16[8,3584]{1,0:T(8,128)(2,1)S(1)}, bf16[8,3584]{1,0:T(8,128)(2,1)S(1)}, u32[]{:S(2)}, u32[]{:S(2)}) %collective-permute-start.4) | collective-permute-done | bytes 57376 | tf_op jit(solution)/shard_map/ppermute | solution.py:325
  24.2 2.1 %shard_map.76 = (bf16[8,10752]{1,0:T(8,128)(2,1)S(1)}, bf16[8,10752]{1,0:T(8,128)(2,1)S(1)}, bf16[8,10752]{1,0:T(8,128)(2,1)S(1)}, bf16[8,3584]{1,0:T(8,128)(2,1...) custom-call(bf16[8,10752]{1,0:T(8,128)(2,1)S(1)} %get-tuple-element.48.refs_3_.refs_0_, ...), custom_call_target="tpu_custom_call" | custom-call | tf_op jit(solution)/shard_map/pallas_call | solution.py:223
  26.3 0.6 collective-permute-start.13
  26.9 0.1 collective-permute-start.20
  27.0 0.5 collective-permute-start.32
  27.5 0.1 collective-permute-start.21
  27.5 0.4 collective-permute-start.22
  28.0 0.2 collective-permute-done.20.refs_3_
  28.2 0.2 collective-permute-start.14
  28.3 0.4 collective-permute-done.21.refs_4_
  28.7 0.2 collective-permute-start.6
  28.9 0.3 collective-permute-start.7
  29.2 2.1 %shard_map.83 = (bf16[8,10752]{1,0:T(8,128)(2,1)S(1)}, bf16[8,10752]{1,0:T(8,128)(2,1)S(1)}, bf16[8,10752]{1,0:T(8,128)(2,1)S(1)}, bf16[8,3584]{1,0:T(8,128)(2,1...) custom-call(bf16[8,10752]{1,0:T(8,128)(2,1)S(1)} %collective-permute-done.9.refs_1_.refs_0_, ...), custom_call_target="tpu_custom_call" | custom-call | tf_op jit(solution)/shard_map/pallas_call | solution.py:223
  31.3 0.3 collective-permute-start.23
  31.6 0.3 collective-permute-start.24
  31.9 1.0 %collective-permute-done.13.whole_ref.refs_1_ = bf16[8,10752]{1,0:T(8,128)(2,1)S(1)} collective-permute-done((bf16[8,10752]{1,0:T(8,128)(2,1)S(1)}, bf16[8,10752]{1,0:T(8,128)(2,1)S(1)}, u32[]{:S(2)}, u32[]{:S(2)}) %collective-permute-start.13) | collective-permute-done | bytes 172064 | tf_op jit(solution)/shard_map/ppermute | solution.py:322
  32.9 0.6 collective-permute-start.15
  33.5 0.1 collective-permute-start.16
  33.6 0.4 collective-permute-start.17
  34.0 0.1 collective-permute-done.25.refs_2_
  34.1 0.2 collective-permute-start.33
  34.3 0.4 collective-permute-start.34
  34.7 0.2 collective-permute-start.35
  34.8 0.4 collective-permute-start.43
  35.2 0.6 %collective-permute-start.44 = (bf16[8,10752]{1,0:T(8,128)(2,1)S(1)}, bf16[8,10752]{1,0:T(8,128)(2,1)S(1)}, u32[]{:S(2)}, u32[]{:S(2)}) collective-permute-start(bf16[8,10752]{1,0:T(8,128)(2,1)S(1)} %shard_map.84.refs_9_), channel_id=1, source_target_pairs={{0,2},{1,3},{2,0},{3,1},{4,6},{5,7},{6,4},{7,5},{8,10},{9,11},{10,... | collective-permute-start | bytes 516104 | tf_op jit(solution)/shard_map/ppermute | solution.py:322
  35.9 2.1 %shard_map.85 = (bf16[8,10752]{1,0:T(8,128)(2,1)S(1)}, bf16[8,10752]{1,0:T(8,128)(2,1)S(1)}, bf16[8,10752]{1,0:T(8,128)(2,1)S(1)}, bf16[8,3584]{1,0:T(8,128)(2,1...) custom-call(bf16[8,10752]{1,0:T(8,128)(2,1)S(1)} %shard_map.80.refs_0_, ...), custom_call_target="tpu_custom_call" | custom-call | tf_op jit(solution)/shard_map/pallas_call | solution.py:223
  38.0 0.1 collective-permute-start.27
  38.1 0.5 collective-permute-start.28
  38.5 0.1 collective-permute-start.29
  38.6 2.1 %shard_map.91 = (bf16[8,10752]{1,0:T(8,128)(2,1)S(1)}, bf16[8,10752]{1,0:T(8,128)(2,1)S(1)}, bf16[8,10752]{1,0:T(8,128)(2,1)S(1)}, bf16[8,3584]{1,0:T(8,128)(2,1...) custom-call(bf16[8,10752]{1,0:T(8,128)(2,1)S(1)} %collective-permute-done.11.refs_0_, ...), custom_call_target="tpu_custom_call" | custom-call | tf_op jit(solution)/shard_map/pallas_call | solution.py:223
  40.8 0.5 collective-permute-start.37
  41.2 0.1 collective-permute-start.38
  41.3 0.4 collective-permute-start.39
  41.8 0.4 collective-permute-done.37.refs_0_
  42.1 0.4 collective-permute-start.8
  42.5 0.2 collective-permute-start.26
  42.7 1.5 %collective-permute-start.30 = (bf16[8,10752]{1,0:T(8,128)(2,1)S(1)}, bf16[8,10752]{1,0:T(8,128)(2,1)S(1)}, u32[]{:S(2)}, u32[]{:S(2)}) collective-permute-start(bf16[8,10752]{1,0:T(8,128)(2,1)S(1)} %shard_map.86), channel_id=1, source_target_pairs={{0,2},{1,3},{2,0},{3,1},{4,6},{5,7},{6,4},{7,5},{8,10},{9,11},{10,... | collective-permute-start | bytes 516104 | tf_op jit(solution)/shard_map/ppermute | solution.py:322
  44.3 0.1 collective-permute-start.36
  44.4 0.6 collective-permute-start.40
  45.1 3.4 %collective-permute-start.45 = (bf16[8,10752]{1,0:T(8,128)(2,1)S(1)}, bf16[8,10752]{1,0:T(8,128)(2,1)S(1)}, u32[]{:S(2)}, u32[]{:S(2)}) collective-permute-start(bf16[8,10752]{1,0:T(8,128)(2,1)S(1)} %shard_map.94), channel_id=1, source_target_pairs={{0,12},{1,13},{2,14},{3,15},{4,8},{5,9},{6,10},{7,11},{8,4},{9,5},... | collective-permute-start | bytes 516104 | tf_op jit(solution)/shard_map/ppermute | solution.py:319
  48.6 0.1 collective-permute-start.5
  48.7 1.3 %collective-permute-done.30.refs_2_ = bf16[8,10752]{1,0:T(8,128)(2,1)S(1)} collective-permute-done((bf16[8,10752]{1,0:T(8,128)(2,1)S(1)}, bf16[8,10752]{1,0:T(8,128)(2,1)S(1)}, u32[]{:S(2)}, u32[]{:S(2)}) %collective-permute-start.30) | collective-permute-done | bytes 172064 | tf_op jit(solution)/shard_map/ppermute | solution.py:322
  50.0 1.3 %collective-permute-start.42 = (bf16[8,10752]{1,0:T(8,128)(2,1)S(1)}, bf16[8,10752]{1,0:T(8,128)(2,1)S(1)}, u32[]{:S(2)}, u32[]{:S(2)}) collective-permute-start(bf16[8,10752]{1,0:T(8,128)(2,1)S(1)} %shard_map.87.refs_1_), channel_id=1, source_target_pairs={{0,8},{1,9},{2,10},{3,11},{4,12},{5,13},{6,14},{7,15},{8,0},{9,1},... | collective-permute-start | bytes 516104 | tf_op jit(solution)/shard_map/ppermute | solution.py:319
  51.4 1.1 %collective-permute-start.31 = (bf16[8,10752]{1,0:T(8,128)(2,1)S(1)}, bf16[8,10752]{1,0:T(8,128)(2,1)S(1)}, u32[]{:S(2)}, u32[]{:S(2)}) collective-permute-start(bf16[8,10752]{1,0:T(8,128)(2,1)S(1)} %shard_map.88), channel_id=1, source_target_pairs={{0,2},{1,3},{2,0},{3,1},{4,6},{5,7},{6,4},{7,5},{8,10},{9,11},{10,... | collective-permute-start | bytes 516104 | tf_op jit(solution)/shard_map/ppermute | solution.py:322
  52.4 1.0 %collective-permute-done.40.refs_2_ = bf16[8,10752]{1,0:T(8,128)(2,1)S(1)} collective-permute-done((bf16[8,10752]{1,0:T(8,128)(2,1)S(1)}, bf16[8,10752]{1,0:T(8,128)(2,1)S(1)}, u32[]{:S(2)}, u32[]{:S(2)}) %collective-permute-start.40) | collective-permute-done | bytes 172064 | tf_op jit(solution)/shard_map/ppermute | solution.py:322
  53.5 1.8 %collective-permute-start.41 = (bf16[8,10752]{1,0:T(8,128)(2,1)S(1)}, bf16[8,10752]{1,0:T(8,128)(2,1)S(1)}, u32[]{:S(2)}, u32[]{:S(2)}) collective-permute-start(bf16[8,10752]{1,0:T(8,128)(2,1)S(1)} %shard_map.93), channel_id=1, source_target_pairs={{0,4},{1,5},{2,6},{3,7},{4,0},{5,1},{6,2},{7,3},{8,12},{9,13},{10,... | collective-permute-start | bytes 516104 | tf_op jit(solution)/shard_map/ppermute | solution.py:319
  55.4 0.1 collective-permute-start.46
  55.5 6.8 %collective-permute-done.42 = bf16[8,10752]{1,0:T(8,128)(2,1)S(1)} collective-permute-done((bf16[8,10752]{1,0:T(8,128)(2,1)S(1)}, bf16[8,10752]{1,0:T(8,128)(2,1)S(1)}, u32[]{:S(2)}, u32[]{:S(2)}) %collective-permute-start.42) | collective-permute-done | bytes 172064 | tf_op jit(solution)/shard_map/ppermute | solution.py:319
  62.4 0.3 collective-permute-done.41.refs_1_
  62.8 1.9 %shard_map.96 = bf16[16,7168]{1,0:T(8,128)(2,1)} custom-call(s32[4]{0:T(128)S(1)} %copy-done.1, s32[2,16]{1,0:T(2,128)S(1)} %bitcast.3, f32[2,16]{1,0:T(2,128)S(1)} %bitcast.4, bf16[8,10752]{1,0:T(8,128)(2,1)S(1)} %shard_map.89.refs_0_, bf16[8,10752]{1,0:T(8,128)(2,1)S(1)} %collective-permute-done.41.refs_1_, f32[8,10752]{1,0:T(8,128)S(1)} %convert_element_type.3.refs_2_, ...), custom_call_target="tpu_custom_call" | custom-call | flops 44040192 | bytes 1146880 | tf_op jit(solution)/shard_map/pallas_call | solution.py:272
  (61 shorter events, 0.6 us)
Async XLA Ops:
  1.5 11.1 %collective-permute-start = (bf16[8,10752]{1,0:T(8,128)(2,1)S(1)}, bf16[8,10752]{1,0:T(8,128)(2,1)S(1)}, u32[]{:S(2)}, u32[]{:S(2)}) collective-permute-start(bf16[8,10752]{1,0:T(8,128)(2,1)S(1)} %get-tuple-element.48.refs_3_.refs_0_), channel_id=1, source_target_pairs={{0,2},{1,3},{2,0},{3,1},{4,6},{5,7},{6,4},{7,5},{8,10},{9,11},{10,... | collective-permute-start | bytes 516104 | tf_op jit(solution)/shard_map/ppermute | solution.py:322
  4.5 8.6 %collective-permute-start.9 = (bf16[8,10752]{1,0:T(8,128)(2,1)S(1)}, bf16[8,10752]{1,0:T(8,128)(2,1)S(1)}, u32[]{:S(2)}, u32[]{:S(2)}) collective-permute-start(bf16[8,10752]{1,0:T(8,128)(2,1)S(1)} %get-tuple-element.62), channel_id=1, source_target_pairs={{0,12},{1,13},{2,14},{3,15},{4,8},{5,9},{6,10},{7,11},{8,4},{9,5},... | collective-permute-start | bytes 516104 | tf_op jit(solution)/shard_map/ppermute | solution.py:319
  12.4 7.1 %collective-permute-start.11 = (bf16[8,10752]{1,0:T(8,128)(2,1)S(1)}, bf16[8,10752]{1,0:T(8,128)(2,1)S(1)}, u32[]{:S(2)}, u32[]{:S(2)}) collective-permute-start(bf16[8,10752]{1,0:T(8,128)(2,1)S(1)} %shard_map.79), channel_id=1, source_target_pairs={{0,4},{1,5},{2,6},{3,7},{4,0},{5,1},{6,2},{7,3},{8,12},{9,13},{10,... | collective-permute-start | bytes 516104 | tf_op jit(solution)/shard_map/ppermute | solution.py:319
  12.4 9.0 %collective-permute-start.1 = (bf16[8,10752]{1,0:T(8,128)(2,1)S(1)}, bf16[8,10752]{1,0:T(8,128)(2,1)S(1)}, u32[]{:S(2)}, u32[]{:S(2)}) collective-permute-start(bf16[8,10752]{1,0:T(8,128)(2,1)S(1)} %get-tuple-element.48.refs_3_.refs_0_), channel_id=1, source_target_pairs={{0,1},{1,0},{2,3},{3,2},{4,5},{5,4},{6,7},{7,6},{8,9},{9,8},{10,11... | collective-permute-start | bytes 516104 | tf_op jit(solution)/shard_map/ppermute | solution.py:325
  12.5 8.9 %collective-permute-start.2 = (bf16[8,3584]{1,0:T(8,128)(2,1)S(1)}, bf16[8,3584]{1,0:T(8,128)(2,1)S(1)}, u32[]{:S(2)}, u32[]{:S(2)}) collective-permute-start(bf16[8,3584]{1,0:T(8,128)(2,1)S(1)} %get-tuple-element.49), channel_id=1, source_target_pairs={{0,1},{1,0},{2,3},{3,2},{4,5},{5,4},{6,7},{7,6},{8,9},{9,8},{10,11... | collective-permute-start | bytes 172040 | tf_op jit(solution)/shard_map/ppermute | solution.py:325
  13.1 13.1 %collective-permute-start.10 = (bf16[8,10752]{1,0:T(8,128)(2,1)S(1)}, bf16[8,10752]{1,0:T(8,128)(2,1)S(1)}, u32[]{:S(2)}, u32[]{:S(2)}) collective-permute-start(bf16[8,10752]{1,0:T(8,128)(2,1)S(1)} %shard_map.78), channel_id=1, source_target_pairs={{0,8},{1,9},{2,10},{3,11},{4,12},{5,13},{6,14},{7,15},{8,0},{9,1},... | collective-permute-start | bytes 516104 | tf_op jit(solution)/shard_map/ppermute | solution.py:319
  19.4 6.9 %collective-permute-start.12 = (bf16[8,10752]{1,0:T(8,128)(2,1)S(1)}, bf16[8,10752]{1,0:T(8,128)(2,1)S(1)}, u32[]{:S(2)}, u32[]{:S(2)}) collective-permute-start(bf16[8,10752]{1,0:T(8,128)(2,1)S(1)} %collective-permute-done.11.refs_0_), channel_id=1, source_target_pairs={{0,2},{1,3},{2,0},{3,1},{4,6},{5,7},{6,4},{7,5},{8,10},{9,11},{10,... | collective-permute-start | bytes 516104 | tf_op jit(solution)/shard_map/ppermute | solution.py:322
  19.9 6.9 %collective-permute-start.18 = (bf16[8,10752]{1,0:T(8,128)(2,1)S(1)}, bf16[8,10752]{1,0:T(8,128)(2,1)S(1)}, u32[]{:S(2)}, u32[]{:S(2)}) collective-permute-start(bf16[8,10752]{1,0:T(8,128)(2,1)S(1)} %collective-permute-done.9.refs_1_.refs_0_), channel_id=1, source_target_pairs={{0,2},{1,3},{2,0},{3,1},{4,6},{5,7},{6,4},{7,5},{8,10},{9,11},{10,... | collective-permute-start | bytes 516104 | tf_op jit(solution)/shard_map/ppermute | solution.py:322
  21.4 6.1 %collective-permute-start.19 = (bf16[8,10752]{1,0:T(8,128)(2,1)S(1)}, bf16[8,10752]{1,0:T(8,128)(2,1)S(1)}, u32[]{:S(2)}, u32[]{:S(2)}) collective-permute-start(bf16[8,10752]{1,0:T(8,128)(2,1)S(1)} %collective-permute-done.9.refs_1_.refs_0_), channel_id=1, source_target_pairs={{0,1},{1,0},{2,3},{3,2},{4,5},{5,4},{6,7},{7,6},{8,9},{9,8},{10,11... | collective-permute-start | bytes 516104 | tf_op jit(solution)/shard_map/ppermute | solution.py:325
  21.5 1.5 %collective-permute-start.3 = (bf16[8,3584]{1,0:T(8,128)(2,1)S(1)}, bf16[8,3584]{1,0:T(8,128)(2,1)S(1)}, u32[]{:S(2)}, u32[]{:S(2)}) collective-permute-start(bf16[8,3584]{1,0:T(8,128)(2,1)S(1)} %get-tuple-element.50), channel_id=1, source_target_pairs={{0,1},{1,0},{2,3},{3,2},{4,5},{5,4},{6,7},{7,6},{8,9},{9,8},{10,11... | collective-permute-start | bytes 172040 | tf_op jit(solution)/shard_map/ppermute | solution.py:325
  22.9 1.2 %collective-permute-start.4 = (bf16[8,3584]{1,0:T(8,128)(2,1)S(1)}, bf16[8,3584]{1,0:T(8,128)(2,1)S(1)}, u32[]{:S(2)}, u32[]{:S(2)}) collective-permute-start(bf16[8,3584]{1,0:T(8,128)(2,1)S(1)} %get-tuple-element.51), channel_id=1, source_target_pairs={{0,1},{1,0},{2,3},{3,2},{4,5},{5,4},{6,7},{7,6},{8,9},{9,8},{10,11... | collective-permute-start | bytes 172040 | tf_op jit(solution)/shard_map/ppermute | solution.py:325
  26.3 6.6 %collective-permute-start.13 = (bf16[8,10752]{1,0:T(8,128)(2,1)S(1)}, bf16[8,10752]{1,0:T(8,128)(2,1)S(1)}, u32[]{:S(2)}, u32[]{:S(2)}) collective-permute-start(bf16[8,10752]{1,0:T(8,128)(2,1)S(1)} %shard_map.80.refs_0_), channel_id=1, source_target_pairs={{0,2},{1,3},{2,0},{3,1},{4,6},{5,7},{6,4},{7,5},{8,10},{9,11},{10,... | collective-permute-start | bytes 516104 | tf_op jit(solution)/shard_map/ppermute | solution.py:322
  26.9 1.3 %collective-permute-start.20 = (bf16[8,3584]{1,0:T(8,128)(2,1)S(1)}, bf16[8,3584]{1,0:T(8,128)(2,1)S(1)}, u32[]{:S(2)}, u32[]{:S(2)}) collective-permute-start(bf16[8,3584]{1,0:T(8,128)(2,1)S(1)} %get-tuple-element.67), channel_id=1, source_target_pairs={{0,1},{1,0},{2,3},{3,2},{4,5},{5,4},{6,7},{7,6},{8,9},{9,8},{10,11... | collective-permute-start | bytes 172040 | tf_op jit(solution)/shard_map/ppermute | solution.py:325
  27.0 6.0 %collective-permute-start.32 = (bf16[8,10752]{1,0:T(8,128)(2,1)S(1)}, bf16[8,10752]{1,0:T(8,128)(2,1)S(1)}, u32[]{:S(2)}, u32[]{:S(2)}) collective-permute-start(bf16[8,10752]{1,0:T(8,128)(2,1)S(1)} %collective-permute-done.11.refs_0_), channel_id=1, source_target_pairs={{0,1},{1,0},{2,3},{3,2},{4,5},{5,4},{6,7},{7,6},{8,9},{9,8},{10,11... | collective-permute-start | bytes 516104 | tf_op jit(solution)/shard_map/ppermute | solution.py:325
  27.5 1.2 %collective-permute-start.21 = (bf16[8,3584]{1,0:T(8,128)(2,1)S(1)}, bf16[8,3584]{1,0:T(8,128)(2,1)S(1)}, u32[]{:S(2)}, u32[]{:S(2)}) collective-permute-start(bf16[8,3584]{1,0:T(8,128)(2,1)S(1)} %get-tuple-element.68), channel_id=1, source_target_pairs={{0,1},{1,0},{2,3},{3,2},{4,5},{5,4},{6,7},{7,6},{8,9},{9,8},{10,11... | collective-permute-start | bytes 172040 | tf_op jit(solution)/shard_map/ppermute | solution.py:325
  27.5 1.4 %collective-permute-start.22 = (bf16[8,3584]{1,0:T(8,128)(2,1)S(1)}, bf16[8,3584]{1,0:T(8,128)(2,1)S(1)}, u32[]{:S(2)}, u32[]{:S(2)}) collective-permute-start(bf16[8,3584]{1,0:T(8,128)(2,1)S(1)} %get-tuple-element.69), channel_id=1, source_target_pairs={{0,1},{1,0},{2,3},{3,2},{4,5},{5,4},{6,7},{7,6},{8,9},{9,8},{10,11... | collective-permute-start | bytes 172040 | tf_op jit(solution)/shard_map/ppermute | solution.py:325
  28.2 6.1 %collective-permute-start.14 = (bf16[8,10752]{1,0:T(8,128)(2,1)S(1)}, bf16[8,10752]{1,0:T(8,128)(2,1)S(1)}, u32[]{:S(2)}, u32[]{:S(2)}) collective-permute-start(bf16[8,10752]{1,0:T(8,128)(2,1)S(1)} %shard_map.80.refs_0_), channel_id=1, source_target_pairs={{0,1},{1,0},{2,3},{3,2},{4,5},{5,4},{6,7},{7,6},{8,9},{9,8},{10,11... | collective-permute-start | bytes 516104 | tf_op jit(solution)/shard_map/ppermute | solution.py:325
  28.7 2.6 %collective-permute-start.6 = (bf16[8,3584]{1,0:T(8,128)(2,1)S(1)}, bf16[8,3584]{1,0:T(8,128)(2,1)S(1)}, u32[]{:S(2)}, u32[]{:S(2)}) collective-permute-start(bf16[8,3584]{1,0:T(8,128)(2,1)S(1)} %get-tuple-element.58.refs_1_), channel_id=1, source_target_pairs={{0,1},{1,0},{2,3},{3,2},{4,5},{5,4},{6,7},{7,6},{8,9},{9,8},{10,11... | collective-permute-start | bytes 172040 | tf_op jit(solution)/shard_map/ppermute | solution.py:325
  28.9 2.7 %collective-permute-start.7 = (bf16[8,3584]{1,0:T(8,128)(2,1)S(1)}, bf16[8,3584]{1,0:T(8,128)(2,1)S(1)}, u32[]{:S(2)}, u32[]{:S(2)}) collective-permute-start(bf16[8,3584]{1,0:T(8,128)(2,1)S(1)} %get-tuple-element.59), channel_id=1, source_target_pairs={{0,1},{1,0},{2,3},{3,2},{4,5},{5,4},{6,7},{7,6},{8,9},{9,8},{10,11... | collective-permute-start | bytes 172040 | tf_op jit(solution)/shard_map/ppermute | solution.py:325
  31.3 2.2 %collective-permute-start.23 = (bf16[8,3584]{1,0:T(8,128)(2,1)S(1)}, bf16[8,3584]{1,0:T(8,128)(2,1)S(1)}, u32[]{:S(2)}, u32[]{:S(2)}) collective-permute-start(bf16[8,3584]{1,0:T(8,128)(2,1)S(1)} %get-tuple-element.71), channel_id=1, source_target_pairs={{0,1},{1,0},{2,3},{3,2},{4,5},{5,4},{6,7},{7,6},{8,9},{9,8},{10,11... | collective-permute-start | bytes 172040 | tf_op jit(solution)/shard_map/ppermute | solution.py:325
  31.6 2.0 %collective-permute-start.24 = (bf16[8,3584]{1,0:T(8,128)(2,1)S(1)}, bf16[8,3584]{1,0:T(8,128)(2,1)S(1)}, u32[]{:S(2)}, u32[]{:S(2)}) collective-permute-start(bf16[8,3584]{1,0:T(8,128)(2,1)S(1)} %get-tuple-element.72), channel_id=1, source_target_pairs={{0,1},{1,0},{2,3},{3,2},{4,5},{5,4},{6,7},{7,6},{8,9},{9,8},{10,11... | collective-permute-start | bytes 172040 | tf_op jit(solution)/shard_map/ppermute | solution.py:325
  32.9 1.2 %collective-permute-start.25 = (bf16[8,3584]{1,0:T(8,128)(2,1)S(1)}, bf16[8,3584]{1,0:T(8,128)(2,1)S(1)}, u32[]{:S(2)}, u32[]{:S(2)}) collective-permute-start(bf16[8,3584]{1,0:T(8,128)(2,1)S(1)} %get-tuple-element.73), channel_id=1, source_target_pairs={{0,1},{1,0},{2,3},{3,2},{4,5},{5,4},{6,7},{7,6},{8,9},{9,8},{10,11... | collective-permute-start | bytes 172040 | tf_op jit(solution)/shard_map/ppermute | solution.py:325
  32.9 1.7 %collective-permute-start.15 = (bf16[8,3584]{1,0:T(8,128)(2,1)S(1)}, bf16[8,3584]{1,0:T(8,128)(2,1)S(1)}, u32[]{:S(2)}, u32[]{:S(2)}) collective-permute-start(bf16[8,3584]{1,0:T(8,128)(2,1)S(1)} %get-tuple-element.64), channel_id=1, source_target_pairs={{0,1},{1,0},{2,3},{3,2},{4,5},{5,4},{6,7},{7,6},{8,9},{9,8},{10,11... | collective-permute-start | bytes 172040 | tf_op jit(solution)/shard_map/ppermute | solution.py:325
  33.5 1.3 %collective-permute-start.16 = (bf16[8,3584]{1,0:T(8,128)(2,1)S(1)}, bf16[8,3584]{1,0:T(8,128)(2,1)S(1)}, u32[]{:S(2)}, u32[]{:S(2)}) collective-permute-start(bf16[8,3584]{1,0:T(8,128)(2,1)S(1)} %get-tuple-element.65), channel_id=1, source_target_pairs={{0,1},{1,0},{2,3},{3,2},{4,5},{5,4},{6,7},{7,6},{8,9},{9,8},{10,11... | collective-permute-start | bytes 172040 | tf_op jit(solution)/shard_map/ppermute | solution.py:325
  33.6 1.6 %collective-permute-start.17 = (bf16[8,3584]{1,0:T(8,128)(2,1)S(1)}, bf16[8,3584]{1,0:T(8,128)(2,1)S(1)}, u32[]{:S(2)}, u32[]{:S(2)}) collective-permute-start(bf16[8,3584]{1,0:T(8,128)(2,1)S(1)} %get-tuple-element.66), channel_id=1, source_target_pairs={{0,1},{1,0},{2,3},{3,2},{4,5},{5,4},{6,7},{7,6},{8,9},{9,8},{10,11... | collective-permute-start | bytes 172040 | tf_op jit(solution)/shard_map/ppermute | solution.py:325
  34.1 3.8 %collective-permute-start.33 = (bf16[8,3584]{1,0:T(8,128)(2,1)S(1)}, bf16[8,3584]{1,0:T(8,128)(2,1)S(1)}, u32[]{:S(2)}, u32[]{:S(2)}) collective-permute-start(bf16[8,3584]{1,0:T(8,128)(2,1)S(1)} %get-tuple-element.80), channel_id=1, source_target_pairs={{0,1},{1,0},{2,3},{3,2},{4,5},{5,4},{6,7},{7,6},{8,9},{9,8},{10,11... | collective-permute-start | bytes 172040 | tf_op jit(solution)/shard_map/ppermute | solution.py:325
  34.3 3.7 %collective-permute-start.34 = (bf16[8,3584]{1,0:T(8,128)(2,1)S(1)}, bf16[8,3584]{1,0:T(8,128)(2,1)S(1)}, u32[]{:S(2)}, u32[]{:S(2)}) collective-permute-start(bf16[8,3584]{1,0:T(8,128)(2,1)S(1)} %get-tuple-element.81), channel_id=1, source_target_pairs={{0,1},{1,0},{2,3},{3,2},{4,5},{5,4},{6,7},{7,6},{8,9},{9,8},{10,11... | collective-permute-start | bytes 172040 | tf_op jit(solution)/shard_map/ppermute | solution.py:325
  34.7 3.9 %collective-permute-start.35 = (bf16[8,3584]{1,0:T(8,128)(2,1)S(1)}, bf16[8,3584]{1,0:T(8,128)(2,1)S(1)}, u32[]{:S(2)}, u32[]{:S(2)}) collective-permute-start(bf16[8,3584]{1,0:T(8,128)(2,1)S(1)} %get-tuple-element.82), channel_id=1, source_target_pairs={{0,1},{1,0},{2,3},{3,2},{4,5},{5,4},{6,7},{7,6},{8,9},{9,8},{10,11... | collective-permute-start | bytes 172040 | tf_op jit(solution)/shard_map/ppermute | solution.py:325
  34.8 9.4 %collective-permute-start.43 = (bf16[8,10752]{1,0:T(8,128)(2,1)S(1)}, bf16[8,10752]{1,0:T(8,128)(2,1)S(1)}, u32[]{:S(2)}, u32[]{:S(2)}) collective-permute-start(bf16[8,10752]{1,0:T(8,128)(2,1)S(1)} %get-tuple-element.90), channel_id=1, source_target_pairs={{0,1},{1,0},{2,3},{3,2},{4,5},{5,4},{6,7},{7,6},{8,9},{9,8},{10,11... | collective-permute-start | bytes 516104 | tf_op jit(solution)/shard_map/ppermute | solution.py:325
  35.2 9.2 %collective-permute-start.44 = (bf16[8,10752]{1,0:T(8,128)(2,1)S(1)}, bf16[8,10752]{1,0:T(8,128)(2,1)S(1)}, u32[]{:S(2)}, u32[]{:S(2)}) collective-permute-start(bf16[8,10752]{1,0:T(8,128)(2,1)S(1)} %shard_map.84.refs_9_), channel_id=1, source_target_pairs={{0,2},{1,3},{2,0},{3,1},{4,6},{5,7},{6,4},{7,5},{8,10},{9,11},{10,... | collective-permute-start | bytes 516104 | tf_op jit(solution)/shard_map/ppermute | solution.py:322
  38.0 2.8 %collective-permute-start.27 = (bf16[8,3584]{1,0:T(8,128)(2,1)S(1)}, bf16[8,3584]{1,0:T(8,128)(2,1)S(1)}, u32[]{:S(2)}, u32[]{:S(2)}) collective-permute-start(bf16[8,3584]{1,0:T(8,128)(2,1)S(1)} %get-tuple-element.77.refs_9_), channel_id=1, source_target_pairs={{0,1},{1,0},{2,3},{3,2},{4,5},{5,4},{6,7},{7,6},{8,9},{9,8},{10,11... | collective-permute-start | bytes 172040 | tf_op jit(solution)/shard_map/ppermute | solution.py:325
  38.1 3.2 %collective-permute-start.28 = (bf16[8,3584]{1,0:T(8,128)(2,1)S(1)}, bf16[8,3584]{1,0:T(8,128)(2,1)S(1)}, u32[]{:S(2)}, u32[]{:S(2)}) collective-permute-start(bf16[8,3584]{1,0:T(8,128)(2,1)S(1)} %get-tuple-element.78), channel_id=1, source_target_pairs={{0,1},{1,0},{2,3},{3,2},{4,5},{5,4},{6,7},{7,6},{8,9},{9,8},{10,11... | collective-permute-start | bytes 172040 | tf_op jit(solution)/shard_map/ppermute | solution.py:325
  38.5 2.8 %collective-permute-start.29 = (bf16[8,3584]{1,0:T(8,128)(2,1)S(1)}, bf16[8,3584]{1,0:T(8,128)(2,1)S(1)}, u32[]{:S(2)}, u32[]{:S(2)}) collective-permute-start(bf16[8,3584]{1,0:T(8,128)(2,1)S(1)} %get-tuple-element.79), channel_id=1, source_target_pairs={{0,1},{1,0},{2,3},{3,2},{4,5},{5,4},{6,7},{7,6},{8,9},{9,8},{10,11... | collective-permute-start | bytes 172040 | tf_op jit(solution)/shard_map/ppermute | solution.py:325
  40.7 22.0 %copy-start = (s32[16,2]{0,1:T(2,128)S(1)}, s32[16,2]{0,1:T(2,128)}, u32[]{:S(2)}) copy-start(s32[16,2]{0,1:T(2,128)} %param.8) | copy-start | bytes 388
  40.7 22.0 %copy-start.1 = (s32[4]{0:T(128)S(1)}, s32[4]{0:T(128)}, u32[]{:S(2)}) copy-start(s32[4]{0:T(128)} %placement_ref.3) | copy-start | bytes 52
  40.7 22.0 %copy-start.2 = (f32[16,2]{0,1:T(2,128)S(1)}, f32[16,2]{0,1:T(2,128)}, u32[]{:S(2)}) copy-start(f32[16,2]{0,1:T(2,128)} %param.9) | copy-start | bytes 388
  40.8 1.4 %collective-permute-start.37 = (bf16[8,3584]{1,0:T(8,128)(2,1)S(1)}, bf16[8,3584]{1,0:T(8,128)(2,1)S(1)}, u32[]{:S(2)}, u32[]{:S(2)}) collective-permute-start(bf16[8,3584]{1,0:T(8,128)(2,1)S(1)} %get-tuple-element.86), channel_id=1, source_target_pairs={{0,1},{1,0},{2,3},{3,2},{4,5},{5,4},{6,7},{7,6},{8,9},{9,8},{10,11... | collective-permute-start | bytes 172040 | tf_op jit(solution)/shard_map/ppermute | solution.py:325
  41.2 1.2 %collective-permute-start.38 = (bf16[8,3584]{1,0:T(8,128)(2,1)S(1)}, bf16[8,3584]{1,0:T(8,128)(2,1)S(1)}, u32[]{:S(2)}, u32[]{:S(2)}) collective-permute-start(bf16[8,3584]{1,0:T(8,128)(2,1)S(1)} %get-tuple-element.87), channel_id=1, source_target_pairs={{0,1},{1,0},{2,3},{3,2},{4,5},{5,4},{6,7},{7,6},{8,9},{9,8},{10,11... | collective-permute-start | bytes 172040 | tf_op jit(solution)/shard_map/ppermute | solution.py:325
  41.3 1.4 %collective-permute-start.39 = (bf16[8,3584]{1,0:T(8,128)(2,1)S(1)}, bf16[8,3584]{1,0:T(8,128)(2,1)S(1)}, u32[]{:S(2)}, u32[]{:S(2)}) collective-permute-start(bf16[8,3584]{1,0:T(8,128)(2,1)S(1)} %get-tuple-element.88), channel_id=1, source_target_pairs={{0,1},{1,0},{2,3},{3,2},{4,5},{5,4},{6,7},{7,6},{8,9},{9,8},{10,11... | collective-permute-start | bytes 172040 | tf_op jit(solution)/shard_map/ppermute | solution.py:325
  42.1 2.9 %collective-permute-start.8 = (bf16[8,3584]{1,0:T(8,128)(2,1)S(1)}, bf16[8,3584]{1,0:T(8,128)(2,1)S(1)}, u32[]{:S(2)}, u32[]{:S(2)}) collective-permute-start(bf16[8,3584]{1,0:T(8,128)(2,1)S(1)} %get-tuple-element.60), channel_id=1, source_target_pairs={{0,1},{1,0},{2,3},{3,2},{4,5},{5,4},{6,7},{7,6},{8,9},{9,8},{10,11... | collective-permute-start | bytes 172040 | tf_op jit(solution)/shard_map/ppermute | solution.py:325
  42.5 6.1 %collective-permute-start.26 = (bf16[8,10752]{1,0:T(8,128)(2,1)S(1)}, bf16[8,10752]{1,0:T(8,128)(2,1)S(1)}, u32[]{:S(2)}, u32[]{:S(2)}) collective-permute-start(bf16[8,10752]{1,0:T(8,128)(2,1)S(1)} %get-tuple-element.75), channel_id=1, source_target_pairs={{0,1},{1,0},{2,3},{3,2},{4,5},{5,4},{6,7},{7,6},{8,9},{9,8},{10,11... | collective-permute-start | bytes 516104 | tf_op jit(solution)/shard_map/ppermute | solution.py:325
  42.7 7.3 %collective-permute-start.30 = (bf16[8,10752]{1,0:T(8,128)(2,1)S(1)}, bf16[8,10752]{1,0:T(8,128)(2,1)S(1)}, u32[]{:S(2)}, u32[]{:S(2)}) collective-permute-start(bf16[8,10752]{1,0:T(8,128)(2,1)S(1)} %shard_map.86), channel_id=1, source_target_pairs={{0,2},{1,3},{2,0},{3,1},{4,6},{5,7},{6,4},{7,5},{8,10},{9,11},{10,... | collective-permute-start | bytes 516104 | tf_op jit(solution)/shard_map/ppermute | solution.py:322
  44.3 7.1 %collective-permute-start.36 = (bf16[8,10752]{1,0:T(8,128)(2,1)S(1)}, bf16[8,10752]{1,0:T(8,128)(2,1)S(1)}, u32[]{:S(2)}, u32[]{:S(2)}) collective-permute-start(bf16[8,10752]{1,0:T(8,128)(2,1)S(1)} %get-tuple-element.84), channel_id=1, source_target_pairs={{0,1},{1,0},{2,3},{3,2},{4,5},{5,4},{6,7},{7,6},{8,9},{9,8},{10,11... | collective-permute-start | bytes 516104 | tf_op jit(solution)/shard_map/ppermute | solution.py:325
  44.4 9.0 %collective-permute-start.40 = (bf16[8,10752]{1,0:T(8,128)(2,1)S(1)}, bf16[8,10752]{1,0:T(8,128)(2,1)S(1)}, u32[]{:S(2)}, u32[]{:S(2)}) collective-permute-start(bf16[8,10752]{1,0:T(8,128)(2,1)S(1)} %shard_map.92), channel_id=1, source_target_pairs={{0,2},{1,3},{2,0},{3,1},{4,6},{5,7},{6,4},{7,5},{8,10},{9,11},{10,... | collective-permute-start | bytes 516104 | tf_op jit(solution)/shard_map/ppermute | solution.py:322
  45.1 10.3 %collective-permute-start.45 = (bf16[8,10752]{1,0:T(8,128)(2,1)S(1)}, bf16[8,10752]{1,0:T(8,128)(2,1)S(1)}, u32[]{:S(2)}, u32[]{:S(2)}) collective-permute-start(bf16[8,10752]{1,0:T(8,128)(2,1)S(1)} %shard_map.94), channel_id=1, source_target_pairs={{0,12},{1,13},{2,14},{3,15},{4,8},{5,9},{6,10},{7,11},{8,4},{9,5},... | collective-permute-start | bytes 516104 | tf_op jit(solution)/shard_map/ppermute | solution.py:319
  48.6 13.7 %collective-permute-start.5 = (bf16[8,10752]{1,0:T(8,128)(2,1)S(1)}, bf16[8,10752]{1,0:T(8,128)(2,1)S(1)}, u32[]{:S(2)}, u32[]{:S(2)}) collective-permute-start(bf16[8,10752]{1,0:T(8,128)(2,1)S(1)} %get-tuple-element.56), channel_id=1, source_target_pairs={{0,1},{1,0},{2,3},{3,2},{4,5},{5,4},{6,7},{7,6},{8,9},{9,8},{10,11... | collective-permute-start | bytes 516104 | tf_op jit(solution)/shard_map/ppermute | solution.py:325
  50.0 12.2 %collective-permute-start.42 = (bf16[8,10752]{1,0:T(8,128)(2,1)S(1)}, bf16[8,10752]{1,0:T(8,128)(2,1)S(1)}, u32[]{:S(2)}, u32[]{:S(2)}) collective-permute-start(bf16[8,10752]{1,0:T(8,128)(2,1)S(1)} %shard_map.87.refs_1_), channel_id=1, source_target_pairs={{0,8},{1,9},{2,10},{3,11},{4,12},{5,13},{6,14},{7,15},{8,0},{9,1},... | collective-permute-start | bytes 516104 | tf_op jit(solution)/shard_map/ppermute | solution.py:319
  51.4 11.0 %collective-permute-start.31 = (bf16[8,10752]{1,0:T(8,128)(2,1)S(1)}, bf16[8,10752]{1,0:T(8,128)(2,1)S(1)}, u32[]{:S(2)}, u32[]{:S(2)}) collective-permute-start(bf16[8,10752]{1,0:T(8,128)(2,1)S(1)} %shard_map.88), channel_id=1, source_target_pairs={{0,2},{1,3},{2,0},{3,1},{4,6},{5,7},{6,4},{7,5},{8,10},{9,11},{10,... | collective-permute-start | bytes 516104 | tf_op jit(solution)/shard_map/ppermute | solution.py:322
  53.5 9.2 %collective-permute-start.41 = (bf16[8,10752]{1,0:T(8,128)(2,1)S(1)}, bf16[8,10752]{1,0:T(8,128)(2,1)S(1)}, u32[]{:S(2)}, u32[]{:S(2)}) collective-permute-start(bf16[8,10752]{1,0:T(8,128)(2,1)S(1)} %shard_map.93), channel_id=1, source_target_pairs={{0,4},{1,5},{2,6},{3,7},{4,0},{5,1},{6,2},{7,3},{8,12},{9,13},{10,... | collective-permute-start | bytes 516104 | tf_op jit(solution)/shard_map/ppermute | solution.py:319
  55.4 7.0 %collective-permute-start.46 = (bf16[8,10112]{1,0:T(8,128)(2,1)S(1)}, bf16[8,10112]{1,0:T(8,128)(2,1)S(1)}, u32[]{:S(2)}, u32[]{:S(2)}) collective-permute-start(bf16[8,10112]{1,0:T(8,128)(2,1)S(1)} %shard_map.95), channel_id=1, source_target_pairs={{0,1},{1,0},{2,3},{3,2},{4,5},{5,4},{6,7},{7,6},{8,9},{9,8},{10,11... | collective-permute-start | bytes 485384 | tf_op jit(solution)/shard_map/ppermute | solution.py:325

commit v10 on v8

--- a/solution.py
+++ b/solution.py
@@ -93,6 +93,21 @@
     pass
 
 
+def clear(*refs):
+    refs[-1][...] = jnp.zeros_like(refs[-1])
+
+
+def token(after):
+    return pl.pallas_call(
+        clear,
+        out_shape=pltpu.VMEM(after.shape, after.dtype),
+        in_specs=[ANYWHERE],
+        out_specs=VMEM,
+        compiler_params=pltpu.CompilerParams(vmem_limit_bytes=VMEM_BYTES),
+        cost_estimate=NO_COST,
+    )(after)
+
+
 def when(value, after):
     if not after:
         return value
@@ -133,15 +148,14 @@
     )(*[pltpu.with_memory_space_constraint(w, pltpu.HBM) for w in weights], after)
 
 
-def experts_kernel(*refs):
-    straight_ref, across_ref, straight_other_ref, across_other_ref = refs[:4]
-    gate_ref, up_ref, down_ref = refs[4:7]
-    out_refs = refs[-4:]
-    pieces = (straight_ref, across_ref, straight_other_ref, across_other_ref)
+def experts_kernel(count, *refs):
+    pieces = refs[:count]
+    gate_ref, up_ref, down_ref = refs[count : count + 3]
+    out_refs = refs[-count:]
     width, hid = gate_ref.shape
     middle = width // 2
-    height = straight_ref.shape[0]
-    total = len(pieces) * height
+    height = pieces[0].shape[0]
+    total = count * height
     rest = jnp.concatenate([p[:, width:] for p in pieces], axis=0)
     left = jnp.concatenate([p[:, :middle] for p in pieces] + [rest], axis=0)
     right = jnp.concatenate([p[:, middle:width] for p in pieces] + [rest], axis=0)
@@ -177,20 +191,16 @@
 
 
 def run_experts(pieces, weights, after):
-    width, hid = weights[0].shape
-    height, packed_width = pieces[0].shape
-    rows = len(pieces) * height
-    shape = pltpu.VMEM((height, packed_width), jnp.bfloat16)
-    operands = [in_vmem(p) for p in pieces] + [in_vmem(w) for w in weights]
-    return pl.pallas_call(
-        experts_kernel,
-        out_shape=[shape] * len(pieces),
-        in_specs=[VMEM] * 7 + [ANYWHERE] * len(after),
-        out_specs=[VMEM] * len(pieces),
-        compiler_params=pltpu.CompilerParams(vmem_limit_bytes=VMEM_BYTES),
-        cost_estimate=pl.CostEstimate(
-            flops=0, bytes_accessed=4 * width * hid, transcendentals=0
-        ),
+    count = len(pieces)
+    shape = pltpu.VMEM(pieces[0].shape, jnp.bfloat16)
+    operands = [in_vmem(value) for value in [*pieces, *weights]]
+    return pl.pallas_call(
+        functools.partial(experts_kernel, count),
+        out_shape=[shape] * count,
+        in_specs=[VMEM] * len(operands) + [ANYWHERE] * len(after),
+        out_specs=[VMEM] * count,
+        compiler_params=pltpu.CompilerParams(vmem_limit_bytes=VMEM_BYTES),
+        cost_estimate=NO_COST,
     )(*operands, *after)
 
 
@@ -211,7 +221,6 @@
         terms.append(jnp.where(named & (slot == wanted), weight, 0.0))
     term = jnp.concatenate(terms, axis=0)
     row = lax.broadcasted_iota(jnp.int32, term.shape, 0) % rows
-    rest = jnp.concatenate([r[:, width:] for r in results], axis=0)
     for side in range(2):
         first = half + side * quarter
         mine = jnp.where((row < half) | ((row >= first) & (row < first + quarter)), term, 0.0)
@@ -223,7 +232,7 @@
         pieces = []
         for r in results:
             pieces += [r[:, side * middle : (side + 1) * middle], r[:, width:]]
-        rhs = jnp.concatenate(pieces, axis=0)
+        rhs = jnp.concatenate([p.astype(jnp.bfloat16) for p in pieces], axis=0)
         value = lax.dot_general(
             lhs, rhs, (((0,), (0,)), ((), ())), preferred_element_type=jnp.float32
         )
@@ -287,49 +296,49 @@
     straight, across, results = {}, {}, {}
     both, home, kept, sent = {}, {}, {}, {}
 
-    def compute(k, after):
-        theirs = [along_core(straight[k]), along_core(across[k])]
-        out = run_experts([straight[k], across[k]] + theirs, weights, after)
-        sent[k] = out[3]
-        both[k] = add(out[1], along_core(out[3]))
-        kept[k] = out[0], along_core(out[2])
+    def compute(blocks, after):
+        pieces = []
+        for k in blocks:
+            pieces += [straight[k], across[k], along_core(straight[k]), along_core(across[k])]
+        out = run_experts(pieces, weights, after)
+        for i, k in enumerate(blocks):
+            sent[k] = out[4 * i + 3]
+            both[k] = add(out[4 * i + 1], along_core(out[4 * i + 3]))
+            kept[k] = out[4 * i], along_core(out[4 * i + 2])
 
     def go_home(k, after):
-        back = along_y(both[k] if k else when(both[k], after))
-        home[k] = add(*kept[k], back)
-        results[k] = along_z(when(home[k], after), k) if k else home[k]
+        home[k] = add(*kept[k], along_y(when(both[k], after)))
+        results[k] = along_z(home[k], k) if k else home[k]
 
     buckets = list(pack(placement, ids, tokens, n_blocks, parts))
     weights = load((gate_weight, up_weight, down_weight), buckets[0])
     straight[0] = buckets[0]
     across[0] = along_y(straight[0])
-    compute(0, [])
-    second, marks = None, []
+    second = None
     for g, group in enumerate(groups):
         first = group[0]
         if g == 0:
             straight[first] = along_z(buckets[first], first)
             across[first] = along_y(straight[first])
-            compute(first, [])
-            go_home(first, [])
+            compute([0, first], [])
         else:
             previous = groups[g - 1][0]
             straight[first] = along_z(when(buckets[first], [straight[previous], across[0]]), first)
-            after = [sent[0]] + ([across[second]] if second else [])
-            straight[first] = when(straight[first], after)
+            straight[first] = when(straight[first], [across[second], across[previous]])
             across[first] = along_y(straight[first])
-            compute(first, [both[previous]])
-            go_home(first, [])
-            marks.append(along_core(results[previous]))
-        if second:
-            compute(second, [sent[first]])
+            go_home(previous, [])
+            compute([second, first], [both[previous]])
             go_home(second, [])
-        second = group[1] if len(group) > 1 else None
-        if second:
+        if len(group) > 1:
+            second = group[1]
             straight[second] = along_z(when(buckets[second], [weights[0]] if g == 0 else []), second)
             across[second] = along_y(straight[second])
+    go_home(last, [])
+    marks = [along_core(token(results[group[0]])) for group in groups[:-1]]
+    results[last] = results[last].astype(jnp.float32)
     go_home(0, [home[last]])
-    return mix(placement, ids, gates.T, [results[k] for k in range(n_blocks)], marks, n_blocks, parts)
+    results = [results[k] for k in range(n_blocks)]
+    return mix(placement, ids, gates.T, results, marks, n_blocks, parts)
 
 
 def solution(mesh):

time: 64.4 us -> 61.9 us (0.961)
  waiting for transfers between devices: 23.3 us -> 28 us
  Pallas kernels: 16.3 us -> 11.7 us
  starting transfers between devices: 24.5 us -> 21.8 us
    pallas_call x4 -> x3, Pallas kernels: 8.28 us -> 3.74 us  [the longest x2 3.73 us: run_experts(): pl.pallas_call(functools.partial(experts_kernel, count), out_shape=[shape...]
    ppermute x6, starting transfers between devices: 15.7 us -> 11.2 us  [along_z(): return lax.ppermute(value, 'node', pairs)]
    ppermute x8, waiting for transfers between devices: 6.62 us -> 9.59 us  [along_y(): return lax.ppermute(value, 'node', [(i, i ^ 2) for i in range(devices)])]
    ppermute x6, waiting for transfers between devices: 15.8 us -> 18.1 us  [along_z(): return lax.ppermute(value, 'node', pairs)]
    ppermute x17, starting transfers between devices: 2.62 us -> 3.63 us  [along_core(): return lax.ppermute(value, 'node', [(i, i ^ 1) for i in range(devices)])]
    ppermute x8, starting transfers between devices: 6.13 us -> 6.9 us  [along_y(): return lax.ppermute(value, 'node', [(i, i ^ 2) for i in range(devices)])]
  transfers between devices with their start and end apart: 31 -> 31, of which waited for: 10 -> 12; matrix products, arithmetic and copies ran while one was open for 0% -> 0% of each run, Pallas kernels for 20% -> 14%
where the time goes in v10:
time: 61.9 us; the launch traced here: 61.7 us
  waiting for transfers between devices  28 us (45%)
  starting transfers between devices  21.8 us (35%)
  Pallas kernels  11.7 us (19%)
    ppermute x6, waiting for transfers between devices, along_z(): return lax.ppermute(value, 'node', pairs)  18.1 us
    ppermute x6, starting transfers between devices, along_z(): return lax.ppermute(value, 'node', pairs)  11.2 us
    ppermute x8, waiting for transfers between devices, along_y(): return lax.ppermute(value, 'node', [(i, i ^ 2) for i in range(devices)])  9.59 us
    ppermute x8, starting transfers between devices, along_y(): return lax.ppermute(value, 'node', [(i, i ^ 2) for i in range(devices)])  6.9 us
    pallas_call x1, Pallas kernels, load(): pl.pallas_call(load_kernel, out_shape=[pltpu.VMEM(w.shape, w.dtype) for w...  4.24 us
    pallas_call x2, Pallas kernels, run_experts(): pl.pallas_call(functools.partial(experts_kernel, count), out_shape=[shape...  3.73 us
    ppermute x17, starting transfers between devices, along_core(): return lax.ppermute(value, 'node', [(i, i ^ 1) for i in range(devices)])  3.63 us
    pallas_call x1, Pallas kernels, mix(): pl.pallas_call(functools.partial(mix_kernel, n_blocks, parts), out_shape=...  1.86 us
  transfers between devices with their start and end apart: 31, of which 12 were waited for; matrix products, arithmetic and copies ran while one was open for 0% of the time, Pallas kernels for 14%

profile of v10, /device:TPU:0, one launch (start us, length us, event | category | flops | bytes accessed | tf_op | source)
XLA Modules:
  0.0 61.7 jit_solution(1359388680332117620)
XLA Ops:
  0.0 1.5 %shard_map.73 = (bf16[8,10752]{1,0:T(8,128)(2,1)S(1)}, bf16[8,10752]{1,0:T(8,128)(2,1)S(1)}, bf16[8,10752]{1,0:T(8,128)(2,1)S(1)}, bf16[8,10752]{1,0:T(8,128)(2,1)S(1)}) custom-call(s32[4]{0:T(128)} %placement_ref.3, s32[2,16]{1,0:T(2,128)} %bitcast.2, bf16[16,7168]{1,0:T(8,128)(2,1)} %tokens_ref.1), custom_call_target="tpu_custom_call" | custom-call | tf_op jit(solution)/shard_map/pallas_call | solution.py:82
  1.5 5.1 %collective-permute-start.3 = (bf16[8,10752]{1,0:T(8,128)(2,1)S(1)}, bf16[8,10752]{1,0:T(8,128)(2,1)S(1)}, u32[]{:S(2)}, u32[]{:S(2)}) collective-permute-start(bf16[8,10752]{1,0:T(8,128)(2,1)S(1)} %get-tuple-element.29), channel_id=1, source_target_pairs={{0,12},{1,13},{2,14},{3,15},{4,8},{5,9},{6,10},{7,11},{8,4},{9,5},... | collective-permute-start | bytes 516104 | tf_op jit(solution)/shard_map/ppermute | solution.py:285
  6.6 1.5 %collective-permute-start = (bf16[8,10752]{1,0:T(8,128)(2,1)S(1)}, bf16[8,10752]{1,0:T(8,128)(2,1)S(1)}, u32[]{:S(2)}, u32[]{:S(2)}) collective-permute-start(bf16[8,10752]{1,0:T(8,128)(2,1)S(1)} %get-tuple-element.28.refs_3_.refs_0_), channel_id=1, source_target_pairs={{0,2},{1,3},{2,0},{3,1},{4,6},{5,7},{6,4},{7,5},{8,10},{9,11},{10,... | collective-permute-start | bytes 516104 | tf_op jit(solution)/shard_map/ppermute | solution.py:288
  8.1 4.2 %shard_map.74 = (bf16[7168,256]{1,0:T(8,128)(2,1)S(1)}, bf16[7168,256]{1,0:T(8,128)(2,1)S(1)}, bf16[256,7168]{1,0:T(8,128)(2,1)S(1)}) custom-call(bf16[7168,256]{1,0:T(8,128)(2,1)} %refs_0_.1, bf16[7168,256]{1,0:T(8,128)(2,1)} %refs_1_.1, bf16[256,7168]{1,0:T(8,128)(2,1)} %refs_2_.1, bf16[8,10752]{1,0:T(8,128)(2,1)S(1)} %get-tuple-element.28.refs_3_.refs_0_), custom_call_target="tpu_custom_call" | custom-call | tf_op jit(solution)/shard_map/pallas_call | solution.py:140
  12.4 0.1 collective-permute-start.9
  12.4 0.0 collective-permute-done.3.refs_4_.refs_1_
  12.4 0.6 collective-permute-start.4
  13.0 0.0 collective-permute-done.refs_1_.refs_2_
  13.0 3.9 %collective-permute-start.13 = (bf16[8,10752]{1,0:T(8,128)(2,1)S(1)}, bf16[8,10752]{1,0:T(8,128)(2,1)S(1)}, u32[]{:S(2)}, u32[]{:S(2)}) collective-permute-start(bf16[8,10752]{1,0:T(8,128)(2,1)S(1)} %shard_map.78), channel_id=1, source_target_pairs={{0,8},{1,9},{2,10},{3,11},{4,12},{5,13},{6,14},{7,15},{8,0},{9,1},... | collective-permute-start | bytes 516104 | tf_op jit(solution)/shard_map/ppermute | solution.py:285
  16.9 2.4 %collective-permute-done.9.refs_0_ = bf16[8,10752]{1,0:T(8,128)(2,1)S(1)} collective-permute-done((bf16[8,10752]{1,0:T(8,128)(2,1)S(1)}, bf16[8,10752]{1,0:T(8,128)(2,1)S(1)}, u32[]{:S(2)}, u32[]{:S(2)}) %collective-permute-start.9) | collective-permute-done | bytes 172064 | tf_op jit(solution)/shard_map/ppermute | solution.py:285
  19.3 0.4 collective-permute-start.10
  19.7 0.0 collective-permute-start.1
  19.7 0.5 collective-permute-start.5
  20.2 0.0 collective-permute-done.4.refs_5_.refs_2_
  20.2 0.0 collective-permute-start.2
  20.2 3.6 %collective-permute-done.13.refs_0_ = bf16[8,10752]{1,0:T(8,128)(2,1)S(1)} collective-permute-done((bf16[8,10752]{1,0:T(8,128)(2,1)S(1)}, bf16[8,10752]{1,0:T(8,128)(2,1)S(1)}, u32[]{:S(2)}, u32[]{:S(2)}) %collective-permute-start.13) | collective-permute-done | bytes 172064 | tf_op jit(solution)/shard_map/ppermute | solution.py:285
  23.8 0.0 collective-permute-start.6
  23.8 0.9 %collective-permute-done.10.refs_1_ = bf16[8,10752]{1,0:T(8,128)(2,1)S(1)} collective-permute-done((bf16[8,10752]{1,0:T(8,128)(2,1)S(1)}, bf16[8,10752]{1,0:T(8,128)(2,1)S(1)}, u32[]{:S(2)}, u32[]{:S(2)}) %collective-permute-start.10) | collective-permute-done | bytes 172064 | tf_op jit(solution)/shard_map/ppermute | solution.py:288
  24.7 0.4 collective-permute-start.14
  25.1 0.0 collective-permute-done.1.refs_2_
  25.1 0.0 collective-permute-done.5.refs_6_
  25.1 0.1 collective-permute-done.6.refs_7_
  25.2 1.9 %shard_map.75 = (bf16[8,10752]{1,0:T(8,128)(2,1)S(1)}, bf16[8,10752]{1,0:T(8,128)(2,1)S(1)}, bf16[8,10752]{1,0:T(8,128)(2,1)S(1)}, bf16[8,10752]{1,0:T(8,128)(2,...) custom-call(bf16[8,10752]{1,0:T(8,128)(2,1)S(1)} %get-tuple-element., ...), custom_call_target="tpu_custom_call" | custom-call | tf_op jit(solution)/shard_map/pallas_call | solution.py:197
  27.1 0.2 collective-permute-start.17
  27.3 0.4 collective-permute-start.11
  27.7 0.1 collective-permute-start.15
  27.8 0.4 collective-permute-start.12
  28.2 2.4 %collective-permute-done.14.refs_5_ = bf16[8,10752]{1,0:T(8,128)(2,1)S(1)} collective-permute-done((bf16[8,10752]{1,0:T(8,128)(2,1)S(1)}, bf16[8,10752]{1,0:T(8,128)(2,1)S(1)}, u32[]{:S(2)}, u32[]{:S(2)}) %collective-permute-start.14) | collective-permute-done | bytes 172064 | tf_op jit(solution)/shard_map/ppermute | solution.py:288
  30.6 0.5 collective-permute-start.27
  31.2 0.7 %collective-permute-start.28 = (bf16[8,10752]{1,0:T(8,128)(2,1)S(1)}, bf16[8,10752]{1,0:T(8,128)(2,1)S(1)}, u32[]{:S(2)}, u32[]{:S(2)}) collective-permute-start(bf16[8,10752]{1,0:T(8,128)(2,1)S(1)} %shard_map.80.refs_11_), channel_id=1, source_target_pairs={{0,2},{1,3},{2,0},{3,1},{4,6},{5,7},{6,4},{7,5},{8,10},{9,11},{10,... | collective-permute-start | bytes 516104 | tf_op jit(solution)/shard_map/ppermute | solution.py:288
  31.9 0.0 collective-permute-done.12.refs_3_
  31.9 0.1 collective-permute-done.16.refs_7_
  32.0 1.9 %shard_map.81 = (bf16[8,10752]{1,0:T(8,128)(2,1)S(1)}, bf16[8,10752]{1,0:T(8,128)(2,1)S(1)}, bf16[8,10752]{1,0:T(8,128)(2,1)S(1)}, bf16[8,10752]{1,0:T(8,128)(2,...) custom-call(bf16[8,10752]{1,0:T(8,128)(2,1)S(1)} %collective-permute, ...), custom_call_target="tpu_custom_call" | custom-call | tf_op jit(solution)/shard_map/pallas_call | solution.py:197
  33.9 0.0 copy-start
  33.9 0.0 copy-start.1
  33.9 0.0 copy-start.2
  33.9 0.2 collective-permute-start.19
  34.1 0.4 collective-permute-start.23
  34.5 0.1 collective-permute-start.8
  34.6 0.0 collective-permute-done.27.refs_1_
  34.7 2.9 %collective-permute-done.28.refs_2_ = bf16[8,10752]{1,0:T(8,128)(2,1)S(1)} collective-permute-done((bf16[8,10752]{1,0:T(8,128)(2,1)S(1)}, bf16[8,10752]{1,0:T(8,128)(2,1)S(1)}, u32[]{:S(2)}, u32[]{:S(2)}) %collective-permute-start.28) | collective-permute-done | bytes 172064 | tf_op jit(solution)/shard_map/ppermute | solution.py:288
  37.5 0.1 shard_map.88
  37.6 1.9 %collective-permute-start.29 = (bf16[8,10752]{1,0:T(8,128)(2,1)S(1)}, bf16[8,10752]{1,0:T(8,128)(2,1)S(1)}, u32[]{:S(2)}, u32[]{:S(2)}) collective-permute-start(bf16[8,10752]{1,0:T(8,128)(2,1)S(1)} %shard_map.88), channel_id=1, source_target_pairs={{0,12},{1,13},{2,14},{3,15},{4,8},{5,9},{6,10},{7,11},{8,4},{9,5},... | collective-permute-start | bytes 516104 | tf_op jit(solution)/shard_map/ppermute | solution.py:285
  39.5 0.0 collective-permute-start.18
  39.6 0.6 collective-permute-start.20
  40.2 0.0 collective-permute-done.23.refs_1_
  40.2 0.2 collective-permute-start.22
  40.4 0.0 collective-permute-done.8.refs_1_
  40.5 1.6 %collective-permute-start.24 = (bf16[8,10752]{1,0:T(8,128)(2,1)S(1)}, bf16[8,10752]{1,0:T(8,128)(2,1)S(1)}, u32[]{:S(2)}, u32[]{:S(2)}) collective-permute-start(bf16[8,10752]{1,0:T(8,128)(2,1)S(1)} %shard_map.86), channel_id=1, source_target_pairs={{0,2},{1,3},{2,0},{3,1},{4,6},{5,7},{6,4},{7,5},{8,10},{9,11},{10,... | collective-permute-start | bytes 516104 | tf_op jit(solution)/shard_map/ppermute | solution.py:288
  42.1 3.0 %collective-permute-done.29.refs_0_.refs_3_ = bf16[8,10752]{1,0:T(8,128)(2,1)S(1)} collective-permute-done((bf16[8,10752]{1,0:T(8,128)(2,1)S(1)}, bf16[8,10752]{1,0:T(8,128)(2,1)S(1)}, u32[]{:S(2)}, u32[]{:S(2)}) %collective-permute-start.29) | collective-permute-done | bytes 172064 | tf_op jit(solution)/shard_map/ppermute | solution.py:285
  45.0 0.6 collective-permute-start.30
  45.6 1.2 %collective-permute-done.20.refs_2_ = bf16[8,10752]{1,0:T(8,128)(2,1)S(1)} collective-permute-done((bf16[8,10752]{1,0:T(8,128)(2,1)S(1)}, bf16[8,10752]{1,0:T(8,128)(2,1)S(1)}, u32[]{:S(2)}, u32[]{:S(2)}) %collective-permute-start.20) | collective-permute-done | bytes 172064 | tf_op jit(solution)/shard_map/ppermute | solution.py:288
  46.8 0.1 shard_map.83.refs_1_
  46.9 0.2 collective-permute-start.26
  47.1 1.2 %collective-permute-start.21 = (bf16[8,10752]{1,0:T(8,128)(2,1)S(1)}, bf16[8,10752]{1,0:T(8,128)(2,1)S(1)}, u32[]{:S(2)}, u32[]{:S(2)}) collective-permute-start(bf16[8,10752]{1,0:T(8,128)(2,1)S(1)} %shard_map.84), channel_id=1, source_target_pairs={{0,2},{1,3},{2,0},{3,1},{4,6},{5,7},{6,4},{7,5},{8,10},{9,11},{10,... | collective-permute-start | bytes 516104 | tf_op jit(solution)/shard_map/ppermute | solution.py:288
  48.3 2.2 %collective-permute-done.24.refs_2_ = bf16[8,10752]{1,0:T(8,128)(2,1)S(1)} collective-permute-done((bf16[8,10752]{1,0:T(8,128)(2,1)S(1)}, bf16[8,10752]{1,0:T(8,128)(2,1)S(1)}, u32[]{:S(2)}, u32[]{:S(2)}) %collective-permute-start.24) | collective-permute-done | bytes 172064 | tf_op jit(solution)/shard_map/ppermute | solution.py:288
  50.5 0.1 shard_map.87
  50.6 0.1 collective-permute-start.25
  50.6 6.4 %collective-permute-done.26 = bf16[8,10752]{1,0:T(8,128)(2,1)S(1)} collective-permute-done((bf16[8,10752]{1,0:T(8,128)(2,1)S(1)}, bf16[8,10752]{1,0:T(8,128)(2,1)S(1)}, u32[]{:S(2)}, u32[]{:S(2)}) %collective-permute-start.26) | collective-permute-done | bytes 172064 | tf_op jit(solution)/shard_map/ppermute | solution.py:285
  57.0 0.0 collective-permute-done.7.refs_1_
  57.1 0.0 collective-permute-done.21.refs_2_
  57.1 0.1 shard_map.85.refs_0_
  57.2 2.7 %collective-permute-done.25.refs_1_ = bf16[8,10752]{1,0:T(8,128)(2,1)S(1)} collective-permute-done((bf16[8,10752]{1,0:T(8,128)(2,1)S(1)}, bf16[8,10752]{1,0:T(8,128)(2,1)S(1)}, u32[]{:S(2)}, u32[]{:S(2)}) %collective-permute-start.25) | collective-permute-done | bytes 172064 | tf_op jit(solution)/shard_map/ppermute | solution.py:285
  59.8 1.9 %shard_map.90 = bf16[16,7168]{1,0:T(8,128)(2,1)} custom-call(s32[4]{0:T(128)S(1)} %copy-done.1, s32[2,16]{1,0:T(2,128)S(1)} %bitcast.3, f32[2,16]{1,0:T(2,128)S(1)} %bitcast.4, bf16[8,10752]{1,0:T(8,128)(2,1)S(1)} %shard_map.85.refs_0_, bf16[8,10752]{1,0:T(8,128)(2,1)S(1)} %collective-permute-done.25.refs_1_, f32[8,10752]{1,0:T(8,128)S(1)} %convert_element_type.3.refs_2_, ...), custom_call_target="tpu_custom_call" | custom-call | flops 44040192 | bytes 1146880 | tf_op jit(solution)/shard_map/pallas_call | solution.py:246
  (23 shorter events, 0.2 us)
Async XLA Ops:
  1.5 11.0 %collective-permute-start.3 = (bf16[8,10752]{1,0:T(8,128)(2,1)S(1)}, bf16[8,10752]{1,0:T(8,128)(2,1)S(1)}, u32[]{:S(2)}, u32[]{:S(2)}) collective-permute-start(bf16[8,10752]{1,0:T(8,128)(2,1)S(1)} %get-tuple-element.29), channel_id=1, source_target_pairs={{0,12},{1,13},{2,14},{3,15},{4,8},{5,9},{6,10},{7,11},{8,4},{9,5},... | collective-permute-start | bytes 516104 | tf_op jit(solution)/shard_map/ppermute | solution.py:285
  6.6 6.4 %collective-permute-start = (bf16[8,10752]{1,0:T(8,128)(2,1)S(1)}, bf16[8,10752]{1,0:T(8,128)(2,1)S(1)}, u32[]{:S(2)}, u32[]{:S(2)}) collective-permute-start(bf16[8,10752]{1,0:T(8,128)(2,1)S(1)} %get-tuple-element.28.refs_3_.refs_0_), channel_id=1, source_target_pairs={{0,2},{1,3},{2,0},{3,1},{4,6},{5,7},{6,4},{7,5},{8,10},{9,11},{10,... | collective-permute-start | bytes 516104 | tf_op jit(solution)/shard_map/ppermute | solution.py:288
  12.4 7.0 %collective-permute-start.9 = (bf16[8,10752]{1,0:T(8,128)(2,1)S(1)}, bf16[8,10752]{1,0:T(8,128)(2,1)S(1)}, u32[]{:S(2)}, u32[]{:S(2)}) collective-permute-start(bf16[8,10752]{1,0:T(8,128)(2,1)S(1)} %shard_map.77), channel_id=1, source_target_pairs={{0,4},{1,5},{2,6},{3,7},{4,0},{5,1},{6,2},{7,3},{8,12},{9,13},{10,... | collective-permute-start | bytes 516104 | tf_op jit(solution)/shard_map/ppermute | solution.py:285
  12.4 7.8 %collective-permute-start.4 = (bf16[8,10752]{1,0:T(8,128)(2,1)S(1)}, bf16[8,10752]{1,0:T(8,128)(2,1)S(1)}, u32[]{:S(2)}, u32[]{:S(2)}) collective-permute-start(bf16[8,10752]{1,0:T(8,128)(2,1)S(1)} %collective-permute-done.3.refs_4_.refs_1_), channel_id=1, source_target_pairs={{0,2},{1,3},{2,0},{3,1},{4,6},{5,7},{6,4},{7,5},{8,10},{9,11},{10,... | collective-permute-start | bytes 516104 | tf_op jit(solution)/shard_map/ppermute | solution.py:288
  13.0 10.8 %collective-permute-start.13 = (bf16[8,10752]{1,0:T(8,128)(2,1)S(1)}, bf16[8,10752]{1,0:T(8,128)(2,1)S(1)}, u32[]{:S(2)}, u32[]{:S(2)}) collective-permute-start(bf16[8,10752]{1,0:T(8,128)(2,1)S(1)} %shard_map.78), channel_id=1, source_target_pairs={{0,8},{1,9},{2,10},{3,11},{4,12},{5,13},{6,14},{7,15},{8,0},{9,1},... | collective-permute-start | bytes 516104 | tf_op jit(solution)/shard_map/ppermute | solution.py:285
  19.3 5.4 %collective-permute-start.10 = (bf16[8,10752]{1,0:T(8,128)(2,1)S(1)}, bf16[8,10752]{1,0:T(8,128)(2,1)S(1)}, u32[]{:S(2)}, u32[]{:S(2)}) collective-permute-start(bf16[8,10752]{1,0:T(8,128)(2,1)S(1)} %collective-permute-done.9.refs_0_), channel_id=1, source_target_pairs={{0,2},{1,3},{2,0},{3,1},{4,6},{5,7},{6,4},{7,5},{8,10},{9,11},{10,... | collective-permute-start | bytes 516104 | tf_op jit(solution)/shard_map/ppermute | solution.py:288
  19.7 5.4 %collective-permute-start.1 = (bf16[8,10752]{1,0:T(8,128)(2,1)S(1)}, bf16[8,10752]{1,0:T(8,128)(2,1)S(1)}, u32[]{:S(2)}, u32[]{:S(2)}) collective-permute-start(bf16[8,10752]{1,0:T(8,128)(2,1)S(1)} %get-tuple-element.28.refs_3_.refs_0_), channel_id=1, source_target_pairs={{0,1},{1,0},{2,3},{3,2},{4,5},{5,4},{6,7},{7,6},{8,9},{9,8},{10,11... | collective-permute-start | bytes 516104 | tf_op jit(solution)/shard_map/ppermute | solution.py:291
  19.7 5.4 %collective-permute-start.5 = (bf16[8,10752]{1,0:T(8,128)(2,1)S(1)}, bf16[8,10752]{1,0:T(8,128)(2,1)S(1)}, u32[]{:S(2)}, u32[]{:S(2)}) collective-permute-start(bf16[8,10752]{1,0:T(8,128)(2,1)S(1)} %collective-permute-done.3.refs_4_.refs_1_), channel_id=1, source_target_pairs={{0,1},{1,0},{2,3},{3,2},{4,5},{5,4},{6,7},{7,6},{8,9},{9,8},{10,11... | collective-permute-start | bytes 516104 | tf_op jit(solution)/shard_map/ppermute | solution.py:291
  20.2 4.9 %collective-permute-start.2 = (bf16[8,10752]{1,0:T(8,128)(2,1)S(1)}, bf16[8,10752]{1,0:T(8,128)(2,1)S(1)}, u32[]{:S(2)}, u32[]{:S(2)}) collective-permute-start(bf16[8,10752]{1,0:T(8,128)(2,1)S(1)} %collective-permute-done.refs_1_.refs_2_), channel_id=1, source_target_pairs={{0,1},{1,0},{2,3},{3,2},{4,5},{5,4},{6,7},{7,6},{8,9},{9,8},{10,11... | collective-permute-start | bytes 516104 | tf_op jit(solution)/shard_map/ppermute | solution.py:291
  23.8 1.4 %collective-permute-start.6 = (bf16[8,10752]{1,0:T(8,128)(2,1)S(1)}, bf16[8,10752]{1,0:T(8,128)(2,1)S(1)}, u32[]{:S(2)}, u32[]{:S(2)}) collective-permute-start(bf16[8,10752]{1,0:T(8,128)(2,1)S(1)} %collective-permute-done.4.refs_5_.refs_2_), channel_id=1, source_target_pairs={{0,1},{1,0},{2,3},{3,2},{4,5},{5,4},{6,7},{7,6},{8,9},{9,8},{10,11... | collective-permute-start | bytes 516104 | tf_op jit(solution)/shard_map/ppermute | solution.py:291
  24.7 5.9 %collective-permute-start.14 = (bf16[8,10752]{1,0:T(8,128)(2,1)S(1)}, bf16[8,10752]{1,0:T(8,128)(2,1)S(1)}, u32[]{:S(2)}, u32[]{:S(2)}) collective-permute-start(bf16[8,10752]{1,0:T(8,128)(2,1)S(1)} %shard_map.79.refs_4_), channel_id=1, source_target_pairs={{0,2},{1,3},{2,0},{3,1},{4,6},{5,7},{6,4},{7,5},{8,10},{9,11},{10,... | collective-permute-start | bytes 516104 | tf_op jit(solution)/shard_map/ppermute | solution.py:288
  27.1 3.5 %collective-permute-start.17 = (bf16[8,10752]{1,0:T(8,128)(2,1)S(1)}, bf16[8,10752]{1,0:T(8,128)(2,1)S(1)}, u32[]{:S(2)}, u32[]{:S(2)}) collective-permute-start(bf16[8,10752]{1,0:T(8,128)(2,1)S(1)} %get-tuple-element.40), channel_id=1, source_target_pairs={{0,1},{1,0},{2,3},{3,2},{4,5},{5,4},{6,7},{7,6},{8,9},{9,8},{10,11... | collective-permute-start | bytes 516104 | tf_op jit(solution)/shard_map/ppermute | solution.py:291
  27.3 3.9 %collective-permute-start.11 = (bf16[8,10752]{1,0:T(8,128)(2,1)S(1)}, bf16[8,10752]{1,0:T(8,128)(2,1)S(1)}, u32[]{:S(2)}, u32[]{:S(2)}) collective-permute-start(bf16[8,10752]{1,0:T(8,128)(2,1)S(1)} %collective-permute-done.9.refs_0_), channel_id=1, source_target_pairs={{0,1},{1,0},{2,3},{3,2},{4,5},{5,4},{6,7},{7,6},{8,9},{9,8},{10,11... | collective-permute-start | bytes 516104 | tf_op jit(solution)/shard_map/ppermute | solution.py:291
  27.7 4.2 %collective-permute-start.15 = (bf16[8,10752]{1,0:T(8,128)(2,1)S(1)}, bf16[8,10752]{1,0:T(8,128)(2,1)S(1)}, u32[]{:S(2)}, u32[]{:S(2)}) collective-permute-start(bf16[8,10752]{1,0:T(8,128)(2,1)S(1)} %shard_map.79.refs_4_), channel_id=1, source_target_pairs={{0,1},{1,0},{2,3},{3,2},{4,5},{5,4},{6,7},{7,6},{8,9},{9,8},{10,11... | collective-permute-start | bytes 516104 | tf_op jit(solution)/shard_map/ppermute | solution.py:291
  27.8 4.1 %collective-permute-start.12 = (bf16[8,10752]{1,0:T(8,128)(2,1)S(1)}, bf16[8,10752]{1,0:T(8,128)(2,1)S(1)}, u32[]{:S(2)}, u32[]{:S(2)}) collective-permute-start(bf16[8,10752]{1,0:T(8,128)(2,1)S(1)} %collective-permute-done.10.refs_1_), channel_id=1, source_target_pairs={{0,1},{1,0},{2,3},{3,2},{4,5},{5,4},{6,7},{7,6},{8,9},{9,8},{10,11... | collective-permute-start | bytes 516104 | tf_op jit(solution)/shard_map/ppermute | solution.py:291
  30.6 1.4 %collective-permute-start.16 = (bf16[8,10752]{1,0:T(8,128)(2,1)S(1)}, bf16[8,10752]{1,0:T(8,128)(2,1)S(1)}, u32[]{:S(2)}, u32[]{:S(2)}) collective-permute-start(bf16[8,10752]{1,0:T(8,128)(2,1)S(1)} %collective-permute-done.14.refs_5_), channel_id=1, source_target_pairs={{0,1},{1,0},{2,3},{3,2},{4,5},{5,4},{6,7},{7,6},{8,9},{9,8},{10,11... | collective-permute-start | bytes 516104 | tf_op jit(solution)/shard_map/ppermute | solution.py:291
  30.6 4.0 %collective-permute-start.27 = (bf16[8,10752]{1,0:T(8,128)(2,1)S(1)}, bf16[8,10752]{1,0:T(8,128)(2,1)S(1)}, u32[]{:S(2)}, u32[]{:S(2)}) collective-permute-start(bf16[8,10752]{1,0:T(8,128)(2,1)S(1)} %get-tuple-element.50), channel_id=1, source_target_pairs={{0,1},{1,0},{2,3},{3,2},{4,5},{5,4},{6,7},{7,6},{8,9},{9,8},{10,11... | collective-permute-start | bytes 516104 | tf_op jit(solution)/shard_map/ppermute | solution.py:291
  31.2 6.3 %collective-permute-start.28 = (bf16[8,10752]{1,0:T(8,128)(2,1)S(1)}, bf16[8,10752]{1,0:T(8,128)(2,1)S(1)}, u32[]{:S(2)}, u32[]{:S(2)}) collective-permute-start(bf16[8,10752]{1,0:T(8,128)(2,1)S(1)} %shard_map.80.refs_11_), channel_id=1, source_target_pairs={{0,2},{1,3},{2,0},{3,1},{4,6},{5,7},{6,4},{7,5},{8,10},{9,11},{10,... | collective-permute-start | bytes 516104 | tf_op jit(solution)/shard_map/ppermute | solution.py:288
  33.9 25.9 %copy-start = (s32[16,2]{0,1:T(2,128)S(1)}, s32[16,2]{0,1:T(2,128)}, u32[]{:S(2)}) copy-start(s32[16,2]{0,1:T(2,128)} %param.8) | copy-start | bytes 388
  33.9 25.9 %copy-start.1 = (s32[4]{0:T(128)S(1)}, s32[4]{0:T(128)}, u32[]{:S(2)}) copy-start(s32[4]{0:T(128)} %placement_ref.3) | copy-start | bytes 52
  33.9 25.9 %copy-start.2 = (f32[16,2]{0,1:T(2,128)S(1)}, f32[16,2]{0,1:T(2,128)}, u32[]{:S(2)}) copy-start(f32[16,2]{0,1:T(2,128)} %param.9) | copy-start | bytes 388
  33.9 5.6 %collective-permute-start.19 = (bf16[8,10752]{1,0:T(8,128)(2,1)S(1)}, bf16[8,10752]{1,0:T(8,128)(2,1)S(1)}, u32[]{:S(2)}, u32[]{:S(2)}) collective-permute-start(bf16[8,10752]{1,0:T(8,128)(2,1)S(1)} %get-tuple-element.44), channel_id=1, source_target_pairs={{0,1},{1,0},{2,3},{3,2},{4,5},{5,4},{6,7},{7,6},{8,9},{9,8},{10,11... | collective-permute-start | bytes 516104 | tf_op jit(solution)/shard_map/ppermute | solution.py:291
  34.1 6.0 %collective-permute-start.23 = (bf16[8,10752]{1,0:T(8,128)(2,1)S(1)}, bf16[8,10752]{1,0:T(8,128)(2,1)S(1)}, u32[]{:S(2)}, u32[]{:S(2)}) collective-permute-start(bf16[8,10752]{1,0:T(8,128)(2,1)S(1)} %get-tuple-element.48), channel_id=1, source_target_pairs={{0,1},{1,0},{2,3},{3,2},{4,5},{5,4},{6,7},{7,6},{8,9},{9,8},{10,11... | collective-permute-start | bytes 516104 | tf_op jit(solution)/shard_map/ppermute | solution.py:291
  34.5 5.9 %collective-permute-start.8 = (bf16[8,10752]{1,0:T(8,128)(2,1)S(1)}, bf16[8,10752]{1,0:T(8,128)(2,1)S(1)}, u32[]{:S(2)}, u32[]{:S(2)}) collective-permute-start(bf16[8,10752]{1,0:T(8,128)(2,1)S(1)} %get-tuple-element.36), channel_id=1, source_target_pairs={{0,1},{1,0},{2,3},{3,2},{4,5},{5,4},{6,7},{7,6},{8,9},{9,8},{10,11... | collective-permute-start | bytes 516104 | tf_op jit(solution)/shard_map/ppermute | solution.py:291
  37.6 7.4 %collective-permute-start.29 = (bf16[8,10752]{1,0:T(8,128)(2,1)S(1)}, bf16[8,10752]{1,0:T(8,128)(2,1)S(1)}, u32[]{:S(2)}, u32[]{:S(2)}) collective-permute-start(bf16[8,10752]{1,0:T(8,128)(2,1)S(1)} %shard_map.88), channel_id=1, source_target_pairs={{0,12},{1,13},{2,14},{3,15},{4,8},{5,9},{6,10},{7,11},{8,4},{9,5},... | collective-permute-start | bytes 516104 | tf_op jit(solution)/shard_map/ppermute | solution.py:285
  39.5 5.5 %collective-permute-start.18 = (bf16[8,10752]{1,0:T(8,128)(2,1)S(1)}, bf16[8,10752]{1,0:T(8,128)(2,1)S(1)}, u32[]{:S(2)}, u32[]{:S(2)}) collective-permute-start(bf16[8,10752]{1,0:T(8,128)(2,1)S(1)} %get-tuple-element.42), channel_id=1, source_target_pairs={{0,1},{1,0},{2,3},{3,2},{4,5},{5,4},{6,7},{7,6},{8,9},{9,8},{10,11... | collective-permute-start | bytes 516104 | tf_op jit(solution)/shard_map/ppermute | solution.py:291
  39.6 7.2 %collective-permute-start.20 = (bf16[8,10752]{1,0:T(8,128)(2,1)S(1)}, bf16[8,10752]{1,0:T(8,128)(2,1)S(1)}, u32[]{:S(2)}, u32[]{:S(2)}) collective-permute-start(bf16[8,10752]{1,0:T(8,128)(2,1)S(1)} %shard_map.82), channel_id=1, source_target_pairs={{0,2},{1,3},{2,0},{3,1},{4,6},{5,7},{6,4},{7,5},{8,10},{9,11},{10,... | collective-permute-start | bytes 516104 | tf_op jit(solution)/shard_map/ppermute | solution.py:288
  40.2 6.9 %collective-permute-start.22 = (bf16[8,10752]{1,0:T(8,128)(2,1)S(1)}, bf16[8,10752]{1,0:T(8,128)(2,1)S(1)}, u32[]{:S(2)}, u32[]{:S(2)}) collective-permute-start(bf16[8,10752]{1,0:T(8,128)(2,1)S(1)} %get-tuple-element.46), channel_id=1, source_target_pairs={{0,1},{1,0},{2,3},{3,2},{4,5},{5,4},{6,7},{7,6},{8,9},{9,8},{10,11... | collective-permute-start | bytes 516104 | tf_op jit(solution)/shard_map/ppermute | solution.py:291
  40.5 10.0 %collective-permute-start.24 = (bf16[8,10752]{1,0:T(8,128)(2,1)S(1)}, bf16[8,10752]{1,0:T(8,128)(2,1)S(1)}, u32[]{:S(2)}, u32[]{:S(2)}) collective-permute-start(bf16[8,10752]{1,0:T(8,128)(2,1)S(1)} %shard_map.86), channel_id=1, source_target_pairs={{0,2},{1,3},{2,0},{3,1},{4,6},{5,7},{6,4},{7,5},{8,10},{9,11},{10,... | collective-permute-start | bytes 516104 | tf_op jit(solution)/shard_map/ppermute | solution.py:288
  45.0 12.0 %collective-permute-start.7 = (bf16[8,10752]{1,0:T(8,128)(2,1)S(1)}, bf16[8,10752]{1,0:T(8,128)(2,1)S(1)}, u32[]{:S(2)}, u32[]{:S(2)}) collective-permute-start(bf16[8,10752]{1,0:T(8,128)(2,1)S(1)} %get-tuple-element.34), channel_id=1, source_target_pairs={{0,1},{1,0},{2,3},{3,2},{4,5},{5,4},{6,7},{7,6},{8,9},{9,8},{10,11... | collective-permute-start | bytes 516104 | tf_op jit(solution)/shard_map/ppermute | solution.py:291
  45.0 12.1 %collective-permute-start.30 = (bf16[8,10752]{1,0:T(8,128)(2,1)S(1)}, bf16[8,10752]{1,0:T(8,128)(2,1)S(1)}, u32[]{:S(2)}, u32[]{:S(2)}) collective-permute-start(bf16[8,10752]{1,0:T(8,128)(2,1)S(1)} %shard_map.89), channel_id=1, source_target_pairs={{0,1},{1,0},{2,3},{3,2},{4,5},{5,4},{6,7},{7,6},{8,9},{9,8},{10,11... | collective-permute-start | bytes 516104 | tf_op jit(solution)/shard_map/ppermute | solution.py:291
  46.9 10.1 %collective-permute-start.26 = (bf16[8,10752]{1,0:T(8,128)(2,1)S(1)}, bf16[8,10752]{1,0:T(8,128)(2,1)S(1)}, u32[]{:S(2)}, u32[]{:S(2)}) collective-permute-start(bf16[8,10752]{1,0:T(8,128)(2,1)S(1)} %shard_map.83.refs_1_), channel_id=1, source_target_pairs={{0,8},{1,9},{2,10},{3,11},{4,12},{5,13},{6,14},{7,15},{8,0},{9,1},... | collective-permute-start | bytes 516104 | tf_op jit(solution)/shard_map/ppermute | solution.py:285
  47.1 10.0 %collective-permute-start.21 = (bf16[8,10752]{1,0:T(8,128)(2,1)S(1)}, bf16[8,10752]{1,0:T(8,128)(2,1)S(1)}, u32[]{:S(2)}, u32[]{:S(2)}) collective-permute-start(bf16[8,10752]{1,0:T(8,128)(2,1)S(1)} %shard_map.84), channel_id=1, source_target_pairs={{0,2},{1,3},{2,0},{3,1},{4,6},{5,7},{6,4},{7,5},{8,10},{9,11},{10,... | collective-permute-start | bytes 516104 | tf_op jit(solution)/shard_map/ppermute | solution.py:288
  50.6 9.3 %collective-permute-start.25 = (bf16[8,10752]{1,0:T(8,128)(2,1)S(1)}, bf16[8,10752]{1,0:T(8,128)(2,1)S(1)}, u32[]{:S(2)}, u32[]{:S(2)}) collective-permute-start(bf16[8,10752]{1,0:T(8,128)(2,1)S(1)} %shard_map.87), channel_id=1, source_target_pairs={{0,4},{1,5},{2,6},{3,7},{4,0},{5,1},{6,2},{7,3},{8,12},{9,13},{10,... | collective-permute-start | bytes 516104 | tf_op jit(solution)/shard_map/ppermute | solution.py:285

commit v11 on v10

--- a/solution.py
+++ b/solution.py
@@ -97,10 +97,11 @@
     refs[-1][...] = jnp.zeros_like(refs[-1])
 
 
-def token(after):
+def token(after, percent):
+    rows, width = after.shape
     return pl.pallas_call(
         clear,
-        out_shape=pltpu.VMEM(after.shape, after.dtype),
+        out_shape=pltpu.VMEM((rows, width * percent // 12800 * 128), after.dtype),
         in_specs=[ANYWHERE],
         out_specs=VMEM,
         compiler_params=pltpu.CompilerParams(vmem_limit_bytes=VMEM_BYTES),
@@ -292,7 +293,7 @@
 
     ids = expert_ids.T
     groups = [[n_blocks - d, d] for d in range(1, n_blocks // 2)] + [[n_blocks // 2]]
-    last = groups[-1][0]
+    last, early = groups[-1][0], [group[0] for group in groups[:-1]]
     straight, across, results = {}, {}, {}
     both, home, kept, sent = {}, {}, {}, {}
 
@@ -308,6 +309,8 @@
 
     def go_home(k, after):
         home[k] = add(*kept[k], along_y(when(both[k], after)))
+        if k in early:
+            home[k] = when(home[k], [along_core(token(home[k], 20))])
         results[k] = along_z(home[k], k) if k else home[k]
 
     buckets = list(pack(placement, ids, tokens, n_blocks, parts))
@@ -323,7 +326,7 @@
             compute([0, first], [])
         else:
             previous = groups[g - 1][0]
-            straight[first] = along_z(when(buckets[first], [straight[previous], across[0]]), first)
+            straight[first] = along_z(when(buckets[first], [straight[previous]]), first)
             straight[first] = when(straight[first], [across[second], across[previous]])
             across[first] = along_y(straight[first])
             go_home(previous, [])
@@ -334,8 +337,7 @@
             straight[second] = along_z(when(buckets[second], [weights[0]] if g == 0 else []), second)
             across[second] = along_y(straight[second])
     go_home(last, [])
-    marks = [along_core(token(results[group[0]])) for group in groups[:-1]]
-    results[last] = results[last].astype(jnp.float32)
+    marks = [along_core(token(results[k], 85)) for k in early]
     go_home(0, [home[last]])
     results = [results[k] for k in range(n_blocks)]
     return mix(placement, ids, gates.T, results, marks, n_blocks, parts)

time: 61.9 us -> 60.2 us (0.973)
  waiting for transfers between devices: 28 us -> 19.8 us
  starting transfers between devices: 21.8 us -> 28.2 us
    ppermute x6, waiting for transfers between devices: 18.1 us -> 10.7 us  [along_z(): return lax.ppermute(value, 'node', pairs)]
    ppermute x8, starting transfers between devices: 6.9 us -> 11.5 us  [along_y(): return lax.ppermute(value, 'node', [(i, i ^ 2) for i in range(devices)])]
    ppermute x6, starting transfers between devices: 11.2 us -> 12.7 us  [along_z(): return lax.ppermute(value, 'node', pairs)]
    ppermute x17 -> x18, starting transfers between devices: 3.63 us -> 3.97 us  [along_core(): return lax.ppermute(value, 'node', [(i, i ^ 1) for i in range(devices)])]
  transfers between devices with their start and end apart: 31 -> 32, of which waited for: 12 -> 9; matrix products, arithmetic and copies ran while one was open for 0% -> 0% of each run, Pallas kernels for 14% -> 14%
where the time goes in v11:
time: 60.2 us; the launch traced here: 60 us
  starting transfers between devices  28.2 us (47%)
  waiting for transfers between devices  19.8 us (33%)
  Pallas kernels  11.8 us (20%)
    ppermute x6, starting transfers between devices, along_z(): return lax.ppermute(value, 'node', pairs)  12.7 us
    ppermute x8, starting transfers between devices, along_y(): return lax.ppermute(value, 'node', [(i, i ^ 2) for i in range(devices)])  11.5 us
    ppermute x6, waiting for transfers between devices, along_z(): return lax.ppermute(value, 'node', pairs)  10.7 us
    ppermute x8, waiting for transfers between devices, along_y(): return lax.ppermute(value, 'node', [(i, i ^ 2) for i in range(devices)])  9.03 us
    pallas_call x1, Pallas kernels, load(): pl.pallas_call(load_kernel, out_shape=[pltpu.VMEM(w.shape, w.dtype) for w...  4.24 us
    ppermute x18, starting transfers between devices, along_core(): return lax.ppermute(value, 'node', [(i, i ^ 1) for i in range(devices)])  3.97 us
    pallas_call x2, Pallas kernels, run_experts(): pl.pallas_call(functools.partial(experts_kernel, count), out_shape=[shape...  3.77 us
    pallas_call x1, Pallas kernels, mix(): pl.pallas_call(functools.partial(mix_kernel, n_blocks, parts), out_shape=...  1.85 us
  transfers between devices with their start and end apart: 32, of which 9 were waited for; matrix products, arithmetic and copies ran while one was open for 0% of the time, Pallas kernels for 14%

profile of v11, /device:TPU:0, one launch (start us, length us, event | category | flops | bytes accessed | tf_op | source)
XLA Modules:
  0.0 60.0 jit_solution(9993954691083925042)
XLA Ops:
  0.0 1.5 %shard_map.73 = (bf16[8,10752]{1,0:T(8,128)(2,1)S(1)}, bf16[8,10752]{1,0:T(8,128)(2,1)S(1)}, bf16[8,10752]{1,0:T(8,128)(2,1)S(1)}, bf16[8,10752]{1,0:T(8,128)(2,1)S(1)}) custom-call(s32[4]{0:T(128)} %placement_ref.3, s32[2,16]{1,0:T(2,128)} %bitcast.2, bf16[16,7168]{1,0:T(8,128)(2,1)} %tokens_ref.1), custom_call_target="tpu_custom_call" | custom-call | tf_op jit(solution)/shard_map/pallas_call | solution.py:82
  1.5 5.1 %collective-permute-start.3 = (bf16[8,10752]{1,0:T(8,128)(2,1)S(1)}, bf16[8,10752]{1,0:T(8,128)(2,1)S(1)}, u32[]{:S(2)}, u32[]{:S(2)}) collective-permute-start(bf16[8,10752]{1,0:T(8,128)(2,1)S(1)} %get-tuple-element.29), channel_id=1, source_target_pairs={{0,12},{1,13},{2,14},{3,15},{4,8},{5,9},{6,10},{7,11},{8,4},{9,5},... | collective-permute-start | bytes 516104 | tf_op jit(solution)/shard_map/ppermute | solution.py:286
  6.6 4.2 %shard_map.74 = (bf16[7168,256]{1,0:T(8,128)(2,1)S(1)}, bf16[7168,256]{1,0:T(8,128)(2,1)S(1)}, bf16[256,7168]{1,0:T(8,128)(2,1)S(1)}) custom-call(bf16[7168,256]{1,0:T(8,128)(2,1)} %refs_0_.1, bf16[7168,256]{1,0:T(8,128)(2,1)} %refs_1_.1, bf16[256,7168]{1,0:T(8,128)(2,1)} %refs_2_.1, bf16[8,10752]{1,0:T(8,128)(2,1)S(1)} %get-tuple-element.28.refs_3_.refs_0_), custom_call_target="tpu_custom_call" | custom-call | tf_op jit(solution)/shard_map/pallas_call | solution.py:141
  10.8 0.1 collective-permute-start.9
  10.9 1.6 %collective-permute-start = (bf16[8,10752]{1,0:T(8,128)(2,1)S(1)}, bf16[8,10752]{1,0:T(8,128)(2,1)S(1)}, u32[]{:S(2)}, u32[]{:S(2)}) collective-permute-start(bf16[8,10752]{1,0:T(8,128)(2,1)S(1)} %get-tuple-element.28.refs_3_.refs_0_), channel_id=1, source_target_pairs={{0,2},{1,3},{2,0},{3,1},{4,6},{5,7},{6,4},{7,5},{8,10},{9,11},{10,... | collective-permute-start | bytes 516104 | tf_op jit(solution)/shard_map/ppermute | solution.py:289
  12.5 0.0 collective-permute-done.3.refs_4_.refs_1_
  12.5 2.9 %collective-permute-start.13 = (bf16[8,10752]{1,0:T(8,128)(2,1)S(1)}, bf16[8,10752]{1,0:T(8,128)(2,1)S(1)}, u32[]{:S(2)}, u32[]{:S(2)}) collective-permute-start(bf16[8,10752]{1,0:T(8,128)(2,1)S(1)} %shard_map.78), channel_id=1, source_target_pairs={{0,8},{1,9},{2,10},{3,11},{4,12},{5,13},{6,14},{7,15},{8,0},{9,1},... | collective-permute-start | bytes 516104 | tf_op jit(solution)/shard_map/ppermute | solution.py:286
  15.4 1.5 %collective-permute-start.4 = (bf16[8,10752]{1,0:T(8,128)(2,1)S(1)}, bf16[8,10752]{1,0:T(8,128)(2,1)S(1)}, u32[]{:S(2)}, u32[]{:S(2)}) collective-permute-start(bf16[8,10752]{1,0:T(8,128)(2,1)S(1)} %collective-permute-done.3.refs_4_.refs_1_), channel_id=1, source_target_pairs={{0,2},{1,3},{2,0},{3,1},{4,6},{5,7},{6,4},{7,5},{8,10},{9,11},{10,... | collective-permute-start | bytes 516104 | tf_op jit(solution)/shard_map/ppermute | solution.py:289
  16.9 1.1 %collective-permute-done.9.refs_0_ = bf16[8,10752]{1,0:T(8,128)(2,1)S(1)} collective-permute-done((bf16[8,10752]{1,0:T(8,128)(2,1)S(1)}, bf16[8,10752]{1,0:T(8,128)(2,1)S(1)}, u32[]{:S(2)}, u32[]{:S(2)}) %collective-permute-start.9) | collective-permute-done | bytes 172064 | tf_op jit(solution)/shard_map/ppermute | solution.py:286
  17.9 1.7 %collective-permute-start.10 = (bf16[8,10752]{1,0:T(8,128)(2,1)S(1)}, bf16[8,10752]{1,0:T(8,128)(2,1)S(1)}, u32[]{:S(2)}, u32[]{:S(2)}) collective-permute-start(bf16[8,10752]{1,0:T(8,128)(2,1)S(1)} %collective-permute-done.9.refs_0_), channel_id=1, source_target_pairs={{0,2},{1,3},{2,0},{3,1},{4,6},{5,7},{6,4},{7,5},{8,10},{9,11},{10,... | collective-permute-start | bytes 516104 | tf_op jit(solution)/shard_map/ppermute | solution.py:289
  19.6 0.0 collective-permute-start.1
  19.6 0.0 collective-permute-done.refs_1_
  19.6 0.5 collective-permute-start.5
  20.1 2.6 %collective-permute-done.13.refs_0_ = bf16[8,10752]{1,0:T(8,128)(2,1)S(1)} collective-permute-done((bf16[8,10752]{1,0:T(8,128)(2,1)S(1)}, bf16[8,10752]{1,0:T(8,128)(2,1)S(1)}, u32[]{:S(2)}, u32[]{:S(2)}) %collective-permute-start.13) | collective-permute-done | bytes 172064 | tf_op jit(solution)/shard_map/ppermute | solution.py:286
  22.7 0.0 collective-permute-start.2
  22.7 0.5 collective-permute-start.6
  23.2 1.0 %collective-permute-done.10.refs_1_ = bf16[8,10752]{1,0:T(8,128)(2,1)S(1)} collective-permute-done((bf16[8,10752]{1,0:T(8,128)(2,1)S(1)}, bf16[8,10752]{1,0:T(8,128)(2,1)S(1)}, u32[]{:S(2)}, u32[]{:S(2)}) %collective-permute-start.10) | collective-permute-done | bytes 172064 | tf_op jit(solution)/shard_map/ppermute | solution.py:289
  24.2 1.5 %collective-permute-start.14 = (bf16[8,10752]{1,0:T(8,128)(2,1)S(1)}, bf16[8,10752]{1,0:T(8,128)(2,1)S(1)}, u32[]{:S(2)}, u32[]{:S(2)}) collective-permute-start(bf16[8,10752]{1,0:T(8,128)(2,1)S(1)} %shard_map.79.refs_4_), channel_id=1, source_target_pairs={{0,2},{1,3},{2,0},{3,1},{4,6},{5,7},{6,4},{7,5},{8,10},{9,11},{10,... | collective-permute-start | bytes 516104 | tf_op jit(solution)/shard_map/ppermute | solution.py:289
  25.7 0.0 collective-permute-done.6.refs_7_
  25.7 1.9 %shard_map.75 = (bf16[8,10752]{1,0:T(8,128)(2,1)S(1)}, bf16[8,10752]{1,0:T(8,128)(2,1)S(1)}, bf16[8,10752]{1,0:T(8,128)(2,1)S(1)}, bf16[8,10752]{1,0:T(8,128)(2,...) custom-call(bf16[8,10752]{1,0:T(8,128)(2,1)S(1)} %get-tuple-element., ...), custom_call_target="tpu_custom_call" | custom-call | tf_op jit(solution)/shard_map/pallas_call | solution.py:198
  27.6 0.1 collective-permute-start.17
  27.7 0.5 collective-permute-start.11
  28.2 0.1 collective-permute-start.15
  28.3 0.4 collective-permute-start.12
  28.7 0.9 %collective-permute-done.14.refs_5_ = bf16[8,10752]{1,0:T(8,128)(2,1)S(1)} collective-permute-done((bf16[8,10752]{1,0:T(8,128)(2,1)S(1)}, bf16[8,10752]{1,0:T(8,128)(2,1)S(1)}, u32[]{:S(2)}, u32[]{:S(2)}) %collective-permute-start.14) | collective-permute-done | bytes 172064 | tf_op jit(solution)/shard_map/ppermute | solution.py:289
  29.6 0.0 collective-permute-start.16
  29.6 0.0 collective-permute-done.17.refs_1_
  29.6 0.5 collective-permute-start.27
  30.2 0.0 collective-permute-done.11.refs_2_
  30.2 1.6 %collective-permute-start.28 = (bf16[8,10752]{1,0:T(8,128)(2,1)S(1)}, bf16[8,10752]{1,0:T(8,128)(2,1)S(1)}, u32[]{:S(2)}, u32[]{:S(2)}) collective-permute-start(bf16[8,10752]{1,0:T(8,128)(2,1)S(1)} %shard_map.80.refs_11_), channel_id=1, source_target_pairs={{0,2},{1,3},{2,0},{3,1},{4,6},{5,7},{6,4},{7,5},{8,10},{9,11},{10,... | collective-permute-start | bytes 516104 | tf_op jit(solution)/shard_map/ppermute | solution.py:289
  31.8 0.0 collective-permute-done.16.refs_7_
  31.8 1.9 %shard_map.81 = (bf16[8,10752]{1,0:T(8,128)(2,1)S(1)}, bf16[8,10752]{1,0:T(8,128)(2,1)S(1)}, bf16[8,10752]{1,0:T(8,128)(2,1)S(1)}, bf16[8,10752]{1,0:T(8,128)(2,...) custom-call(bf16[8,10752]{1,0:T(8,128)(2,1)S(1)} %collective-permute, ...), custom_call_target="tpu_custom_call" | custom-call | tf_op jit(solution)/shard_map/pallas_call | solution.py:198
  33.7 0.0 copy-start
  33.7 0.0 copy-start.1
  33.7 0.0 copy-start.2
  33.7 0.1 collective-permute-start.19
  33.8 0.5 collective-permute-start.23
  34.3 0.1 collective-permute-start.8
  34.3 2.2 %collective-permute-done.28.refs_2_ = bf16[8,10752]{1,0:T(8,128)(2,1)S(1)} collective-permute-done((bf16[8,10752]{1,0:T(8,128)(2,1)S(1)}, bf16[8,10752]{1,0:T(8,128)(2,1)S(1)}, u32[]{:S(2)}, u32[]{:S(2)}) %collective-permute-start.28) | collective-permute-done | bytes 172064 | tf_op jit(solution)/shard_map/ppermute | solution.py:289
  36.5 0.1 shard_map.88.refs_0_
  36.6 0.1 collective-permute-start.29
  36.7 0.5 collective-permute-start.18
  37.2 1.6 %collective-permute-start.20 = (bf16[8,10752]{1,0:T(8,128)(2,1)S(1)}, bf16[8,10752]{1,0:T(8,128)(2,1)S(1)}, u32[]{:S(2)}, u32[]{:S(2)}) collective-permute-start(bf16[8,10752]{1,0:T(8,128)(2,1)S(1)} %shard_map.82), channel_id=1, source_target_pairs={{0,2},{1,3},{2,0},{3,1},{4,6},{5,7},{6,4},{7,5},{8,10},{9,11},{10,... | collective-permute-start | bytes 516104 | tf_op jit(solution)/shard_map/ppermute | solution.py:289
  38.8 0.0 collective-permute-start.22
  38.9 0.0 collective-permute-done.29.refs_1_
  38.9 0.6 collective-permute-start.24
  39.4 2.3 %collective-permute-start.30 = (bf16[8,10752]{1,0:T(8,128)(2,1)S(1)}, bf16[8,10752]{1,0:T(8,128)(2,1)S(1)}, u32[]{:S(2)}, u32[]{:S(2)}) collective-permute-start(bf16[8,10752]{1,0:T(8,128)(2,1)S(1)} %shard_map.90), channel_id=1, source_target_pairs={{0,12},{1,13},{2,14},{3,15},{4,8},{5,9},{6,10},{7,11},{8,4},{9,5},... | collective-permute-start | bytes 516104 | tf_op jit(solution)/shard_map/ppermute | solution.py:286
  41.8 0.0 collective-permute-done.18.refs_1_
  41.8 0.1 collective-permute-start.7
  41.9 2.7 %collective-permute-done.20.refs_2_ = bf16[8,10752]{1,0:T(8,128)(2,1)S(1)} collective-permute-done((bf16[8,10752]{1,0:T(8,128)(2,1)S(1)}, bf16[8,10752]{1,0:T(8,128)(2,1)S(1)}, u32[]{:S(2)}, u32[]{:S(2)}) %collective-permute-start.20) | collective-permute-done | bytes 172064 | tf_op jit(solution)/shard_map/ppermute | solution.py:289
  44.5 0.1 shard_map.83.refs_1_
  44.6 0.8 %collective-permute-start.26 = (bf16[8,10752]{1,0:T(8,128)(2,1)S(1)}, bf16[8,10752]{1,0:T(8,128)(2,1)S(1)}, u32[]{:S(2)}, u32[]{:S(2)}) collective-permute-start(bf16[8,10752]{1,0:T(8,128)(2,1)S(1)} %shard_map.83.refs_1_), channel_id=1, source_target_pairs={{0,8},{1,9},{2,10},{3,11},{4,12},{5,13},{6,14},{7,15},{8,0},{9,1},... | collective-permute-start | bytes 516104 | tf_op jit(solution)/shard_map/ppermute | solution.py:286
  45.4 1.5 %collective-permute-start.21 = (bf16[8,10752]{1,0:T(8,128)(2,1)S(1)}, bf16[8,10752]{1,0:T(8,128)(2,1)S(1)}, u32[]{:S(2)}, u32[]{:S(2)}) collective-permute-start(bf16[8,10752]{1,0:T(8,128)(2,1)S(1)} %shard_map.84), channel_id=1, source_target_pairs={{0,2},{1,3},{2,0},{3,1},{4,6},{5,7},{6,4},{7,5},{8,10},{9,11},{10,... | collective-permute-start | bytes 516104 | tf_op jit(solution)/shard_map/ppermute | solution.py:289
  46.9 1.3 %collective-permute-done.24.refs_2_ = bf16[8,10752]{1,0:T(8,128)(2,1)S(1)} collective-permute-done((bf16[8,10752]{1,0:T(8,128)(2,1)S(1)}, bf16[8,10752]{1,0:T(8,128)(2,1)S(1)}, u32[]{:S(2)}, u32[]{:S(2)}) %collective-permute-start.24) | collective-permute-done | bytes 172064 | tf_op jit(solution)/shard_map/ppermute | solution.py:289
  48.2 0.1 shard_map.87
  48.3 1.6 %collective-permute-start.25 = (bf16[8,10752]{1,0:T(8,128)(2,1)S(1)}, bf16[8,10752]{1,0:T(8,128)(2,1)S(1)}, u32[]{:S(2)}, u32[]{:S(2)}) collective-permute-start(bf16[8,10752]{1,0:T(8,128)(2,1)S(1)} %shard_map.87), channel_id=1, source_target_pairs={{0,4},{1,5},{2,6},{3,7},{4,0},{5,1},{6,2},{7,3},{8,12},{9,13},{10,... | collective-permute-start | bytes 516104 | tf_op jit(solution)/shard_map/ppermute | solution.py:286
  49.9 0.0 collective-permute-done.30.refs_0_.refs_3_
  49.9 0.1 collective-permute-start.31
  50.0 0.0 collective-permute-done.7.refs_1_
  50.0 1.0 %collective-permute-done.21.refs_2_ = bf16[8,10752]{1,0:T(8,128)(2,1)S(1)} collective-permute-done((bf16[8,10752]{1,0:T(8,128)(2,1)S(1)}, bf16[8,10752]{1,0:T(8,128)(2,1)S(1)}, u32[]{:S(2)}, u32[]{:S(2)}) %collective-permute-start.21) | collective-permute-done | bytes 172064 | tf_op jit(solution)/shard_map/ppermute | solution.py:289
  51.0 0.1 shard_map.85.refs_0_
  51.1 7.0 %collective-permute-done.26.refs_2_ = bf16[8,10752]{1,0:T(8,128)(2,1)S(1)} collective-permute-done((bf16[8,10752]{1,0:T(8,128)(2,1)S(1)}, bf16[8,10752]{1,0:T(8,128)(2,1)S(1)}, u32[]{:S(2)}, u32[]{:S(2)}) %collective-permute-start.26) | collective-permute-done | bytes 172064 | tf_op jit(solution)/shard_map/ppermute | solution.py:286
  58.1 0.0 collective-permute-done.25.refs_1_
  58.1 1.9 %shard_map.92 = bf16[16,7168]{1,0:T(8,128)(2,1)} custom-call(s32[4]{0:T(128)S(1)} %copy-done.1, s32[2,16]{1,0:T(2,128)S(1)} %bitcast.3, f32[2,16]{1,0:T(2,128)S(1)} %bitcast.4, bf16[8,10752]{1,0:T(8,128)(2,1)S(1)} %shard_map.85.refs_0_, bf16[8,10752]{1,0:T(8,128)(2,1)S(1)} %collective-permute-done.25.refs_1_, ...), custom_call_target="tpu_custom_call" | custom-call | flops 44040192 | bytes 1146880 | tf_op jit(solution)/shard_map/pallas_call | solution.py:247
  (26 shorter events, 0.2 us)
Async XLA Ops:
  1.5 11.0 %collective-permute-start.3 = (bf16[8,10752]{1,0:T(8,128)(2,1)S(1)}, bf16[8,10752]{1,0:T(8,128)(2,1)S(1)}, u32[]{:S(2)}, u32[]{:S(2)}) collective-permute-start(bf16[8,10752]{1,0:T(8,128)(2,1)S(1)} %get-tuple-element.29), channel_id=1, source_target_pairs={{0,12},{1,13},{2,14},{3,15},{4,8},{5,9},{6,10},{7,11},{8,4},{9,5},... | collective-permute-start | bytes 516104 | tf_op jit(solution)/shard_map/ppermute | solution.py:286
  10.8 7.1 %collective-permute-start.9 = (bf16[8,10752]{1,0:T(8,128)(2,1)S(1)}, bf16[8,10752]{1,0:T(8,128)(2,1)S(1)}, u32[]{:S(2)}, u32[]{:S(2)}) collective-permute-start(bf16[8,10752]{1,0:T(8,128)(2,1)S(1)} %shard_map.77), channel_id=1, source_target_pairs={{0,4},{1,5},{2,6},{3,7},{4,0},{5,1},{6,2},{7,3},{8,12},{9,13},{10,... | collective-permute-start | bytes 516104 | tf_op jit(solution)/shard_map/ppermute | solution.py:286
  10.9 8.7 %collective-permute-start = (bf16[8,10752]{1,0:T(8,128)(2,1)S(1)}, bf16[8,10752]{1,0:T(8,128)(2,1)S(1)}, u32[]{:S(2)}, u32[]{:S(2)}) collective-permute-start(bf16[8,10752]{1,0:T(8,128)(2,1)S(1)} %get-tuple-element.28.refs_3_.refs_0_), channel_id=1, source_target_pairs={{0,2},{1,3},{2,0},{3,1},{4,6},{5,7},{6,4},{7,5},{8,10},{9,11},{10,... | collective-permute-start | bytes 516104 | tf_op jit(solution)/shard_map/ppermute | solution.py:289
  12.5 10.2 %collective-permute-start.13 = (bf16[8,10752]{1,0:T(8,128)(2,1)S(1)}, bf16[8,10752]{1,0:T(8,128)(2,1)S(1)}, u32[]{:S(2)}, u32[]{:S(2)}) collective-permute-start(bf16[8,10752]{1,0:T(8,128)(2,1)S(1)} %shard_map.78), channel_id=1, source_target_pairs={{0,8},{1,9},{2,10},{3,11},{4,12},{5,13},{6,14},{7,15},{8,0},{9,1},... | collective-permute-start | bytes 516104 | tf_op jit(solution)/shard_map/ppermute | solution.py:286
  15.4 7.3 %collective-permute-start.4 = (bf16[8,10752]{1,0:T(8,128)(2,1)S(1)}, bf16[8,10752]{1,0:T(8,128)(2,1)S(1)}, u32[]{:S(2)}, u32[]{:S(2)}) collective-permute-start(bf16[8,10752]{1,0:T(8,128)(2,1)S(1)} %collective-permute-done.3.refs_4_.refs_1_), channel_id=1, source_target_pairs={{0,2},{1,3},{2,0},{3,1},{4,6},{5,7},{6,4},{7,5},{8,10},{9,11},{10,... | collective-permute-start | bytes 516104 | tf_op jit(solution)/shard_map/ppermute | solution.py:289
  17.9 6.2 %collective-permute-start.10 = (bf16[8,10752]{1,0:T(8,128)(2,1)S(1)}, bf16[8,10752]{1,0:T(8,128)(2,1)S(1)}, u32[]{:S(2)}, u32[]{:S(2)}) collective-permute-start(bf16[8,10752]{1,0:T(8,128)(2,1)S(1)} %collective-permute-done.9.refs_0_), channel_id=1, source_target_pairs={{0,2},{1,3},{2,0},{3,1},{4,6},{5,7},{6,4},{7,5},{8,10},{9,11},{10,... | collective-permute-start | bytes 516104 | tf_op jit(solution)/shard_map/ppermute | solution.py:289
  19.6 6.1 %collective-permute-start.1 = (bf16[8,10752]{1,0:T(8,128)(2,1)S(1)}, bf16[8,10752]{1,0:T(8,128)(2,1)S(1)}, u32[]{:S(2)}, u32[]{:S(2)}) collective-permute-start(bf16[8,10752]{1,0:T(8,128)(2,1)S(1)} %get-tuple-element.28.refs_3_.refs_0_), channel_id=1, source_target_pairs={{0,1},{1,0},{2,3},{3,2},{4,5},{5,4},{6,7},{7,6},{8,9},{9,8},{10,11... | collective-permute-start | bytes 516104 | tf_op jit(solution)/shard_map/ppermute | solution.py:292
  19.6 6.1 %collective-permute-start.5 = (bf16[8,10752]{1,0:T(8,128)(2,1)S(1)}, bf16[8,10752]{1,0:T(8,128)(2,1)S(1)}, u32[]{:S(2)}, u32[]{:S(2)}) collective-permute-start(bf16[8,10752]{1,0:T(8,128)(2,1)S(1)} %collective-permute-done.3.refs_4_.refs_1_), channel_id=1, source_target_pairs={{0,1},{1,0},{2,3},{3,2},{4,5},{5,4},{6,7},{7,6},{8,9},{9,8},{10,11... | collective-permute-start | bytes 516104 | tf_op jit(solution)/shard_map/ppermute | solution.py:292
  22.7 3.0 %collective-permute-start.2 = (bf16[8,10752]{1,0:T(8,128)(2,1)S(1)}, bf16[8,10752]{1,0:T(8,128)(2,1)S(1)}, u32[]{:S(2)}, u32[]{:S(2)}) collective-permute-start(bf16[8,10752]{1,0:T(8,128)(2,1)S(1)} %collective-permute-done.refs_1_), channel_id=1, source_target_pairs={{0,1},{1,0},{2,3},{3,2},{4,5},{5,4},{6,7},{7,6},{8,9},{9,8},{10,11... | collective-permute-start | bytes 516104 | tf_op jit(solution)/shard_map/ppermute | solution.py:292
  22.7 3.0 %collective-permute-start.6 = (bf16[8,10752]{1,0:T(8,128)(2,1)S(1)}, bf16[8,10752]{1,0:T(8,128)(2,1)S(1)}, u32[]{:S(2)}, u32[]{:S(2)}) collective-permute-start(bf16[8,10752]{1,0:T(8,128)(2,1)S(1)} %collective-permute-done.4.refs_5_.refs_2_), channel_id=1, source_target_pairs={{0,1},{1,0},{2,3},{3,2},{4,5},{5,4},{6,7},{7,6},{8,9},{9,8},{10,11... | collective-permute-start | bytes 516104 | tf_op jit(solution)/shard_map/ppermute | solution.py:292
  24.2 5.4 %collective-permute-start.14 = (bf16[8,10752]{1,0:T(8,128)(2,1)S(1)}, bf16[8,10752]{1,0:T(8,128)(2,1)S(1)}, u32[]{:S(2)}, u32[]{:S(2)}) collective-permute-start(bf16[8,10752]{1,0:T(8,128)(2,1)S(1)} %shard_map.79.refs_4_), channel_id=1, source_target_pairs={{0,2},{1,3},{2,0},{3,1},{4,6},{5,7},{6,4},{7,5},{8,10},{9,11},{10,... | collective-permute-start | bytes 516104 | tf_op jit(solution)/shard_map/ppermute | solution.py:289
  27.6 2.0 %collective-permute-start.17 = (bf16[8,10752]{1,0:T(8,128)(2,1)S(1)}, bf16[8,10752]{1,0:T(8,128)(2,1)S(1)}, u32[]{:S(2)}, u32[]{:S(2)}) collective-permute-start(bf16[8,10752]{1,0:T(8,128)(2,1)S(1)} %get-tuple-element.40), channel_id=1, source_target_pairs={{0,1},{1,0},{2,3},{3,2},{4,5},{5,4},{6,7},{7,6},{8,9},{9,8},{10,11... | collective-permute-start | bytes 516104 | tf_op jit(solution)/shard_map/ppermute | solution.py:292
  27.7 2.5 %collective-permute-start.11 = (bf16[8,10752]{1,0:T(8,128)(2,1)S(1)}, bf16[8,10752]{1,0:T(8,128)(2,1)S(1)}, u32[]{:S(2)}, u32[]{:S(2)}) collective-permute-start(bf16[8,10752]{1,0:T(8,128)(2,1)S(1)} %collective-permute-done.9.refs_0_), channel_id=1, source_target_pairs={{0,1},{1,0},{2,3},{3,2},{4,5},{5,4},{6,7},{7,6},{8,9},{9,8},{10,11... | collective-permute-start | bytes 516104 | tf_op jit(solution)/shard_map/ppermute | solution.py:292
  28.2 3.6 %collective-permute-start.15 = (bf16[8,10752]{1,0:T(8,128)(2,1)S(1)}, bf16[8,10752]{1,0:T(8,128)(2,1)S(1)}, u32[]{:S(2)}, u32[]{:S(2)}) collective-permute-start(bf16[8,10752]{1,0:T(8,128)(2,1)S(1)} %shard_map.79.refs_4_), channel_id=1, source_target_pairs={{0,1},{1,0},{2,3},{3,2},{4,5},{5,4},{6,7},{7,6},{8,9},{9,8},{10,11... | collective-permute-start | bytes 516104 | tf_op jit(solution)/shard_map/ppermute | solution.py:292
  28.3 3.5 %collective-permute-start.12 = (bf16[8,10752]{1,0:T(8,128)(2,1)S(1)}, bf16[8,10752]{1,0:T(8,128)(2,1)S(1)}, u32[]{:S(2)}, u32[]{:S(2)}) collective-permute-start(bf16[8,10752]{1,0:T(8,128)(2,1)S(1)} %collective-permute-done.10.refs_1_), channel_id=1, source_target_pairs={{0,1},{1,0},{2,3},{3,2},{4,5},{5,4},{6,7},{7,6},{8,9},{9,8},{10,11... | collective-permute-start | bytes 516104 | tf_op jit(solution)/shard_map/ppermute | solution.py:292
  29.6 2.2 %collective-permute-start.16 = (bf16[8,10752]{1,0:T(8,128)(2,1)S(1)}, bf16[8,10752]{1,0:T(8,128)(2,1)S(1)}, u32[]{:S(2)}, u32[]{:S(2)}) collective-permute-start(bf16[8,10752]{1,0:T(8,128)(2,1)S(1)} %collective-permute-done.14.refs_5_), channel_id=1, source_target_pairs={{0,1},{1,0},{2,3},{3,2},{4,5},{5,4},{6,7},{7,6},{8,9},{9,8},{10,11... | collective-permute-start | bytes 516104 | tf_op jit(solution)/shard_map/ppermute | solution.py:292
  29.6 4.7 %collective-permute-start.27 = (bf16[8,10752]{1,0:T(8,128)(2,1)S(1)}, bf16[8,10752]{1,0:T(8,128)(2,1)S(1)}, u32[]{:S(2)}, u32[]{:S(2)}) collective-permute-start(bf16[8,10752]{1,0:T(8,128)(2,1)S(1)} %get-tuple-element.50), channel_id=1, source_target_pairs={{0,1},{1,0},{2,3},{3,2},{4,5},{5,4},{6,7},{7,6},{8,9},{9,8},{10,11... | collective-permute-start | bytes 516104 | tf_op jit(solution)/shard_map/ppermute | solution.py:292
  30.2 6.3 %collective-permute-start.28 = (bf16[8,10752]{1,0:T(8,128)(2,1)S(1)}, bf16[8,10752]{1,0:T(8,128)(2,1)S(1)}, u32[]{:S(2)}, u32[]{:S(2)}) collective-permute-start(bf16[8,10752]{1,0:T(8,128)(2,1)S(1)} %shard_map.80.refs_11_), channel_id=1, source_target_pairs={{0,2},{1,3},{2,0},{3,1},{4,6},{5,7},{6,4},{7,5},{8,10},{9,11},{10,... | collective-permute-start | bytes 516104 | tf_op jit(solution)/shard_map/ppermute | solution.py:289
  33.7 24.5 %copy-start = (s32[16,2]{0,1:T(2,128)S(1)}, s32[16,2]{0,1:T(2,128)}, u32[]{:S(2)}) copy-start(s32[16,2]{0,1:T(2,128)} %param.8) | copy-start | bytes 388
  33.7 24.5 %copy-start.1 = (s32[4]{0:T(128)S(1)}, s32[4]{0:T(128)}, u32[]{:S(2)}) copy-start(s32[4]{0:T(128)} %placement_ref.3) | copy-start | bytes 52
  33.7 24.5 %copy-start.2 = (f32[16,2]{0,1:T(2,128)S(1)}, f32[16,2]{0,1:T(2,128)}, u32[]{:S(2)}) copy-start(f32[16,2]{0,1:T(2,128)} %param.9) | copy-start | bytes 388
  33.7 3.5 %collective-permute-start.19 = (bf16[8,10752]{1,0:T(8,128)(2,1)S(1)}, bf16[8,10752]{1,0:T(8,128)(2,1)S(1)}, u32[]{:S(2)}, u32[]{:S(2)}) collective-permute-start(bf16[8,10752]{1,0:T(8,128)(2,1)S(1)} %get-tuple-element.44), channel_id=1, source_target_pairs={{0,1},{1,0},{2,3},{3,2},{4,5},{5,4},{6,7},{7,6},{8,9},{9,8},{10,11... | collective-permute-start | bytes 516104 | tf_op jit(solution)/shard_map/ppermute | solution.py:292
  33.8 5.0 %collective-permute-start.23 = (bf16[8,10752]{1,0:T(8,128)(2,1)S(1)}, bf16[8,10752]{1,0:T(8,128)(2,1)S(1)}, u32[]{:S(2)}, u32[]{:S(2)}) collective-permute-start(bf16[8,10752]{1,0:T(8,128)(2,1)S(1)} %get-tuple-element.48), channel_id=1, source_target_pairs={{0,1},{1,0},{2,3},{3,2},{4,5},{5,4},{6,7},{7,6},{8,9},{9,8},{10,11... | collective-permute-start | bytes 516104 | tf_op jit(solution)/shard_map/ppermute | solution.py:292
  34.3 5.2 %collective-permute-start.8 = (bf16[8,10752]{1,0:T(8,128)(2,1)S(1)}, bf16[8,10752]{1,0:T(8,128)(2,1)S(1)}, u32[]{:S(2)}, u32[]{:S(2)}) collective-permute-start(bf16[8,10752]{1,0:T(8,128)(2,1)S(1)} %get-tuple-element.36), channel_id=1, source_target_pairs={{0,1},{1,0},{2,3},{3,2},{4,5},{5,4},{6,7},{7,6},{8,9},{9,8},{10,11... | collective-permute-start | bytes 516104 | tf_op jit(solution)/shard_map/ppermute | solution.py:292
  36.6 2.3 %collective-permute-start.29 = (bf16[8,2048]{1,0:T(8,128)(2,1)S(1)}, bf16[8,2048]{1,0:T(8,128)(2,1)S(1)}, u32[]{:S(2)}, u32[]{:S(2)}) collective-permute-start(bf16[8,2048]{1,0:T(8,128)(2,1)S(1)} %shard_map.89), channel_id=1, source_target_pairs={{0,1},{1,0},{2,3},{3,2},{4,5},{5,4},{6,7},{7,6},{8,9},{9,8},{10,11... | collective-permute-start | bytes 98312 | tf_op jit(solution)/shard_map/ppermute | solution.py:292
  36.7 5.1 %collective-permute-start.18 = (bf16[8,10752]{1,0:T(8,128)(2,1)S(1)}, bf16[8,10752]{1,0:T(8,128)(2,1)S(1)}, u32[]{:S(2)}, u32[]{:S(2)}) collective-permute-start(bf16[8,10752]{1,0:T(8,128)(2,1)S(1)} %get-tuple-element.42), channel_id=1, source_target_pairs={{0,1},{1,0},{2,3},{3,2},{4,5},{5,4},{6,7},{7,6},{8,9},{9,8},{10,11... | collective-permute-start | bytes 516104 | tf_op jit(solution)/shard_map/ppermute | solution.py:292
  37.2 7.3 %collective-permute-start.20 = (bf16[8,10752]{1,0:T(8,128)(2,1)S(1)}, bf16[8,10752]{1,0:T(8,128)(2,1)S(1)}, u32[]{:S(2)}, u32[]{:S(2)}) collective-permute-start(bf16[8,10752]{1,0:T(8,128)(2,1)S(1)} %shard_map.82), channel_id=1, source_target_pairs={{0,2},{1,3},{2,0},{3,1},{4,6},{5,7},{6,4},{7,5},{8,10},{9,11},{10,... | collective-permute-start | bytes 516104 | tf_op jit(solution)/shard_map/ppermute | solution.py:289
  38.8 6.6 %collective-permute-start.22 = (bf16[8,10752]{1,0:T(8,128)(2,1)S(1)}, bf16[8,10752]{1,0:T(8,128)(2,1)S(1)}, u32[]{:S(2)}, u32[]{:S(2)}) collective-permute-start(bf16[8,10752]{1,0:T(8,128)(2,1)S(1)} %get-tuple-element.46), channel_id=1, source_target_pairs={{0,1},{1,0},{2,3},{3,2},{4,5},{5,4},{6,7},{7,6},{8,9},{9,8},{10,11... | collective-permute-start | bytes 516104 | tf_op jit(solution)/shard_map/ppermute | solution.py:292
  38.9 9.3 %collective-permute-start.24 = (bf16[8,10752]{1,0:T(8,128)(2,1)S(1)}, bf16[8,10752]{1,0:T(8,128)(2,1)S(1)}, u32[]{:S(2)}, u32[]{:S(2)}) collective-permute-start(bf16[8,10752]{1,0:T(8,128)(2,1)S(1)} %shard_map.86), channel_id=1, source_target_pairs={{0,2},{1,3},{2,0},{3,1},{4,6},{5,7},{6,4},{7,5},{8,10},{9,11},{10,... | collective-permute-start | bytes 516104 | tf_op jit(solution)/shard_map/ppermute | solution.py:289
  39.4 10.5 %collective-permute-start.30 = (bf16[8,10752]{1,0:T(8,128)(2,1)S(1)}, bf16[8,10752]{1,0:T(8,128)(2,1)S(1)}, u32[]{:S(2)}, u32[]{:S(2)}) collective-permute-start(bf16[8,10752]{1,0:T(8,128)(2,1)S(1)} %shard_map.90), channel_id=1, source_target_pairs={{0,12},{1,13},{2,14},{3,15},{4,8},{5,9},{6,10},{7,11},{8,4},{9,5},... | collective-permute-start | bytes 516104 | tf_op jit(solution)/shard_map/ppermute | solution.py:286
  41.8 8.2 %collective-permute-start.7 = (bf16[8,10752]{1,0:T(8,128)(2,1)S(1)}, bf16[8,10752]{1,0:T(8,128)(2,1)S(1)}, u32[]{:S(2)}, u32[]{:S(2)}) collective-permute-start(bf16[8,10752]{1,0:T(8,128)(2,1)S(1)} %get-tuple-element.34), channel_id=1, source_target_pairs={{0,1},{1,0},{2,3},{3,2},{4,5},{5,4},{6,7},{7,6},{8,9},{9,8},{10,11... | collective-permute-start | bytes 516104 | tf_op jit(solution)/shard_map/ppermute | solution.py:292
  44.6 13.5 %collective-permute-start.26 = (bf16[8,10752]{1,0:T(8,128)(2,1)S(1)}, bf16[8,10752]{1,0:T(8,128)(2,1)S(1)}, u32[]{:S(2)}, u32[]{:S(2)}) collective-permute-start(bf16[8,10752]{1,0:T(8,128)(2,1)S(1)} %shard_map.83.refs_1_), channel_id=1, source_target_pairs={{0,8},{1,9},{2,10},{3,11},{4,12},{5,13},{6,14},{7,15},{8,0},{9,1},... | collective-permute-start | bytes 516104 | tf_op jit(solution)/shard_map/ppermute | solution.py:286
  45.4 5.6 %collective-permute-start.21 = (bf16[8,10752]{1,0:T(8,128)(2,1)S(1)}, bf16[8,10752]{1,0:T(8,128)(2,1)S(1)}, u32[]{:S(2)}, u32[]{:S(2)}) collective-permute-start(bf16[8,10752]{1,0:T(8,128)(2,1)S(1)} %shard_map.84), channel_id=1, source_target_pairs={{0,2},{1,3},{2,0},{3,1},{4,6},{5,7},{6,4},{7,5},{8,10},{9,11},{10,... | collective-permute-start | bytes 516104 | tf_op jit(solution)/shard_map/ppermute | solution.py:289
  48.3 9.8 %collective-permute-start.25 = (bf16[8,10752]{1,0:T(8,128)(2,1)S(1)}, bf16[8,10752]{1,0:T(8,128)(2,1)S(1)}, u32[]{:S(2)}, u32[]{:S(2)}) collective-permute-start(bf16[8,10752]{1,0:T(8,128)(2,1)S(1)} %shard_map.87), channel_id=1, source_target_pairs={{0,4},{1,5},{2,6},{3,7},{4,0},{5,1},{6,2},{7,3},{8,12},{9,13},{10,... | collective-permute-start | bytes 516104 | tf_op jit(solution)/shard_map/ppermute | solution.py:286
  49.9 8.2 %collective-permute-start.31 = (bf16[8,9088]{1,0:T(8,128)(2,1)S(1)}, bf16[8,9088]{1,0:T(8,128)(2,1)S(1)}, u32[]{:S(2)}, u32[]{:S(2)}) collective-permute-start(bf16[8,9088]{1,0:T(8,128)(2,1)S(1)} %shard_map.91), channel_id=1, source_target_pairs={{0,1},{1,0},{2,3},{3,2},{4,5},{5,4},{6,7},{7,6},{8,9},{9,8},{10,11... | collective-permute-start | bytes 436232 | tf_op jit(solution)/shard_map/ppermute | solution.py:292

commit v12 on v11

--- a/solution.py
+++ b/solution.py
@@ -12,6 +12,8 @@
 SMEM = pl.BlockSpec(memory_space=pltpu.SMEM)
 ANYWHERE = pl.BlockSpec(memory_space=pl.ANY)
 LOADS = 4
+EXTRA = 512
+SHARE = 94
 N1, N2, N3, N4 = 30,30,30,30
 NO_COST = pl.CostEstimate(flops=0, bytes_accessed=0, transcendentals=0)
 
@@ -232,7 +234,7 @@
         lhs = jnp.concatenate([high, mid, low], axis=1)
         pieces = []
         for r in results:
-            pieces += [r[:, side * middle : (side + 1) * middle], r[:, width:]]
+            pieces += [r[:, side * middle : (side + 1) * middle], r[:, width : width + middle]]
         rhs = jnp.concatenate([p.astype(jnp.bfloat16) for p in pieces], axis=0)
         value = lax.dot_general(
             lhs, rhs, (((0,), (0,)), ((), ())), preferred_element_type=jnp.float32
@@ -262,13 +264,17 @@
     total = refs[0][...].astype(jnp.float32)
     for ref in refs[1:-1]:
         total = total + ref[...].astype(jnp.float32)
-    refs[-1][...] = total.astype(refs[-1].dtype)
-
-
-def add(*values):
+    width = total.shape[1]
+    refs[-1][:, :width] = total.astype(refs[-1].dtype)
+    if refs[-1].shape[1] > width:
+        refs[-1][:, width:] = jnp.zeros_like(refs[-1][:, width:])
+
+
+def add(*values, extra=0):
+    rows, width = values[0].shape
     return pl.pallas_call(
         add_kernel,
-        out_shape=pltpu.VMEM(values[0].shape, values[0].dtype),
+        out_shape=pltpu.VMEM((rows, width + extra), values[0].dtype),
         in_specs=[VMEM] * len(values),
         out_specs=VMEM,
         compiler_params=pltpu.CompilerParams(vmem_limit_bytes=VMEM_BYTES),
@@ -308,9 +314,8 @@
             kept[k] = out[4 * i], along_core(out[4 * i + 2])
 
     def go_home(k, after):
-        home[k] = add(*kept[k], along_y(when(both[k], after)))
-        if k in early:
-            home[k] = when(home[k], [along_core(token(home[k], 20))])
+        back = along_y(when(both[k], after))
+        home[k] = add(*kept[k], back, extra=EXTRA if k in early else 0)
         results[k] = along_z(home[k], k) if k else home[k]
 
     buckets = list(pack(placement, ids, tokens, n_blocks, parts))
@@ -337,7 +342,7 @@
             straight[second] = along_z(when(buckets[second], [weights[0]] if g == 0 else []), second)
             across[second] = along_y(straight[second])
     go_home(last, [])
-    marks = [along_core(token(results[k], 85)) for k in early]
+    marks = [along_core(token(results[k], SHARE)) for k in early]
     go_home(0, [home[last]])
     results = [results[k] for k in range(n_blocks)]
     return mix(placement, ids, gates.T, results, marks, n_blocks, parts)

time: 60.2 us -> 61.2 us (1.017)
  waiting for transfers between devices: 19.8 us -> 22.4 us
  starting transfers between devices: 28.2 us -> 26.6 us
    ppermute x8, waiting for transfers between devices: 9.03 us -> 12.8 us  [along_y(): return lax.ppermute(value, 'node', [(i, i ^ 2) for i in range(devices)])]
    ppermute x6, starting transfers between devices: 12.7 us -> 11.5 us  [along_z(): return lax.ppermute(value, 'node', pairs)]
    ppermute x6, waiting for transfers between devices: 10.7 us -> 9.53 us  [along_z(): return lax.ppermute(value, 'node', pairs)]
    ppermute x18 -> x17, starting transfers between devices: 3.97 us -> 3.63 us  [along_core(): return lax.ppermute(value, 'node', [(i, i ^ 1) for i in range(devices)])]
  transfers between devices with their start and end apart: 32 -> 31, of which waited for: 9 -> 10; matrix products, arithmetic and copies ran while one was open for 0% -> 0% of each run, Pallas kernels for 14% -> 14%
where the time goes in v12:
time: 61.2 us; the launch traced here: 61 us
  starting transfers between devices  26.6 us (43%)
  waiting for transfers between devices  22.4 us (37%)
  Pallas kernels  11.8 us (19%)
    ppermute x8, waiting for transfers between devices, along_y(): return lax.ppermute(value, 'node', [(i, i ^ 2) for i in range(devices)])  12.8 us
    ppermute x8, starting transfers between devices, along_y(): return lax.ppermute(value, 'node', [(i, i ^ 2) for i in range(devices)])  11.5 us
    ppermute x6, starting transfers between devices, along_z(): return lax.ppermute(value, 'node', pairs)  11.5 us
    ppermute x6, waiting for transfers between devices, along_z(): return lax.ppermute(value, 'node', pairs)  9.53 us
    pallas_call x1, Pallas kernels, load(): pl.pallas_call(load_kernel, out_shape=[pltpu.VMEM(w.shape, w.dtype) for w...  4.24 us
    pallas_call x2, Pallas kernels, run_experts(): pl.pallas_call(functools.partial(experts_kernel, count), out_shape=[shape...  3.77 us
    ppermute x17, starting transfers between devices, along_core(): return lax.ppermute(value, 'node', [(i, i ^ 1) for i in range(devices)])  3.63 us
    pallas_call x1, Pallas kernels, mix(): pl.pallas_call(functools.partial(mix_kernel, n_blocks, parts), out_shape=...  1.85 us
  transfers between devices with their start and end apart: 31, of which 10 were waited for; matrix products, arithmetic and copies ran while one was open for 0% of the time, Pallas kernels for 14%

profile of v12, /device:TPU:0, one launch (start us, length us, event | category | flops | bytes accessed | tf_op | source)
XLA Modules:
  0.0 61.0 jit_solution(2407405464265251110)
XLA Ops:
  0.0 1.5 %shard_map.73 = (bf16[8,10752]{1,0:T(8,128)(2,1)S(1)}, bf16[8,10752]{1,0:T(8,128)(2,1)S(1)}, bf16[8,10752]{1,0:T(8,128)(2,1)S(1)}, bf16[8,10752]{1,0:T(8,128)(2,1)S(1)}) custom-call(s32[4]{0:T(128)} %placement_ref.3, s32[2,16]{1,0:T(2,128)} %bitcast.2, bf16[16,7168]{1,0:T(8,128)(2,1)} %tokens_ref.1), custom_call_target="tpu_custom_call" | custom-call | tf_op jit(solution)/shard_map/pallas_call | solution.py:84
  1.5 5.1 %collective-permute-start.3 = (bf16[8,10752]{1,0:T(8,128)(2,1)S(1)}, bf16[8,10752]{1,0:T(8,128)(2,1)S(1)}, u32[]{:S(2)}, u32[]{:S(2)}) collective-permute-start(bf16[8,10752]{1,0:T(8,128)(2,1)S(1)} %get-tuple-element.29), channel_id=1, source_target_pairs={{0,12},{1,13},{2,14},{3,15},{4,8},{5,9},{6,10},{7,11},{8,4},{9,5},... | collective-permute-start | bytes 516104 | tf_op jit(solution)/shard_map/ppermute | solution.py:292
  6.6 4.2 %shard_map.74 = (bf16[7168,256]{1,0:T(8,128)(2,1)S(1)}, bf16[7168,256]{1,0:T(8,128)(2,1)S(1)}, bf16[256,7168]{1,0:T(8,128)(2,1)S(1)}) custom-call(bf16[7168,256]{1,0:T(8,128)(2,1)} %refs_0_.1, bf16[7168,256]{1,0:T(8,128)(2,1)} %refs_1_.1, bf16[256,7168]{1,0:T(8,128)(2,1)} %refs_2_.1, bf16[8,10752]{1,0:T(8,128)(2,1)S(1)} %get-tuple-element.28.refs_3_.refs_0_), custom_call_target="tpu_custom_call" | custom-call | tf_op jit(solution)/shard_map/pallas_call | solution.py:143
  10.8 0.1 collective-permute-start.9
  10.9 1.6 %collective-permute-start = (bf16[8,10752]{1,0:T(8,128)(2,1)S(1)}, bf16[8,10752]{1,0:T(8,128)(2,1)S(1)}, u32[]{:S(2)}, u32[]{:S(2)}) collective-permute-start(bf16[8,10752]{1,0:T(8,128)(2,1)S(1)} %get-tuple-element.28.refs_3_.refs_0_), channel_id=1, source_target_pairs={{0,2},{1,3},{2,0},{3,1},{4,6},{5,7},{6,4},{7,5},{8,10},{9,11},{10,... | collective-permute-start | bytes 516104 | tf_op jit(solution)/shard_map/ppermute | solution.py:295
  12.5 0.0 collective-permute-done.3.refs_4_.refs_1_
  12.5 2.9 %collective-permute-start.13 = (bf16[8,10752]{1,0:T(8,128)(2,1)S(1)}, bf16[8,10752]{1,0:T(8,128)(2,1)S(1)}, u32[]{:S(2)}, u32[]{:S(2)}) collective-permute-start(bf16[8,10752]{1,0:T(8,128)(2,1)S(1)} %shard_map.78), channel_id=1, source_target_pairs={{0,8},{1,9},{2,10},{3,11},{4,12},{5,13},{6,14},{7,15},{8,0},{9,1},... | collective-permute-start | bytes 516104 | tf_op jit(solution)/shard_map/ppermute | solution.py:292
  15.4 1.5 %collective-permute-start.4 = (bf16[8,10752]{1,0:T(8,128)(2,1)S(1)}, bf16[8,10752]{1,0:T(8,128)(2,1)S(1)}, u32[]{:S(2)}, u32[]{:S(2)}) collective-permute-start(bf16[8,10752]{1,0:T(8,128)(2,1)S(1)} %collective-permute-done.3.refs_4_.refs_1_), channel_id=1, source_target_pairs={{0,2},{1,3},{2,0},{3,1},{4,6},{5,7},{6,4},{7,5},{8,10},{9,11},{10,... | collective-permute-start | bytes 516104 | tf_op jit(solution)/shard_map/ppermute | solution.py:295
  16.9 1.1 %collective-permute-done.9.refs_0_ = bf16[8,10752]{1,0:T(8,128)(2,1)S(1)} collective-permute-done((bf16[8,10752]{1,0:T(8,128)(2,1)S(1)}, bf16[8,10752]{1,0:T(8,128)(2,1)S(1)}, u32[]{:S(2)}, u32[]{:S(2)}) %collective-permute-start.9) | collective-permute-done | bytes 172064 | tf_op jit(solution)/shard_map/ppermute | solution.py:292
  17.9 1.7 %collective-permute-start.10 = (bf16[8,10752]{1,0:T(8,128)(2,1)S(1)}, bf16[8,10752]{1,0:T(8,128)(2,1)S(1)}, u32[]{:S(2)}, u32[]{:S(2)}) collective-permute-start(bf16[8,10752]{1,0:T(8,128)(2,1)S(1)} %collective-permute-done.9.refs_0_), channel_id=1, source_target_pairs={{0,2},{1,3},{2,0},{3,1},{4,6},{5,7},{6,4},{7,5},{8,10},{9,11},{10,... | collective-permute-start | bytes 516104 | tf_op jit(solution)/shard_map/ppermute | solution.py:295
  19.6 0.0 collective-permute-start.1
  19.6 0.0 collective-permute-done.refs_1_
  19.6 0.5 collective-permute-start.5
  20.1 2.6 %collective-permute-done.13.refs_0_ = bf16[8,10752]{1,0:T(8,128)(2,1)S(1)} collective-permute-done((bf16[8,10752]{1,0:T(8,128)(2,1)S(1)}, bf16[8,10752]{1,0:T(8,128)(2,1)S(1)}, u32[]{:S(2)}, u32[]{:S(2)}) %collective-permute-start.13) | collective-permute-done | bytes 172064 | tf_op jit(solution)/shard_map/ppermute | solution.py:292
  22.7 0.0 collective-permute-start.2
  22.7 0.5 collective-permute-start.6
  23.2 1.0 %collective-permute-done.10.refs_1_ = bf16[8,10752]{1,0:T(8,128)(2,1)S(1)} collective-permute-done((bf16[8,10752]{1,0:T(8,128)(2,1)S(1)}, bf16[8,10752]{1,0:T(8,128)(2,1)S(1)}, u32[]{:S(2)}, u32[]{:S(2)}) %collective-permute-start.10) | collective-permute-done | bytes 172064 | tf_op jit(solution)/shard_map/ppermute | solution.py:295
  24.2 1.5 %collective-permute-start.14 = (bf16[8,10752]{1,0:T(8,128)(2,1)S(1)}, bf16[8,10752]{1,0:T(8,128)(2,1)S(1)}, u32[]{:S(2)}, u32[]{:S(2)}) collective-permute-start(bf16[8,10752]{1,0:T(8,128)(2,1)S(1)} %shard_map.79.refs_4_), channel_id=1, source_target_pairs={{0,2},{1,3},{2,0},{3,1},{4,6},{5,7},{6,4},{7,5},{8,10},{9,11},{10,... | collective-permute-start | bytes 516104 | tf_op jit(solution)/shard_map/ppermute | solution.py:295
  25.7 0.0 collective-permute-done.6.refs_7_
  25.7 1.9 %shard_map.75 = (bf16[8,10752]{1,0:T(8,128)(2,1)S(1)}, bf16[8,10752]{1,0:T(8,128)(2,1)S(1)}, bf16[8,10752]{1,0:T(8,128)(2,1)S(1)}, bf16[8,10752]{1,0:T(8,128)(2,...) custom-call(bf16[8,10752]{1,0:T(8,128)(2,1)S(1)} %get-tuple-element., ...), custom_call_target="tpu_custom_call" | custom-call | tf_op jit(solution)/shard_map/pallas_call | solution.py:200
  27.6 0.1 collective-permute-start.17
  27.7 0.5 collective-permute-start.11
  28.2 0.1 collective-permute-start.15
  28.3 0.4 collective-permute-start.12
  28.7 0.9 %collective-permute-done.14.refs_5_ = bf16[8,10752]{1,0:T(8,128)(2,1)S(1)} collective-permute-done((bf16[8,10752]{1,0:T(8,128)(2,1)S(1)}, bf16[8,10752]{1,0:T(8,128)(2,1)S(1)}, u32[]{:S(2)}, u32[]{:S(2)}) %collective-permute-start.14) | collective-permute-done | bytes 172064 | tf_op jit(solution)/shard_map/ppermute | solution.py:295
  29.6 0.0 collective-permute-start.16
  29.6 0.0 collective-permute-done.17.refs_1_
  29.6 0.5 collective-permute-start.27
  30.2 0.0 collective-permute-done.11.refs_2_
  30.2 1.6 %collective-permute-start.28 = (bf16[8,10752]{1,0:T(8,128)(2,1)S(1)}, bf16[8,10752]{1,0:T(8,128)(2,1)S(1)}, u32[]{:S(2)}, u32[]{:S(2)}) collective-permute-start(bf16[8,10752]{1,0:T(8,128)(2,1)S(1)} %shard_map.80.refs_11_), channel_id=1, source_target_pairs={{0,2},{1,3},{2,0},{3,1},{4,6},{5,7},{6,4},{7,5},{8,10},{9,11},{10,... | collective-permute-start | bytes 516104 | tf_op jit(solution)/shard_map/ppermute | solution.py:295
  31.8 0.0 collective-permute-done.16.refs_7_
  31.8 1.9 %shard_map.81 = (bf16[8,10752]{1,0:T(8,128)(2,1)S(1)}, bf16[8,10752]{1,0:T(8,128)(2,1)S(1)}, bf16[8,10752]{1,0:T(8,128)(2,1)S(1)}, bf16[8,10752]{1,0:T(8,128)(2,...) custom-call(bf16[8,10752]{1,0:T(8,128)(2,1)S(1)} %collective-permute, ...), custom_call_target="tpu_custom_call" | custom-call | tf_op jit(solution)/shard_map/pallas_call | solution.py:200
  33.7 0.0 copy-start
  33.7 0.0 copy-start.1
  33.7 0.0 copy-start.2
  33.7 0.1 collective-permute-start.19
  33.8 0.5 collective-permute-start.23
  34.3 0.1 collective-permute-start.8
  34.3 2.2 %collective-permute-done.28.refs_2_ = bf16[8,10752]{1,0:T(8,128)(2,1)S(1)} collective-permute-done((bf16[8,10752]{1,0:T(8,128)(2,1)S(1)}, bf16[8,10752]{1,0:T(8,128)(2,1)S(1)}, u32[]{:S(2)}, u32[]{:S(2)}) %collective-permute-start.28) | collective-permute-done | bytes 172064 | tf_op jit(solution)/shard_map/ppermute | solution.py:295
  36.5 0.1 shard_map.88
  36.6 2.3 %collective-permute-start.29 = (bf16[8,11264]{1,0:T(8,128)(2,1)S(1)}, bf16[8,11264]{1,0:T(8,128)(2,1)S(1)}, u32[]{:S(2)}, u32[]{:S(2)}) collective-permute-start(bf16[8,11264]{1,0:T(8,128)(2,1)S(1)} %shard_map.88), channel_id=1, source_target_pairs={{0,12},{1,13},{2,14},{3,15},{4,8},{5,9},{6,10},{7,11},{8,4},{9,5},... | collective-permute-start | bytes 540680 | tf_op jit(solution)/shard_map/ppermute | solution.py:292
  39.0 1.6 %collective-permute-start.20 = (bf16[8,10752]{1,0:T(8,128)(2,1)S(1)}, bf16[8,10752]{1,0:T(8,128)(2,1)S(1)}, u32[]{:S(2)}, u32[]{:S(2)}) collective-permute-start(bf16[8,10752]{1,0:T(8,128)(2,1)S(1)} %shard_map.82), channel_id=1, source_target_pairs={{0,2},{1,3},{2,0},{3,1},{4,6},{5,7},{6,4},{7,5},{8,10},{9,11},{10,... | collective-permute-start | bytes 516104 | tf_op jit(solution)/shard_map/ppermute | solution.py:295
  40.5 0.0 collective-permute-done.23.refs_1_
  40.5 0.2 collective-permute-start.22
  40.8 0.0 collective-permute-done.8.refs_1_
  40.8 0.6 collective-permute-start.24
  41.5 0.0 collective-permute-done.18.refs_1_
  41.5 0.1 collective-permute-start.7
  41.6 4.7 %collective-permute-done.20.refs_2_ = bf16[8,10752]{1,0:T(8,128)(2,1)S(1)} collective-permute-done((bf16[8,10752]{1,0:T(8,128)(2,1)S(1)}, bf16[8,10752]{1,0:T(8,128)(2,1)S(1)}, u32[]{:S(2)}, u32[]{:S(2)}) %collective-permute-start.20) | collective-permute-done | bytes 172064 | tf_op jit(solution)/shard_map/ppermute | solution.py:295
  46.2 0.1 shard_map.83.refs_1_
  46.3 0.9 %collective-permute-start.26 = (bf16[8,10752]{1,0:T(8,128)(2,1)S(1)}, bf16[8,10752]{1,0:T(8,128)(2,1)S(1)}, u32[]{:S(2)}, u32[]{:S(2)}) collective-permute-start(bf16[8,10752]{1,0:T(8,128)(2,1)S(1)} %shard_map.83.refs_1_), channel_id=1, source_target_pairs={{0,8},{1,9},{2,10},{3,11},{4,12},{5,13},{6,14},{7,15},{8,0},{9,1},... | collective-permute-start | bytes 516104 | tf_op jit(solution)/shard_map/ppermute | solution.py:292
  47.2 1.5 %collective-permute-start.21 = (bf16[8,10752]{1,0:T(8,128)(2,1)S(1)}, bf16[8,10752]{1,0:T(8,128)(2,1)S(1)}, u32[]{:S(2)}, u32[]{:S(2)}) collective-permute-start(bf16[8,10752]{1,0:T(8,128)(2,1)S(1)} %shard_map.84), channel_id=1, source_target_pairs={{0,2},{1,3},{2,0},{3,1},{4,6},{5,7},{6,4},{7,5},{8,10},{9,11},{10,... | collective-permute-start | bytes 516104 | tf_op jit(solution)/shard_map/ppermute | solution.py:295
  48.7 1.2 %collective-permute-done.24.refs_2_ = bf16[8,10752]{1,0:T(8,128)(2,1)S(1)} collective-permute-done((bf16[8,10752]{1,0:T(8,128)(2,1)S(1)}, bf16[8,10752]{1,0:T(8,128)(2,1)S(1)}, u32[]{:S(2)}, u32[]{:S(2)}) %collective-permute-start.24) | collective-permute-done | bytes 172064 | tf_op jit(solution)/shard_map/ppermute | solution.py:295
  49.9 0.1 shard_map.87
  50.0 0.2 collective-permute-start.25
  50.1 0.0 collective-permute-done.29.refs_0_.refs_3_
  50.1 0.1 collective-permute-start.30
  50.2 0.0 collective-permute-done.7.refs_1_
  50.2 3.0 %collective-permute-done.21.refs_2_ = bf16[8,10752]{1,0:T(8,128)(2,1)S(1)} collective-permute-done((bf16[8,10752]{1,0:T(8,128)(2,1)S(1)}, bf16[8,10752]{1,0:T(8,128)(2,1)S(1)}, u32[]{:S(2)}, u32[]{:S(2)}) %collective-permute-start.21) | collective-permute-done | bytes 172064 | tf_op jit(solution)/shard_map/ppermute | solution.py:295
  53.2 0.1 shard_map.85.refs_0_
  53.3 2.3 %collective-permute-done.26.refs_2_ = bf16[8,10752]{1,0:T(8,128)(2,1)S(1)} collective-permute-done((bf16[8,10752]{1,0:T(8,128)(2,1)S(1)}, bf16[8,10752]{1,0:T(8,128)(2,1)S(1)}, u32[]{:S(2)}, u32[]{:S(2)}) %collective-permute-start.26) | collective-permute-done | bytes 172064 | tf_op jit(solution)/shard_map/ppermute | solution.py:292
  55.6 3.6 %collective-permute-done.25.refs_1_ = bf16[8,10752]{1,0:T(8,128)(2,1)S(1)} collective-permute-done((bf16[8,10752]{1,0:T(8,128)(2,1)S(1)}, bf16[8,10752]{1,0:T(8,128)(2,1)S(1)}, u32[]{:S(2)}, u32[]{:S(2)}) %collective-permute-start.25) | collective-permute-done | bytes 172064 | tf_op jit(solution)/shard_map/ppermute | solution.py:292
  59.2 0.0 collective-permute-done.30.refs_4_
  59.2 1.9 %shard_map.90 = bf16[16,7168]{1,0:T(8,128)(2,1)} custom-call(s32[4]{0:T(128)S(1)} %copy-done.1, s32[2,16]{1,0:T(2,128)S(1)} %bitcast.3, f32[2,16]{1,0:T(2,128)S(1)} %bitcast.4, bf16[8,10752]{1,0:T(8,128)(2,1)S(1)} %shard_map.85.refs_0_, bf16[8,10752]{1,0:T(8,128)(2,1)S(1)} %collective-permute-done.25.refs_1_, ...), custom_call_target="tpu_custom_call" | custom-call | flops 44040192 | bytes 1146880 | tf_op jit(solution)/shard_map/pallas_call | solution.py:249
  (22 shorter events, 0.2 us)
Async XLA Ops:
  1.5 11.0 %collective-permute-start.3 = (bf16[8,10752]{1,0:T(8,128)(2,1)S(1)}, bf16[8,10752]{1,0:T(8,128)(2,1)S(1)}, u32[]{:S(2)}, u32[]{:S(2)}) collective-permute-start(bf16[8,10752]{1,0:T(8,128)(2,1)S(1)} %get-tuple-element.29), channel_id=1, source_target_pairs={{0,12},{1,13},{2,14},{3,15},{4,8},{5,9},{6,10},{7,11},{8,4},{9,5},... | collective-permute-start | bytes 516104 | tf_op jit(solution)/shard_map/ppermute | solution.py:292
  10.8 7.1 %collective-permute-start.9 = (bf16[8,10752]{1,0:T(8,128)(2,1)S(1)}, bf16[8,10752]{1,0:T(8,128)(2,1)S(1)}, u32[]{:S(2)}, u32[]{:S(2)}) collective-permute-start(bf16[8,10752]{1,0:T(8,128)(2,1)S(1)} %shard_map.77), channel_id=1, source_target_pairs={{0,4},{1,5},{2,6},{3,7},{4,0},{5,1},{6,2},{7,3},{8,12},{9,13},{10,... | collective-permute-start | bytes 516104 | tf_op jit(solution)/shard_map/ppermute | solution.py:292
  10.9 8.7 %collective-permute-start = (bf16[8,10752]{1,0:T(8,128)(2,1)S(1)}, bf16[8,10752]{1,0:T(8,128)(2,1)S(1)}, u32[]{:S(2)}, u32[]{:S(2)}) collective-permute-start(bf16[8,10752]{1,0:T(8,128)(2,1)S(1)} %get-tuple-element.28.refs_3_.refs_0_), channel_id=1, source_target_pairs={{0,2},{1,3},{2,0},{3,1},{4,6},{5,7},{6,4},{7,5},{8,10},{9,11},{10,... | collective-permute-start | bytes 516104 | tf_op jit(solution)/shard_map/ppermute | solution.py:295
  12.5 10.2 %collective-permute-start.13 = (bf16[8,10752]{1,0:T(8,128)(2,1)S(1)}, bf16[8,10752]{1,0:T(8,128)(2,1)S(1)}, u32[]{:S(2)}, u32[]{:S(2)}) collective-permute-start(bf16[8,10752]{1,0:T(8,128)(2,1)S(1)} %shard_map.78), channel_id=1, source_target_pairs={{0,8},{1,9},{2,10},{3,11},{4,12},{5,13},{6,14},{7,15},{8,0},{9,1},... | collective-permute-start | bytes 516104 | tf_op jit(solution)/shard_map/ppermute | solution.py:292
  15.4 7.3 %collective-permute-start.4 = (bf16[8,10752]{1,0:T(8,128)(2,1)S(1)}, bf16[8,10752]{1,0:T(8,128)(2,1)S(1)}, u32[]{:S(2)}, u32[]{:S(2)}) collective-permute-start(bf16[8,10752]{1,0:T(8,128)(2,1)S(1)} %collective-permute-done.3.refs_4_.refs_1_), channel_id=1, source_target_pairs={{0,2},{1,3},{2,0},{3,1},{4,6},{5,7},{6,4},{7,5},{8,10},{9,11},{10,... | collective-permute-start | bytes 516104 | tf_op jit(solution)/shard_map/ppermute | solution.py:295
  17.9 6.2 %collective-permute-start.10 = (bf16[8,10752]{1,0:T(8,128)(2,1)S(1)}, bf16[8,10752]{1,0:T(8,128)(2,1)S(1)}, u32[]{:S(2)}, u32[]{:S(2)}) collective-permute-start(bf16[8,10752]{1,0:T(8,128)(2,1)S(1)} %collective-permute-done.9.refs_0_), channel_id=1, source_target_pairs={{0,2},{1,3},{2,0},{3,1},{4,6},{5,7},{6,4},{7,5},{8,10},{9,11},{10,... | collective-permute-start | bytes 516104 | tf_op jit(solution)/shard_map/ppermute | solution.py:295
  19.6 6.1 %collective-permute-start.1 = (bf16[8,10752]{1,0:T(8,128)(2,1)S(1)}, bf16[8,10752]{1,0:T(8,128)(2,1)S(1)}, u32[]{:S(2)}, u32[]{:S(2)}) collective-permute-start(bf16[8,10752]{1,0:T(8,128)(2,1)S(1)} %get-tuple-element.28.refs_3_.refs_0_), channel_id=1, source_target_pairs={{0,1},{1,0},{2,3},{3,2},{4,5},{5,4},{6,7},{7,6},{8,9},{9,8},{10,11... | collective-permute-start | bytes 516104 | tf_op jit(solution)/shard_map/ppermute | solution.py:298
  19.6 6.1 %collective-permute-start.5 = (bf16[8,10752]{1,0:T(8,128)(2,1)S(1)}, bf16[8,10752]{1,0:T(8,128)(2,1)S(1)}, u32[]{:S(2)}, u32[]{:S(2)}) collective-permute-start(bf16[8,10752]{1,0:T(8,128)(2,1)S(1)} %collective-permute-done.3.refs_4_.refs_1_), channel_id=1, source_target_pairs={{0,1},{1,0},{2,3},{3,2},{4,5},{5,4},{6,7},{7,6},{8,9},{9,8},{10,11... | collective-permute-start | bytes 516104 | tf_op jit(solution)/shard_map/ppermute | solution.py:298
  22.7 3.0 %collective-permute-start.2 = (bf16[8,10752]{1,0:T(8,128)(2,1)S(1)}, bf16[8,10752]{1,0:T(8,128)(2,1)S(1)}, u32[]{:S(2)}, u32[]{:S(2)}) collective-permute-start(bf16[8,10752]{1,0:T(8,128)(2,1)S(1)} %collective-permute-done.refs_1_), channel_id=1, source_target_pairs={{0,1},{1,0},{2,3},{3,2},{4,5},{5,4},{6,7},{7,6},{8,9},{9,8},{10,11... | collective-permute-start | bytes 516104 | tf_op jit(solution)/shard_map/ppermute | solution.py:298
  22.7 3.0 %collective-permute-start.6 = (bf16[8,10752]{1,0:T(8,128)(2,1)S(1)}, bf16[8,10752]{1,0:T(8,128)(2,1)S(1)}, u32[]{:S(2)}, u32[]{:S(2)}) collective-permute-start(bf16[8,10752]{1,0:T(8,128)(2,1)S(1)} %collective-permute-done.4.refs_5_.refs_2_), channel_id=1, source_target_pairs={{0,1},{1,0},{2,3},{3,2},{4,5},{5,4},{6,7},{7,6},{8,9},{9,8},{10,11... | collective-permute-start | bytes 516104 | tf_op jit(solution)/shard_map/ppermute | solution.py:298
  24.2 5.4 %collective-permute-start.14 = (bf16[8,10752]{1,0:T(8,128)(2,1)S(1)}, bf16[8,10752]{1,0:T(8,128)(2,1)S(1)}, u32[]{:S(2)}, u32[]{:S(2)}) collective-permute-start(bf16[8,10752]{1,0:T(8,128)(2,1)S(1)} %shard_map.79.refs_4_), channel_id=1, source_target_pairs={{0,2},{1,3},{2,0},{3,1},{4,6},{5,7},{6,4},{7,5},{8,10},{9,11},{10,... | collective-permute-start | bytes 516104 | tf_op jit(solution)/shard_map/ppermute | solution.py:295
  27.6 2.0 %collective-permute-start.17 = (bf16[8,10752]{1,0:T(8,128)(2,1)S(1)}, bf16[8,10752]{1,0:T(8,128)(2,1)S(1)}, u32[]{:S(2)}, u32[]{:S(2)}) collective-permute-start(bf16[8,10752]{1,0:T(8,128)(2,1)S(1)} %get-tuple-element.40), channel_id=1, source_target_pairs={{0,1},{1,0},{2,3},{3,2},{4,5},{5,4},{6,7},{7,6},{8,9},{9,8},{10,11... | collective-permute-start | bytes 516104 | tf_op jit(solution)/shard_map/ppermute | solution.py:298
  27.7 2.5 %collective-permute-start.11 = (bf16[8,10752]{1,0:T(8,128)(2,1)S(1)}, bf16[8,10752]{1,0:T(8,128)(2,1)S(1)}, u32[]{:S(2)}, u32[]{:S(2)}) collective-permute-start(bf16[8,10752]{1,0:T(8,128)(2,1)S(1)} %collective-permute-done.9.refs_0_), channel_id=1, source_target_pairs={{0,1},{1,0},{2,3},{3,2},{4,5},{5,4},{6,7},{7,6},{8,9},{9,8},{10,11... | collective-permute-start | bytes 516104 | tf_op jit(solution)/shard_map/ppermute | solution.py:298
  28.2 3.6 %collective-permute-start.15 = (bf16[8,10752]{1,0:T(8,128)(2,1)S(1)}, bf16[8,10752]{1,0:T(8,128)(2,1)S(1)}, u32[]{:S(2)}, u32[]{:S(2)}) collective-permute-start(bf16[8,10752]{1,0:T(8,128)(2,1)S(1)} %shard_map.79.refs_4_), channel_id=1, source_target_pairs={{0,1},{1,0},{2,3},{3,2},{4,5},{5,4},{6,7},{7,6},{8,9},{9,8},{10,11... | collective-permute-start | bytes 516104 | tf_op jit(solution)/shard_map/ppermute | solution.py:298
  28.3 3.5 %collective-permute-start.12 = (bf16[8,10752]{1,0:T(8,128)(2,1)S(1)}, bf16[8,10752]{1,0:T(8,128)(2,1)S(1)}, u32[]{:S(2)}, u32[]{:S(2)}) collective-permute-start(bf16[8,10752]{1,0:T(8,128)(2,1)S(1)} %collective-permute-done.10.refs_1_), channel_id=1, source_target_pairs={{0,1},{1,0},{2,3},{3,2},{4,5},{5,4},{6,7},{7,6},{8,9},{9,8},{10,11... | collective-permute-start | bytes 516104 | tf_op jit(solution)/shard_map/ppermute | solution.py:298
  29.6 2.2 %collective-permute-start.16 = (bf16[8,10752]{1,0:T(8,128)(2,1)S(1)}, bf16[8,10752]{1,0:T(8,128)(2,1)S(1)}, u32[]{:S(2)}, u32[]{:S(2)}) collective-permute-start(bf16[8,10752]{1,0:T(8,128)(2,1)S(1)} %collective-permute-done.14.refs_5_), channel_id=1, source_target_pairs={{0,1},{1,0},{2,3},{3,2},{4,5},{5,4},{6,7},{7,6},{8,9},{9,8},{10,11... | collective-permute-start | bytes 516104 | tf_op jit(solution)/shard_map/ppermute | solution.py:298
  29.6 4.7 %collective-permute-start.27 = (bf16[8,10752]{1,0:T(8,128)(2,1)S(1)}, bf16[8,10752]{1,0:T(8,128)(2,1)S(1)}, u32[]{:S(2)}, u32[]{:S(2)}) collective-permute-start(bf16[8,10752]{1,0:T(8,128)(2,1)S(1)} %get-tuple-element.50), channel_id=1, source_target_pairs={{0,1},{1,0},{2,3},{3,2},{4,5},{5,4},{6,7},{7,6},{8,9},{9,8},{10,11... | collective-permute-start | bytes 516104 | tf_op jit(solution)/shard_map/ppermute | solution.py:298
  30.2 6.3 %collective-permute-start.28 = (bf16[8,10752]{1,0:T(8,128)(2,1)S(1)}, bf16[8,10752]{1,0:T(8,128)(2,1)S(1)}, u32[]{:S(2)}, u32[]{:S(2)}) collective-permute-start(bf16[8,10752]{1,0:T(8,128)(2,1)S(1)} %shard_map.80.refs_11_), channel_id=1, source_target_pairs={{0,2},{1,3},{2,0},{3,1},{4,6},{5,7},{6,4},{7,5},{8,10},{9,11},{10,... | collective-permute-start | bytes 516104 | tf_op jit(solution)/shard_map/ppermute | solution.py:295
  33.7 25.5 %copy-start = (s32[16,2]{0,1:T(2,128)S(1)}, s32[16,2]{0,1:T(2,128)}, u32[]{:S(2)}) copy-start(s32[16,2]{0,1:T(2,128)} %param.8) | copy-start | bytes 388
  33.7 25.5 %copy-start.1 = (s32[4]{0:T(128)S(1)}, s32[4]{0:T(128)}, u32[]{:S(2)}) copy-start(s32[4]{0:T(128)} %placement_ref.3) | copy-start | bytes 52
  33.7 25.5 %copy-start.2 = (f32[16,2]{0,1:T(2,128)S(1)}, f32[16,2]{0,1:T(2,128)}, u32[]{:S(2)}) copy-start(f32[16,2]{0,1:T(2,128)} %param.9) | copy-start | bytes 388
  33.7 5.2 %collective-permute-start.19 = (bf16[8,10752]{1,0:T(8,128)(2,1)S(1)}, bf16[8,10752]{1,0:T(8,128)(2,1)S(1)}, u32[]{:S(2)}, u32[]{:S(2)}) collective-permute-start(bf16[8,10752]{1,0:T(8,128)(2,1)S(1)} %get-tuple-element.44), channel_id=1, source_target_pairs={{0,1},{1,0},{2,3},{3,2},{4,5},{5,4},{6,7},{7,6},{8,9},{9,8},{10,11... | collective-permute-start | bytes 516104 | tf_op jit(solution)/shard_map/ppermute | solution.py:298
  33.8 6.8 %collective-permute-start.23 = (bf16[8,10752]{1,0:T(8,128)(2,1)S(1)}, bf16[8,10752]{1,0:T(8,128)(2,1)S(1)}, u32[]{:S(2)}, u32[]{:S(2)}) collective-permute-start(bf16[8,10752]{1,0:T(8,128)(2,1)S(1)} %get-tuple-element.48), channel_id=1, source_target_pairs={{0,1},{1,0},{2,3},{3,2},{4,5},{5,4},{6,7},{7,6},{8,9},{9,8},{10,11... | collective-permute-start | bytes 516104 | tf_op jit(solution)/shard_map/ppermute | solution.py:298
  34.3 6.6 %collective-permute-start.8 = (bf16[8,10752]{1,0:T(8,128)(2,1)S(1)}, bf16[8,10752]{1,0:T(8,128)(2,1)S(1)}, u32[]{:S(2)}, u32[]{:S(2)}) collective-permute-start(bf16[8,10752]{1,0:T(8,128)(2,1)S(1)} %get-tuple-element.36), channel_id=1, source_target_pairs={{0,1},{1,0},{2,3},{3,2},{4,5},{5,4},{6,7},{7,6},{8,9},{9,8},{10,11... | collective-permute-start | bytes 516104 | tf_op jit(solution)/shard_map/ppermute | solution.py:298
  36.6 13.5 %collective-permute-start.29 = (bf16[8,11264]{1,0:T(8,128)(2,1)S(1)}, bf16[8,11264]{1,0:T(8,128)(2,1)S(1)}, u32[]{:S(2)}, u32[]{:S(2)}) collective-permute-start(bf16[8,11264]{1,0:T(8,128)(2,1)S(1)} %shard_map.88), channel_id=1, source_target_pairs={{0,12},{1,13},{2,14},{3,15},{4,8},{5,9},{6,10},{7,11},{8,4},{9,5},... | collective-permute-start | bytes 540680 | tf_op jit(solution)/shard_map/ppermute | solution.py:292
  38.9 2.5 %collective-permute-start.18 = (bf16[8,10752]{1,0:T(8,128)(2,1)S(1)}, bf16[8,10752]{1,0:T(8,128)(2,1)S(1)}, u32[]{:S(2)}, u32[]{:S(2)}) collective-permute-start(bf16[8,10752]{1,0:T(8,128)(2,1)S(1)} %get-tuple-element.42), channel_id=1, source_target_pairs={{0,1},{1,0},{2,3},{3,2},{4,5},{5,4},{6,7},{7,6},{8,9},{9,8},{10,11... | collective-permute-start | bytes 516104 | tf_op jit(solution)/shard_map/ppermute | solution.py:298
  39.0 7.2 %collective-permute-start.20 = (bf16[8,10752]{1,0:T(8,128)(2,1)S(1)}, bf16[8,10752]{1,0:T(8,128)(2,1)S(1)}, u32[]{:S(2)}, u32[]{:S(2)}) collective-permute-start(bf16[8,10752]{1,0:T(8,128)(2,1)S(1)} %shard_map.82), channel_id=1, source_target_pairs={{0,2},{1,3},{2,0},{3,1},{4,6},{5,7},{6,4},{7,5},{8,10},{9,11},{10,... | collective-permute-start | bytes 516104 | tf_op jit(solution)/shard_map/ppermute | solution.py:295
  40.5 6.7 %collective-permute-start.22 = (bf16[8,10752]{1,0:T(8,128)(2,1)S(1)}, bf16[8,10752]{1,0:T(8,128)(2,1)S(1)}, u32[]{:S(2)}, u32[]{:S(2)}) collective-permute-start(bf16[8,10752]{1,0:T(8,128)(2,1)S(1)} %get-tuple-element.46), channel_id=1, source_target_pairs={{0,1},{1,0},{2,3},{3,2},{4,5},{5,4},{6,7},{7,6},{8,9},{9,8},{10,11... | collective-permute-start | bytes 516104 | tf_op jit(solution)/shard_map/ppermute | solution.py:298
  40.8 9.1 %collective-permute-start.24 = (bf16[8,10752]{1,0:T(8,128)(2,1)S(1)}, bf16[8,10752]{1,0:T(8,128)(2,1)S(1)}, u32[]{:S(2)}, u32[]{:S(2)}) collective-permute-start(bf16[8,10752]{1,0:T(8,128)(2,1)S(1)} %shard_map.86), channel_id=1, source_target_pairs={{0,2},{1,3},{2,0},{3,1},{4,6},{5,7},{6,4},{7,5},{8,10},{9,11},{10,... | collective-permute-start | bytes 516104 | tf_op jit(solution)/shard_map/ppermute | solution.py:295
  41.5 8.8 %collective-permute-start.7 = (bf16[8,10752]{1,0:T(8,128)(2,1)S(1)}, bf16[8,10752]{1,0:T(8,128)(2,1)S(1)}, u32[]{:S(2)}, u32[]{:S(2)}) collective-permute-start(bf16[8,10752]{1,0:T(8,128)(2,1)S(1)} %get-tuple-element.34), channel_id=1, source_target_pairs={{0,1},{1,0},{2,3},{3,2},{4,5},{5,4},{6,7},{7,6},{8,9},{9,8},{10,11... | collective-permute-start | bytes 516104 | tf_op jit(solution)/shard_map/ppermute | solution.py:298
  46.3 9.3 %collective-permute-start.26 = (bf16[8,10752]{1,0:T(8,128)(2,1)S(1)}, bf16[8,10752]{1,0:T(8,128)(2,1)S(1)}, u32[]{:S(2)}, u32[]{:S(2)}) collective-permute-start(bf16[8,10752]{1,0:T(8,128)(2,1)S(1)} %shard_map.83.refs_1_), channel_id=1, source_target_pairs={{0,8},{1,9},{2,10},{3,11},{4,12},{5,13},{6,14},{7,15},{8,0},{9,1},... | collective-permute-start | bytes 516104 | tf_op jit(solution)/shard_map/ppermute | solution.py:292
  47.2 6.0 %collective-permute-start.21 = (bf16[8,10752]{1,0:T(8,128)(2,1)S(1)}, bf16[8,10752]{1,0:T(8,128)(2,1)S(1)}, u32[]{:S(2)}, u32[]{:S(2)}) collective-permute-start(bf16[8,10752]{1,0:T(8,128)(2,1)S(1)} %shard_map.84), channel_id=1, source_target_pairs={{0,2},{1,3},{2,0},{3,1},{4,6},{5,7},{6,4},{7,5},{8,10},{9,11},{10,... | collective-permute-start | bytes 516104 | tf_op jit(solution)/shard_map/ppermute | solution.py:295
  50.0 9.2 %collective-permute-start.25 = (bf16[8,10752]{1,0:T(8,128)(2,1)S(1)}, bf16[8,10752]{1,0:T(8,128)(2,1)S(1)}, u32[]{:S(2)}, u32[]{:S(2)}) collective-permute-start(bf16[8,10752]{1,0:T(8,128)(2,1)S(1)} %shard_map.87), channel_id=1, source_target_pairs={{0,4},{1,5},{2,6},{3,7},{4,0},{5,1},{6,2},{7,3},{8,12},{9,13},{10,... | collective-permute-start | bytes 516104 | tf_op jit(solution)/shard_map/ppermute | solution.py:292
  50.1 9.0 %collective-permute-start.30 = (bf16[8,10496]{1,0:T(8,128)(2,1)S(1)}, bf16[8,10496]{1,0:T(8,128)(2,1)S(1)}, u32[]{:S(2)}, u32[]{:S(2)}) collective-permute-start(bf16[8,10496]{1,0:T(8,128)(2,1)S(1)} %shard_map.89), channel_id=1, source_target_pairs={{0,1},{1,0},{2,3},{3,2},{4,5},{5,4},{6,7},{7,6},{8,9},{9,8},{10,11... | collective-permute-start | bytes 503816 | tf_op jit(solution)/shard_map/ppermute | solution.py:298

commit v13 on v11

--- a/solution.py
+++ b/solution.py
@@ -292,7 +292,8 @@
         return lax.ppermute(value, "node", [(i, i ^ 1) for i in range(devices)])
 
     ids = expert_ids.T
-    groups = [[n_blocks - d, d] for d in range(1, n_blocks // 2)] + [[n_blocks // 2]]
+    far = [n_blocks // 2] + [n_blocks - d for d in range(1, n_blocks // 2)]
+    groups = [[far[d - 1], d] for d in range(1, n_blocks // 2)] + [far[-1:]]
     last, early = groups[-1][0], [group[0] for group in groups[:-1]]
     straight, across, results = {}, {}, {}
     both, home, kept, sent = {}, {}, {}, {}

time: 60.2 us -> 61 us (1.013)
  waiting for transfers between devices: 19.8 us -> 24.9 us
  starting transfers between devices: 28.2 us -> 24 us
    ppermute x8, waiting for transfers between devices: 9.03 us -> 14.3 us  [along_y(): return lax.ppermute(value, 'node', [(i, i ^ 2) for i in range(devices)])]
    ppermute x6, starting transfers between devices: 12.7 us -> 9.95 us  [along_z(): return lax.ppermute(value, 'node', pairs)]
    ppermute x8, starting transfers between devices: 11.5 us -> 10.3 us  [along_y(): return lax.ppermute(value, 'node', [(i, i ^ 2) for i in range(devices)])]
  transfers between devices with their start and end apart: 32 -> 32, of which waited for: 9 -> 11; matrix products, arithmetic and copies ran while one was open for 0% -> 0% of each run, Pallas kernels for 14% -> 14%
where the time goes in v13:
time: 61 us; the launch traced here: 60.9 us
  waiting for transfers between devices  24.9 us (41%)
  starting transfers between devices  24 us (39%)
  Pallas kernels  11.8 us (19%)
    ppermute x8, waiting for transfers between devices, along_y(): return lax.ppermute(value, 'node', [(i, i ^ 2) for i in range(devices)])  14.3 us
    ppermute x6, waiting for transfers between devices, along_z(): return lax.ppermute(value, 'node', pairs)  10.5 us
    ppermute x8, starting transfers between devices, along_y(): return lax.ppermute(value, 'node', [(i, i ^ 2) for i in range(devices)])  10.3 us
    ppermute x6, starting transfers between devices, along_z(): return lax.ppermute(value, 'node', pairs)  9.95 us
    pallas_call x1, Pallas kernels, load(): pl.pallas_call(load_kernel, out_shape=[pltpu.VMEM(w.shape, w.dtype) for w...  4.24 us
    pallas_call x2, Pallas kernels, run_experts(): pl.pallas_call(functools.partial(experts_kernel, count), out_shape=[shape...  3.76 us
    ppermute x18, starting transfers between devices, along_core(): return lax.ppermute(value, 'node', [(i, i ^ 1) for i in range(devices)])  3.68 us
    pallas_call x1, Pallas kernels, mix(): pl.pallas_call(functools.partial(mix_kernel, n_blocks, parts), out_shape=...  1.86 us
  transfers between devices with their start and end apart: 32, of which 11 were waited for; matrix products, arithmetic and copies ran while one was open for 0% of the time, Pallas kernels for 14%

profile of v13, /device:TPU:0, one launch (start us, length us, event | category | flops | bytes accessed | tf_op | source)
XLA Modules:
  0.0 60.9 jit_solution(10303201850528591596)
XLA Ops:
  0.0 1.5 %shard_map.73 = (bf16[8,10752]{1,0:T(8,128)(2,1)S(1)}, bf16[8,10752]{1,0:T(8,128)(2,1)S(1)}, bf16[8,10752]{1,0:T(8,128)(2,1)S(1)}, bf16[8,10752]{1,0:T(8,128)(2,1)S(1)}) custom-call(s32[4]{0:T(128)} %placement_ref.3, s32[2,16]{1,0:T(2,128)} %bitcast.2, bf16[16,7168]{1,0:T(8,128)(2,1)} %tokens_ref.1), custom_call_target="tpu_custom_call" | custom-call | tf_op jit(solution)/shard_map/pallas_call | solution.py:82
  1.5 4.1 %collective-permute-start.3 = (bf16[8,10752]{1,0:T(8,128)(2,1)S(1)}, bf16[8,10752]{1,0:T(8,128)(2,1)S(1)}, u32[]{:S(2)}, u32[]{:S(2)}) collective-permute-start(bf16[8,10752]{1,0:T(8,128)(2,1)S(1)} %get-tuple-element.29), channel_id=1, source_target_pairs={{0,8},{1,9},{2,10},{3,11},{4,12},{5,13},{6,14},{7,15},{8,0},{9,1},... | collective-permute-start | bytes 516104 | tf_op jit(solution)/shard_map/ppermute | solution.py:286
  5.6 4.2 %shard_map.74 = (bf16[7168,256]{1,0:T(8,128)(2,1)S(1)}, bf16[7168,256]{1,0:T(8,128)(2,1)S(1)}, bf16[256,7168]{1,0:T(8,128)(2,1)S(1)}) custom-call(bf16[7168,256]{1,0:T(8,128)(2,1)} %refs_0_.1, bf16[7168,256]{1,0:T(8,128)(2,1)} %refs_1_.1, bf16[256,7168]{1,0:T(8,128)(2,1)} %refs_2_.1, bf16[8,10752]{1,0:T(8,128)(2,1)S(1)} %get-tuple-element.28.refs_3_.refs_0_), custom_call_target="tpu_custom_call" | custom-call | tf_op jit(solution)/shard_map/pallas_call | solution.py:141
  9.8 1.6 %collective-permute-start.9 = (bf16[8,10752]{1,0:T(8,128)(2,1)S(1)}, bf16[8,10752]{1,0:T(8,128)(2,1)S(1)}, u32[]{:S(2)}, u32[]{:S(2)}) collective-permute-start(bf16[8,10752]{1,0:T(8,128)(2,1)S(1)} %shard_map.77), channel_id=1, source_target_pairs={{0,4},{1,5},{2,6},{3,7},{4,0},{5,1},{6,2},{7,3},{8,12},{9,13},{10,... | collective-permute-start | bytes 516104 | tf_op jit(solution)/shard_map/ppermute | solution.py:286
  11.5 1.5 %collective-permute-start = (bf16[8,10752]{1,0:T(8,128)(2,1)S(1)}, bf16[8,10752]{1,0:T(8,128)(2,1)S(1)}, u32[]{:S(2)}, u32[]{:S(2)}) collective-permute-start(bf16[8,10752]{1,0:T(8,128)(2,1)S(1)} %get-tuple-element.28.refs_3_.refs_0_), channel_id=1, source_target_pairs={{0,2},{1,3},{2,0},{3,1},{4,6},{5,7},{6,4},{7,5},{8,10},{9,11},{10,... | collective-permute-start | bytes 516104 | tf_op jit(solution)/shard_map/ppermute | solution.py:289
  13.0 0.7 %collective-permute-done.3.refs_4_.refs_1_ = bf16[8,10752]{1,0:T(8,128)(2,1)S(1)} collective-permute-done((bf16[8,10752]{1,0:T(8,128)(2,1)S(1)}, bf16[8,10752]{1,0:T(8,128)(2,1)S(1)}, u32[]{:S(2)}, u32[]{:S(2)}) %collective-permute-start.3) | collective-permute-done | bytes 172064 | tf_op jit(solution)/shard_map/ppermute | solution.py:286
  13.7 3.5 %collective-permute-start.13 = (bf16[8,10752]{1,0:T(8,128)(2,1)S(1)}, bf16[8,10752]{1,0:T(8,128)(2,1)S(1)}, u32[]{:S(2)}, u32[]{:S(2)}) collective-permute-start(bf16[8,10752]{1,0:T(8,128)(2,1)S(1)} %shard_map.78), channel_id=1, source_target_pairs={{0,12},{1,13},{2,14},{3,15},{4,8},{5,9},{6,10},{7,11},{8,4},{9,5},... | collective-permute-start | bytes 516104 | tf_op jit(solution)/shard_map/ppermute | solution.py:286
  17.3 1.5 %collective-permute-start.4 = (bf16[8,10752]{1,0:T(8,128)(2,1)S(1)}, bf16[8,10752]{1,0:T(8,128)(2,1)S(1)}, u32[]{:S(2)}, u32[]{:S(2)}) collective-permute-start(bf16[8,10752]{1,0:T(8,128)(2,1)S(1)} %collective-permute-done.3.refs_4_.refs_1_), channel_id=1, source_target_pairs={{0,2},{1,3},{2,0},{3,1},{4,6},{5,7},{6,4},{7,5},{8,10},{9,11},{10,... | collective-permute-start | bytes 516104 | tf_op jit(solution)/shard_map/ppermute | solution.py:289
  18.8 0.0 collective-permute-done.9.refs_0_
  18.8 0.5 collective-permute-start.10
  19.3 0.0 collective-permute-start.1
  19.3 0.0 collective-permute-done.refs_1_
  19.3 0.5 collective-permute-start.5
  19.8 2.1 %collective-permute-done.13.refs_0_ = bf16[8,10752]{1,0:T(8,128)(2,1)S(1)} collective-permute-done((bf16[8,10752]{1,0:T(8,128)(2,1)S(1)}, bf16[8,10752]{1,0:T(8,128)(2,1)S(1)}, u32[]{:S(2)}, u32[]{:S(2)}) %collective-permute-start.13) | collective-permute-done | bytes 172064 | tf_op jit(solution)/shard_map/ppermute | solution.py:286
  21.9 0.0 collective-permute-start.2
  21.9 2.7 %collective-permute-done.4.refs_5_.refs_2_ = bf16[8,10752]{1,0:T(8,128)(2,1)S(1)} collective-permute-done((bf16[8,10752]{1,0:T(8,128)(2,1)S(1)}, bf16[8,10752]{1,0:T(8,128)(2,1)S(1)}, u32[]{:S(2)}, u32[]{:S(2)}) %collective-permute-start.4) | collective-permute-done | bytes 172064 | tf_op jit(solution)/shard_map/ppermute | solution.py:289
  24.6 0.0 collective-permute-start.6
  24.6 2.4 %collective-permute-done.10.refs_1_ = bf16[8,10752]{1,0:T(8,128)(2,1)S(1)} collective-permute-done((bf16[8,10752]{1,0:T(8,128)(2,1)S(1)}, bf16[8,10752]{1,0:T(8,128)(2,1)S(1)}, u32[]{:S(2)}, u32[]{:S(2)}) %collective-permute-start.10) | collective-permute-done | bytes 172064 | tf_op jit(solution)/shard_map/ppermute | solution.py:289
  26.9 1.5 %collective-permute-start.14 = (bf16[8,10752]{1,0:T(8,128)(2,1)S(1)}, bf16[8,10752]{1,0:T(8,128)(2,1)S(1)}, u32[]{:S(2)}, u32[]{:S(2)}) collective-permute-start(bf16[8,10752]{1,0:T(8,128)(2,1)S(1)} %shard_map.79.refs_4_), channel_id=1, source_target_pairs={{0,2},{1,3},{2,0},{3,1},{4,6},{5,7},{6,4},{7,5},{8,10},{9,11},{10,... | collective-permute-start | bytes 516104 | tf_op jit(solution)/shard_map/ppermute | solution.py:289
  28.4 0.0 collective-permute-done.1.refs_2_
  28.4 0.0 collective-permute-done.5.refs_6_
  28.4 0.0 collective-permute-done.2.refs_3_
  28.4 0.0 collective-permute-done.6.refs_7_
  28.5 1.9 %shard_map.75 = (bf16[8,10752]{1,0:T(8,128)(2,1)S(1)}, bf16[8,10752]{1,0:T(8,128)(2,1)S(1)}, bf16[8,10752]{1,0:T(8,128)(2,1)S(1)}, bf16[8,10752]{1,0:T(8,128)(2,...) custom-call(bf16[8,10752]{1,0:T(8,128)(2,1)S(1)} %get-tuple-element., ...), custom_call_target="tpu_custom_call" | custom-call | tf_op jit(solution)/shard_map/pallas_call | solution.py:198
  30.3 0.1 collective-permute-start.17
  30.4 0.5 collective-permute-start.11
  30.9 0.1 collective-permute-start.15
  31.0 0.4 collective-permute-start.12
  31.4 0.9 %collective-permute-done.14.refs_5_ = bf16[8,10752]{1,0:T(8,128)(2,1)S(1)} collective-permute-done((bf16[8,10752]{1,0:T(8,128)(2,1)S(1)}, bf16[8,10752]{1,0:T(8,128)(2,1)S(1)}, u32[]{:S(2)}, u32[]{:S(2)}) %collective-permute-start.14) | collective-permute-done | bytes 172064 | tf_op jit(solution)/shard_map/ppermute | solution.py:289
  32.3 0.0 collective-permute-start.16
  32.3 0.0 collective-permute-done.17.refs_1_
  32.3 0.5 collective-permute-start.26
  32.9 0.0 collective-permute-done.11.refs_2_
  32.9 1.6 %collective-permute-start.27 = (bf16[8,10752]{1,0:T(8,128)(2,1)S(1)}, bf16[8,10752]{1,0:T(8,128)(2,1)S(1)}, u32[]{:S(2)}, u32[]{:S(2)}) collective-permute-start(bf16[8,10752]{1,0:T(8,128)(2,1)S(1)} %shard_map.80.refs_11_), channel_id=1, source_target_pairs={{0,2},{1,3},{2,0},{3,1},{4,6},{5,7},{6,4},{7,5},{8,10},{9,11},{10,... | collective-permute-start | bytes 516104 | tf_op jit(solution)/shard_map/ppermute | solution.py:289
  34.5 0.0 collective-permute-done.15.refs_6_
  34.5 0.0 collective-permute-done.12.refs_3_
  34.5 1.9 %shard_map.81 = (bf16[8,10752]{1,0:T(8,128)(2,1)S(1)}, bf16[8,10752]{1,0:T(8,128)(2,1)S(1)}, bf16[8,10752]{1,0:T(8,128)(2,1)S(1)}, bf16[8,10752]{1,0:T(8,128)(2,...) custom-call(bf16[8,10752]{1,0:T(8,128)(2,1)S(1)} %collective-permute, ...), custom_call_target="tpu_custom_call" | custom-call | tf_op jit(solution)/shard_map/pallas_call | solution.py:198
  36.4 0.0 copy-start
  36.4 0.0 copy-start.1
  36.4 0.0 copy-start.2
  36.4 0.1 collective-permute-start.19
  36.5 0.5 collective-permute-start.23
  37.0 0.1 collective-permute-start.8
  37.1 2.2 %collective-permute-done.27.refs_2_ = bf16[8,10752]{1,0:T(8,128)(2,1)S(1)} collective-permute-done((bf16[8,10752]{1,0:T(8,128)(2,1)S(1)}, bf16[8,10752]{1,0:T(8,128)(2,1)S(1)}, u32[]{:S(2)}, u32[]{:S(2)}) %collective-permute-start.27) | collective-permute-done | bytes 172064 | tf_op jit(solution)/shard_map/ppermute | solution.py:289
  39.2 0.1 shard_map.88.refs_0_
  39.3 0.1 collective-permute-start.28
  39.4 0.5 collective-permute-start.18
  39.9 1.6 %collective-permute-start.20 = (bf16[8,10752]{1,0:T(8,128)(2,1)S(1)}, bf16[8,10752]{1,0:T(8,128)(2,1)S(1)}, u32[]{:S(2)}, u32[]{:S(2)}) collective-permute-start(bf16[8,10752]{1,0:T(8,128)(2,1)S(1)} %shard_map.82), channel_id=1, source_target_pairs={{0,2},{1,3},{2,0},{3,1},{4,6},{5,7},{6,4},{7,5},{8,10},{9,11},{10,... | collective-permute-start | bytes 516104 | tf_op jit(solution)/shard_map/ppermute | solution.py:289
  41.6 0.6 collective-permute-start.24
  42.2 0.3 collective-permute-start.7
  42.5 4.7 %collective-permute-done.20.refs_2_ = bf16[8,10752]{1,0:T(8,128)(2,1)S(1)} collective-permute-done((bf16[8,10752]{1,0:T(8,128)(2,1)S(1)}, bf16[8,10752]{1,0:T(8,128)(2,1)S(1)}, u32[]{:S(2)}, u32[]{:S(2)}) %collective-permute-start.20) | collective-permute-done | bytes 172064 | tf_op jit(solution)/shard_map/ppermute | solution.py:289
  47.2 0.1 shard_map.83.refs_1_
  47.3 0.6 collective-permute-start.30
  47.9 1.5 %collective-permute-start.21 = (bf16[8,10752]{1,0:T(8,128)(2,1)S(1)}, bf16[8,10752]{1,0:T(8,128)(2,1)S(1)}, u32[]{:S(2)}, u32[]{:S(2)}) collective-permute-start(bf16[8,10752]{1,0:T(8,128)(2,1)S(1)} %shard_map.84), channel_id=1, source_target_pairs={{0,2},{1,3},{2,0},{3,1},{4,6},{5,7},{6,4},{7,5},{8,10},{9,11},{10,... | collective-permute-start | bytes 516104 | tf_op jit(solution)/shard_map/ppermute | solution.py:289
  49.4 1.5 %collective-permute-done.24.refs_2_ = bf16[8,10752]{1,0:T(8,128)(2,1)S(1)} collective-permute-done((bf16[8,10752]{1,0:T(8,128)(2,1)S(1)}, bf16[8,10752]{1,0:T(8,128)(2,1)S(1)}, u32[]{:S(2)}, u32[]{:S(2)}) %collective-permute-start.24) | collective-permute-done | bytes 172064 | tf_op jit(solution)/shard_map/ppermute | solution.py:289
  50.9 0.1 shard_map.87
  51.0 0.1 collective-permute-start.25
  51.1 3.3 %collective-permute-done.29.refs_0_.refs_2_ = bf16[8,10752]{1,0:T(8,128)(2,1)S(1)} collective-permute-done((bf16[8,10752]{1,0:T(8,128)(2,1)S(1)}, bf16[8,10752]{1,0:T(8,128)(2,1)S(1)}, u32[]{:S(2)}, u32[]{:S(2)}) %collective-permute-start.29) | collective-permute-done | bytes 172064 | tf_op jit(solution)/shard_map/ppermute | solution.py:286
  54.4 0.1 collective-permute-start.31
  54.5 0.0 collective-permute-done.7.refs_1_
  54.5 0.1 shard_map.85.refs_0_
  54.6 1.2 %collective-permute-done.30.refs_3_ = bf16[8,10752]{1,0:T(8,128)(2,1)S(1)} collective-permute-done((bf16[8,10752]{1,0:T(8,128)(2,1)S(1)}, bf16[8,10752]{1,0:T(8,128)(2,1)S(1)}, u32[]{:S(2)}, u32[]{:S(2)}) %collective-permute-start.30) | collective-permute-done | bytes 172064 | tf_op jit(solution)/shard_map/ppermute | solution.py:286
  55.8 3.2 %collective-permute-done.25.refs_1_ = bf16[8,10752]{1,0:T(8,128)(2,1)S(1)} collective-permute-done((bf16[8,10752]{1,0:T(8,128)(2,1)S(1)}, bf16[8,10752]{1,0:T(8,128)(2,1)S(1)}, u32[]{:S(2)}, u32[]{:S(2)}) %collective-permute-start.25) | collective-permute-done | bytes 172064 | tf_op jit(solution)/shard_map/ppermute | solution.py:286
  59.0 1.9 %shard_map.92 = bf16[16,7168]{1,0:T(8,128)(2,1)} custom-call(s32[4]{0:T(128)S(1)} %copy-done.1, s32[2,16]{1,0:T(2,128)S(1)} %bitcast.3, f32[2,16]{1,0:T(2,128)S(1)} %bitcast.4, bf16[8,10752]{1,0:T(8,128)(2,1)S(1)} %shard_map.85.refs_0_, bf16[8,10752]{1,0:T(8,128)(2,1)S(1)} %collective-permute-done.25.refs_1_, ...), custom_call_target="tpu_custom_call" | custom-call | flops 44040192 | bytes 1146880 | tf_op jit(solution)/shard_map/pallas_call | solution.py:247
  (26 shorter events, 0.2 us)
Async XLA Ops:
  1.5 12.3 %collective-permute-start.3 = (bf16[8,10752]{1,0:T(8,128)(2,1)S(1)}, bf16[8,10752]{1,0:T(8,128)(2,1)S(1)}, u32[]{:S(2)}, u32[]{:S(2)}) collective-permute-start(bf16[8,10752]{1,0:T(8,128)(2,1)S(1)} %get-tuple-element.29), channel_id=1, source_target_pairs={{0,8},{1,9},{2,10},{3,11},{4,12},{5,13},{6,14},{7,15},{8,0},{9,1},... | collective-permute-start | bytes 516104 | tf_op jit(solution)/shard_map/ppermute | solution.py:286
  9.8 9.0 %collective-permute-start.9 = (bf16[8,10752]{1,0:T(8,128)(2,1)S(1)}, bf16[8,10752]{1,0:T(8,128)(2,1)S(1)}, u32[]{:S(2)}, u32[]{:S(2)}) collective-permute-start(bf16[8,10752]{1,0:T(8,128)(2,1)S(1)} %shard_map.77), channel_id=1, source_target_pairs={{0,4},{1,5},{2,6},{3,7},{4,0},{5,1},{6,2},{7,3},{8,12},{9,13},{10,... | collective-permute-start | bytes 516104 | tf_op jit(solution)/shard_map/ppermute | solution.py:286
  11.5 7.8 %collective-permute-start = (bf16[8,10752]{1,0:T(8,128)(2,1)S(1)}, bf16[8,10752]{1,0:T(8,128)(2,1)S(1)}, u32[]{:S(2)}, u32[]{:S(2)}) collective-permute-start(bf16[8,10752]{1,0:T(8,128)(2,1)S(1)} %get-tuple-element.28.refs_3_.refs_0_), channel_id=1, source_target_pairs={{0,2},{1,3},{2,0},{3,1},{4,6},{5,7},{6,4},{7,5},{8,10},{9,11},{10,... | collective-permute-start | bytes 516104 | tf_op jit(solution)/shard_map/ppermute | solution.py:289
  13.7 8.1 %collective-permute-start.13 = (bf16[8,10752]{1,0:T(8,128)(2,1)S(1)}, bf16[8,10752]{1,0:T(8,128)(2,1)S(1)}, u32[]{:S(2)}, u32[]{:S(2)}) collective-permute-start(bf16[8,10752]{1,0:T(8,128)(2,1)S(1)} %shard_map.78), channel_id=1, source_target_pairs={{0,12},{1,13},{2,14},{3,15},{4,8},{5,9},{6,10},{7,11},{8,4},{9,5},... | collective-permute-start | bytes 516104 | tf_op jit(solution)/shard_map/ppermute | solution.py:286
  17.3 7.3 %collective-permute-start.4 = (bf16[8,10752]{1,0:T(8,128)(2,1)S(1)}, bf16[8,10752]{1,0:T(8,128)(2,1)S(1)}, u32[]{:S(2)}, u32[]{:S(2)}) collective-permute-start(bf16[8,10752]{1,0:T(8,128)(2,1)S(1)} %collective-permute-done.3.refs_4_.refs_1_), channel_id=1, source_target_pairs={{0,2},{1,3},{2,0},{3,1},{4,6},{5,7},{6,4},{7,5},{8,10},{9,11},{10,... | collective-permute-start | bytes 516104 | tf_op jit(solution)/shard_map/ppermute | solution.py:289
  18.8 8.1 %collective-permute-start.10 = (bf16[8,10752]{1,0:T(8,128)(2,1)S(1)}, bf16[8,10752]{1,0:T(8,128)(2,1)S(1)}, u32[]{:S(2)}, u32[]{:S(2)}) collective-permute-start(bf16[8,10752]{1,0:T(8,128)(2,1)S(1)} %collective-permute-done.9.refs_0_), channel_id=1, source_target_pairs={{0,2},{1,3},{2,0},{3,1},{4,6},{5,7},{6,4},{7,5},{8,10},{9,11},{10,... | collective-permute-start | bytes 516104 | tf_op jit(solution)/shard_map/ppermute | solution.py:289
  19.3 9.1 %collective-permute-start.1 = (bf16[8,10752]{1,0:T(8,128)(2,1)S(1)}, bf16[8,10752]{1,0:T(8,128)(2,1)S(1)}, u32[]{:S(2)}, u32[]{:S(2)}) collective-permute-start(bf16[8,10752]{1,0:T(8,128)(2,1)S(1)} %get-tuple-element.28.refs_3_.refs_0_), channel_id=1, source_target_pairs={{0,1},{1,0},{2,3},{3,2},{4,5},{5,4},{6,7},{7,6},{8,9},{9,8},{10,11... | collective-permute-start | bytes 516104 | tf_op jit(solution)/shard_map/ppermute | solution.py:292
  19.3 9.1 %collective-permute-start.5 = (bf16[8,10752]{1,0:T(8,128)(2,1)S(1)}, bf16[8,10752]{1,0:T(8,128)(2,1)S(1)}, u32[]{:S(2)}, u32[]{:S(2)}) collective-permute-start(bf16[8,10752]{1,0:T(8,128)(2,1)S(1)} %collective-permute-done.3.refs_4_.refs_1_), channel_id=1, source_target_pairs={{0,1},{1,0},{2,3},{3,2},{4,5},{5,4},{6,7},{7,6},{8,9},{9,8},{10,11... | collective-permute-start | bytes 516104 | tf_op jit(solution)/shard_map/ppermute | solution.py:292
  21.9 6.6 %collective-permute-start.2 = (bf16[8,10752]{1,0:T(8,128)(2,1)S(1)}, bf16[8,10752]{1,0:T(8,128)(2,1)S(1)}, u32[]{:S(2)}, u32[]{:S(2)}) collective-permute-start(bf16[8,10752]{1,0:T(8,128)(2,1)S(1)} %collective-permute-done.refs_1_), channel_id=1, source_target_pairs={{0,1},{1,0},{2,3},{3,2},{4,5},{5,4},{6,7},{7,6},{8,9},{9,8},{10,11... | collective-permute-start | bytes 516104 | tf_op jit(solution)/shard_map/ppermute | solution.py:292
  24.6 3.9 %collective-permute-start.6 = (bf16[8,10752]{1,0:T(8,128)(2,1)S(1)}, bf16[8,10752]{1,0:T(8,128)(2,1)S(1)}, u32[]{:S(2)}, u32[]{:S(2)}) collective-permute-start(bf16[8,10752]{1,0:T(8,128)(2,1)S(1)} %collective-permute-done.4.refs_5_.refs_2_), channel_id=1, source_target_pairs={{0,1},{1,0},{2,3},{3,2},{4,5},{5,4},{6,7},{7,6},{8,9},{9,8},{10,11... | collective-permute-start | bytes 516104 | tf_op jit(solution)/shard_map/ppermute | solution.py:292
  26.9 5.4 %collective-permute-start.14 = (bf16[8,10752]{1,0:T(8,128)(2,1)S(1)}, bf16[8,10752]{1,0:T(8,128)(2,1)S(1)}, u32[]{:S(2)}, u32[]{:S(2)}) collective-permute-start(bf16[8,10752]{1,0:T(8,128)(2,1)S(1)} %shard_map.79.refs_4_), channel_id=1, source_target_pairs={{0,2},{1,3},{2,0},{3,1},{4,6},{5,7},{6,4},{7,5},{8,10},{9,11},{10,... | collective-permute-start | bytes 516104 | tf_op jit(solution)/shard_map/ppermute | solution.py:289
  30.3 2.0 %collective-permute-start.17 = (bf16[8,10752]{1,0:T(8,128)(2,1)S(1)}, bf16[8,10752]{1,0:T(8,128)(2,1)S(1)}, u32[]{:S(2)}, u32[]{:S(2)}) collective-permute-start(bf16[8,10752]{1,0:T(8,128)(2,1)S(1)} %get-tuple-element.40), channel_id=1, source_target_pairs={{0,1},{1,0},{2,3},{3,2},{4,5},{5,4},{6,7},{7,6},{8,9},{9,8},{10,11... | collective-permute-start | bytes 516104 | tf_op jit(solution)/shard_map/ppermute | solution.py:292
  30.4 2.5 %collective-permute-start.11 = (bf16[8,10752]{1,0:T(8,128)(2,1)S(1)}, bf16[8,10752]{1,0:T(8,128)(2,1)S(1)}, u32[]{:S(2)}, u32[]{:S(2)}) collective-permute-start(bf16[8,10752]{1,0:T(8,128)(2,1)S(1)} %collective-permute-done.9.refs_0_), channel_id=1, source_target_pairs={{0,1},{1,0},{2,3},{3,2},{4,5},{5,4},{6,7},{7,6},{8,9},{9,8},{10,11... | collective-permute-start | bytes 516104 | tf_op jit(solution)/shard_map/ppermute | solution.py:292
  30.9 3.6 %collective-permute-start.15 = (bf16[8,10752]{1,0:T(8,128)(2,1)S(1)}, bf16[8,10752]{1,0:T(8,128)(2,1)S(1)}, u32[]{:S(2)}, u32[]{:S(2)}) collective-permute-start(bf16[8,10752]{1,0:T(8,128)(2,1)S(1)} %shard_map.79.refs_4_), channel_id=1, source_target_pairs={{0,1},{1,0},{2,3},{3,2},{4,5},{5,4},{6,7},{7,6},{8,9},{9,8},{10,11... | collective-permute-start | bytes 516104 | tf_op jit(solution)/shard_map/ppermute | solution.py:292
  31.0 3.5 %collective-permute-start.12 = (bf16[8,10752]{1,0:T(8,128)(2,1)S(1)}, bf16[8,10752]{1,0:T(8,128)(2,1)S(1)}, u32[]{:S(2)}, u32[]{:S(2)}) collective-permute-start(bf16[8,10752]{1,0:T(8,128)(2,1)S(1)} %collective-permute-done.10.refs_1_), channel_id=1, source_target_pairs={{0,1},{1,0},{2,3},{3,2},{4,5},{5,4},{6,7},{7,6},{8,9},{9,8},{10,11... | collective-permute-start | bytes 516104 | tf_op jit(solution)/shard_map/ppermute | solution.py:292
  32.3 2.2 %collective-permute-start.16 = (bf16[8,10752]{1,0:T(8,128)(2,1)S(1)}, bf16[8,10752]{1,0:T(8,128)(2,1)S(1)}, u32[]{:S(2)}, u32[]{:S(2)}) collective-permute-start(bf16[8,10752]{1,0:T(8,128)(2,1)S(1)} %collective-permute-done.14.refs_5_), channel_id=1, source_target_pairs={{0,1},{1,0},{2,3},{3,2},{4,5},{5,4},{6,7},{7,6},{8,9},{9,8},{10,11... | collective-permute-start | bytes 516104 | tf_op jit(solution)/shard_map/ppermute | solution.py:292
  32.3 4.7 %collective-permute-start.26 = (bf16[8,10752]{1,0:T(8,128)(2,1)S(1)}, bf16[8,10752]{1,0:T(8,128)(2,1)S(1)}, u32[]{:S(2)}, u32[]{:S(2)}) collective-permute-start(bf16[8,10752]{1,0:T(8,128)(2,1)S(1)} %get-tuple-element.50), channel_id=1, source_target_pairs={{0,1},{1,0},{2,3},{3,2},{4,5},{5,4},{6,7},{7,6},{8,9},{9,8},{10,11... | collective-permute-start | bytes 516104 | tf_op jit(solution)/shard_map/ppermute | solution.py:292
  32.9 6.3 %collective-permute-start.27 = (bf16[8,10752]{1,0:T(8,128)(2,1)S(1)}, bf16[8,10752]{1,0:T(8,128)(2,1)S(1)}, u32[]{:S(2)}, u32[]{:S(2)}) collective-permute-start(bf16[8,10752]{1,0:T(8,128)(2,1)S(1)} %shard_map.80.refs_11_), channel_id=1, source_target_pairs={{0,2},{1,3},{2,0},{3,1},{4,6},{5,7},{6,4},{7,5},{8,10},{9,11},{10,... | collective-permute-start | bytes 516104 | tf_op jit(solution)/shard_map/ppermute | solution.py:289
  36.4 22.6 %copy-start = (s32[16,2]{0,1:T(2,128)S(1)}, s32[16,2]{0,1:T(2,128)}, u32[]{:S(2)}) copy-start(s32[16,2]{0,1:T(2,128)} %param.8) | copy-start | bytes 388
  36.4 22.6 %copy-start.1 = (s32[4]{0:T(128)S(1)}, s32[4]{0:T(128)}, u32[]{:S(2)}) copy-start(s32[4]{0:T(128)} %placement_ref.3) | copy-start | bytes 52
  36.4 22.6 %copy-start.2 = (f32[16,2]{0,1:T(2,128)S(1)}, f32[16,2]{0,1:T(2,128)}, u32[]{:S(2)}) copy-start(f32[16,2]{0,1:T(2,128)} %param.9) | copy-start | bytes 388
  36.4 3.5 %collective-permute-start.19 = (bf16[8,10752]{1,0:T(8,128)(2,1)S(1)}, bf16[8,10752]{1,0:T(8,128)(2,1)S(1)}, u32[]{:S(2)}, u32[]{:S(2)}) collective-permute-start(bf16[8,10752]{1,0:T(8,128)(2,1)S(1)} %get-tuple-element.44), channel_id=1, source_target_pairs={{0,1},{1,0},{2,3},{3,2},{4,5},{5,4},{6,7},{7,6},{8,9},{9,8},{10,11... | collective-permute-start | bytes 516104 | tf_op jit(solution)/shard_map/ppermute | solution.py:292
  36.5 5.0 %collective-permute-start.23 = (bf16[8,10752]{1,0:T(8,128)(2,1)S(1)}, bf16[8,10752]{1,0:T(8,128)(2,1)S(1)}, u32[]{:S(2)}, u32[]{:S(2)}) collective-permute-start(bf16[8,10752]{1,0:T(8,128)(2,1)S(1)} %get-tuple-element.48), channel_id=1, source_target_pairs={{0,1},{1,0},{2,3},{3,2},{4,5},{5,4},{6,7},{7,6},{8,9},{9,8},{10,11... | collective-permute-start | bytes 516104 | tf_op jit(solution)/shard_map/ppermute | solution.py:292
  37.0 5.2 %collective-permute-start.8 = (bf16[8,10752]{1,0:T(8,128)(2,1)S(1)}, bf16[8,10752]{1,0:T(8,128)(2,1)S(1)}, u32[]{:S(2)}, u32[]{:S(2)}) collective-permute-start(bf16[8,10752]{1,0:T(8,128)(2,1)S(1)} %get-tuple-element.36), channel_id=1, source_target_pairs={{0,1},{1,0},{2,3},{3,2},{4,5},{5,4},{6,7},{7,6},{8,9},{9,8},{10,11... | collective-permute-start | bytes 516104 | tf_op jit(solution)/shard_map/ppermute | solution.py:292
  39.3 2.3 %collective-permute-start.28 = (bf16[8,2048]{1,0:T(8,128)(2,1)S(1)}, bf16[8,2048]{1,0:T(8,128)(2,1)S(1)}, u32[]{:S(2)}, u32[]{:S(2)}) collective-permute-start(bf16[8,2048]{1,0:T(8,128)(2,1)S(1)} %shard_map.89), channel_id=1, source_target_pairs={{0,1},{1,0},{2,3},{3,2},{4,5},{5,4},{6,7},{7,6},{8,9},{9,8},{10,11... | collective-permute-start | bytes 98312 | tf_op jit(solution)/shard_map/ppermute | solution.py:292
  39.4 2.8 %collective-permute-start.18 = (bf16[8,10752]{1,0:T(8,128)(2,1)S(1)}, bf16[8,10752]{1,0:T(8,128)(2,1)S(1)}, u32[]{:S(2)}, u32[]{:S(2)}) collective-permute-start(bf16[8,10752]{1,0:T(8,128)(2,1)S(1)} %get-tuple-element.42), channel_id=1, source_target_pairs={{0,1},{1,0},{2,3},{3,2},{4,5},{5,4},{6,7},{7,6},{8,9},{9,8},{10,11... | collective-permute-start | bytes 516104 | tf_op jit(solution)/shard_map/ppermute | solution.py:292
  39.9 7.3 %collective-permute-start.20 = (bf16[8,10752]{1,0:T(8,128)(2,1)S(1)}, bf16[8,10752]{1,0:T(8,128)(2,1)S(1)}, u32[]{:S(2)}, u32[]{:S(2)}) collective-permute-start(bf16[8,10752]{1,0:T(8,128)(2,1)S(1)} %shard_map.82), channel_id=1, source_target_pairs={{0,2},{1,3},{2,0},{3,1},{4,6},{5,7},{6,4},{7,5},{8,10},{9,11},{10,... | collective-permute-start | bytes 516104 | tf_op jit(solution)/shard_map/ppermute | solution.py:289
  41.5 6.4 %collective-permute-start.22 = (bf16[8,10752]{1,0:T(8,128)(2,1)S(1)}, bf16[8,10752]{1,0:T(8,128)(2,1)S(1)}, u32[]{:S(2)}, u32[]{:S(2)}) collective-permute-start(bf16[8,10752]{1,0:T(8,128)(2,1)S(1)} %get-tuple-element.46), channel_id=1, source_target_pairs={{0,1},{1,0},{2,3},{3,2},{4,5},{5,4},{6,7},{7,6},{8,9},{9,8},{10,11... | collective-permute-start | bytes 516104 | tf_op jit(solution)/shard_map/ppermute | solution.py:292
  41.6 9.3 %collective-permute-start.24 = (bf16[8,10752]{1,0:T(8,128)(2,1)S(1)}, bf16[8,10752]{1,0:T(8,128)(2,1)S(1)}, u32[]{:S(2)}, u32[]{:S(2)}) collective-permute-start(bf16[8,10752]{1,0:T(8,128)(2,1)S(1)} %shard_map.86), channel_id=1, source_target_pairs={{0,2},{1,3},{2,0},{3,1},{4,6},{5,7},{6,4},{7,5},{8,10},{9,11},{10,... | collective-permute-start | bytes 516104 | tf_op jit(solution)/shard_map/ppermute | solution.py:289
  42.2 12.2 %collective-permute-start.29 = (bf16[8,10752]{1,0:T(8,128)(2,1)S(1)}, bf16[8,10752]{1,0:T(8,128)(2,1)S(1)}, u32[]{:S(2)}, u32[]{:S(2)}) collective-permute-start(bf16[8,10752]{1,0:T(8,128)(2,1)S(1)} %shard_map.90), channel_id=1, source_target_pairs={{0,8},{1,9},{2,10},{3,11},{4,12},{5,13},{6,14},{7,15},{8,0},{9,1},... | collective-permute-start | bytes 516104 | tf_op jit(solution)/shard_map/ppermute | solution.py:286
  42.2 12.2 %collective-permute-start.7 = (bf16[8,10752]{1,0:T(8,128)(2,1)S(1)}, bf16[8,10752]{1,0:T(8,128)(2,1)S(1)}, u32[]{:S(2)}, u32[]{:S(2)}) collective-permute-start(bf16[8,10752]{1,0:T(8,128)(2,1)S(1)} %get-tuple-element.34), channel_id=1, source_target_pairs={{0,1},{1,0},{2,3},{3,2},{4,5},{5,4},{6,7},{7,6},{8,9},{9,8},{10,11... | collective-permute-start | bytes 516104 | tf_op jit(solution)/shard_map/ppermute | solution.py:292
  47.3 8.5 %collective-permute-start.30 = (bf16[8,10752]{1,0:T(8,128)(2,1)S(1)}, bf16[8,10752]{1,0:T(8,128)(2,1)S(1)}, u32[]{:S(2)}, u32[]{:S(2)}) collective-permute-start(bf16[8,10752]{1,0:T(8,128)(2,1)S(1)} %shard_map.83.refs_1_), channel_id=1, source_target_pairs={{0,12},{1,13},{2,14},{3,15},{4,8},{5,9},{6,10},{7,11},{8,4},{9,5},... | collective-permute-start | bytes 516104 | tf_op jit(solution)/shard_map/ppermute | solution.py:286
  47.9 6.6 %collective-permute-start.21 = (bf16[8,10752]{1,0:T(8,128)(2,1)S(1)}, bf16[8,10752]{1,0:T(8,128)(2,1)S(1)}, u32[]{:S(2)}, u32[]{:S(2)}) collective-permute-start(bf16[8,10752]{1,0:T(8,128)(2,1)S(1)} %shard_map.84), channel_id=1, source_target_pairs={{0,2},{1,3},{2,0},{3,1},{4,6},{5,7},{6,4},{7,5},{8,10},{9,11},{10,... | collective-permute-start | bytes 516104 | tf_op jit(solution)/shard_map/ppermute | solution.py:289
  51.0 8.0 %collective-permute-start.25 = (bf16[8,10752]{1,0:T(8,128)(2,1)S(1)}, bf16[8,10752]{1,0:T(8,128)(2,1)S(1)}, u32[]{:S(2)}, u32[]{:S(2)}) collective-permute-start(bf16[8,10752]{1,0:T(8,128)(2,1)S(1)} %shard_map.87), channel_id=1, source_target_pairs={{0,4},{1,5},{2,6},{3,7},{4,0},{5,1},{6,2},{7,3},{8,12},{9,13},{10,... | collective-permute-start | bytes 516104 | tf_op jit(solution)/shard_map/ppermute | solution.py:286
  54.4 4.6 %collective-permute-start.31 = (bf16[8,9088]{1,0:T(8,128)(2,1)S(1)}, bf16[8,9088]{1,0:T(8,128)(2,1)S(1)}, u32[]{:S(2)}, u32[]{:S(2)}) collective-permute-start(bf16[8,9088]{1,0:T(8,128)(2,1)S(1)} %shard_map.91), channel_id=1, source_target_pairs={{0,1},{1,0},{2,3},{3,2},{4,5},{5,4},{6,7},{7,6},{8,9},{9,8},{10,11... | collective-permute-start | bytes 436232 | tf_op jit(solution)/shard_map/ppermute | solution.py:292

commit v14 on v11

--- a/solution.py
+++ b/solution.py
@@ -326,7 +326,7 @@
             compute([0, first], [])
         else:
             previous = groups[g - 1][0]
-            straight[first] = along_z(when(buckets[first], [straight[previous]]), first)
+            straight[first] = along_z(when(buckets[first], [straight[previous], across[0]]), first)
             straight[first] = when(straight[first], [across[second], across[previous]])
             across[first] = along_y(straight[first])
             go_home(previous, [])

time: 60.2 us -> 60.3 us (level)
  waiting for transfers between devices: 19.8 us -> 27.1 us
  starting transfers between devices: 28.2 us -> 21 us
    ppermute x8, waiting for transfers between devices: 9.03 us -> 14.4 us  [along_y(): return lax.ppermute(value, 'node', [(i, i ^ 2) for i in range(devices)])]
    ppermute x8, starting transfers between devices: 11.5 us -> 6.42 us  [along_y(): return lax.ppermute(value, 'node', [(i, i ^ 2) for i in range(devices)])]
    ppermute x6, starting transfers between devices: 12.7 us -> 11 us  [along_z(): return lax.ppermute(value, 'node', pairs)]
    ppermute x6, waiting for transfers between devices: 10.7 us -> 12.4 us  [along_z(): return lax.ppermute(value, 'node', pairs)]
  transfers between devices with their start and end apart: 32 -> 32, of which waited for: 9 -> 13; matrix products, arithmetic and copies ran while one was open for 0% -> 0% of each run, Pallas kernels for 14% -> 14%
where the time goes in v14:
time: 60.3 us; the launch traced here: 60.1 us
  waiting for transfers between devices  27.1 us (45%)
  starting transfers between devices  21 us (35%)
  Pallas kernels  11.7 us (19%)
    ppermute x8, waiting for transfers between devices, along_y(): return lax.ppermute(value, 'node', [(i, i ^ 2) for i in range(devices)])  14.4 us
    ppermute x6, waiting for transfers between devices, along_z(): return lax.ppermute(value, 'node', pairs)  12.4 us
    ppermute x6, starting transfers between devices, along_z(): return lax.ppermute(value, 'node', pairs)  11 us
    ppermute x8, starting transfers between devices, along_y(): return lax.ppermute(value, 'node', [(i, i ^ 2) for i in range(devices)])  6.42 us
    pallas_call x1, Pallas kernels, load(): pl.pallas_call(load_kernel, out_shape=[pltpu.VMEM(w.shape, w.dtype) for w...  4.24 us
    pallas_call x2, Pallas kernels, run_experts(): pl.pallas_call(functools.partial(experts_kernel, count), out_shape=[shape...  3.73 us
    ppermute x18, starting transfers between devices, along_core(): return lax.ppermute(value, 'node', [(i, i ^ 1) for i in range(devices)])  3.54 us
    pallas_call x1, Pallas kernels, mix(): pl.pallas_call(functools.partial(mix_kernel, n_blocks, parts), out_shape=...  1.86 us
  transfers between devices with their start and end apart: 32, of which 13 were waited for; matrix products, arithmetic and copies ran while one was open for 0% of the time, Pallas kernels for 14%

profile of v14, /device:TPU:0, one launch (start us, length us, event | category | flops | bytes accessed | tf_op | source)
XLA Modules:
  0.0 60.1 jit_solution(4174881719552658132)
XLA Ops:
  0.0 1.5 %shard_map.73 = (bf16[8,10752]{1,0:T(8,128)(2,1)S(1)}, bf16[8,10752]{1,0:T(8,128)(2,1)S(1)}, bf16[8,10752]{1,0:T(8,128)(2,1)S(1)}, bf16[8,10752]{1,0:T(8,128)(2,1)S(1)}) custom-call(s32[4]{0:T(128)} %placement_ref.3, s32[2,16]{1,0:T(2,128)} %bitcast.2, bf16[16,7168]{1,0:T(8,128)(2,1)} %tokens_ref.1), custom_call_target="tpu_custom_call" | custom-call | tf_op jit(solution)/shard_map/pallas_call | solution.py:82
  1.5 5.1 %collective-permute-start.3 = (bf16[8,10752]{1,0:T(8,128)(2,1)S(1)}, bf16[8,10752]{1,0:T(8,128)(2,1)S(1)}, u32[]{:S(2)}, u32[]{:S(2)}) collective-permute-start(bf16[8,10752]{1,0:T(8,128)(2,1)S(1)} %get-tuple-element.29), channel_id=1, source_target_pairs={{0,12},{1,13},{2,14},{3,15},{4,8},{5,9},{6,10},{7,11},{8,4},{9,5},... | collective-permute-start | bytes 516104 | tf_op jit(solution)/shard_map/ppermute | solution.py:286
  6.6 1.5 %collective-permute-start = (bf16[8,10752]{1,0:T(8,128)(2,1)S(1)}, bf16[8,10752]{1,0:T(8,128)(2,1)S(1)}, u32[]{:S(2)}, u32[]{:S(2)}) collective-permute-start(bf16[8,10752]{1,0:T(8,128)(2,1)S(1)} %get-tuple-element.28.refs_3_.refs_0_), channel_id=1, source_target_pairs={{0,2},{1,3},{2,0},{3,1},{4,6},{5,7},{6,4},{7,5},{8,10},{9,11},{10,... | collective-permute-start | bytes 516104 | tf_op jit(solution)/shard_map/ppermute | solution.py:289
  8.1 4.2 %shard_map.74 = (bf16[7168,256]{1,0:T(8,128)(2,1)S(1)}, bf16[7168,256]{1,0:T(8,128)(2,1)S(1)}, bf16[256,7168]{1,0:T(8,128)(2,1)S(1)}) custom-call(bf16[7168,256]{1,0:T(8,128)(2,1)} %refs_0_.1, bf16[7168,256]{1,0:T(8,128)(2,1)} %refs_1_.1, bf16[256,7168]{1,0:T(8,128)(2,1)} %refs_2_.1, bf16[8,10752]{1,0:T(8,128)(2,1)S(1)} %get-tuple-element.28.refs_3_.refs_0_), custom_call_target="tpu_custom_call" | custom-call | tf_op jit(solution)/shard_map/pallas_call | solution.py:141
  12.4 0.1 collective-permute-start.9
  12.4 0.0 collective-permute-done.3.refs_4_.refs_1_
  12.4 0.6 collective-permute-start.4
  13.0 0.0 collective-permute-done.refs_1_.refs_2_
  13.0 3.9 %collective-permute-start.13 = (bf16[8,10752]{1,0:T(8,128)(2,1)S(1)}, bf16[8,10752]{1,0:T(8,128)(2,1)S(1)}, u32[]{:S(2)}, u32[]{:S(2)}) collective-permute-start(bf16[8,10752]{1,0:T(8,128)(2,1)S(1)} %shard_map.78), channel_id=1, source_target_pairs={{0,8},{1,9},{2,10},{3,11},{4,12},{5,13},{6,14},{7,15},{8,0},{9,1},... | collective-permute-start | bytes 516104 | tf_op jit(solution)/shard_map/ppermute | solution.py:286
  16.9 2.4 %collective-permute-done.9.refs_0_ = bf16[8,10752]{1,0:T(8,128)(2,1)S(1)} collective-permute-done((bf16[8,10752]{1,0:T(8,128)(2,1)S(1)}, bf16[8,10752]{1,0:T(8,128)(2,1)S(1)}, u32[]{:S(2)}, u32[]{:S(2)}) %collective-permute-start.9) | collective-permute-done | bytes 172064 | tf_op jit(solution)/shard_map/ppermute | solution.py:286
  19.3 0.4 collective-permute-start.10
  19.7 0.0 collective-permute-start.1
  19.7 0.5 collective-permute-start.5
  20.2 0.0 collective-permute-done.4.refs_5_.refs_2_
  20.2 0.0 collective-permute-start.2
  20.2 3.6 %collective-permute-done.13.refs_0_ = bf16[8,10752]{1,0:T(8,128)(2,1)S(1)} collective-permute-done((bf16[8,10752]{1,0:T(8,128)(2,1)S(1)}, bf16[8,10752]{1,0:T(8,128)(2,1)S(1)}, u32[]{:S(2)}, u32[]{:S(2)}) %collective-permute-start.13) | collective-permute-done | bytes 172064 | tf_op jit(solution)/shard_map/ppermute | solution.py:286
  23.8 0.9 %collective-permute-done.10.refs_1_ = bf16[8,10752]{1,0:T(8,128)(2,1)S(1)} collective-permute-done((bf16[8,10752]{1,0:T(8,128)(2,1)S(1)}, bf16[8,10752]{1,0:T(8,128)(2,1)S(1)}, u32[]{:S(2)}, u32[]{:S(2)}) %collective-permute-start.10) | collective-permute-done | bytes 172064 | tf_op jit(solution)/shard_map/ppermute | solution.py:289
  24.7 0.4 collective-permute-start.14
  25.1 0.0 collective-permute-done.1.refs_2_
  25.1 0.0 collective-permute-done.5.refs_6_
  25.1 0.0 collective-permute-done.2.refs_3_
  25.1 0.1 collective-permute-done.6.refs_7_
  25.2 1.9 %shard_map.75 = (bf16[8,10752]{1,0:T(8,128)(2,1)S(1)}, bf16[8,10752]{1,0:T(8,128)(2,1)S(1)}, bf16[8,10752]{1,0:T(8,128)(2,1)S(1)}, bf16[8,10752]{1,0:T(8,128)(2,...) custom-call(bf16[8,10752]{1,0:T(8,128)(2,1)S(1)} %get-tuple-element., ...), custom_call_target="tpu_custom_call" | custom-call | tf_op jit(solution)/shard_map/pallas_call | solution.py:198
  27.1 0.2 collective-permute-start.17
  27.3 0.4 collective-permute-start.11
  27.7 0.1 collective-permute-start.15
  27.8 0.4 collective-permute-start.12
  28.2 2.4 %collective-permute-done.14.refs_5_ = bf16[8,10752]{1,0:T(8,128)(2,1)S(1)} collective-permute-done((bf16[8,10752]{1,0:T(8,128)(2,1)S(1)}, bf16[8,10752]{1,0:T(8,128)(2,1)S(1)}, u32[]{:S(2)}, u32[]{:S(2)}) %collective-permute-start.14) | collective-permute-done | bytes 172064 | tf_op jit(solution)/shard_map/ppermute | solution.py:289
  30.6 0.0 collective-permute-start.16
  30.6 0.0 collective-permute-done.17.refs_1_
  30.6 0.5 collective-permute-start.27
  31.2 0.0 collective-permute-done.11.refs_2_
  31.2 0.7 %collective-permute-start.28 = (bf16[8,10752]{1,0:T(8,128)(2,1)S(1)}, bf16[8,10752]{1,0:T(8,128)(2,1)S(1)}, u32[]{:S(2)}, u32[]{:S(2)}) collective-permute-start(bf16[8,10752]{1,0:T(8,128)(2,1)S(1)} %shard_map.80.refs_11_), channel_id=1, source_target_pairs={{0,2},{1,3},{2,0},{3,1},{4,6},{5,7},{6,4},{7,5},{8,10},{9,11},{10,... | collective-permute-start | bytes 516104 | tf_op jit(solution)/shard_map/ppermute | solution.py:289
  31.9 0.0 collective-permute-done.15.refs_6_
  31.9 0.1 collective-permute-done.16.refs_7_
  32.0 1.9 %shard_map.81 = (bf16[8,10752]{1,0:T(8,128)(2,1)S(1)}, bf16[8,10752]{1,0:T(8,128)(2,1)S(1)}, bf16[8,10752]{1,0:T(8,128)(2,1)S(1)}, bf16[8,10752]{1,0:T(8,128)(2,...) custom-call(bf16[8,10752]{1,0:T(8,128)(2,1)S(1)} %collective-permute, ...), custom_call_target="tpu_custom_call" | custom-call | tf_op jit(solution)/shard_map/pallas_call | solution.py:198
  33.9 0.0 copy-start
  33.9 0.0 copy-start.1
  33.9 0.0 copy-start.2
  33.9 0.2 collective-permute-start.19
  34.1 0.4 collective-permute-start.23
  34.5 0.1 collective-permute-start.8
  34.7 2.9 %collective-permute-done.28.refs_2_ = bf16[8,10752]{1,0:T(8,128)(2,1)S(1)} collective-permute-done((bf16[8,10752]{1,0:T(8,128)(2,1)S(1)}, bf16[8,10752]{1,0:T(8,128)(2,1)S(1)}, u32[]{:S(2)}, u32[]{:S(2)}) %collective-permute-start.28) | collective-permute-done | bytes 172064 | tf_op jit(solution)/shard_map/ppermute | solution.py:289
  37.5 0.1 shard_map.88.refs_0_
  37.6 0.1 collective-permute-start.29
  37.7 0.5 collective-permute-start.18
  38.2 0.7 %collective-permute-start.20 = (bf16[8,10752]{1,0:T(8,128)(2,1)S(1)}, bf16[8,10752]{1,0:T(8,128)(2,1)S(1)}, u32[]{:S(2)}, u32[]{:S(2)}) collective-permute-start(bf16[8,10752]{1,0:T(8,128)(2,1)S(1)} %shard_map.82), channel_id=1, source_target_pairs={{0,2},{1,3},{2,0},{3,1},{4,6},{5,7},{6,4},{7,5},{8,10},{9,11},{10,... | collective-permute-start | bytes 516104 | tf_op jit(solution)/shard_map/ppermute | solution.py:289
  39.0 1.5 %collective-permute-start.24 = (bf16[8,10752]{1,0:T(8,128)(2,1)S(1)}, bf16[8,10752]{1,0:T(8,128)(2,1)S(1)}, u32[]{:S(2)}, u32[]{:S(2)}) collective-permute-start(bf16[8,10752]{1,0:T(8,128)(2,1)S(1)} %shard_map.86), channel_id=1, source_target_pairs={{0,2},{1,3},{2,0},{3,1},{4,6},{5,7},{6,4},{7,5},{8,10},{9,11},{10,... | collective-permute-start | bytes 516104 | tf_op jit(solution)/shard_map/ppermute | solution.py:289
  40.5 1.8 %collective-permute-start.30 = (bf16[8,10752]{1,0:T(8,128)(2,1)S(1)}, bf16[8,10752]{1,0:T(8,128)(2,1)S(1)}, u32[]{:S(2)}, u32[]{:S(2)}) collective-permute-start(bf16[8,10752]{1,0:T(8,128)(2,1)S(1)} %shard_map.90), channel_id=1, source_target_pairs={{0,12},{1,13},{2,14},{3,15},{4,8},{5,9},{6,10},{7,11},{8,4},{9,5},... | collective-permute-start | bytes 516104 | tf_op jit(solution)/shard_map/ppermute | solution.py:286
  42.4 0.1 collective-permute-start.7
  42.5 3.1 %collective-permute-done.20.refs_2_ = bf16[8,10752]{1,0:T(8,128)(2,1)S(1)} collective-permute-done((bf16[8,10752]{1,0:T(8,128)(2,1)S(1)}, bf16[8,10752]{1,0:T(8,128)(2,1)S(1)}, u32[]{:S(2)}, u32[]{:S(2)}) %collective-permute-start.20) | collective-permute-done | bytes 172064 | tf_op jit(solution)/shard_map/ppermute | solution.py:289
  45.5 0.1 shard_map.83.refs_1_
  45.6 0.1 collective-permute-start.26
  45.7 0.7 %collective-permute-start.21 = (bf16[8,10752]{1,0:T(8,128)(2,1)S(1)}, bf16[8,10752]{1,0:T(8,128)(2,1)S(1)}, u32[]{:S(2)}, u32[]{:S(2)}) collective-permute-start(bf16[8,10752]{1,0:T(8,128)(2,1)S(1)} %shard_map.84), channel_id=1, source_target_pairs={{0,2},{1,3},{2,0},{3,1},{4,6},{5,7},{6,4},{7,5},{8,10},{9,11},{10,... | collective-permute-start | bytes 516104 | tf_op jit(solution)/shard_map/ppermute | solution.py:289
  46.4 2.8 %collective-permute-done.24.refs_2_ = bf16[8,10752]{1,0:T(8,128)(2,1)S(1)} collective-permute-done((bf16[8,10752]{1,0:T(8,128)(2,1)S(1)}, bf16[8,10752]{1,0:T(8,128)(2,1)S(1)}, u32[]{:S(2)}, u32[]{:S(2)}) %collective-permute-start.24) | collective-permute-done | bytes 172064 | tf_op jit(solution)/shard_map/ppermute | solution.py:289
  49.2 0.1 shard_map.87
  49.3 0.1 collective-permute-start.25
  49.4 0.2 collective-permute-done.30.refs_0_.refs_3_
  49.6 0.1 collective-permute-start.31
  49.7 2.4 %collective-permute-done.21.refs_2_ = bf16[8,10752]{1,0:T(8,128)(2,1)S(1)} collective-permute-done((bf16[8,10752]{1,0:T(8,128)(2,1)S(1)}, bf16[8,10752]{1,0:T(8,128)(2,1)S(1)}, u32[]{:S(2)}, u32[]{:S(2)}) %collective-permute-start.21) | collective-permute-done | bytes 172064 | tf_op jit(solution)/shard_map/ppermute | solution.py:289
  52.0 0.1 shard_map.85.refs_0_
  52.1 4.5 %collective-permute-done.26.refs_2_ = bf16[8,10752]{1,0:T(8,128)(2,1)S(1)} collective-permute-done((bf16[8,10752]{1,0:T(8,128)(2,1)S(1)}, bf16[8,10752]{1,0:T(8,128)(2,1)S(1)}, u32[]{:S(2)}, u32[]{:S(2)}) %collective-permute-start.26) | collective-permute-done | bytes 172064 | tf_op jit(solution)/shard_map/ppermute | solution.py:286
  56.6 1.6 %collective-permute-done.25.refs_1_ = bf16[8,10752]{1,0:T(8,128)(2,1)S(1)} collective-permute-done((bf16[8,10752]{1,0:T(8,128)(2,1)S(1)}, bf16[8,10752]{1,0:T(8,128)(2,1)S(1)}, u32[]{:S(2)}, u32[]{:S(2)}) %collective-permute-start.25) | collective-permute-done | bytes 172064 | tf_op jit(solution)/shard_map/ppermute | solution.py:286
  58.2 1.9 %shard_map.92 = bf16[16,7168]{1,0:T(8,128)(2,1)} custom-call(s32[4]{0:T(128)S(1)} %copy-done.1, s32[2,16]{1,0:T(2,128)S(1)} %bitcast.3, f32[2,16]{1,0:T(2,128)S(1)} %bitcast.4, bf16[8,10752]{1,0:T(8,128)(2,1)S(1)} %shard_map.85.refs_0_, bf16[8,10752]{1,0:T(8,128)(2,1)S(1)} %collective-permute-done.25.refs_1_, ...), custom_call_target="tpu_custom_call" | custom-call | flops 44040192 | bytes 1146880 | tf_op jit(solution)/shard_map/pallas_call | solution.py:247
  (26 shorter events, 0.2 us)
Async XLA Ops:
  1.5 11.0 %collective-permute-start.3 = (bf16[8,10752]{1,0:T(8,128)(2,1)S(1)}, bf16[8,10752]{1,0:T(8,128)(2,1)S(1)}, u32[]{:S(2)}, u32[]{:S(2)}) collective-permute-start(bf16[8,10752]{1,0:T(8,128)(2,1)S(1)} %get-tuple-element.29), channel_id=1, source_target_pairs={{0,12},{1,13},{2,14},{3,15},{4,8},{5,9},{6,10},{7,11},{8,4},{9,5},... | collective-permute-start | bytes 516104 | tf_op jit(solution)/shard_map/ppermute | solution.py:286
  6.6 6.4 %collective-permute-start = (bf16[8,10752]{1,0:T(8,128)(2,1)S(1)}, bf16[8,10752]{1,0:T(8,128)(2,1)S(1)}, u32[]{:S(2)}, u32[]{:S(2)}) collective-permute-start(bf16[8,10752]{1,0:T(8,128)(2,1)S(1)} %get-tuple-element.28.refs_3_.refs_0_), channel_id=1, source_target_pairs={{0,2},{1,3},{2,0},{3,1},{4,6},{5,7},{6,4},{7,5},{8,10},{9,11},{10,... | collective-permute-start | bytes 516104 | tf_op jit(solution)/shard_map/ppermute | solution.py:289
  12.4 7.0 %collective-permute-start.9 = (bf16[8,10752]{1,0:T(8,128)(2,1)S(1)}, bf16[8,10752]{1,0:T(8,128)(2,1)S(1)}, u32[]{:S(2)}, u32[]{:S(2)}) collective-permute-start(bf16[8,10752]{1,0:T(8,128)(2,1)S(1)} %shard_map.77), channel_id=1, source_target_pairs={{0,4},{1,5},{2,6},{3,7},{4,0},{5,1},{6,2},{7,3},{8,12},{9,13},{10,... | collective-permute-start | bytes 516104 | tf_op jit(solution)/shard_map/ppermute | solution.py:286
  12.4 7.8 %collective-permute-start.4 = (bf16[8,10752]{1,0:T(8,128)(2,1)S(1)}, bf16[8,10752]{1,0:T(8,128)(2,1)S(1)}, u32[]{:S(2)}, u32[]{:S(2)}) collective-permute-start(bf16[8,10752]{1,0:T(8,128)(2,1)S(1)} %collective-permute-done.3.refs_4_.refs_1_), channel_id=1, source_target_pairs={{0,2},{1,3},{2,0},{3,1},{4,6},{5,7},{6,4},{7,5},{8,10},{9,11},{10,... | collective-permute-start | bytes 516104 | tf_op jit(solution)/shard_map/ppermute | solution.py:289
  13.0 10.8 %collective-permute-start.13 = (bf16[8,10752]{1,0:T(8,128)(2,1)S(1)}, bf16[8,10752]{1,0:T(8,128)(2,1)S(1)}, u32[]{:S(2)}, u32[]{:S(2)}) collective-permute-start(bf16[8,10752]{1,0:T(8,128)(2,1)S(1)} %shard_map.78), channel_id=1, source_target_pairs={{0,8},{1,9},{2,10},{3,11},{4,12},{5,13},{6,14},{7,15},{8,0},{9,1},... | collective-permute-start | bytes 516104 | tf_op jit(solution)/shard_map/ppermute | solution.py:286
  19.3 5.4 %collective-permute-start.10 = (bf16[8,10752]{1,0:T(8,128)(2,1)S(1)}, bf16[8,10752]{1,0:T(8,128)(2,1)S(1)}, u32[]{:S(2)}, u32[]{:S(2)}) collective-permute-start(bf16[8,10752]{1,0:T(8,128)(2,1)S(1)} %collective-permute-done.9.refs_0_), channel_id=1, source_target_pairs={{0,2},{1,3},{2,0},{3,1},{4,6},{5,7},{6,4},{7,5},{8,10},{9,11},{10,... | collective-permute-start | bytes 516104 | tf_op jit(solution)/shard_map/ppermute | solution.py:289
  19.7 5.4 %collective-permute-start.1 = (bf16[8,10752]{1,0:T(8,128)(2,1)S(1)}, bf16[8,10752]{1,0:T(8,128)(2,1)S(1)}, u32[]{:S(2)}, u32[]{:S(2)}) collective-permute-start(bf16[8,10752]{1,0:T(8,128)(2,1)S(1)} %get-tuple-element.28.refs_3_.refs_0_), channel_id=1, source_target_pairs={{0,1},{1,0},{2,3},{3,2},{4,5},{5,4},{6,7},{7,6},{8,9},{9,8},{10,11... | collective-permute-start | bytes 516104 | tf_op jit(solution)/shard_map/ppermute | solution.py:292
  19.7 5.4 %collective-permute-start.5 = (bf16[8,10752]{1,0:T(8,128)(2,1)S(1)}, bf16[8,10752]{1,0:T(8,128)(2,1)S(1)}, u32[]{:S(2)}, u32[]{:S(2)}) collective-permute-start(bf16[8,10752]{1,0:T(8,128)(2,1)S(1)} %collective-permute-done.3.refs_4_.refs_1_), channel_id=1, source_target_pairs={{0,1},{1,0},{2,3},{3,2},{4,5},{5,4},{6,7},{7,6},{8,9},{9,8},{10,11... | collective-permute-start | bytes 516104 | tf_op jit(solution)/shard_map/ppermute | solution.py:292
  20.2 4.9 %collective-permute-start.2 = (bf16[8,10752]{1,0:T(8,128)(2,1)S(1)}, bf16[8,10752]{1,0:T(8,128)(2,1)S(1)}, u32[]{:S(2)}, u32[]{:S(2)}) collective-permute-start(bf16[8,10752]{1,0:T(8,128)(2,1)S(1)} %collective-permute-done.refs_1_.refs_2_), channel_id=1, source_target_pairs={{0,1},{1,0},{2,3},{3,2},{4,5},{5,4},{6,7},{7,6},{8,9},{9,8},{10,11... | collective-permute-start | bytes 516104 | tf_op jit(solution)/shard_map/ppermute | solution.py:292
  23.8 1.4 %collective-permute-start.6 = (bf16[8,10752]{1,0:T(8,128)(2,1)S(1)}, bf16[8,10752]{1,0:T(8,128)(2,1)S(1)}, u32[]{:S(2)}, u32[]{:S(2)}) collective-permute-start(bf16[8,10752]{1,0:T(8,128)(2,1)S(1)} %collective-permute-done.4.refs_5_.refs_2_), channel_id=1, source_target_pairs={{0,1},{1,0},{2,3},{3,2},{4,5},{5,4},{6,7},{7,6},{8,9},{9,8},{10,11... | collective-permute-start | bytes 516104 | tf_op jit(solution)/shard_map/ppermute | solution.py:292
  24.7 5.9 %collective-permute-start.14 = (bf16[8,10752]{1,0:T(8,128)(2,1)S(1)}, bf16[8,10752]{1,0:T(8,128)(2,1)S(1)}, u32[]{:S(2)}, u32[]{:S(2)}) collective-permute-start(bf16[8,10752]{1,0:T(8,128)(2,1)S(1)} %shard_map.79.refs_4_), channel_id=1, source_target_pairs={{0,2},{1,3},{2,0},{3,1},{4,6},{5,7},{6,4},{7,5},{8,10},{9,11},{10,... | collective-permute-start | bytes 516104 | tf_op jit(solution)/shard_map/ppermute | solution.py:289
  27.1 3.5 %collective-permute-start.17 = (bf16[8,10752]{1,0:T(8,128)(2,1)S(1)}, bf16[8,10752]{1,0:T(8,128)(2,1)S(1)}, u32[]{:S(2)}, u32[]{:S(2)}) collective-permute-start(bf16[8,10752]{1,0:T(8,128)(2,1)S(1)} %get-tuple-element.40), channel_id=1, source_target_pairs={{0,1},{1,0},{2,3},{3,2},{4,5},{5,4},{6,7},{7,6},{8,9},{9,8},{10,11... | collective-permute-start | bytes 516104 | tf_op jit(solution)/shard_map/ppermute | solution.py:292
  27.3 3.9 %collective-permute-start.11 = (bf16[8,10752]{1,0:T(8,128)(2,1)S(1)}, bf16[8,10752]{1,0:T(8,128)(2,1)S(1)}, u32[]{:S(2)}, u32[]{:S(2)}) collective-permute-start(bf16[8,10752]{1,0:T(8,128)(2,1)S(1)} %collective-permute-done.9.refs_0_), channel_id=1, source_target_pairs={{0,1},{1,0},{2,3},{3,2},{4,5},{5,4},{6,7},{7,6},{8,9},{9,8},{10,11... | collective-permute-start | bytes 516104 | tf_op jit(solution)/shard_map/ppermute | solution.py:292
  27.7 4.2 %collective-permute-start.15 = (bf16[8,10752]{1,0:T(8,128)(2,1)S(1)}, bf16[8,10752]{1,0:T(8,128)(2,1)S(1)}, u32[]{:S(2)}, u32[]{:S(2)}) collective-permute-start(bf16[8,10752]{1,0:T(8,128)(2,1)S(1)} %shard_map.79.refs_4_), channel_id=1, source_target_pairs={{0,1},{1,0},{2,3},{3,2},{4,5},{5,4},{6,7},{7,6},{8,9},{9,8},{10,11... | collective-permute-start | bytes 516104 | tf_op jit(solution)/shard_map/ppermute | solution.py:292
  27.8 4.1 %collective-permute-start.12 = (bf16[8,10752]{1,0:T(8,128)(2,1)S(1)}, bf16[8,10752]{1,0:T(8,128)(2,1)S(1)}, u32[]{:S(2)}, u32[]{:S(2)}) collective-permute-start(bf16[8,10752]{1,0:T(8,128)(2,1)S(1)} %collective-permute-done.10.refs_1_), channel_id=1, source_target_pairs={{0,1},{1,0},{2,3},{3,2},{4,5},{5,4},{6,7},{7,6},{8,9},{9,8},{10,11... | collective-permute-start | bytes 516104 | tf_op jit(solution)/shard_map/ppermute | solution.py:292
  30.6 1.4 %collective-permute-start.16 = (bf16[8,10752]{1,0:T(8,128)(2,1)S(1)}, bf16[8,10752]{1,0:T(8,128)(2,1)S(1)}, u32[]{:S(2)}, u32[]{:S(2)}) collective-permute-start(bf16[8,10752]{1,0:T(8,128)(2,1)S(1)} %collective-permute-done.14.refs_5_), channel_id=1, source_target_pairs={{0,1},{1,0},{2,3},{3,2},{4,5},{5,4},{6,7},{7,6},{8,9},{9,8},{10,11... | collective-permute-start | bytes 516104 | tf_op jit(solution)/shard_map/ppermute | solution.py:292
  30.6 4.0 %collective-permute-start.27 = (bf16[8,10752]{1,0:T(8,128)(2,1)S(1)}, bf16[8,10752]{1,0:T(8,128)(2,1)S(1)}, u32[]{:S(2)}, u32[]{:S(2)}) collective-permute-start(bf16[8,10752]{1,0:T(8,128)(2,1)S(1)} %get-tuple-element.50), channel_id=1, source_target_pairs={{0,1},{1,0},{2,3},{3,2},{4,5},{5,4},{6,7},{7,6},{8,9},{9,8},{10,11... | collective-permute-start | bytes 516104 | tf_op jit(solution)/shard_map/ppermute | solution.py:292
  31.2 6.3 %collective-permute-start.28 = (bf16[8,10752]{1,0:T(8,128)(2,1)S(1)}, bf16[8,10752]{1,0:T(8,128)(2,1)S(1)}, u32[]{:S(2)}, u32[]{:S(2)}) collective-permute-start(bf16[8,10752]{1,0:T(8,128)(2,1)S(1)} %shard_map.80.refs_11_), channel_id=1, source_target_pairs={{0,2},{1,3},{2,0},{3,1},{4,6},{5,7},{6,4},{7,5},{8,10},{9,11},{10,... | collective-permute-start | bytes 516104 | tf_op jit(solution)/shard_map/ppermute | solution.py:289
  33.9 24.3 %copy-start = (s32[16,2]{0,1:T(2,128)S(1)}, s32[16,2]{0,1:T(2,128)}, u32[]{:S(2)}) copy-start(s32[16,2]{0,1:T(2,128)} %param.8) | copy-start | bytes 388
  33.9 24.3 %copy-start.1 = (s32[4]{0:T(128)S(1)}, s32[4]{0:T(128)}, u32[]{:S(2)}) copy-start(s32[4]{0:T(128)} %placement_ref.3) | copy-start | bytes 52
  33.9 24.3 %copy-start.2 = (f32[16,2]{0,1:T(2,128)S(1)}, f32[16,2]{0,1:T(2,128)}, u32[]{:S(2)}) copy-start(f32[16,2]{0,1:T(2,128)} %param.9) | copy-start | bytes 388
  33.9 4.3 %collective-permute-start.19 = (bf16[8,10752]{1,0:T(8,128)(2,1)S(1)}, bf16[8,10752]{1,0:T(8,128)(2,1)S(1)}, u32[]{:S(2)}, u32[]{:S(2)}) collective-permute-start(bf16[8,10752]{1,0:T(8,128)(2,1)S(1)} %get-tuple-element.44), channel_id=1, source_target_pairs={{0,1},{1,0},{2,3},{3,2},{4,5},{5,4},{6,7},{7,6},{8,9},{9,8},{10,11... | collective-permute-start | bytes 516104 | tf_op jit(solution)/shard_map/ppermute | solution.py:292
  34.1 4.8 %collective-permute-start.23 = (bf16[8,10752]{1,0:T(8,128)(2,1)S(1)}, bf16[8,10752]{1,0:T(8,128)(2,1)S(1)}, u32[]{:S(2)}, u32[]{:S(2)}) collective-permute-start(bf16[8,10752]{1,0:T(8,128)(2,1)S(1)} %get-tuple-element.48), channel_id=1, source_target_pairs={{0,1},{1,0},{2,3},{3,2},{4,5},{5,4},{6,7},{7,6},{8,9},{9,8},{10,11... | collective-permute-start | bytes 516104 | tf_op jit(solution)/shard_map/ppermute | solution.py:292
  34.5 6.0 %collective-permute-start.8 = (bf16[8,10752]{1,0:T(8,128)(2,1)S(1)}, bf16[8,10752]{1,0:T(8,128)(2,1)S(1)}, u32[]{:S(2)}, u32[]{:S(2)}) collective-permute-start(bf16[8,10752]{1,0:T(8,128)(2,1)S(1)} %get-tuple-element.36), channel_id=1, source_target_pairs={{0,1},{1,0},{2,3},{3,2},{4,5},{5,4},{6,7},{7,6},{8,9},{9,8},{10,11... | collective-permute-start | bytes 516104 | tf_op jit(solution)/shard_map/ppermute | solution.py:292
  37.6 1.4 %collective-permute-start.29 = (bf16[8,2048]{1,0:T(8,128)(2,1)S(1)}, bf16[8,2048]{1,0:T(8,128)(2,1)S(1)}, u32[]{:S(2)}, u32[]{:S(2)}) collective-permute-start(bf16[8,2048]{1,0:T(8,128)(2,1)S(1)} %shard_map.89), channel_id=1, source_target_pairs={{0,1},{1,0},{2,3},{3,2},{4,5},{5,4},{6,7},{7,6},{8,9},{9,8},{10,11... | collective-permute-start | bytes 98312 | tf_op jit(solution)/shard_map/ppermute | solution.py:292
  37.7 4.7 %collective-permute-start.18 = (bf16[8,10752]{1,0:T(8,128)(2,1)S(1)}, bf16[8,10752]{1,0:T(8,128)(2,1)S(1)}, u32[]{:S(2)}, u32[]{:S(2)}) collective-permute-start(bf16[8,10752]{1,0:T(8,128)(2,1)S(1)} %get-tuple-element.42), channel_id=1, source_target_pairs={{0,1},{1,0},{2,3},{3,2},{4,5},{5,4},{6,7},{7,6},{8,9},{9,8},{10,11... | collective-permute-start | bytes 516104 | tf_op jit(solution)/shard_map/ppermute | solution.py:292
  38.2 7.3 %collective-permute-start.20 = (bf16[8,10752]{1,0:T(8,128)(2,1)S(1)}, bf16[8,10752]{1,0:T(8,128)(2,1)S(1)}, u32[]{:S(2)}, u32[]{:S(2)}) collective-permute-start(bf16[8,10752]{1,0:T(8,128)(2,1)S(1)} %shard_map.82), channel_id=1, source_target_pairs={{0,2},{1,3},{2,0},{3,1},{4,6},{5,7},{6,4},{7,5},{8,10},{9,11},{10,... | collective-permute-start | bytes 516104 | tf_op jit(solution)/shard_map/ppermute | solution.py:289
  38.9 6.8 %collective-permute-start.22 = (bf16[8,10752]{1,0:T(8,128)(2,1)S(1)}, bf16[8,10752]{1,0:T(8,128)(2,1)S(1)}, u32[]{:S(2)}, u32[]{:S(2)}) collective-permute-start(bf16[8,10752]{1,0:T(8,128)(2,1)S(1)} %get-tuple-element.46), channel_id=1, source_target_pairs={{0,1},{1,0},{2,3},{3,2},{4,5},{5,4},{6,7},{7,6},{8,9},{9,8},{10,11... | collective-permute-start | bytes 516104 | tf_op jit(solution)/shard_map/ppermute | solution.py:292
  39.0 10.2 %collective-permute-start.24 = (bf16[8,10752]{1,0:T(8,128)(2,1)S(1)}, bf16[8,10752]{1,0:T(8,128)(2,1)S(1)}, u32[]{:S(2)}, u32[]{:S(2)}) collective-permute-start(bf16[8,10752]{1,0:T(8,128)(2,1)S(1)} %shard_map.86), channel_id=1, source_target_pairs={{0,2},{1,3},{2,0},{3,1},{4,6},{5,7},{6,4},{7,5},{8,10},{9,11},{10,... | collective-permute-start | bytes 516104 | tf_op jit(solution)/shard_map/ppermute | solution.py:289
  40.5 9.1 %collective-permute-start.30 = (bf16[8,10752]{1,0:T(8,128)(2,1)S(1)}, bf16[8,10752]{1,0:T(8,128)(2,1)S(1)}, u32[]{:S(2)}, u32[]{:S(2)}) collective-permute-start(bf16[8,10752]{1,0:T(8,128)(2,1)S(1)} %shard_map.90), channel_id=1, source_target_pairs={{0,12},{1,13},{2,14},{3,15},{4,8},{5,9},{6,10},{7,11},{8,4},{9,5},... | collective-permute-start | bytes 516104 | tf_op jit(solution)/shard_map/ppermute | solution.py:286
  42.4 7.3 %collective-permute-start.7 = (bf16[8,10752]{1,0:T(8,128)(2,1)S(1)}, bf16[8,10752]{1,0:T(8,128)(2,1)S(1)}, u32[]{:S(2)}, u32[]{:S(2)}) collective-permute-start(bf16[8,10752]{1,0:T(8,128)(2,1)S(1)} %get-tuple-element.34), channel_id=1, source_target_pairs={{0,1},{1,0},{2,3},{3,2},{4,5},{5,4},{6,7},{7,6},{8,9},{9,8},{10,11... | collective-permute-start | bytes 516104 | tf_op jit(solution)/shard_map/ppermute | solution.py:292
  45.6 11.0 %collective-permute-start.26 = (bf16[8,10752]{1,0:T(8,128)(2,1)S(1)}, bf16[8,10752]{1,0:T(8,128)(2,1)S(1)}, u32[]{:S(2)}, u32[]{:S(2)}) collective-permute-start(bf16[8,10752]{1,0:T(8,128)(2,1)S(1)} %shard_map.83.refs_1_), channel_id=1, source_target_pairs={{0,8},{1,9},{2,10},{3,11},{4,12},{5,13},{6,14},{7,15},{8,0},{9,1},... | collective-permute-start | bytes 516104 | tf_op jit(solution)/shard_map/ppermute | solution.py:286
  45.7 6.3 %collective-permute-start.21 = (bf16[8,10752]{1,0:T(8,128)(2,1)S(1)}, bf16[8,10752]{1,0:T(8,128)(2,1)S(1)}, u32[]{:S(2)}, u32[]{:S(2)}) collective-permute-start(bf16[8,10752]{1,0:T(8,128)(2,1)S(1)} %shard_map.84), channel_id=1, source_target_pairs={{0,2},{1,3},{2,0},{3,1},{4,6},{5,7},{6,4},{7,5},{8,10},{9,11},{10,... | collective-permute-start | bytes 516104 | tf_op jit(solution)/shard_map/ppermute | solution.py:289
  49.3 8.9 %collective-permute-start.25 = (bf16[8,10752]{1,0:T(8,128)(2,1)S(1)}, bf16[8,10752]{1,0:T(8,128)(2,1)S(1)}, u32[]{:S(2)}, u32[]{:S(2)}) collective-permute-start(bf16[8,10752]{1,0:T(8,128)(2,1)S(1)} %shard_map.87), channel_id=1, source_target_pairs={{0,4},{1,5},{2,6},{3,7},{4,0},{5,1},{6,2},{7,3},{8,12},{9,13},{10,... | collective-permute-start | bytes 516104 | tf_op jit(solution)/shard_map/ppermute | solution.py:286
  49.6 8.6 %collective-permute-start.31 = (bf16[8,9088]{1,0:T(8,128)(2,1)S(1)}, bf16[8,9088]{1,0:T(8,128)(2,1)S(1)}, u32[]{:S(2)}, u32[]{:S(2)}) collective-permute-start(bf16[8,9088]{1,0:T(8,128)(2,1)S(1)} %shard_map.91), channel_id=1, source_target_pairs={{0,1},{1,0},{2,3},{3,2},{4,5},{5,4},{6,7},{7,6},{8,9},{9,8},{10,11... | collective-permute-start | bytes 436232 | tf_op jit(solution)/shard_map/ppermute | solution.py:292

commit v15 on v11

--- a/solution.py
+++ b/solution.py
@@ -206,7 +206,7 @@
 
 
 def mix_kernel(n_blocks, parts, placement_ref, ids_ref, gates_ref, *refs):
-    results, out_ref = refs[:n_blocks], refs[-1]
+    results, (out_hbm, out_ref, sems) = refs[:n_blocks], refs[-3:]
     rows, width = out_ref.shape
     half, quarter, middle = rows // 2, rows // 4, width // 2
     block = lax.axis_index("node") // parts
@@ -222,6 +222,7 @@
         terms.append(jnp.where(named & (slot == wanted), weight, 0.0))
     term = jnp.concatenate(terms, axis=0)
     row = lax.broadcasted_iota(jnp.int32, term.shape, 0) % rows
+    copies = []
     for side in range(2):
         first = half + side * quarter
         mine = jnp.where((row < half) | ((row >= first) & (row < first + quarter)), term, 0.0)
@@ -239,6 +240,14 @@
         )
         value = value[:rows] + value[rows : 2 * rows] + value[2 * rows :]
         out_ref[:, side * middle : (side + 1) * middle] = value.astype(jnp.bfloat16)
+        half_columns = pl.ds(side * middle, middle)
+        copy = pltpu.make_async_copy(
+            out_ref.at[:, half_columns], out_hbm.at[:, half_columns], sems.at[side]
+        )
+        copy.start()
+        copies.append(copy)
+    for copy in copies:
+        copy.wait()
 
 
 def mix(placement, ids, gates, results, after, n_blocks, parts):
@@ -248,7 +257,8 @@
         functools.partial(mix_kernel, n_blocks, parts),
         out_shape=jax.ShapeDtypeStruct((rows, width), jnp.bfloat16),
         in_specs=[SMEM] + [VMEM] * (2 + n_blocks) + [ANYWHERE] * len(after),
-        out_specs=VMEM,
+        out_specs=pl.BlockSpec(memory_space=pltpu.HBM),
+        scratch_shapes=[pltpu.VMEM((rows, width), jnp.bfloat16), pltpu.SemaphoreType.DMA((2,))],
         compiler_params=pltpu.CompilerParams(vmem_limit_bytes=VMEM_BYTES),
         cost_estimate=pl.CostEstimate(
             flops=6 * n_blocks * rows * rows * width,

time: 60.2 us -> 60.1 us (level)
  no operation moved by 1% of the time
where the time goes in v15:
time: 60.1 us; the launch traced here: 60 us
  starting transfers between devices  28.2 us (47%)
  waiting for transfers between devices  19.8 us (33%)
  Pallas kernels  11.7 us (19%)
    ppermute x6, starting transfers between devices, along_z(): return lax.ppermute(value, 'node', pairs)  12.7 us
    ppermute x8, starting transfers between devices, along_y(): return lax.ppermute(value, 'node', [(i, i ^ 2) for i in range(devices)])  11.5 us
    ppermute x6, waiting for transfers between devices, along_z(): return lax.ppermute(value, 'node', pairs)  10.7 us
    ppermute x8, waiting for transfers between devices, along_y(): return lax.ppermute(value, 'node', [(i, i ^ 2) for i in range(devices)])  9.03 us
    pallas_call x1, Pallas kernels, load(): pl.pallas_call(load_kernel, out_shape=[pltpu.VMEM(w.shape, w.dtype) for w...  4.24 us
    ppermute x18, starting transfers between devices, along_core(): return lax.ppermute(value, 'node', [(i, i ^ 1) for i in range(devices)])  3.97 us
    pallas_call x2, Pallas kernels, run_experts(): pl.pallas_call(functools.partial(experts_kernel, count), out_shape=[shape...  3.77 us
    pallas_call x1, Pallas kernels, mix(): pl.pallas_call(functools.partial(mix_kernel, n_blocks, parts), out_shape=...  1.83 us
  transfers between devices with their start and end apart: 32, of which 9 were waited for; matrix products, arithmetic and copies ran while one was open for 0% of the time, Pallas kernels for 14%

profile of v15, /device:TPU:0, one launch (start us, length us, event | category | flops | bytes accessed | tf_op | source)
XLA Modules:
  0.0 60.0 jit_solution(7706862443051401608)
XLA Ops:
  0.0 1.5 %shard_map.73 = (bf16[8,10752]{1,0:T(8,128)(2,1)S(1)}, bf16[8,10752]{1,0:T(8,128)(2,1)S(1)}, bf16[8,10752]{1,0:T(8,128)(2,1)S(1)}, bf16[8,10752]{1,0:T(8,128)(2,1)S(1)}) custom-call(s32[4]{0:T(128)} %placement_ref.3, s32[2,16]{1,0:T(2,128)} %bitcast.2, bf16[16,7168]{1,0:T(8,128)(2,1)} %tokens_ref.1), custom_call_target="tpu_custom_call" | custom-call | tf_op jit(solution)/shard_map/pallas_call | solution.py:82
  1.5 5.1 %collective-permute-start.3 = (bf16[8,10752]{1,0:T(8,128)(2,1)S(1)}, bf16[8,10752]{1,0:T(8,128)(2,1)S(1)}, u32[]{:S(2)}, u32[]{:S(2)}) collective-permute-start(bf16[8,10752]{1,0:T(8,128)(2,1)S(1)} %get-tuple-element.29), channel_id=1, source_target_pairs={{0,12},{1,13},{2,14},{3,15},{4,8},{5,9},{6,10},{7,11},{8,4},{9,5},... | collective-permute-start | bytes 516104 | tf_op jit(solution)/shard_map/ppermute | solution.py:296
  6.6 4.2 %shard_map.74 = (bf16[7168,256]{1,0:T(8,128)(2,1)S(1)}, bf16[7168,256]{1,0:T(8,128)(2,1)S(1)}, bf16[256,7168]{1,0:T(8,128)(2,1)S(1)}) custom-call(bf16[7168,256]{1,0:T(8,128)(2,1)} %refs_0_.1, bf16[7168,256]{1,0:T(8,128)(2,1)} %refs_1_.1, bf16[256,7168]{1,0:T(8,128)(2,1)} %refs_2_.1, bf16[8,10752]{1,0:T(8,128)(2,1)S(1)} %get-tuple-element.28.refs_3_.refs_0_), custom_call_target="tpu_custom_call" | custom-call | tf_op jit(solution)/shard_map/pallas_call | solution.py:141
  10.8 0.1 collective-permute-start.9
  10.9 1.6 %collective-permute-start = (bf16[8,10752]{1,0:T(8,128)(2,1)S(1)}, bf16[8,10752]{1,0:T(8,128)(2,1)S(1)}, u32[]{:S(2)}, u32[]{:S(2)}) collective-permute-start(bf16[8,10752]{1,0:T(8,128)(2,1)S(1)} %get-tuple-element.28.refs_3_.refs_0_), channel_id=1, source_target_pairs={{0,2},{1,3},{2,0},{3,1},{4,6},{5,7},{6,4},{7,5},{8,10},{9,11},{10,... | collective-permute-start | bytes 516104 | tf_op jit(solution)/shard_map/ppermute | solution.py:299
  12.5 2.9 %collective-permute-start.13 = (bf16[8,10752]{1,0:T(8,128)(2,1)S(1)}, bf16[8,10752]{1,0:T(8,128)(2,1)S(1)}, u32[]{:S(2)}, u32[]{:S(2)}) collective-permute-start(bf16[8,10752]{1,0:T(8,128)(2,1)S(1)} %shard_map.78), channel_id=1, source_target_pairs={{0,8},{1,9},{2,10},{3,11},{4,12},{5,13},{6,14},{7,15},{8,0},{9,1},... | collective-permute-start | bytes 516104 | tf_op jit(solution)/shard_map/ppermute | solution.py:296
  15.4 1.5 %collective-permute-start.4 = (bf16[8,10752]{1,0:T(8,128)(2,1)S(1)}, bf16[8,10752]{1,0:T(8,128)(2,1)S(1)}, u32[]{:S(2)}, u32[]{:S(2)}) collective-permute-start(bf16[8,10752]{1,0:T(8,128)(2,1)S(1)} %collective-permute-done.3.refs_4_.refs_1_), channel_id=1, source_target_pairs={{0,2},{1,3},{2,0},{3,1},{4,6},{5,7},{6,4},{7,5},{8,10},{9,11},{10,... | collective-permute-start | bytes 516104 | tf_op jit(solution)/shard_map/ppermute | solution.py:299
  16.9 1.1 %collective-permute-done.9.refs_0_ = bf16[8,10752]{1,0:T(8,128)(2,1)S(1)} collective-permute-done((bf16[8,10752]{1,0:T(8,128)(2,1)S(1)}, bf16[8,10752]{1,0:T(8,128)(2,1)S(1)}, u32[]{:S(2)}, u32[]{:S(2)}) %collective-permute-start.9) | collective-permute-done | bytes 172064 | tf_op jit(solution)/shard_map/ppermute | solution.py:296
  17.9 1.7 %collective-permute-start.10 = (bf16[8,10752]{1,0:T(8,128)(2,1)S(1)}, bf16[8,10752]{1,0:T(8,128)(2,1)S(1)}, u32[]{:S(2)}, u32[]{:S(2)}) collective-permute-start(bf16[8,10752]{1,0:T(8,128)(2,1)S(1)} %collective-permute-done.9.refs_0_), channel_id=1, source_target_pairs={{0,2},{1,3},{2,0},{3,1},{4,6},{5,7},{6,4},{7,5},{8,10},{9,11},{10,... | collective-permute-start | bytes 516104 | tf_op jit(solution)/shard_map/ppermute | solution.py:299
  19.6 0.0 collective-permute-start.1
  19.6 0.0 collective-permute-done.refs_1_
  19.6 0.5 collective-permute-start.5
  20.1 2.6 %collective-permute-done.13.refs_0_ = bf16[8,10752]{1,0:T(8,128)(2,1)S(1)} collective-permute-done((bf16[8,10752]{1,0:T(8,128)(2,1)S(1)}, bf16[8,10752]{1,0:T(8,128)(2,1)S(1)}, u32[]{:S(2)}, u32[]{:S(2)}) %collective-permute-start.13) | collective-permute-done | bytes 172064 | tf_op jit(solution)/shard_map/ppermute | solution.py:296
  22.7 0.5 collective-permute-start.6
  23.2 1.0 %collective-permute-done.10.refs_1_ = bf16[8,10752]{1,0:T(8,128)(2,1)S(1)} collective-permute-done((bf16[8,10752]{1,0:T(8,128)(2,1)S(1)}, bf16[8,10752]{1,0:T(8,128)(2,1)S(1)}, u32[]{:S(2)}, u32[]{:S(2)}) %collective-permute-start.10) | collective-permute-done | bytes 172064 | tf_op jit(solution)/shard_map/ppermute | solution.py:299
  24.2 1.5 %collective-permute-start.14 = (bf16[8,10752]{1,0:T(8,128)(2,1)S(1)}, bf16[8,10752]{1,0:T(8,128)(2,1)S(1)}, u32[]{:S(2)}, u32[]{:S(2)}) collective-permute-start(bf16[8,10752]{1,0:T(8,128)(2,1)S(1)} %shard_map.79.refs_4_), channel_id=1, source_target_pairs={{0,2},{1,3},{2,0},{3,1},{4,6},{5,7},{6,4},{7,5},{8,10},{9,11},{10,... | collective-permute-start | bytes 516104 | tf_op jit(solution)/shard_map/ppermute | solution.py:299
  25.7 0.0 collective-permute-done.1.refs_2_
  25.7 0.0 collective-permute-done.5.refs_6_
  25.7 0.0 collective-permute-done.2.refs_3_
  25.7 1.9 %shard_map.75 = (bf16[8,10752]{1,0:T(8,128)(2,1)S(1)}, bf16[8,10752]{1,0:T(8,128)(2,1)S(1)}, bf16[8,10752]{1,0:T(8,128)(2,1)S(1)}, bf16[8,10752]{1,0:T(8,128)(2,...) custom-call(bf16[8,10752]{1,0:T(8,128)(2,1)S(1)} %get-tuple-element., ...), custom_call_target="tpu_custom_call" | custom-call | tf_op jit(solution)/shard_map/pallas_call | solution.py:198
  27.6 0.1 collective-permute-start.17
  27.7 0.5 collective-permute-start.11
  28.2 0.1 collective-permute-start.15
  28.3 0.4 collective-permute-start.12
  28.7 0.9 %collective-permute-done.14.refs_5_ = bf16[8,10752]{1,0:T(8,128)(2,1)S(1)} collective-permute-done((bf16[8,10752]{1,0:T(8,128)(2,1)S(1)}, bf16[8,10752]{1,0:T(8,128)(2,1)S(1)}, u32[]{:S(2)}, u32[]{:S(2)}) %collective-permute-start.14) | collective-permute-done | bytes 172064 | tf_op jit(solution)/shard_map/ppermute | solution.py:299
  29.6 0.5 collective-permute-start.27
  30.2 1.6 %collective-permute-start.28 = (bf16[8,10752]{1,0:T(8,128)(2,1)S(1)}, bf16[8,10752]{1,0:T(8,128)(2,1)S(1)}, u32[]{:S(2)}, u32[]{:S(2)}) collective-permute-start(bf16[8,10752]{1,0:T(8,128)(2,1)S(1)} %shard_map.80.refs_11_), channel_id=1, source_target_pairs={{0,2},{1,3},{2,0},{3,1},{4,6},{5,7},{6,4},{7,5},{8,10},{9,11},{10,... | collective-permute-start | bytes 516104 | tf_op jit(solution)/shard_map/ppermute | solution.py:299
  31.8 0.0 collective-permute-done.15.refs_6_
  31.8 0.0 collective-permute-done.12.refs_3_
  31.8 0.0 collective-permute-done.16.refs_7_
  31.8 1.9 %shard_map.81 = (bf16[8,10752]{1,0:T(8,128)(2,1)S(1)}, bf16[8,10752]{1,0:T(8,128)(2,1)S(1)}, bf16[8,10752]{1,0:T(8,128)(2,1)S(1)}, bf16[8,10752]{1,0:T(8,128)(2,...) custom-call(bf16[8,10752]{1,0:T(8,128)(2,1)S(1)} %collective-permute, ...), custom_call_target="tpu_custom_call" | custom-call | tf_op jit(solution)/shard_map/pallas_call | solution.py:198
  33.7 0.0 copy-start
  33.7 0.0 copy-start.1
  33.7 0.0 copy-start.2
  33.7 0.1 collective-permute-start.19
  33.8 0.5 collective-permute-start.23
  34.3 0.1 collective-permute-start.8
  34.3 0.0 collective-permute-done.27.refs_1_
  34.3 2.2 %collective-permute-done.28.refs_2_ = bf16[8,10752]{1,0:T(8,128)(2,1)S(1)} collective-permute-done((bf16[8,10752]{1,0:T(8,128)(2,1)S(1)}, bf16[8,10752]{1,0:T(8,128)(2,1)S(1)}, u32[]{:S(2)}, u32[]{:S(2)}) %collective-permute-start.28) | collective-permute-done | bytes 172064 | tf_op jit(solution)/shard_map/ppermute | solution.py:299
  36.5 0.1 shard_map.88.refs_0_
  36.6 0.1 collective-permute-start.29
  36.7 0.5 collective-permute-start.18
  37.2 0.0 collective-permute-done.19.refs_1_
  37.2 1.6 %collective-permute-start.20 = (bf16[8,10752]{1,0:T(8,128)(2,1)S(1)}, bf16[8,10752]{1,0:T(8,128)(2,1)S(1)}, u32[]{:S(2)}, u32[]{:S(2)}) collective-permute-start(bf16[8,10752]{1,0:T(8,128)(2,1)S(1)} %shard_map.82), channel_id=1, source_target_pairs={{0,2},{1,3},{2,0},{3,1},{4,6},{5,7},{6,4},{7,5},{8,10},{9,11},{10,... | collective-permute-start | bytes 516104 | tf_op jit(solution)/shard_map/ppermute | solution.py:299
  38.8 0.0 collective-permute-done.23.refs_1_
  38.8 0.0 collective-permute-start.22
  38.9 0.0 collective-permute-done.29.refs_1_
  38.9 0.6 collective-permute-start.24
  39.4 0.0 collective-permute-done.8.refs_1_
  39.4 2.3 %collective-permute-start.30 = (bf16[8,10752]{1,0:T(8,128)(2,1)S(1)}, bf16[8,10752]{1,0:T(8,128)(2,1)S(1)}, u32[]{:S(2)}, u32[]{:S(2)}) collective-permute-start(bf16[8,10752]{1,0:T(8,128)(2,1)S(1)} %shard_map.90), channel_id=1, source_target_pairs={{0,12},{1,13},{2,14},{3,15},{4,8},{5,9},{6,10},{7,11},{8,4},{9,5},... | collective-permute-start | bytes 516104 | tf_op jit(solution)/shard_map/ppermute | solution.py:296
  41.8 0.1 collective-permute-start.7
  41.9 2.7 %collective-permute-done.20.refs_2_ = bf16[8,10752]{1,0:T(8,128)(2,1)S(1)} collective-permute-done((bf16[8,10752]{1,0:T(8,128)(2,1)S(1)}, bf16[8,10752]{1,0:T(8,128)(2,1)S(1)}, u32[]{:S(2)}, u32[]{:S(2)}) %collective-permute-start.20) | collective-permute-done | bytes 172064 | tf_op jit(solution)/shard_map/ppermute | solution.py:299
  44.5 0.1 shard_map.83.refs_1_
  44.6 0.8 %collective-permute-start.26 = (bf16[8,10752]{1,0:T(8,128)(2,1)S(1)}, bf16[8,10752]{1,0:T(8,128)(2,1)S(1)}, u32[]{:S(2)}, u32[]{:S(2)}) collective-permute-start(bf16[8,10752]{1,0:T(8,128)(2,1)S(1)} %shard_map.83.refs_1_), channel_id=1, source_target_pairs={{0,8},{1,9},{2,10},{3,11},{4,12},{5,13},{6,14},{7,15},{8,0},{9,1},... | collective-permute-start | bytes 516104 | tf_op jit(solution)/shard_map/ppermute | solution.py:296
  45.4 0.0 collective-permute-done.22.refs_1_
  45.4 1.5 %collective-permute-start.21 = (bf16[8,10752]{1,0:T(8,128)(2,1)S(1)}, bf16[8,10752]{1,0:T(8,128)(2,1)S(1)}, u32[]{:S(2)}, u32[]{:S(2)}) collective-permute-start(bf16[8,10752]{1,0:T(8,128)(2,1)S(1)} %shard_map.84), channel_id=1, source_target_pairs={{0,2},{1,3},{2,0},{3,1},{4,6},{5,7},{6,4},{7,5},{8,10},{9,11},{10,... | collective-permute-start | bytes 516104 | tf_op jit(solution)/shard_map/ppermute | solution.py:299
  46.9 1.3 %collective-permute-done.24.refs_2_ = bf16[8,10752]{1,0:T(8,128)(2,1)S(1)} collective-permute-done((bf16[8,10752]{1,0:T(8,128)(2,1)S(1)}, bf16[8,10752]{1,0:T(8,128)(2,1)S(1)}, u32[]{:S(2)}, u32[]{:S(2)}) %collective-permute-start.24) | collective-permute-done | bytes 172064 | tf_op jit(solution)/shard_map/ppermute | solution.py:299
  48.2 0.1 shard_map.87
  48.3 1.6 %collective-permute-start.25 = (bf16[8,10752]{1,0:T(8,128)(2,1)S(1)}, bf16[8,10752]{1,0:T(8,128)(2,1)S(1)}, u32[]{:S(2)}, u32[]{:S(2)}) collective-permute-start(bf16[8,10752]{1,0:T(8,128)(2,1)S(1)} %shard_map.87), channel_id=1, source_target_pairs={{0,4},{1,5},{2,6},{3,7},{4,0},{5,1},{6,2},{7,3},{8,12},{9,13},{10,... | collective-permute-start | bytes 516104 | tf_op jit(solution)/shard_map/ppermute | solution.py:296
  49.9 0.1 collective-permute-start.31
  50.0 1.0 %collective-permute-done.21.refs_2_ = bf16[8,10752]{1,0:T(8,128)(2,1)S(1)} collective-permute-done((bf16[8,10752]{1,0:T(8,128)(2,1)S(1)}, bf16[8,10752]{1,0:T(8,128)(2,1)S(1)}, u32[]{:S(2)}, u32[]{:S(2)}) %collective-permute-start.21) | collective-permute-done | bytes 172064 | tf_op jit(solution)/shard_map/ppermute | solution.py:299
  51.0 0.1 shard_map.85.refs_0_
  51.1 7.0 %collective-permute-done.26.refs_2_ = bf16[8,10752]{1,0:T(8,128)(2,1)S(1)} collective-permute-done((bf16[8,10752]{1,0:T(8,128)(2,1)S(1)}, bf16[8,10752]{1,0:T(8,128)(2,1)S(1)}, u32[]{:S(2)}, u32[]{:S(2)}) %collective-permute-start.26) | collective-permute-done | bytes 172064 | tf_op jit(solution)/shard_map/ppermute | solution.py:296
  58.1 1.8 %shard_map.92 = bf16[16,7168]{1,0:T(8,128)(2,1)} custom-call(s32[4]{0:T(128)S(1)} %copy-done.1, s32[2,16]{1,0:T(2,128)S(1)} %bitcast.3, f32[2,16]{1,0:T(2,128)S(1)} %bitcast.4, bf16[8,10752]{1,0:T(8,128)(2,1)S(1)} %shard_map.85.refs_0_, bf16[8,10752]{1,0:T(8,128)(2,1)S(1)} %collective-permute-done.25.refs_1_, ...), custom_call_target="tpu_custom_call" | custom-call | flops 44040192 | bytes 1146880 | tf_op jit(solution)/shard_map/pallas_call | solution.py:256
  (26 shorter events, 0.2 us)
Async XLA Ops:
  1.5 11.0 %collective-permute-start.3 = (bf16[8,10752]{1,0:T(8,128)(2,1)S(1)}, bf16[8,10752]{1,0:T(8,128)(2,1)S(1)}, u32[]{:S(2)}, u32[]{:S(2)}) collective-permute-start(bf16[8,10752]{1,0:T(8,128)(2,1)S(1)} %get-tuple-element.29), channel_id=1, source_target_pairs={{0,12},{1,13},{2,14},{3,15},{4,8},{5,9},{6,10},{7,11},{8,4},{9,5},... | collective-permute-start | bytes 516104 | tf_op jit(solution)/shard_map/ppermute | solution.py:296
  10.8 7.1 %collective-permute-start.9 = (bf16[8,10752]{1,0:T(8,128)(2,1)S(1)}, bf16[8,10752]{1,0:T(8,128)(2,1)S(1)}, u32[]{:S(2)}, u32[]{:S(2)}) collective-permute-start(bf16[8,10752]{1,0:T(8,128)(2,1)S(1)} %shard_map.77), channel_id=1, source_target_pairs={{0,4},{1,5},{2,6},{3,7},{4,0},{5,1},{6,2},{7,3},{8,12},{9,13},{10,... | collective-permute-start | bytes 516104 | tf_op jit(solution)/shard_map/ppermute | solution.py:296
  10.9 8.7 %collective-permute-start = (bf16[8,10752]{1,0:T(8,128)(2,1)S(1)}, bf16[8,10752]{1,0:T(8,128)(2,1)S(1)}, u32[]{:S(2)}, u32[]{:S(2)}) collective-permute-start(bf16[8,10752]{1,0:T(8,128)(2,1)S(1)} %get-tuple-element.28.refs_3_.refs_0_), channel_id=1, source_target_pairs={{0,2},{1,3},{2,0},{3,1},{4,6},{5,7},{6,4},{7,5},{8,10},{9,11},{10,... | collective-permute-start | bytes 516104 | tf_op jit(solution)/shard_map/ppermute | solution.py:299
  12.5 10.2 %collective-permute-start.13 = (bf16[8,10752]{1,0:T(8,128)(2,1)S(1)}, bf16[8,10752]{1,0:T(8,128)(2,1)S(1)}, u32[]{:S(2)}, u32[]{:S(2)}) collective-permute-start(bf16[8,10752]{1,0:T(8,128)(2,1)S(1)} %shard_map.78), channel_id=1, source_target_pairs={{0,8},{1,9},{2,10},{3,11},{4,12},{5,13},{6,14},{7,15},{8,0},{9,1},... | collective-permute-start | bytes 516104 | tf_op jit(solution)/shard_map/ppermute | solution.py:296
  15.4 7.3 %collective-permute-start.4 = (bf16[8,10752]{1,0:T(8,128)(2,1)S(1)}, bf16[8,10752]{1,0:T(8,128)(2,1)S(1)}, u32[]{:S(2)}, u32[]{:S(2)}) collective-permute-start(bf16[8,10752]{1,0:T(8,128)(2,1)S(1)} %collective-permute-done.3.refs_4_.refs_1_), channel_id=1, source_target_pairs={{0,2},{1,3},{2,0},{3,1},{4,6},{5,7},{6,4},{7,5},{8,10},{9,11},{10,... | collective-permute-start | bytes 516104 | tf_op jit(solution)/shard_map/ppermute | solution.py:299
  17.9 6.2 %collective-permute-start.10 = (bf16[8,10752]{1,0:T(8,128)(2,1)S(1)}, bf16[8,10752]{1,0:T(8,128)(2,1)S(1)}, u32[]{:S(2)}, u32[]{:S(2)}) collective-permute-start(bf16[8,10752]{1,0:T(8,128)(2,1)S(1)} %collective-permute-done.9.refs_0_), channel_id=1, source_target_pairs={{0,2},{1,3},{2,0},{3,1},{4,6},{5,7},{6,4},{7,5},{8,10},{9,11},{10,... | collective-permute-start | bytes 516104 | tf_op jit(solution)/shard_map/ppermute | solution.py:299
  19.6 6.1 %collective-permute-start.1 = (bf16[8,10752]{1,0:T(8,128)(2,1)S(1)}, bf16[8,10752]{1,0:T(8,128)(2,1)S(1)}, u32[]{:S(2)}, u32[]{:S(2)}) collective-permute-start(bf16[8,10752]{1,0:T(8,128)(2,1)S(1)} %get-tuple-element.28.refs_3_.refs_0_), channel_id=1, source_target_pairs={{0,1},{1,0},{2,3},{3,2},{4,5},{5,4},{6,7},{7,6},{8,9},{9,8},{10,11... | collective-permute-start | bytes 516104 | tf_op jit(solution)/shard_map/ppermute | solution.py:302
  19.6 6.1 %collective-permute-start.5 = (bf16[8,10752]{1,0:T(8,128)(2,1)S(1)}, bf16[8,10752]{1,0:T(8,128)(2,1)S(1)}, u32[]{:S(2)}, u32[]{:S(2)}) collective-permute-start(bf16[8,10752]{1,0:T(8,128)(2,1)S(1)} %collective-permute-done.3.refs_4_.refs_1_), channel_id=1, source_target_pairs={{0,1},{1,0},{2,3},{3,2},{4,5},{5,4},{6,7},{7,6},{8,9},{9,8},{10,11... | collective-permute-start | bytes 516104 | tf_op jit(solution)/shard_map/ppermute | solution.py:302
  22.7 3.0 %collective-permute-start.2 = (bf16[8,10752]{1,0:T(8,128)(2,1)S(1)}, bf16[8,10752]{1,0:T(8,128)(2,1)S(1)}, u32[]{:S(2)}, u32[]{:S(2)}) collective-permute-start(bf16[8,10752]{1,0:T(8,128)(2,1)S(1)} %collective-permute-done.refs_1_), channel_id=1, source_target_pairs={{0,1},{1,0},{2,3},{3,2},{4,5},{5,4},{6,7},{7,6},{8,9},{9,8},{10,11... | collective-permute-start | bytes 516104 | tf_op jit(solution)/shard_map/ppermute | solution.py:302
  22.7 3.0 %collective-permute-start.6 = (bf16[8,10752]{1,0:T(8,128)(2,1)S(1)}, bf16[8,10752]{1,0:T(8,128)(2,1)S(1)}, u32[]{:S(2)}, u32[]{:S(2)}) collective-permute-start(bf16[8,10752]{1,0:T(8,128)(2,1)S(1)} %collective-permute-done.4.refs_5_.refs_2_), channel_id=1, source_target_pairs={{0,1},{1,0},{2,3},{3,2},{4,5},{5,4},{6,7},{7,6},{8,9},{9,8},{10,11... | collective-permute-start | bytes 516104 | tf_op jit(solution)/shard_map/ppermute | solution.py:302
  24.2 5.4 %collective-permute-start.14 = (bf16[8,10752]{1,0:T(8,128)(2,1)S(1)}, bf16[8,10752]{1,0:T(8,128)(2,1)S(1)}, u32[]{:S(2)}, u32[]{:S(2)}) collective-permute-start(bf16[8,10752]{1,0:T(8,128)(2,1)S(1)} %shard_map.79.refs_4_), channel_id=1, source_target_pairs={{0,2},{1,3},{2,0},{3,1},{4,6},{5,7},{6,4},{7,5},{8,10},{9,11},{10,... | collective-permute-start | bytes 516104 | tf_op jit(solution)/shard_map/ppermute | solution.py:299
  27.6 2.0 %collective-permute-start.17 = (bf16[8,10752]{1,0:T(8,128)(2,1)S(1)}, bf16[8,10752]{1,0:T(8,128)(2,1)S(1)}, u32[]{:S(2)}, u32[]{:S(2)}) collective-permute-start(bf16[8,10752]{1,0:T(8,128)(2,1)S(1)} %get-tuple-element.40), channel_id=1, source_target_pairs={{0,1},{1,0},{2,3},{3,2},{4,5},{5,4},{6,7},{7,6},{8,9},{9,8},{10,11... | collective-permute-start | bytes 516104 | tf_op jit(solution)/shard_map/ppermute | solution.py:302
  27.7 2.5 %collective-permute-start.11 = (bf16[8,10752]{1,0:T(8,128)(2,1)S(1)}, bf16[8,10752]{1,0:T(8,128)(2,1)S(1)}, u32[]{:S(2)}, u32[]{:S(2)}) collective-permute-start(bf16[8,10752]{1,0:T(8,128)(2,1)S(1)} %collective-permute-done.9.refs_0_), channel_id=1, source_target_pairs={{0,1},{1,0},{2,3},{3,2},{4,5},{5,4},{6,7},{7,6},{8,9},{9,8},{10,11... | collective-permute-start | bytes 516104 | tf_op jit(solution)/shard_map/ppermute | solution.py:302
  28.2 3.6 %collective-permute-start.15 = (bf16[8,10752]{1,0:T(8,128)(2,1)S(1)}, bf16[8,10752]{1,0:T(8,128)(2,1)S(1)}, u32[]{:S(2)}, u32[]{:S(2)}) collective-permute-start(bf16[8,10752]{1,0:T(8,128)(2,1)S(1)} %shard_map.79.refs_4_), channel_id=1, source_target_pairs={{0,1},{1,0},{2,3},{3,2},{4,5},{5,4},{6,7},{7,6},{8,9},{9,8},{10,11... | collective-permute-start | bytes 516104 | tf_op jit(solution)/shard_map/ppermute | solution.py:302
  28.3 3.5 %collective-permute-start.12 = (bf16[8,10752]{1,0:T(8,128)(2,1)S(1)}, bf16[8,10752]{1,0:T(8,128)(2,1)S(1)}, u32[]{:S(2)}, u32[]{:S(2)}) collective-permute-start(bf16[8,10752]{1,0:T(8,128)(2,1)S(1)} %collective-permute-done.10.refs_1_), channel_id=1, source_target_pairs={{0,1},{1,0},{2,3},{3,2},{4,5},{5,4},{6,7},{7,6},{8,9},{9,8},{10,11... | collective-permute-start | bytes 516104 | tf_op jit(solution)/shard_map/ppermute | solution.py:302
  29.6 2.2 %collective-permute-start.16 = (bf16[8,10752]{1,0:T(8,128)(2,1)S(1)}, bf16[8,10752]{1,0:T(8,128)(2,1)S(1)}, u32[]{:S(2)}, u32[]{:S(2)}) collective-permute-start(bf16[8,10752]{1,0:T(8,128)(2,1)S(1)} %collective-permute-done.14.refs_5_), channel_id=1, source_target_pairs={{0,1},{1,0},{2,3},{3,2},{4,5},{5,4},{6,7},{7,6},{8,9},{9,8},{10,11... | collective-permute-start | bytes 516104 | tf_op jit(solution)/shard_map/ppermute | solution.py:302
  29.6 4.7 %collective-permute-start.27 = (bf16[8,10752]{1,0:T(8,128)(2,1)S(1)}, bf16[8,10752]{1,0:T(8,128)(2,1)S(1)}, u32[]{:S(2)}, u32[]{:S(2)}) collective-permute-start(bf16[8,10752]{1,0:T(8,128)(2,1)S(1)} %get-tuple-element.50), channel_id=1, source_target_pairs={{0,1},{1,0},{2,3},{3,2},{4,5},{5,4},{6,7},{7,6},{8,9},{9,8},{10,11... | collective-permute-start | bytes 516104 | tf_op jit(solution)/shard_map/ppermute | solution.py:302
  30.2 6.3 %collective-permute-start.28 = (bf16[8,10752]{1,0:T(8,128)(2,1)S(1)}, bf16[8,10752]{1,0:T(8,128)(2,1)S(1)}, u32[]{:S(2)}, u32[]{:S(2)}) collective-permute-start(bf16[8,10752]{1,0:T(8,128)(2,1)S(1)} %shard_map.80.refs_11_), channel_id=1, source_target_pairs={{0,2},{1,3},{2,0},{3,1},{4,6},{5,7},{6,4},{7,5},{8,10},{9,11},{10,... | collective-permute-start | bytes 516104 | tf_op jit(solution)/shard_map/ppermute | solution.py:299
  33.7 24.5 %copy-start = (s32[16,2]{0,1:T(2,128)S(1)}, s32[16,2]{0,1:T(2,128)}, u32[]{:S(2)}) copy-start(s32[16,2]{0,1:T(2,128)} %param.8) | copy-start | bytes 388
  33.7 24.5 %copy-start.1 = (s32[4]{0:T(128)S(1)}, s32[4]{0:T(128)}, u32[]{:S(2)}) copy-start(s32[4]{0:T(128)} %placement_ref.3) | copy-start | bytes 52
  33.7 24.5 %copy-start.2 = (f32[16,2]{0,1:T(2,128)S(1)}, f32[16,2]{0,1:T(2,128)}, u32[]{:S(2)}) copy-start(f32[16,2]{0,1:T(2,128)} %param.9) | copy-start | bytes 388
  33.7 3.5 %collective-permute-start.19 = (bf16[8,10752]{1,0:T(8,128)(2,1)S(1)}, bf16[8,10752]{1,0:T(8,128)(2,1)S(1)}, u32[]{:S(2)}, u32[]{:S(2)}) collective-permute-start(bf16[8,10752]{1,0:T(8,128)(2,1)S(1)} %get-tuple-element.44), channel_id=1, source_target_pairs={{0,1},{1,0},{2,3},{3,2},{4,5},{5,4},{6,7},{7,6},{8,9},{9,8},{10,11... | collective-permute-start | bytes 516104 | tf_op jit(solution)/shard_map/ppermute | solution.py:302
  33.8 5.0 %collective-permute-start.23 = (bf16[8,10752]{1,0:T(8,128)(2,1)S(1)}, bf16[8,10752]{1,0:T(8,128)(2,1)S(1)}, u32[]{:S(2)}, u32[]{:S(2)}) collective-permute-start(bf16[8,10752]{1,0:T(8,128)(2,1)S(1)} %get-tuple-element.48), channel_id=1, source_target_pairs={{0,1},{1,0},{2,3},{3,2},{4,5},{5,4},{6,7},{7,6},{8,9},{9,8},{10,11... | collective-permute-start | bytes 516104 | tf_op jit(solution)/shard_map/ppermute | solution.py:302
  34.3 5.2 %collective-permute-start.8 = (bf16[8,10752]{1,0:T(8,128)(2,1)S(1)}, bf16[8,10752]{1,0:T(8,128)(2,1)S(1)}, u32[]{:S(2)}, u32[]{:S(2)}) collective-permute-start(bf16[8,10752]{1,0:T(8,128)(2,1)S(1)} %get-tuple-element.36), channel_id=1, source_target_pairs={{0,1},{1,0},{2,3},{3,2},{4,5},{5,4},{6,7},{7,6},{8,9},{9,8},{10,11... | collective-permute-start | bytes 516104 | tf_op jit(solution)/shard_map/ppermute | solution.py:302
  36.6 2.3 %collective-permute-start.29 = (bf16[8,2048]{1,0:T(8,128)(2,1)S(1)}, bf16[8,2048]{1,0:T(8,128)(2,1)S(1)}, u32[]{:S(2)}, u32[]{:S(2)}) collective-permute-start(bf16[8,2048]{1,0:T(8,128)(2,1)S(1)} %shard_map.89), channel_id=1, source_target_pairs={{0,1},{1,0},{2,3},{3,2},{4,5},{5,4},{6,7},{7,6},{8,9},{9,8},{10,11... | collective-permute-start | bytes 98312 | tf_op jit(solution)/shard_map/ppermute | solution.py:302
  36.7 5.1 %collective-permute-start.18 = (bf16[8,10752]{1,0:T(8,128)(2,1)S(1)}, bf16[8,10752]{1,0:T(8,128)(2,1)S(1)}, u32[]{:S(2)}, u32[]{:S(2)}) collective-permute-start(bf16[8,10752]{1,0:T(8,128)(2,1)S(1)} %get-tuple-element.42), channel_id=1, source_target_pairs={{0,1},{1,0},{2,3},{3,2},{4,5},{5,4},{6,7},{7,6},{8,9},{9,8},{10,11... | collective-permute-start | bytes 516104 | tf_op jit(solution)/shard_map/ppermute | solution.py:302
  37.2 7.3 %collective-permute-start.20 = (bf16[8,10752]{1,0:T(8,128)(2,1)S(1)}, bf16[8,10752]{1,0:T(8,128)(2,1)S(1)}, u32[]{:S(2)}, u32[]{:S(2)}) collective-permute-start(bf16[8,10752]{1,0:T(8,128)(2,1)S(1)} %shard_map.82), channel_id=1, source_target_pairs={{0,2},{1,3},{2,0},{3,1},{4,6},{5,7},{6,4},{7,5},{8,10},{9,11},{10,... | collective-permute-start | bytes 516104 | tf_op jit(solution)/shard_map/ppermute | solution.py:299
  38.8 6.6 %collective-permute-start.22 = (bf16[8,10752]{1,0:T(8,128)(2,1)S(1)}, bf16[8,10752]{1,0:T(8,128)(2,1)S(1)}, u32[]{:S(2)}, u32[]{:S(2)}) collective-permute-start(bf16[8,10752]{1,0:T(8,128)(2,1)S(1)} %get-tuple-element.46), channel_id=1, source_target_pairs={{0,1},{1,0},{2,3},{3,2},{4,5},{5,4},{6,7},{7,6},{8,9},{9,8},{10,11... | collective-permute-start | bytes 516104 | tf_op jit(solution)/shard_map/ppermute | solution.py:302
  38.9 9.3 %collective-permute-start.24 = (bf16[8,10752]{1,0:T(8,128)(2,1)S(1)}, bf16[8,10752]{1,0:T(8,128)(2,1)S(1)}, u32[]{:S(2)}, u32[]{:S(2)}) collective-permute-start(bf16[8,10752]{1,0:T(8,128)(2,1)S(1)} %shard_map.86), channel_id=1, source_target_pairs={{0,2},{1,3},{2,0},{3,1},{4,6},{5,7},{6,4},{7,5},{8,10},{9,11},{10,... | collective-permute-start | bytes 516104 | tf_op jit(solution)/shard_map/ppermute | solution.py:299
  39.4 10.5 %collective-permute-start.30 = (bf16[8,10752]{1,0:T(8,128)(2,1)S(1)}, bf16[8,10752]{1,0:T(8,128)(2,1)S(1)}, u32[]{:S(2)}, u32[]{:S(2)}) collective-permute-start(bf16[8,10752]{1,0:T(8,128)(2,1)S(1)} %shard_map.90), channel_id=1, source_target_pairs={{0,12},{1,13},{2,14},{3,15},{4,8},{5,9},{6,10},{7,11},{8,4},{9,5},... | collective-permute-start | bytes 516104 | tf_op jit(solution)/shard_map/ppermute | solution.py:296
  41.8 8.2 %collective-permute-start.7 = (bf16[8,10752]{1,0:T(8,128)(2,1)S(1)}, bf16[8,10752]{1,0:T(8,128)(2,1)S(1)}, u32[]{:S(2)}, u32[]{:S(2)}) collective-permute-start(bf16[8,10752]{1,0:T(8,128)(2,1)S(1)} %get-tuple-element.34), channel_id=1, source_target_pairs={{0,1},{1,0},{2,3},{3,2},{4,5},{5,4},{6,7},{7,6},{8,9},{9,8},{10,11... | collective-permute-start | bytes 516104 | tf_op jit(solution)/shard_map/ppermute | solution.py:302
  44.6 13.5 %collective-permute-start.26 = (bf16[8,10752]{1,0:T(8,128)(2,1)S(1)}, bf16[8,10752]{1,0:T(8,128)(2,1)S(1)}, u32[]{:S(2)}, u32[]{:S(2)}) collective-permute-start(bf16[8,10752]{1,0:T(8,128)(2,1)S(1)} %shard_map.83.refs_1_), channel_id=1, source_target_pairs={{0,8},{1,9},{2,10},{3,11},{4,12},{5,13},{6,14},{7,15},{8,0},{9,1},... | collective-permute-start | bytes 516104 | tf_op jit(solution)/shard_map/ppermute | solution.py:296
  45.4 5.6 %collective-permute-start.21 = (bf16[8,10752]{1,0:T(8,128)(2,1)S(1)}, bf16[8,10752]{1,0:T(8,128)(2,1)S(1)}, u32[]{:S(2)}, u32[]{:S(2)}) collective-permute-start(bf16[8,10752]{1,0:T(8,128)(2,1)S(1)} %shard_map.84), channel_id=1, source_target_pairs={{0,2},{1,3},{2,0},{3,1},{4,6},{5,7},{6,4},{7,5},{8,10},{9,11},{10,... | collective-permute-start | bytes 516104 | tf_op jit(solution)/shard_map/ppermute | solution.py:299
  48.3 9.8 %collective-permute-start.25 = (bf16[8,10752]{1,0:T(8,128)(2,1)S(1)}, bf16[8,10752]{1,0:T(8,128)(2,1)S(1)}, u32[]{:S(2)}, u32[]{:S(2)}) collective-permute-start(bf16[8,10752]{1,0:T(8,128)(2,1)S(1)} %shard_map.87), channel_id=1, source_target_pairs={{0,4},{1,5},{2,6},{3,7},{4,0},{5,1},{6,2},{7,3},{8,12},{9,13},{10,... | collective-permute-start | bytes 516104 | tf_op jit(solution)/shard_map/ppermute | solution.py:296
  49.9 8.2 %collective-permute-start.31 = (bf16[8,9088]{1,0:T(8,128)(2,1)S(1)}, bf16[8,9088]{1,0:T(8,128)(2,1)S(1)}, u32[]{:S(2)}, u32[]{:S(2)}) collective-permute-start(bf16[8,9088]{1,0:T(8,128)(2,1)S(1)} %shard_map.91), channel_id=1, source_target_pairs={{0,1},{1,0},{2,3},{3,2},{4,5},{5,4},{6,7},{7,6},{8,9},{9,8},{10,11... | collective-permute-start | bytes 436232 | tf_op jit(solution)/shard_map/ppermute | solution.py:302
